TPU v7x, 512 devices: a whole 4x8x8 slice. The times are simulated.
512 devices in a mesh: group: 4 (over x_lo, core), dp: 8 (over y), tensor: 16 (over z, x_hi).
Axes of the slice: x: 4 (x_hi: 2, x_lo: 2; x = x_hi * 2 + x_lo), y: 8, z: 8, core: 2. Of those that a mesh axis runs over, the one named last changes fastest.
Arguments:
- activations: bfloat16 [24576, 5120], P(('group', 'dp'), 'tensor'), may hold values from -6 to 6
- norm_gain: float32 [5120], replicated, may hold values from 0.5 to 1.5
- master_weight: float32 [5120, 16, 3, 128], P(('group', 'dp'), 'tensor'), may hold values from -0.078125 to 0.078125
- grad: bfloat16 [5120, 16, 3, 128], P(('group', 'dp'), 'tensor'), may hold values from -12 to 12
- moment: float32 [5120, 16, 3, 128], P(('group', 'dp'), 'tensor'), may hold values from -0.0024414062 to 0.0024414062
- variance: float32 [5120, 16, 3, 128], P(('group', 'dp'), 'tensor'), may hold values from 1.5894572e-09 to 6.357829e-08
- query_gain: float32 [32, 128], P('tensor'), may hold values from 1 to 2.5
- key_gain: float32 [8, 128], replicated, may hold values from 1 to 2.5
- prompt_len: int32 [32], P(('group', 'dp')), may hold values from 192 to 768, as said below
Outputs:
- attended: bfloat16 [24576, 4096], P(('group', 'dp'), 'tensor')
Inputs may be any that keep to these rules, and one draw needn't show every extreme that they name: `prompt_len`: some sequence is full.
All inputs are finite; a program needn't handle non-finite values.
Results may differ from a plain program's by a relative error of at most 0.012.
The roundings to bfloat16 on the way count: a program that leaves them out, or rounds other values in their place, can miss the bound.
Values may be sent and summed in bfloat16 or wider, within the bound.
No kernel may reach another device: no remote copies, remote signals or barrier semaphores. Data moves between devices by JAX's collectives and lax.ppermute only.
A program may use at most 64 MiB of HBM per device.

v0:
```python
import jax
import jax.numpy as jnp
from jax import lax
from jax.sharding import PartitionSpec as P

STEP_SCALE = 0.5
BETA_ONE = 0.9
BETA_TWO = 0.95
ROPE_BASE = 500000.0


def from_partner(array, axis, distance):
    return lax.ppermute(array, axis, [(i, i ^ 1 << distance) for i in range(lax.axis_size(axis))])


def rope_tables(length, head_size):
    positions = jnp.arange(length, dtype=jnp.float32)
    exponent = jnp.arange(head_size // 2, dtype=jnp.float32) * 2.0 / head_size
    inverse = jnp.power(ROPE_BASE, -exponent)
    angles = positions[:, None] * inverse[None, :]
    return (jnp.cos(angles), jnp.sin(angles))


def rotate(inputs, cosine, sine):
    midpoint = inputs.shape[-1] // 2
    front_half = inputs[..., :midpoint]
    back_half = inputs[..., midpoint:]
    return jnp.concatenate(
        [front_half * cosine - back_half * sine, back_half * cosine + front_half * sine], axis=-1
    )


def rms_scaled(inputs, gains):
    return inputs * lax.rsqrt(jnp.mean(inputs * inputs, axis=-1, keepdims=True) + 1e-06) * gains


def shards(
    activations, norm_gain, master_weight, grad, moment, variance, query_gain, key_gain, prompt_len
):
    width_all = norm_gain.shape[0]
    grad_local = grad.astype(jnp.float32)
    sumsq = lax.psum(jnp.sum(grad_local * grad_local), ("group", "dp", "tensor"))
    clip_factor = 1.0 / jnp.sqrt(sumsq + 1e-12)
    clipped = grad_local * clip_factor
    moment_new = BETA_ONE * moment + (1.0 - BETA_ONE) * clipped
    variance_new = BETA_TWO * variance + (1.0 - BETA_TWO) * clipped * clipped
    step_size = STEP_SCALE * width_all ** (-0.5)
    updated = (master_weight - step_size * moment_new / (jnp.sqrt(variance_new) + 1e-08)).astype(
        jnp.bfloat16
    )
    gathered = lax.all_gather(activations, "tensor", axis=1, tiled=True)
    widened = gathered.astype(jnp.float32)
    row_scale = lax.rsqrt(jnp.mean(widened * widened, axis=-1, keepdims=True) + 1e-06)
    normed = (widened * row_scale * norm_gain).astype(jnp.bfloat16)
    seq_rows = normed.shape[0]
    slab_rows = updated.shape[0]
    head_dev = updated.shape[2] - 1
    head_size = updated.shape[3]
    query_cols = head_dev * head_size
    tensor_pos = lax.axis_index("tensor")
    is_even = tensor_pos % 2 == 0
    query_part = updated[:, 0, :head_dev].reshape(slab_rows, query_cols)
    own_part = updated[:, 0, head_dev]
    partner = from_partner(own_part, "tensor", 0)
    key_weight = jnp.where(is_even, own_part, partner)
    value_weight = jnp.where(is_even, partner, own_part)
    relayed = jnp.concatenate([query_part, key_weight, value_weight], axis=1)
    projected = jnp.dot(
        normed,
        lax.all_gather(relayed, ("group", "dp"), axis=0, tiled=True),
        preferred_element_type=jnp.float32,
    )
    cosine, sine = rope_tables(seq_rows, head_size)
    gain_row = lax.dynamic_slice_in_dim(key_gain, tensor_pos // 2, 1, 0)[0]
    query_proj = projected[:, :query_cols].reshape(seq_rows, head_dev, head_size)
    queries = rms_scaled(query_proj, query_gain)
    queries = (rotate(queries, cosine[:, None, :], sine[:, None, :]) * head_size ** (-0.5)).astype(
        jnp.bfloat16
    )
    key_rot = rotate(
        rms_scaled(projected[:, query_cols : query_cols + head_size], gain_row), cosine, sine
    ).astype(jnp.bfloat16)
    value_rows = projected[:, query_cols + head_size :].astype(jnp.bfloat16)
    scores = jnp.einsum("qhe,ke->hqk", queries, key_rot, preferred_element_type=jnp.float32)
    row_pos = jnp.arange(seq_rows, dtype=jnp.int32)[:, None]
    col_pos = jnp.arange(seq_rows, dtype=jnp.int32)[None, :]
    allowed = (col_pos <= row_pos) & (col_pos < prompt_len[0])
    scores = jnp.where(allowed[None], scores, -1e30)
    highest = jnp.max(scores, axis=-1, keepdims=True)
    weights = jnp.exp(scores - highest)
    weights = (weights / jnp.sum(weights, axis=-1, keepdims=True)).astype(jnp.bfloat16)
    output = jnp.einsum("hqk,ke->qhe", weights, value_rows, preferred_element_type=jnp.float32)
    return output.astype(jnp.bfloat16).reshape(seq_rows, query_cols)


def solution(mesh):
    in_specs = (
        P(("group", "dp"), "tensor"),
        P(),
        P(("group", "dp"), "tensor", None, None),
        P(("group", "dp"), "tensor", None, None),
        P(("group", "dp"), "tensor", None, None),
        P(("group", "dp"), "tensor", None, None),
        P("tensor", None),
        P(),
        P(("group", "dp")),
    )
    out_specs = P(("group", "dp"), "tensor")
    return jax.shard_map(shards, mesh=mesh, in_specs=in_specs, out_specs=out_specs, check_vma=False)
```

profile of v0, /device:TPU:1, one launch (start us, length us, event | category | flops | bytes accessed | tf_op | source)
XLA Modules:
  0.0 286.1 jit_solution(6875367453801068412)
XLA Ops:
  6.5 0.0 copy-start
  6.5 0.0 all-gather.3.cloned.1.call-start
  6.5 0.7 all-gather.3.cloned.1.call-update
  7.3 0.0 all-gather.5.cloned.1.call-start
  7.3 2.0 multiply_reduce_fusion.2
  9.3 108.1 %psum.7 = f32[]{:T(128)} all-reduce(f32[]{:T(128)} %multiply_reduce_fusion.2), channel_id=1, replica_groups=mesh['group'=4,'dp'=8,'tensor'=16] {'group','dp','tensor'}, use_global_device_ids=true, to_apply=%region_2.0 | all-reduce | flops 1 | bytes 8 | tf_op jit(solution)/shard_map/psum | solution.py:42
  118.1 2.7 subtract_convert_fusion
  120.8 0.1 slice.38
  120.9 2.6 collective-permute-start
  123.5 0.5 slice_reduce_fusion
  124.1 0.0 copy-start.2
  124.1 3.1 %collective-permute-done = bf16[160,128]{1,0:T(8,128)(2,1)S(1)} collective-permute-done((bf16[160,128]{1,0:T(8,128)(2,1)S(1)}, bf16[160,128]{1,0:T(8,128)(2,1)S(1)}, u32[]{:S(2)}, u32[]{:S(2)}) %collective-permute-start) | collective-permute-done | bytes 40992 | tf_op jit(solution)/shard_map/ppermute | solution.py:13
  127.2 0.7 pad_maximum_fusion
  127.9 0.0 all-gather.5.cloned.1.call-update
  128.6 0.0 copy-done
  128.6 1.1 fusion.10
  129.7 23.2 %all-gather.3.cloned.1.call-done = bf16[768,5120]{0,1:T(8,128)(2,1)} async-done(((bf16[768,320]{0,1:T(8,128)(2,1)}), bf16[768,5120]{0,1:T(8,128)(2,1)}) %all-gather.3.cloned.1.call-update) | async-done | bytes 7864336 | tf_op jit(solution)/shard_map/all_gather | solution.py:51
  152.9 4.9 %fusion.1 = f32[768]{0:T(1024)S(1)} fusion(bf16[768,5120]{0,1:T(8,128)(2,1)} %all-gather.3.cloned.1.call-done), kind=kLoop, calls=%fused_computation.3 | loop fusion | flops 11795712 | bytes 7867392 | tf_op jit(solution)/shard_map/reduce_sum | solution.py:53
  157.8 98.4 %all-gather.5.cloned.1.call-done = bf16[5120,512]{1,0:T(8,128)(2,1)} async-done(((bf16[160,512]{1,0:T(8,128)(2,1)}), bf16[5120,512]{1,0:T(8,128)(2,1)}) %all-gather.5.cloned.1.call-update) | async-done | bytes 5242896 | tf_op jit(solution)/shard_map/all_gather | solution.py:70
  256.2 0.0 copy-done.2
  256.2 9.4 %fusion.4 = f32[768,512]{0,1:T(8,128)S(1)} fusion(bf16[5120,512]{1,0:T(8,128)(2,1)} %all-gather.5.cloned.1.call-done, bf16[768,5120]{0,1:T(8,128)(2,1)} %all-gather.3.cloned.1.call-done, f32[5120]{0:T(1024)S(1)} %copy-done.2, f32[768]{0:T(1024)S(1)} %add_rsqrt_fusion.2), kind=kOutput, calls=%fused_computation.6 | convolution fusion | flops 4042260480 | bytes 14703616 | tf_op jit(solution)/shard_map/dot_general | solution.py:68
  265.6 0.0 copy-start.1
  265.6 0.1 multiply_reduce_fusion
  265.7 0.1 slice.43
  265.8 0.1 multiply_multiply_fusion.1
  265.9 1.5 subtract_convert_fusion.1
  267.4 0.2 copy.13
  267.5 0.9 copy.12
  268.5 0.3 copy.11
  268.7 0.0 copy-done.1
  268.7 0.3 multiply_multiply_fusion
  269.0 1.3 multiply_subtract_fusion
  270.3 5.2 %fusion.28 = (f32[2,768]{1,0:T(2,128)S(1)}, f32[2,768,768]{1,2,0:T(8,128)}) fusion(pred[768,768]{0,1:T(8,128)(4,1)} %fusion.10, bf16[768,64]{0,1:T(8,128)(2,1)} %get-tuple-element.8, bf16[768,64]{0,1:T(8,128)(2,1)} %get-tuple-element.7, f32[768,2,64]{2,0,1:T(8,128)S(1)} %get-tuple-element.6, f32[768,2,64]{2,0,1:T(8,128)S(1)} %get-tuple-element.5), kind=kOutput, calls=%fused_computation.57 | convolution fusion | flops 306512640 | bytes 6297600 | tf_op jit(solution)/shard_map/sub | solution.py:90
  275.5 2.8 fusion.13
  278.3 0.9 copy.16
  (10 shorter events, 0.1 us)
Async XLA Ops:
  6.5 122.0 %copy-start = (f32[8,128]{1,0:T(8,128)S(1)}, f32[8,128]{1,0:T(8,128)}, u32[]{:S(2)}) copy-start(f32[8,128]{1,0:T(8,128)} %param.16) | copy-start | bytes 12292
  6.5 146.4 %all-gather.3.cloned.1.call-start = ((), (), s32[]{:S(2)}) async-start(), calls=%async_computation | async-start | bytes 8355840 | tf_op jit(solution)/shard_map/all_gather | solution.py:51
  7.3 248.9 %all-gather.5.cloned.1.call-start = ((), (), s32[]{:S(2)}) async-start(), calls=%async_computation.1 | async-start | bytes 5406720 | tf_op jit(solution)/shard_map/all_gather | solution.py:70
  120.9 6.3 %collective-permute-start = (bf16[160,128]{1,0:T(8,128)(2,1)S(1)}, bf16[160,128]{1,0:T(8,128)(2,1)S(1)}, u32[]{:S(2)}, u32[]{:S(2)}) collective-permute-start(bf16[160,128]{1,0:T(8,128)(2,1)S(1)} %bitcast.49), channel_id=1, source_target_pairs={{0,1},{1,0},{2,3},{3,2},{4,5},{5,4},{6,7},{7,6},{8,9},{9,8},{10,11... | collective-permute-start | bytes 122888 | tf_op jit(solution)/shard_map/ppermute | solution.py:13
  124.1 132.1 %copy-start.2 = (f32[5120]{0:T(1024)S(1)}, f32[5120]{0:T(1024)}, u32[]{:S(2)}) copy-start(f32[5120]{0:T(1024)} %param.10) | copy-start | bytes 61444
  265.6 3.2 %copy-start.1 = (f32[2,128]{1,0:T(2,128)S(1)}, f32[2,128]{1,0:T(2,128)}, u32[]{:S(2)}) copy-start(f32[2,128]{1,0:T(2,128)} %param.15) | copy-start | bytes 3076
Sparse Core Ops, SparseCore 0:
  10.5 142.3 all-gather.2
  155.0 101.0 all-gather.4
where the time goes:
time: 289 us; the launch traced here: 286 us
  waiting for transfers between devices  125 us (43%)
  blocking collectives  108 us (37%)
  matrix products  17.4 us (6%)
  between operations  14.9 us (5%)
  other arithmetic  14.6 us (5%)
  local copies, waits for them, and re-layouts  2.97 us (1%)
    psum x1, blocking collectives, shards(): lax.psum(jnp.sum(grad_local * grad_local), ('group', 'dp', 'tensor'))  108 us
    all_gather x1, waiting for transfers between devices, shards(): lax.all_gather(relayed, ('group', 'dp'), axis=0, tiled=True)  98.4 us
    all_gather x1, waiting for transfers between devices, shards(): gathered = lax.all_gather(activations, 'tensor', axis=1, tiled=True)  23.2 us
    dot_general x1, matrix products, shards(): jnp.dot(normed, lax.all_gather(relayed, ('group', 'dp'), axis=0, tiled=Tr...  9.39 us
  transfers between devices with their start and end apart: 3, of which 3 were waited for; matrix products, arithmetic and copies ran while one was open for 4% of the time, Pallas kernels for 0%

commit v1 on v0

v1 whole, which is shorter than its diff:
```python
import jax
import jax.numpy as jnp
from jax import lax
from jax.sharding import Mesh, PartitionSpec as P

STEP_SCALE = 0.5
BETA_ONE = 0.9
BETA_TWO = 0.95
ROPE_BASE = 500000.0
AXES = ("xl", "core", "y", "z", "xh")
SIZES = (2, 2, 8, 8, 2)


def rope_tables(length, head_size):
    positions = jnp.arange(length, dtype=jnp.float32)
    exponent = jnp.arange(head_size // 2, dtype=jnp.float32) * 2.0 / head_size
    inverse = jnp.power(ROPE_BASE, -exponent)
    angles = positions[:, None] * inverse[None, :]
    return (jnp.cos(angles), jnp.sin(angles))


def rotate(inputs, cosine, sine):
    midpoint = inputs.shape[-1] // 2
    front_half = inputs[..., :midpoint]
    back_half = inputs[..., midpoint:]
    return jnp.concatenate(
        [front_half * cosine - back_half * sine, back_half * cosine + front_half * sine], axis=-1
    )


def rms_scaled(inputs, gains):
    return inputs * lax.rsqrt(jnp.mean(inputs * inputs, axis=-1, keepdims=True) + 1e-06) * gains


def swap(array, axis):
    return lax.ppermute(array, axis, [(0, 1), (1, 0)])


def global_sum(value):
    count = 1
    for size in SIZES:
        count *= size
    spread = jnp.broadcast_to(value, (count, 128))
    return jnp.sum(lax.all_to_all(spread, AXES, 0, 0, tiled=True)[:, 0])


def to_column(block, step):
    pairs = []
    for y in range(8):
        for slab in range(2):
            pairs.append((y * 2 + slab, (y + step + 2 * slab) % 8 * 2 + (y >> 1) % 2))
    return lax.ppermute(block, ("y", "xh"), pairs)


def shards(
    activations, norm_gain, master_weight, grad, moment, variance, query_gain, key_gain, prompt_len
):
    xl, y, z, xh = (lax.axis_index(a) for a in ("xl", "y", "z", "xh"))
    width_all = norm_gain.shape[0]
    seq_rows, width_part = activations.shape
    slab_rows, _, slab_heads, head_size = grad.shape
    head_dev = slab_heads - 1
    query_cols = head_dev * head_size
    slab_cols = slab_heads * head_size

    gathered = lax.all_gather(activations, "z", axis=1, tiled=True)

    grad_local = grad.astype(jnp.float32)
    sumsq = global_sum(jnp.sum(grad_local * grad_local))
    clip_factor = 1.0 / jnp.sqrt(sumsq + 1e-12)
    clipped = grad_local * clip_factor
    moment_new = BETA_ONE * moment + (1.0 - BETA_ONE) * clipped
    variance_new = BETA_TWO * variance + (1.0 - BETA_TWO) * clipped * clipped
    step_size = STEP_SCALE * width_all ** (-0.5)
    updated = (master_weight - step_size * moment_new / (jnp.sqrt(variance_new) + 1e-08)).astype(
        jnp.bfloat16
    )
    updated = updated.reshape(slab_rows, slab_cols)

    arrived = jnp.stack([to_column(updated, step) for step in range(8)])
    rows = []
    for high in range(2):
        for low in range(2):
            source = high * 4 + xh * 2 + low
            left = lax.dynamic_index_in_dim(arrived, (y - source) & 7, 0, False)
            right = lax.dynamic_index_in_dim(arrived, (y - source - 2) & 7, 0, False)
            rows.append(jnp.concatenate([left, right], axis=1))
    own_rows = jnp.concatenate(rows, axis=0)
    other_rows = swap(own_rows, "xl")
    own_weight = lax.all_gather(own_rows, "core", axis=0, tiled=True)
    other_weight = lax.all_gather(other_rows, "core", axis=0, tiled=True)

    widened = gathered.astype(jnp.float32)
    square = jnp.sum(widened * widened, axis=-1)
    square = square + swap(square, "xh")
    row_scale = lax.rsqrt(square / width_all + 1e-06)
    gain = lax.dynamic_index_in_dim(norm_gain.reshape(8, 2, width_part), xh, 1, False).reshape(-1)
    normed = (widened * row_scale[:, None] * gain).astype(jnp.bfloat16)
    half = normed.shape[1] // 2
    own_normed = lax.dynamic_slice_in_dim(normed, xl * half, half, 1)
    other_normed = lax.dynamic_slice_in_dim(normed, (1 - xl) * half, half, 1)
    partial = jnp.dot(own_normed, own_weight, preferred_element_type=jnp.float32)
    partial += jnp.dot(other_normed, other_weight, preferred_element_type=jnp.float32)

    def picked(slab):
        queries = lax.dynamic_slice_in_dim(partial, slab * slab_cols, query_cols, 1)
        return jnp.concatenate([queries, partial[:, query_cols:slab_cols], partial[:, slab_cols + query_cols :]], axis=1)

    projected = picked(xh) + swap(picked(1 - xh).astype(jnp.bfloat16), "xh").astype(jnp.float32)

    cosine, sine = rope_tables(seq_rows, head_size)
    gain_row = lax.dynamic_slice_in_dim(key_gain, z, 1, 0)[0]
    query_proj = projected[:, :query_cols].reshape(seq_rows, head_dev, head_size)
    queries = rms_scaled(query_proj, query_gain)
    queries = (rotate(queries, cosine[:, None, :], sine[:, None, :]) * head_size ** (-0.5)).astype(
        jnp.bfloat16
    )
    key_rot = rotate(
        rms_scaled(projected[:, query_cols : query_cols + head_size], gain_row), cosine, sine
    ).astype(jnp.bfloat16)
    value_rows = projected[:, query_cols + head_size :].astype(jnp.bfloat16)
    scores = jnp.einsum("qhe,ke->hqk", queries, key_rot, preferred_element_type=jnp.float32)
    row_pos = jnp.arange(seq_rows, dtype=jnp.int32)[:, None]
    col_pos = jnp.arange(seq_rows, dtype=jnp.int32)[None, :]
    allowed = (col_pos <= row_pos) & (col_pos < prompt_len[0])
    scores = jnp.where(allowed[None], scores, -1e30)
    highest = jnp.max(scores, axis=-1, keepdims=True)
    weights = jnp.exp(scores - highest)
    weights = (weights / jnp.sum(weights, axis=-1, keepdims=True)).astype(jnp.bfloat16)
    output = jnp.einsum("hqk,ke->qhe", weights, value_rows, preferred_element_type=jnp.float32)
    return output.astype(jnp.bfloat16).reshape(seq_rows, query_cols)


def solution(mesh):
    fine = Mesh(mesh.devices.reshape(SIZES), AXES)
    rows, cols = ("xl", "core", "y"), ("z", "xh")
    slab = P(rows, cols, None, None)
    in_specs = (P(rows, cols), P(), slab, slab, slab, slab, P(cols, None), P(), P(rows))
    return jax.shard_map(
        shards, mesh=fine, in_specs=in_specs, out_specs=P(rows, cols), check_vma=False
    )
```

time: 289 us -> 208 us (0.72)
  blocking collectives: 108 us -> 38.9 us
  waiting for transfers between devices: 125 us -> 78.4 us
  starting transfers between devices: 2.64 us -> 31.5 us
  other arithmetic: 14.6 us -> 20.1 us
    all_gather x2 -> x3, waiting for transfers between devices: 122 us -> 0.02 us  [the longest x1 0.02 us: shards(): gathered = lax.all_gather(activations, 'z', axis=1, tiled=True)]
    psum x1 -> x0, blocking collectives: 108 us -> none  [shards(): lax.psum(jnp.sum(grad_local * grad_local), ('group', 'dp', 'tensor'))]
    ppermute x1 -> x11, waiting for transfers between devices: 3.06 us -> 77.6 us  [the longest x3 43.1 us: swap(): return lax.ppermute(array, axis, [(0, 1), (1, 0)])]
    all_to_all x0 -> x1, blocking collectives: none -> 38.9 us  [global_sum(): return jnp.sum(lax.all_to_all(spread, AXES, 0, 0, tiled=True)[:, 0])]
    ppermute x1 -> x11, starting transfers between devices: 2.6 us -> 31.4 us  [the longest x8 25.5 us: to_column(): return lax.ppermute(block, ('y', 'xh'), pairs)]
    convert_element_type x0 -> x1, other arithmetic: none -> 4.37 us  [shards(): normed = (widened * row_scale[:, None] * gain).astype(jnp.bfloat16)]
    reduce_sum x2 -> x3, other arithmetic: 6.87 us -> 5.64 us  [the longest x1 2.96 us: shards(): square = jnp.sum(widened * widened, axis=-1)]
    dot_general x1 -> x2, matrix products: 9.39 us -> 10 us  [the longest x1 5.26 us: shards(): jnp.dot(own_normed, own_weight, preferred_element_type=jnp.float32)]
  transfers between devices with their start and end apart: 3 -> 14, of which waited for: 3 -> 6; matrix products, arithmetic and copies ran while one was open for 4% -> 11% of each run, Pallas kernels for 0% -> 0%
where the time goes in v1:
time: 208 us; the launch traced here: 207 us
  waiting for transfers between devices  78.4 us (38%)
  blocking collectives  38.9 us (19%)
  starting transfers between devices  31.5 us (15%)
  other arithmetic  20.1 us (10%)
  matrix products  18 us (9%)
  between operations  14.9 us (7%)
  local copies, waits for them, and re-layouts  4.81 us (2%)
    ppermute x3, waiting for transfers between devices, swap(): return lax.ppermute(array, axis, [(0, 1), (1, 0)])  43.1 us
    all_to_all x1, blocking collectives, global_sum(): return jnp.sum(lax.all_to_all(spread, AXES, 0, 0, tiled=True)[:, 0])  38.9 us
    ppermute x8, waiting for transfers between devices, to_column(): return lax.ppermute(block, ('y', 'xh'), pairs)  34.6 us
    ppermute x8, starting transfers between devices, to_column(): return lax.ppermute(block, ('y', 'xh'), pairs)  25.5 us
    ppermute x3, starting transfers between devices, swap(): return lax.ppermute(array, axis, [(0, 1), (1, 0)])  5.94 us
    dot_general x1, matrix products, shards(): jnp.dot(own_normed, own_weight, preferred_element_type=jnp.float32)  5.26 us
    sub x1, matrix products, shards(): weights = jnp.exp(scores - highest)  5.19 us
    dot_general x1, matrix products, shards(): jnp.dot(other_normed, other_weight, preferred_element_type=jnp.float32)  4.74 us
  transfers between devices with their start and end apart: 14, of which 6 were waited for; matrix products, arithmetic and copies ran while one was open for 11% of the time, Pallas kernels for 0%

profile of v1, /device:TPU:1, one launch (start us, length us, event | category | flops | bytes accessed | tf_op | source)
XLA Modules:
  0.0 206.6 jit_solution(15511190006136124342)
XLA Ops:
  6.5 0.7 all-gather.4.cloned.1.call-update
  7.3 2.0 multiply_reduce_fusion.2
  9.3 0.8 broadcast_in_dim.10
  10.1 38.9 %all_to_all.9 = f32[512,1,128]{2,1,0:T(1,128)S(1)} all-to-all(f32[512,1,128]{2,1,0:T(1,128)S(1)} %broadcast_in_dim.10), channel_id=1, replica_groups=mesh['xl'=2,'core'=2,'y'=8,'z'=8,'xh'=2] {'xl','core','y','z','xh'}, dimensions={0} | all-to-all | bytes 524288 | tf_op jit(solution)/shard_map/all_to_all | solution.py:44
  49.0 0.7 slice_reduce_fusion
  50.3 3.2 %convert_reduce_fusion = bf16[160,3,128]{2,1,0:T(4,128)(2,1)S(1)} fusion(f32[160,1,3,128]{3,1,2,0:T(1,128)} %param.11, f32[160,1,3,128]{3,1,2,0:T(1,128)} %param.14, f32[160,1,3,128]{3,1,2,0:T(1,128)} %param.13, bf16[160,1,3,128]{3,0,2,1:T(8,128)(2,1)} %param.12, f32[]{:T(128)S(6)} %sqrt.6), kind=kLoop, calls=%fused_computation.39 | loop fusion | flops 860160 | bytes 983044 | tf_op jit(solution)/shard_map/convert_element_type | solution.py:75
  53.6 0.7 collective-permute-start.1
  54.3 4.2 %collective-permute-start.8 = (bf16[160,384]{1,0:T(8,128)(2,1)S(1)}, bf16[160,384]{1,0:T(8,128)(2,1)S(1)}, u32[]{:S(2)}, u32[]{:S(2)}) collective-permute-start(bf16[160,384]{1,0:T(8,128)(2,1)S(1)} %bitcast.79), channel_id=1, source_target_pairs={{0,112},{1,16},{16,0},{17,32},{32,17},{33,49},{48,33},{49,65},{64,... | collective-permute-start | bytes 368648 | tf_op jit(solution)/shard_map/ppermute | solution.py:52
  58.5 6.7 %collective-permute-start.7 = (bf16[160,384]{1,0:T(8,128)(2,1)S(1)}, bf16[160,384]{1,0:T(8,128)(2,1)S(1)}, u32[]{:S(2)}, u32[]{:S(2)}) collective-permute-start(bf16[160,384]{1,0:T(8,128)(2,1)S(1)} %bitcast.80), channel_id=1, source_target_pairs={{0,96},{1,0},{16,112},{17,16},{32,1},{33,33},{48,17},{49,49},{64,3... | collective-permute-start | bytes 368648 | tf_op jit(solution)/shard_map/ppermute | solution.py:52
  65.2 1.9 collective-permute-start.6
  67.1 6.3 %collective-permute-start.5 = (bf16[160,384]{1,0:T(8,128)(2,1)S(1)}, bf16[160,384]{1,0:T(8,128)(2,1)S(1)}, u32[]{:S(2)}, u32[]{:S(2)}) collective-permute-start(bf16[160,384]{1,0:T(8,128)(2,1)S(1)} %bitcast.82), channel_id=1, source_target_pairs={{0,64},{1,96},{16,80},{17,112},{32,97},{33,1},{48,113},{49,17},{64... | collective-permute-start | bytes 368648 | tf_op jit(solution)/shard_map/ppermute | solution.py:52
  73.4 1.9 collective-permute-start.2
  75.4 11.6 %collective-permute-done.2 = bf16[160,384]{1,0:T(8,128)(2,1)S(1)} collective-permute-done((bf16[160,384]{1,0:T(8,128)(2,1)S(1)}, bf16[160,384]{1,0:T(8,128)(2,1)S(1)}, u32[]{:S(2)}, u32[]{:S(2)}) %collective-permute-start.2) | collective-permute-done | bytes 122912 | tf_op jit(solution)/shard_map/ppermute | solution.py:52
  87.0 1.9 collective-permute-start.3
  88.9 12.0 %collective-permute-done.3 = bf16[160,384]{1,0:T(8,128)(2,1)S(1)} collective-permute-done((bf16[160,384]{1,0:T(8,128)(2,1)S(1)}, bf16[160,384]{1,0:T(8,128)(2,1)S(1)}, u32[]{:S(2)}, u32[]{:S(2)}) %collective-permute-start.3) | collective-permute-done | bytes 122912 | tf_op jit(solution)/shard_map/ppermute | solution.py:52
  101.0 1.9 collective-permute-start.4
  102.9 10.9 %collective-permute-done.4 = bf16[160,384]{1,0:T(8,128)(2,1)S(1)} collective-permute-done((bf16[160,384]{1,0:T(8,128)(2,1)S(1)}, bf16[160,384]{1,0:T(8,128)(2,1)S(1)}, u32[]{:S(2)}, u32[]{:S(2)}) %collective-permute-start.4) | collective-permute-done | bytes 122912 | tf_op jit(solution)/shard_map/ppermute | solution.py:52
  114.0 0.1 dynamic-slice_bitcast_fusion.7
  114.2 1.1 maximum_maximum_fusion
  115.4 1.9 collective-permute-start.9
  117.3 23.0 %collective-permute-done.9 = bf16[640,768]{1,0:T(8,128)(2,1)S(1)} collective-permute-done((bf16[640,768]{1,0:T(8,128)(2,1)}, bf16[640,768]{1,0:T(8,128)(2,1)S(1)}, u32[]{:S(2)}, u32[]{:S(2)}) %collective-permute-start.9) | collective-permute-done | bytes 983072 | tf_op jit(solution)/shard_map/ppermute | solution.py:36
  140.3 1.0 copy-done.1
  141.3 3.0 %fusion.1 = f32[768]{0:T(1024)S(1)} fusion(bf16[768,2560]{0,1:T(8,128)(2,1)} %all-gather.4.cloned.1.call-done), kind=kLoop, calls=%fused_computation.3 | loop fusion | flops 5897472 | bytes 3935232 | tf_op jit(solution)/shard_map/reduce_sum | solution.py:94
  144.3 2.1 %collective-permute-start = (f32[768]{0:T(1024)S(1)}, f32[768]{0:T(1024)S(1)}, u32[]{:S(2)}, u32[]{:S(2)}) collective-permute-start(f32[768]{0:T(1024)S(1)} %fusion.1), channel_id=1, source_target_pairs={{0,1},{1,0},{2,3},{3,2},{4,5},{5,4},{6,7},{7,6},{8,9},{9,8},{10,11... | collective-permute-start | bytes 9224 | tf_op jit(solution)/shard_map/ppermute | solution.py:36
  146.4 0.1 reshape.108
  146.6 0.1 mul.239
  146.6 3.5 %collective-permute-done = f32[768]{0:T(1024)S(1)} collective-permute-done((f32[768]{0:T(1024)S(1)}, f32[768]{0:T(1024)S(1)}, u32[]{:S(2)}, u32[]{:S(2)}) %collective-permute-start) | collective-permute-done | bytes 3104 | tf_op jit(solution)/shard_map/ppermute | solution.py:36
  150.2 4.4 %fusion.3 = bf16[768,2560]{0,1:T(8,128)(2,1)} fusion(bf16[768,2560]{0,1:T(8,128)(2,1)} %all-gather.4.cloned.1.call-done, f32[2560]{0:T(1024)S(1)} %mul.239, f32[768]{0:T(1024)S(1)} %add_rsqrt_fusion.2), kind=kLoop, calls=%fused_computation.5 | loop fusion | flops 7864320 | bytes 7877632 | tf_op jit(solution)/shard_map/convert_element_type | solution.py:98
  154.5 5.3 %fusion.11 = f32[768,768]{0,1:T(8,128)} fusion(bf16[1280,768]{1,0:T(8,128)(2,1)} %all-gather.6.cloned.1.call-done, bf16[768,2560]{0,1:T(8,128)(2,1)} %fusion.3, s32[]{:T(128)S(6)} %select_n.49), kind=kOutput, calls=%fused_computation.17 | convolution fusion | flops 1509949440 | bytes 6291460 | tf_op jit(solution)/shard_map/dot_general | solution.py:102
  159.8 4.7 %fusion.13 = f32[768,768]{0,1:T(8,128)S(1)} fusion(f32[768,768]{0,1:T(8,128)} %fusion.11, bf16[1280,768]{1,0:T(8,128)(2,1)} %all-gather.8.cloned.1.call-done, bf16[768,2560]{0,1:T(8,128)(2,1)} %fusion.3, s32[]{:T(128)S(6)} %select_n.58), kind=kOutput, calls=%fused_computation.20 | convolution fusion | flops 1510539264 | bytes 8650756 | tf_op jit(solution)/shard_map/dot_general | solution.py:103
  164.6 0.1 pad_maximum_fusion
  164.7 1.9 collective-permute-start.10
  167.3 1.1 fusion.6
  168.4 0.1 fusion.35
  168.5 16.5 %collective-permute-done.10 = bf16[768,512]{0,1:T(8,128)(2,1)} collective-permute-done((bf16[768,512]{0,1:T(8,128)(2,1)S(1)}, bf16[768,512]{0,1:T(8,128)(2,1)}, u32[]{:S(2)}, u32[]{:S(2)}) %collective-permute-start.10) | collective-permute-done | bytes 786464 | tf_op jit(solution)/shard_map/ppermute | solution.py:36
  185.0 1.3 maximum_add_fusion
  186.4 0.1 multiply_reduce_fusion
  186.5 0.1 slice.50
  186.6 0.1 multiply_multiply_fusion.1
  186.7 1.5 subtract_convert_fusion
  188.2 0.2 copy.28
  188.3 0.9 copy.27
  189.3 0.3 copy.26
  189.5 0.3 multiply_multiply_fusion
  189.8 1.3 multiply_subtract_fusion
  191.1 5.2 %fusion.36 = (f32[2,768]{1,0:T(2,128)S(1)}, f32[2,768,768]{1,2,0:T(8,128)}) fusion(pred[768,768]{0,1:T(8,128)(4,1)} %fusion.6, bf16[768,64]{0,1:T(8,128)(2,1)} %get-tuple-element.20, bf16[768,64]{0,1:T(8,128)(2,1)} %get-tuple-element.19, f32[768,2,64]{2,0,1:T(8,128)S(1)} %get-tuple-element.10, f32[768,2,64]{2,0,1:T(8,128)S(1)} %get-tuple-element.9), kind=kOutput, calls=%fused_computation.84 | convolution fusion | flops 306512640 | bytes 6297600 | tf_op jit(solution)/shard_map/sub | solution.py:128
  196.3 2.8 %fusion.16 = bf16[128,2,768]{2,0,1:T(8,128)(2,1)S(1)} fusion(f32[2,768,768]{1,2,0:T(8,128)} %get-tuple-element.24, f32[2,768]{1,0:T(2,128)S(1)} %get-tuple-element.23, f32[768,512]{0,1:T(8,128)S(1)} %maximum_add_fusion), kind=kOutput, calls=%fused_computation.21 | convolution fusion | flops 304545792 | bytes 5314560 | tf_op jit(solution)/shard_map/hqk,ke->qhe/dot_general | solution.py:130
  199.1 0.9 copy.31
  (40 shorter events, 0.6 us)
Async XLA Ops:
  6.5 160.1 %copy-start = (f32[8,128]{1,0:T(8,128)S(1)}, f32[8,128]{1,0:T(8,128)}, u32[]{:S(2)}) copy-start(f32[8,128]{1,0:T(8,128)} %param.16) | copy-start | bytes 12292
  6.5 134.8 %all-gather.4.cloned.1.call-start = ((), (), s32[]{:S(2)}) async-start(), calls=%async_computation.1 | async-start | bytes 4423680 | tf_op jit(solution)/shard_map/all_gather | solution.py:66
  7.3 147.3 %all-gather.6.cloned.1.call-start = ((), (), s32[]{:S(2)}) async-start(), calls=%async_computation.2 | async-start | bytes 2949120 | tf_op jit(solution)/shard_map/all_gather | solution.py:90
  53.6 19.8 %collective-permute-start.1 = (bf16[160,384]{1,0:T(8,128)(2,1)S(1)}, bf16[160,384]{1,0:T(8,128)(2,1)S(1)}, u32[]{:S(2)}, u32[]{:S(2)}) collective-permute-start(bf16[160,384]{1,0:T(8,128)(2,1)S(1)} %bitcast.78), channel_id=1, source_target_pairs={{0,0},{1,32},{16,16},{17,48},{32,33},{33,65},{48,49},{49,81},{64,6... | collective-permute-start | bytes 368648 | tf_op jit(solution)/shard_map/ppermute | solution.py:52
  54.3 59.7 %collective-permute-start.8 = (bf16[160,384]{1,0:T(8,128)(2,1)S(1)}, bf16[160,384]{1,0:T(8,128)(2,1)S(1)}, u32[]{:S(2)}, u32[]{:S(2)}) collective-permute-start(bf16[160,384]{1,0:T(8,128)(2,1)S(1)} %bitcast.79), channel_id=1, source_target_pairs={{0,112},{1,16},{16,0},{17,32},{32,17},{33,49},{48,33},{49,65},{64,... | collective-permute-start | bytes 368648 | tf_op jit(solution)/shard_map/ppermute | solution.py:52
  58.5 55.4 %collective-permute-start.7 = (bf16[160,384]{1,0:T(8,128)(2,1)S(1)}, bf16[160,384]{1,0:T(8,128)(2,1)S(1)}, u32[]{:S(2)}, u32[]{:S(2)}) collective-permute-start(bf16[160,384]{1,0:T(8,128)(2,1)S(1)} %bitcast.80), channel_id=1, source_target_pairs={{0,96},{1,0},{16,112},{17,16},{32,1},{33,33},{48,17},{49,49},{64,3... | collective-permute-start | bytes 368648 | tf_op jit(solution)/shard_map/ppermute | solution.py:52
  65.2 48.7 %collective-permute-start.6 = (bf16[160,384]{1,0:T(8,128)(2,1)S(1)}, bf16[160,384]{1,0:T(8,128)(2,1)S(1)}, u32[]{:S(2)}, u32[]{:S(2)}) collective-permute-start(bf16[160,384]{1,0:T(8,128)(2,1)S(1)} %bitcast.81), channel_id=1, source_target_pairs={{0,80},{1,112},{16,96},{17,0},{32,113},{33,17},{48,1},{49,33},{64,... | collective-permute-start | bytes 368648 | tf_op jit(solution)/shard_map/ppermute | solution.py:52
  67.1 46.8 %collective-permute-start.5 = (bf16[160,384]{1,0:T(8,128)(2,1)S(1)}, bf16[160,384]{1,0:T(8,128)(2,1)S(1)}, u32[]{:S(2)}, u32[]{:S(2)}) collective-permute-start(bf16[160,384]{1,0:T(8,128)(2,1)S(1)} %bitcast.82), channel_id=1, source_target_pairs={{0,64},{1,96},{16,80},{17,112},{32,97},{33,1},{48,113},{49,17},{64... | collective-permute-start | bytes 368648 | tf_op jit(solution)/shard_map/ppermute | solution.py:52
  73.4 13.5 %collective-permute-start.2 = (bf16[160,384]{1,0:T(8,128)(2,1)S(1)}, bf16[160,384]{1,0:T(8,128)(2,1)S(1)}, u32[]{:S(2)}, u32[]{:S(2)}) collective-permute-start(bf16[160,384]{1,0:T(8,128)(2,1)S(1)} %bitcast.83), channel_id=1, source_target_pairs={{0,16},{1,48},{16,32},{17,64},{32,49},{33,81},{48,65},{49,97},{64,... | collective-permute-start | bytes 368648 | tf_op jit(solution)/shard_map/ppermute | solution.py:52
  87.0 14.0 %collective-permute-start.3 = (bf16[160,384]{1,0:T(8,128)(2,1)S(1)}, bf16[160,384]{1,0:T(8,128)(2,1)S(1)}, u32[]{:S(2)}, u32[]{:S(2)}) collective-permute-start(bf16[160,384]{1,0:T(8,128)(2,1)S(1)} %bitcast.84), channel_id=1, source_target_pairs={{0,32},{1,64},{16,48},{17,80},{32,65},{33,97},{48,81},{49,113},{64... | collective-permute-start | bytes 368648 | tf_op jit(solution)/shard_map/ppermute | solution.py:52
  101.0 12.9 %collective-permute-start.4 = (bf16[160,384]{1,0:T(8,128)(2,1)S(1)}, bf16[160,384]{1,0:T(8,128)(2,1)S(1)}, u32[]{:S(2)}, u32[]{:S(2)}) collective-permute-start(bf16[160,384]{1,0:T(8,128)(2,1)S(1)} %bitcast.85), channel_id=1, source_target_pairs={{0,48},{1,80},{16,64},{17,96},{32,81},{33,113},{48,97},{49,1},{64,... | collective-permute-start | bytes 368648 | tf_op jit(solution)/shard_map/ppermute | solution.py:52
  115.3 44.5 %all-gather.8.cloned.1.call-start = ((), (), s32[]{:S(2)}) async-start(), calls=%async_computation.3 | async-start | bytes 2949120 | tf_op jit(solution)/shard_map/all_gather | solution.py:91
  115.4 24.9 %collective-permute-start.9 = (bf16[640,768]{1,0:T(8,128)(2,1)}, bf16[640,768]{1,0:T(8,128)(2,1)S(1)}, u32[]{:S(2)}, u32[]{:S(2)}) collective-permute-start(bf16[640,768]{1,0:T(8,128)(2,1)} %maximum_maximum_fusion), channel_id=1, source_target_pairs={{0,256},{256,0},{1,257},{257,1},{2,258},{258,2},{3,259},{259,3},{4... | collective-permute-start | bytes 2949128 | tf_op jit(solution)/shard_map/ppermute | solution.py:36
  140.3 1.0 copy-start.1
  141.3 5.1 %copy-start.2 = (f32[5120]{0:T(1024)S(1)}, f32[5120]{0:T(1024)}, u32[]{:S(2)}) copy-start(f32[5120]{0:T(1024)} %param.10) | copy-start | bytes 61444
  144.3 5.8 %collective-permute-start = (f32[768]{0:T(1024)S(1)}, f32[768]{0:T(1024)S(1)}, u32[]{:S(2)}, u32[]{:S(2)}) collective-permute-start(f32[768]{0:T(1024)S(1)} %fusion.1), channel_id=1, source_target_pairs={{0,1},{1,0},{2,3},{3,2},{4,5},{5,4},{6,7},{7,6},{8,9},{9,8},{10,11... | collective-permute-start | bytes 9224 | tf_op jit(solution)/shard_map/ppermute | solution.py:36
  164.7 20.3 %collective-permute-start.10 = (bf16[768,512]{0,1:T(8,128)(2,1)S(1)}, bf16[768,512]{0,1:T(8,128)(2,1)}, u32[]{:S(2)}, u32[]{:S(2)}) collective-permute-start(bf16[768,512]{0,1:T(8,128)(2,1)S(1)} %pad_maximum_fusion), channel_id=1, source_target_pairs={{0,1},{1,0},{2,3},{3,2},{4,5},{5,4},{6,7},{7,6},{8,9},{9,8},{10,11... | collective-permute-start | bytes 2359304 | tf_op jit(solution)/shard_map/ppermute | solution.py:36
  186.7 2.9 %copy-start.3 = (f32[2,128]{1,0:T(2,128)S(1)}, f32[2,128]{1,0:T(2,128)}, u32[]{:S(2)}) copy-start(f32[2,128]{1,0:T(2,128)} %param.15) | copy-start | bytes 3076
Sparse Core Ops, SparseCore 0:
  9.4 66.8 all-gather.3
  115.4 13.8 all-gather.5
  141.4 12.7 all-gather.7

commit v2 on v1

v2 whole, which is shorter than its diff:
```python
import functools

import jax
import jax.numpy as jnp
import numpy as np
from jax import lax
from jax.experimental import pallas as pl
from jax.experimental.pallas import tpu as pltpu
from jax.sharding import Mesh, PartitionSpec as P

STEP_SCALE = 0.5
BETA_ONE = 0.9
BETA_TWO = 0.95
ROPE_BASE = 500000.0
AXES = ("xl", "core", "y", "z", "xh")
SIZES = (2, 2, 8, 8, 2)


def rope_tables(length, head_size):
    exponent = np.arange(head_size // 2, dtype=np.float32) * np.float32(2.0) / head_size
    inverse = np.power(np.float64(ROPE_BASE), -exponent.astype(np.float64)).astype(np.float32)
    angles = np.arange(length, dtype=np.float32)[:, None] * inverse[None, :]
    cosine = np.cos(angles.astype(np.float64)).astype(np.float32)
    sine = np.sin(angles.astype(np.float64)).astype(np.float32)
    return np.concatenate([cosine, cosine], axis=1), np.concatenate([-sine, sine], axis=1)


def rms_rotated(inputs, gain, cosine, sine):
    scale = lax.rsqrt(jnp.mean(inputs * inputs, axis=-1, keepdims=True) + 1e-06)
    scaled = inputs * scale * gain
    return scaled * cosine + pltpu.roll(scaled, scaled.shape[-1] // 2, 1) * sine


def assemble_kernel(place_ref, *refs):
    *blocks, out_ref = refs
    rows, cols = blocks[0].shape[1:]
    half = out_ref.shape[0] // 2
    for step, block in enumerate(blocks):
        row = pl.multiple_of(place_ref[0, step] * rows, 32)
        col = pl.multiple_of(place_ref[1, step] * cols, 128)
        for near in range(2):
            out_ref[pl.ds(near * half + row, rows), pl.ds(col, cols)] = block[near]


def assemble(place, blocks):
    rows, cols = blocks[0].shape[1:]
    vmem = pl.BlockSpec(memory_space=pltpu.VMEM)
    return pl.pallas_call(
        assemble_kernel,
        out_shape=jax.ShapeDtypeStruct((len(blocks) * rows, 2 * cols), blocks[0].dtype),
        in_specs=[pl.BlockSpec(memory_space=pltpu.SMEM)] + [vmem] * len(blocks),
        out_specs=vmem,
        compiler_params=pltpu.CompilerParams(vmem_limit_bytes=24 << 20),
        name="assemble",
    )(place, *blocks)


def attend_kernel(tile, limit_ref, own_ref, got_ref, query_gain_ref, key_gain_ref, cos_ref, sin_ref, out_ref):
    length, head = cos_ref.shape
    heads = query_gain_ref.shape[0]
    wide = heads * head
    limit = limit_ref[0]

    def summed(start, rows, col):
        got = got_ref[start : start + rows, col : col + head].astype(jnp.float32)
        return own_ref[start : start + rows, col : col + head] + got

    key_gain = key_gain_ref[...]
    keys = rms_rotated(summed(0, length, wide), key_gain, cos_ref[...], sin_ref[...])
    keys = keys.astype(jnp.bfloat16)
    values = summed(0, length, wide + head).astype(jnp.bfloat16)
    for start in range(0, length, tile):
        seen = start + tile
        row = start + lax.broadcasted_iota(jnp.int32, (tile, seen), 0)
        col = lax.broadcasted_iota(jnp.int32, (tile, seen), 1)
        allowed = (col <= row) & (col < limit)
        cosine, sine = cos_ref[start:seen, :], sin_ref[start:seen, :]
        for j in range(heads):
            query = rms_rotated(summed(start, tile, j * head), query_gain_ref[j : j + 1, :], cosine, sine)
            query = (query * head**-0.5).astype(jnp.bfloat16)
            scores = lax.dot_general(
                query, keys[:seen], (((1,), (1,)), ((), ())), preferred_element_type=jnp.float32
            )
            scores = jnp.where(allowed, scores, -1e30)
            weights = jnp.exp(scores - jnp.max(scores, axis=-1, keepdims=True))
            weights = weights / jnp.sum(weights, axis=-1, keepdims=True)
            output = jnp.dot(weights.astype(jnp.bfloat16), values[:seen], preferred_element_type=jnp.float32)
            out_ref[start:seen, j * head : (j + 1) * head] = output.astype(out_ref.dtype)


def attend(limit, own, got, query_gain, key_gain):
    length = own.shape[0]
    heads, head = query_gain.shape
    cosine, sine = rope_tables(length, head)
    vmem = pl.BlockSpec(memory_space=pltpu.VMEM)
    return pl.pallas_call(
        functools.partial(attend_kernel, 256),
        out_shape=jax.ShapeDtypeStruct((length, heads * head), jnp.bfloat16),
        in_specs=[pl.BlockSpec(memory_space=pltpu.SMEM)] + [vmem] * 6,
        out_specs=vmem,
        compiler_params=pltpu.CompilerParams(vmem_limit_bytes=40 << 20),
        name="attend",
    )(limit, own, got, query_gain, key_gain, cosine, sine)


def swap(array, axis):
    return lax.ppermute(array, axis, [(0, 1), (1, 0)])


def global_sum(value):
    count = 1
    for size in SIZES:
        count *= size
    spread = jnp.broadcast_to(value, (count, 128))
    return jnp.sum(lax.all_to_all(spread, AXES, 0, 0, tiled=True)[:, 0])


def to_column(block, other):
    pairs = []
    for xl in range(2):
        for y in range(8):
            for slab in range(2):
                target = ((xl ^ other) * 8 + (y + 2 * slab) % 8) * 2 + (y >> 1) % 2
                pairs.append(((xl * 8 + y) * 2 + slab, target))
    return lax.ppermute(block, ("xl", "y", "xh"), pairs)


def along(array, axis, step):
    size = lax.axis_size(axis)
    return lax.ppermute(array, axis, [(i, (i + step) % size) for i in range(size)])


def shards(
    activations, norm_gain, master_weight, grad, moment, variance, query_gain, key_gain, prompt_len
):
    xl, core, y, z, xh = (lax.axis_index(a) for a in AXES)
    width_all = norm_gain.shape[0]
    seq_rows, width_part = activations.shape
    slab_rows, _, slab_heads, head_size = grad.shape
    head_dev = slab_heads - 1
    query_cols = head_dev * head_size
    slab_cols = slab_heads * head_size

    gathered = lax.all_gather(activations, "z", axis=1, tiled=True)

    grad_local = grad.astype(jnp.float32)
    sumsq = global_sum(jnp.sum(grad_local * grad_local))
    clip_factor = 1.0 / jnp.sqrt(sumsq + 1e-12)
    clipped = grad_local * clip_factor
    moment_new = BETA_ONE * moment + (1.0 - BETA_ONE) * clipped
    variance_new = BETA_TWO * variance + (1.0 - BETA_TWO) * clipped * clipped
    step_size = STEP_SCALE * width_all ** (-0.5)
    updated = (master_weight - step_size * moment_new / (jnp.sqrt(variance_new) + 1e-08)).astype(
        jnp.bfloat16
    )
    updated = updated.reshape(slab_rows, slab_cols)

    home = jnp.stack([to_column(updated, 0), to_column(updated, 1)])
    arrived = {0: home}
    up = down = home
    up = arrived[1] = along(up, "y", 1)
    down = arrived[7] = along(down, "y", -1)
    up = arrived[2] = along(up, "y", 1)
    down = arrived[6] = along(down, "y", -1)
    gathered, up, down = lax.optimization_barrier((gathered, up, down))

    widened = gathered.astype(jnp.float32)
    square = jnp.sum(widened * widened, axis=-1)
    square = square + swap(square, "xh")
    row_scale = lax.rsqrt(square / width_all + 1e-06)
    gain = lax.dynamic_index_in_dim(norm_gain.reshape(8, 2, width_part), xh, 1, False).reshape(-1)
    normed = (widened * row_scale[:, None] * gain).astype(jnp.bfloat16)

    up = arrived[3] = along(up, "y", 1)
    down = arrived[5] = along(down, "y", -1)
    normed, up = lax.optimization_barrier((normed, up))
    arrived[4] = along(up, "y", 1)

    source = (y - jnp.arange(8)) & 7
    native = ((source >> 1) & 1) == xh
    shifted = (source - 2) & 7
    origin = jnp.where(native, source, shifted)
    place = jnp.stack([(origin >> 2) * 2 + (origin & 1), jnp.where(native, 0, 1)]).astype(jnp.int32)
    own_weight = assemble(place, [arrived[step] for step in range(8)])
    other_weight = swap(own_weight, "core")

    quarter = normed.shape[1] // 4

    def matching(lane):
        near = lax.dynamic_slice_in_dim(normed, (xl * 2 + lane) * quarter, quarter, 1)
        far = lax.dynamic_slice_in_dim(normed, (2 - xl * 2 + lane) * quarter, quarter, 1)
        return jnp.concatenate([near, far], axis=1)

    partial = jnp.dot(matching(core), own_weight, preferred_element_type=jnp.float32)
    partial += jnp.dot(matching(1 - core), other_weight, preferred_element_type=jnp.float32)

    def picked(slab):
        queries = lax.dynamic_slice_in_dim(partial, slab * slab_cols, query_cols, 1)
        return jnp.concatenate([queries, partial[:, query_cols:slab_cols], partial[:, slab_cols + query_cols :]], axis=1)

    got = swap(picked(1 - xh).astype(jnp.bfloat16), "xh")
    gain_row = lax.dynamic_slice_in_dim(key_gain, z, 1, 0)
    return attend(prompt_len, picked(xh), got, query_gain, gain_row)


def solution(mesh):
    fine = Mesh(mesh.devices.reshape(SIZES), AXES)
    rows, cols = ("xl", "core", "y"), ("z", "xh")
    slab = P(rows, cols, None, None)
    in_specs = (P(rows, cols), P(), slab, slab, slab, slab, P(cols, None), P(), P(rows))
    return jax.shard_map(
        shards, mesh=fine, in_specs=in_specs, out_specs=P(rows, cols), check_vma=False
    )
```

time: 208 us -> 172 us (0.83)
  waiting for transfers between devices: 78.4 us -> 34.8 us
  starting transfers between devices: 31.5 us -> 48.2 us
  matrix products: 18 us -> 5.13 us
  other arithmetic: 20.1 us -> 13.2 us
  local copies, waits for them, and re-layouts: 4.81 us -> 10.5 us
  Pallas kernels: 0 us -> 5.6 us
    ppermute x3, waiting for transfers between devices: 43.1 us -> 15.5 us  [swap(): return lax.ppermute(array, axis, [(0, 1), (1, 0)])]
    ppermute x8 -> x9, waiting for transfers between devices: 34.6 us -> 18.6 us  [the longest x7 15.5 us: along(): lax.ppermute(array, axis, [(i, (i + step) % size) for i in range(size)])]
    ppermute x8 -> x9, starting transfers between devices: 25.5 us -> 34.8 us  [the longest x7 31.9 us: along(): lax.ppermute(array, axis, [(i, (i + step) % size) for i in range(size)])]
    dot_general x3 -> x2, matrix products: 12.8 us -> 5.13 us  [the longest x1 3.32 us: shards(): jnp.dot(matching(1 - core), other_weight, preferred_element_type=jnp.floa...]
    ppermute x3, starting transfers between devices: 5.94 us -> 13.4 us  [swap(): return lax.ppermute(array, axis, [(0, 1), (1, 0)])]
    pallas_call x0 -> x2, Pallas kernels: none -> 5.6 us  [the longest x1 4.87 us: attend(): pl.pallas_call(functools.partial(attend_kernel, 256), out_shape=jax.Shape...]
    sub x1 -> x0, matrix products: 5.19 us -> none  [shards(): weights = jnp.exp(scores - highest)]
    unnamed x16 -> x21, local copies, waits for them, and re-layouts: 1.15 us -> 4.61 us
  transfers between devices with their start and end apart: 14 -> 13, of which waited for: 6 -> 7; matrix products, arithmetic and copies ran while one was open for 11% -> 9% of each run, Pallas kernels for 0% -> 0%
where the time goes in v2:
time: 172 us; the launch traced here: 171 us
  starting transfers between devices  48.2 us (28%)
  blocking collectives  38.9 us (23%)
  waiting for transfers between devices  34.8 us (20%)
  between operations  15.1 us (9%)
  other arithmetic  13.2 us (8%)
  local copies, waits for them, and re-layouts  10.5 us (6%)
  Pallas kernels  5.6 us (3%)
  matrix products  5.13 us (3%)
    all_to_all x1, blocking collectives, global_sum(): return jnp.sum(lax.all_to_all(spread, AXES, 0, 0, tiled=True)[:, 0])  38.9 us
    ppermute x7, starting transfers between devices, along(): lax.ppermute(array, axis, [(i, (i + step) % size) for i in range(size)])  31.9 us
    ppermute x7, waiting for transfers between devices, along(): lax.ppermute(array, axis, [(i, (i + step) % size) for i in range(size)])  15.5 us
    ppermute x3, waiting for transfers between devices, swap(): return lax.ppermute(array, axis, [(0, 1), (1, 0)])  15.5 us
    ppermute x3, starting transfers between devices, swap(): return lax.ppermute(array, axis, [(0, 1), (1, 0)])  13.4 us
    pallas_call x1, Pallas kernels, attend(): pl.pallas_call(functools.partial(attend_kernel, 256), out_shape=jax.Shape...  4.87 us
    unnamed x21, local copies, waits for them, and re-layouts  4.61 us
    convert_element_type x1, other arithmetic, shards(): normed = (widened * row_scale[:, None] * gain).astype(jnp.bfloat16)  4.08 us
  transfers between devices with their start and end apart: 13, of which 7 were waited for; matrix products, arithmetic and copies ran while one was open for 9% of the time, Pallas kernels for 0%

profile of v2, /device:TPU:1, one launch (start us, length us, event | category | flops | bytes accessed | tf_op | source)
XLA Modules:
  0.0 171.3 jit_solution(13504654138764492165)
XLA Ops:
  6.5 0.7 all-gather.2.cloned.1.call-update
  7.3 2.0 %multiply_reduce_fusion = f32[]{:T(128)} fusion(bf16[160,1,3,128]{3,0,2,1:T(8,128)(2,1)} %param.14), kind=kLoop, calls=%fused_computation.23 | loop fusion | flops 184319 | bytes 122884 | tf_op jit(solution)/shard_map/reduce_sum | solution.py:147
  9.3 0.8 broadcast_in_dim.10
  10.1 38.9 %all_to_all.9 = f32[512,1,128]{2,1,0:T(1,128)S(1)} all-to-all(f32[512,1,128]{2,1,0:T(1,128)S(1)} %broadcast_in_dim.10), channel_id=1, replica_groups=mesh['xl'=2,'core'=2,'y'=8,'z'=8,'xh'=2] {'xl','core','y','z','xh'}, dimensions={0} | all-to-all | bytes 524288 | tf_op jit(solution)/shard_map/all_to_all | solution.py:115
  48.9 0.7 slice_reduce_fusion
  50.3 3.2 %convert_reduce_fusion = bf16[160,3,128]{2,1,0:T(4,128)(2,1)S(1)} fusion(f32[160,1,3,128]{3,1,2,0:T(1,128)} %param.13, f32[160,1,3,128]{3,1,2,0:T(1,128)} %param.16, f32[160,1,3,128]{3,1,2,0:T(1,128)} %param.15, bf16[160,1,3,128]{3,0,2,1:T(8,128)(2,1)} %param.14, f32[]{:T(128)S(6)} %sqrt.6), kind=kLoop, calls=%fused_computation.22 | loop fusion | flops 860160 | bytes 983044 | tf_op jit(solution)/shard_map/convert_element_type | solution.py:153
  53.5 0.0 copy-start.9
  53.6 2.2 %collective-permute-start.1 = (bf16[160,384]{1,0:T(8,128)(2,1)S(1)}, bf16[160,384]{1,0:T(8,128)(2,1)S(1)}, u32[]{:S(2)}, u32[]{:S(2)}) collective-permute-start(bf16[160,384]{1,0:T(8,128)(2,1)S(1)} %bitcast.11), channel_id=1, source_target_pairs={{0,256},{1,288},{16,272},{17,304},{32,289},{33,321},{48,305},{49,3... | collective-permute-start | bytes 368648 | tf_op jit(solution)/shard_map/ppermute | solution.py:125
  55.8 0.7 collective-permute-start
  56.5 3.1 %collective-permute-done.1 = bf16[160,384]{1,0:T(8,128)(2,1)S(1)} collective-permute-done((bf16[160,384]{1,0:T(8,128)(2,1)S(1)}, bf16[160,384]{1,0:T(8,128)(2,1)S(1)}, u32[]{:S(2)}, u32[]{:S(2)}) %collective-permute-start.1) | collective-permute-done | bytes 122912 | tf_op jit(solution)/shard_map/ppermute | solution.py:125
  59.6 14.4 %collective-permute-start.4 = (bf16[2,160,384]{2,1,0:T(8,128)(2,1)S(1)}, bf16[2,160,384]{2,1,0:T(8,128)(2,1)S(1)}, u32[]{:S(2)}, u32[]{:S(2)}) collective-permute-start(bf16[2,160,384]{2,1,0:T(8,128)(2,1)S(1)} %pad_maximum_fusion.2.refs_0_), channel_id=1, source_target_pairs={{0,112},{16,0},{32,16},{48,32},{64,48},{80,64},{96,80},{112,96},{1... | collective-permute-start | bytes 737288 | tf_op jit(solution)/shard_map/ppermute | solution.py:130
  74.0 1.9 %collective-permute-start.2 = (bf16[2,160,384]{2,1,0:T(8,128)(2,1)S(1)}, bf16[2,160,384]{2,1,0:T(8,128)(2,1)S(1)}, u32[]{:S(2)}, u32[]{:S(2)}) collective-permute-start(bf16[2,160,384]{2,1,0:T(8,128)(2,1)S(1)} %pad_maximum_fusion.2.refs_0_), channel_id=1, source_target_pairs={{0,16},{16,32},{32,48},{48,64},{64,80},{80,96},{96,112},{112,0},{1... | collective-permute-start | bytes 737288 | tf_op jit(solution)/shard_map/ppermute | solution.py:130
  76.0 2.9 %collective-permute-done.4.refs_7_ = bf16[2,160,384]{2,1,0:T(8,128)(2,1)S(1)} collective-permute-done((bf16[2,160,384]{2,1,0:T(8,128)(2,1)S(1)}, bf16[2,160,384]{2,1,0:T(8,128)(2,1)S(1)}, u32[]{:S(2)}, u32[]{:S(2)}) %collective-permute-start.4) | collective-permute-done | bytes 245792 | tf_op jit(solution)/shard_map/ppermute | solution.py:130
  78.9 5.3 %collective-permute-start.5 = (bf16[2,160,384]{2,1,0:T(8,128)(2,1)S(1)}, bf16[2,160,384]{2,1,0:T(8,128)(2,1)S(1)}, u32[]{:S(2)}, u32[]{:S(2)}) collective-permute-start(bf16[2,160,384]{2,1,0:T(8,128)(2,1)S(1)} %collective-permute-done.4.refs_7_), channel_id=1, source_target_pairs={{0,112},{16,0},{32,16},{48,32},{64,48},{80,64},{96,80},{112,96},{1... | collective-permute-start | bytes 737288 | tf_op jit(solution)/shard_map/ppermute | solution.py:130
  84.2 1.9 %collective-permute-start.3 = (bf16[2,160,384]{2,1,0:T(8,128)(2,1)S(1)}, bf16[2,160,384]{2,1,0:T(8,128)(2,1)S(1)}, u32[]{:S(2)}, u32[]{:S(2)}) collective-permute-start(bf16[2,160,384]{2,1,0:T(8,128)(2,1)S(1)} %collective-permute-done.2.refs_1_), channel_id=1, source_target_pairs={{0,16},{16,32},{32,48},{48,64},{64,80},{80,96},{96,112},{112,0},{1... | collective-permute-start | bytes 737288 | tf_op jit(solution)/shard_map/ppermute | solution.py:130
  86.1 2.0 %collective-permute-done.5.refs_6_ = bf16[2,160,384]{2,1,0:T(8,128)(2,1)S(1)} collective-permute-done((bf16[2,160,384]{2,1,0:T(8,128)(2,1)S(1)}, bf16[2,160,384]{2,1,0:T(8,128)(2,1)S(1)}, u32[]{:S(2)}, u32[]{:S(2)}) %collective-permute-start.5) | collective-permute-done | bytes 245792 | tf_op jit(solution)/shard_map/ppermute | solution.py:130
  88.1 5.1 %collective-permute-done.3.refs_2_ = bf16[2,160,384]{2,1,0:T(8,128)(2,1)S(1)} collective-permute-done((bf16[2,160,384]{2,1,0:T(8,128)(2,1)S(1)}, bf16[2,160,384]{2,1,0:T(8,128)(2,1)S(1)}, u32[]{:S(2)}, u32[]{:S(2)}) %collective-permute-start.3) | collective-permute-done | bytes 245792 | tf_op jit(solution)/shard_map/ppermute | solution.py:130
  93.2 3.0 %fusion = f32[768]{0:T(1024)S(1)} fusion(bf16[768,2560]{0,1:T(8,128)(2,1)} %all-gather.2.cloned.1.call-done), kind=kLoop, calls=%fused_computation.2 | loop fusion | flops 5897472 | bytes 3935232 | tf_op jit(solution)/shard_map/reduce_sum | solution.py:168
  96.2 1.9 %collective-permute-start.6 = (f32[768]{0:T(1024)S(1)}, f32[768]{0:T(1024)S(1)}, u32[]{:S(2)}, u32[]{:S(2)}) collective-permute-start(f32[768]{0:T(1024)S(1)} %fusion), channel_id=1, source_target_pairs={{0,1},{1,0},{2,3},{3,2},{4,5},{5,4},{6,7},{7,6},{8,9},{9,8},{10,11... | collective-permute-start | bytes 9224 | tf_op jit(solution)/shard_map/ppermute | solution.py:107
  98.1 0.1 reshape.56
  98.2 0.1 mul.114
  98.3 1.9 %collective-permute-start.7 = (bf16[2,160,384]{2,1,0:T(8,128)(2,1)S(1)}, bf16[2,160,384]{2,1,0:T(8,128)(2,1)S(1)}, u32[]{:S(2)}, u32[]{:S(2)}) collective-permute-start(bf16[2,160,384]{2,1,0:T(8,128)(2,1)S(1)} %collective-permute-done.3.refs_2_), channel_id=1, source_target_pairs={{0,16},{16,32},{32,48},{48,64},{64,80},{80,96},{96,112},{112,0},{1... | collective-permute-start | bytes 737288 | tf_op jit(solution)/shard_map/ppermute | solution.py:130
  100.2 4.6 %collective-permute-start.9 = (bf16[2,160,384]{2,1,0:T(8,128)(2,1)S(1)}, bf16[2,160,384]{2,1,0:T(8,128)(2,1)S(1)}, u32[]{:S(2)}, u32[]{:S(2)}) collective-permute-start(bf16[2,160,384]{2,1,0:T(8,128)(2,1)S(1)} %collective-permute-done.5.refs_6_), channel_id=1, source_target_pairs={{0,112},{16,0},{32,16},{48,32},{64,48},{80,64},{96,80},{112,96},{1... | collective-permute-start | bytes 737288 | tf_op jit(solution)/shard_map/ppermute | solution.py:130
  104.8 4.1 %fusion.2 = bf16[768,2560]{0,1:T(8,128)(2,1)} fusion(bf16[768,2560]{0,1:T(8,128)(2,1)} %all-gather.2.cloned.1.call-done, f32[2560]{0:T(1024)S(1)} %mul.114, f32[768]{0:T(1024)S(1)} %add_rsqrt_fusion), kind=kLoop, calls=%fused_computation.4 | loop fusion | flops 7864320 | bytes 7877632 | tf_op jit(solution)/shard_map/convert_element_type | solution.py:172
  108.9 1.9 %collective-permute-start.8 = (bf16[2,160,384]{2,1,0:T(8,128)(2,1)S(1)}, bf16[2,160,384]{2,1,0:T(8,128)(2,1)S(1)}, u32[]{:S(2)}, u32[]{:S(2)}) collective-permute-start(bf16[2,160,384]{2,1,0:T(8,128)(2,1)S(1)} %collective-permute-done.7.refs_3_), channel_id=1, source_target_pairs={{0,16},{16,32},{32,48},{48,64},{64,80},{80,96},{96,112},{112,0},{1... | collective-permute-start | bytes 737288 | tf_op jit(solution)/shard_map/ppermute | solution.py:130
  110.9 0.7 copy-done.3
  111.6 5.5 %collective-permute-done.8.refs_4_ = bf16[2,160,384]{2,1,0:T(8,128)(2,1)S(1)} collective-permute-done((bf16[2,160,384]{2,1,0:T(8,128)(2,1)S(1)}, bf16[2,160,384]{2,1,0:T(8,128)(2,1)S(1)}, u32[]{:S(2)}, u32[]{:S(2)}) %collective-permute-start.8) | collective-permute-done | bytes 245792 | tf_op jit(solution)/shard_map/ppermute | solution.py:130
  117.1 0.7 copy-done.5
  117.8 0.9 copy-done.4
  118.7 0.9 copy-done.6
  119.7 0.7 assemble.1
  120.4 6.3 %collective-permute-start.10 = (bf16[1280,768]{1,0:T(8,128)(2,1)S(1)}, bf16[1280,768]{1,0:T(8,128)(2,1)}, u32[]{:S(2)}, u32[]{:S(2)}) collective-permute-start(bf16[1280,768]{1,0:T(8,128)(2,1)S(1)} %assemble.1), channel_id=1, source_target_pairs={{0,128},{128,0},{1,129},{129,1},{2,130},{130,2},{3,131},{131,3},{4... | collective-permute-start | bytes 5898248 | tf_op jit(solution)/shard_map/ppermute | solution.py:107
  126.7 2.4 %constant_dynamic-slice_fusion.5 = (bf16[768,640]{0,1:T(8,128)(2,1)S(1)}, bf16[768,640]{0,1:T(8,128)(2,1)S(1)}, bf16[768,640]{0,1:T(8,128)(2,1)S(1)}, bf16[768,640]{0,1:T(8,128)(2,1)S(1)}) fusion(bf16[768,2560]{0,1:T(8,128)(2,1)} %fusion.2, s32[]{:T(128)S(6)} %select_n.48, s32[]{:T(128)S(6)} %select_n.53, s32[]{:T(128)S(6)} %select_n.52, s32[]{:T(128)S(6)} %select_n.49), kind=kLoop, calls=%fused_computation.32 | loop fusion | bytes 7864336 | tf_op jit(solution)/shard_map/dynamic_slice | solution.py:190
  129.1 1.2 collective-permute-done.10
  130.2 3.3 %fusion.7 = f32[768,768]{1,0:T(8,128)S(1)} fusion(bf16[1280,768]{1,0:T(8,128)(2,1)} %collective-permute-done.10, bf16[768,640]{0,1:T(8,128)(2,1)S(1)} %get-tuple-element.16, bf16[768,640]{0,1:T(8,128)(2,1)S(1)} %get-tuple-element.17), kind=kOutput, calls=%fused_computation.9 | convolution fusion | flops 1513881600 | bytes 6291456 | tf_op jit(solution)/shard_map/dot_general | solution.py:195
  133.5 1.8 %fusion.11 = f32[768,768]{1,0:T(8,128)S(1)} fusion(f32[768,768]{1,0:T(8,128)S(1)} %fusion.7, bf16[1280,768]{1,0:T(8,128)(2,1)S(1)} %assemble.1, bf16[768,640]{0,1:T(8,128)(2,1)S(1)} %get-tuple-element.18, bf16[768,640]{0,1:T(8,128)(2,1)S(1)} %get-tuple-element.15), kind=kOutput, calls=%fused_computation.14 | convolution fusion | flops 1514471424 | bytes 8650752 | tf_op jit(solution)/shard_map/dot_general | solution.py:194
  135.4 0.1 fusion.17
  135.5 1.3 copy-done.8
  136.8 0.1 pad_maximum_fusion.1
  136.9 5.1 %collective-permute-start.11 = (bf16[768,512]{1,0:T(8,128)(2,1)S(1)}, bf16[768,512]{1,0:T(8,128)(2,1)S(1)}, u32[]{:S(2)}, u32[]{:S(2)}) collective-permute-start(bf16[768,512]{1,0:T(8,128)(2,1)S(1)} %pad_maximum_fusion.1), channel_id=1, source_target_pairs={{0,1},{1,0},{2,3},{3,2},{4,5},{5,4},{6,7},{7,6},{8,9},{9,8},{10,11... | collective-permute-start | bytes 2359304 | tf_op jit(solution)/shard_map/ppermute | solution.py:107
  142.7 1.2 constant_dynamic-slice_fusion.1
  143.9 0.0 copy-start.1
  143.9 0.0 copy-start.2
  143.9 0.0 copy-start.7
  143.9 1.2 fusion.18
  145.2 0.1 pad_maximum_fusion.own_ref
  145.3 14.3 %collective-permute-done.11.got_ref = bf16[768,512]{1,0:T(8,128)(2,1)S(1)} collective-permute-done((bf16[768,512]{1,0:T(8,128)(2,1)S(1)}, bf16[768,512]{1,0:T(8,128)(2,1)S(1)}, u32[]{:S(2)}, u32[]{:S(2)}) %collective-permute-start.11) | collective-permute-done | bytes 786464 | tf_op jit(solution)/shard_map/ppermute | solution.py:107
  159.6 4.9 %attend.1 = bf16[768,256]{1,0:T(8,128)(2,1)} custom-call(s32[1]{0:T(128)S(6)} %copy.33.limit_ref, f32[768,512]{1,0:T(8,128)S(1)} %pad_maximum_fusion.own_ref, bf16[768,512]{1,0:T(8,128)(2,1)S(1)} %collective-permute-done.11.got_ref, f32[2,128]{1,0:T(2,128)S(1)} %copy-done.7, f32[1,128]{1,0:T(1,128)S(1)} %constant_dynamic-slice_fusion.key_gain_ref, ...), custom_call_target="tpu_custom_call" | custom-call | tf_op jit(solution)/shard_map/attend/pallas_call | solution.py:96
  (26 shorter events, 0.2 us)
Async XLA Ops:
  6.5 136.1 %copy-start = (f32[8,128]{1,0:T(8,128)S(1)}, f32[8,128]{1,0:T(8,128)}, u32[]{:S(2)}) copy-start(f32[8,128]{1,0:T(8,128)} %param.18) | copy-start | bytes 12292
  6.5 86.7 %all-gather.2.cloned.1.call-start = ((), (), s32[]{:S(2)}) async-start(), calls=%async_computation.1 | async-start | bytes 4423680 | tf_op jit(solution)/shard_map/all_gather | solution.py:144
  53.5 44.6 %copy-start.9 = (f32[5120]{0:T(1024)S(1)}, f32[5120]{0:T(1024)}, u32[]{:S(2)}) copy-start(f32[5120]{0:T(1024)} %param.12) | copy-start | bytes 61444
  53.6 6.0 %collective-permute-start.1 = (bf16[160,384]{1,0:T(8,128)(2,1)S(1)}, bf16[160,384]{1,0:T(8,128)(2,1)S(1)}, u32[]{:S(2)}, u32[]{:S(2)}) collective-permute-start(bf16[160,384]{1,0:T(8,128)(2,1)S(1)} %bitcast.11), channel_id=1, source_target_pairs={{0,256},{1,288},{16,272},{17,304},{32,289},{33,321},{48,305},{49,3... | collective-permute-start | bytes 368648 | tf_op jit(solution)/shard_map/ppermute | solution.py:125
  55.8 3.8 %collective-permute-start = (bf16[160,384]{1,0:T(8,128)(2,1)S(1)}, bf16[160,384]{1,0:T(8,128)(2,1)S(1)}, u32[]{:S(2)}, u32[]{:S(2)}) collective-permute-start(bf16[160,384]{1,0:T(8,128)(2,1)S(1)} %bitcast.12), channel_id=1, source_target_pairs={{0,0},{1,32},{16,16},{17,48},{32,33},{33,65},{48,49},{49,81},{64,6... | collective-permute-start | bytes 368648 | tf_op jit(solution)/shard_map/ppermute | solution.py:125
  59.6 19.3 %collective-permute-start.4 = (bf16[2,160,384]{2,1,0:T(8,128)(2,1)S(1)}, bf16[2,160,384]{2,1,0:T(8,128)(2,1)S(1)}, u32[]{:S(2)}, u32[]{:S(2)}) collective-permute-start(bf16[2,160,384]{2,1,0:T(8,128)(2,1)S(1)} %pad_maximum_fusion.2.refs_0_), channel_id=1, source_target_pairs={{0,112},{16,0},{32,16},{48,32},{64,48},{80,64},{96,80},{112,96},{1... | collective-permute-start | bytes 737288 | tf_op jit(solution)/shard_map/ppermute | solution.py:130
  74.0 10.2 %collective-permute-start.2 = (bf16[2,160,384]{2,1,0:T(8,128)(2,1)S(1)}, bf16[2,160,384]{2,1,0:T(8,128)(2,1)S(1)}, u32[]{:S(2)}, u32[]{:S(2)}) collective-permute-start(bf16[2,160,384]{2,1,0:T(8,128)(2,1)S(1)} %pad_maximum_fusion.2.refs_0_), channel_id=1, source_target_pairs={{0,16},{16,32},{32,48},{48,64},{64,80},{80,96},{96,112},{112,0},{1... | collective-permute-start | bytes 737288 | tf_op jit(solution)/shard_map/ppermute | solution.py:130
  78.9 9.3 %collective-permute-start.5 = (bf16[2,160,384]{2,1,0:T(8,128)(2,1)S(1)}, bf16[2,160,384]{2,1,0:T(8,128)(2,1)S(1)}, u32[]{:S(2)}, u32[]{:S(2)}) collective-permute-start(bf16[2,160,384]{2,1,0:T(8,128)(2,1)S(1)} %collective-permute-done.4.refs_7_), channel_id=1, source_target_pairs={{0,112},{16,0},{32,16},{48,32},{64,48},{80,64},{96,80},{112,96},{1... | collective-permute-start | bytes 737288 | tf_op jit(solution)/shard_map/ppermute | solution.py:130
  84.2 9.0 %collective-permute-start.3 = (bf16[2,160,384]{2,1,0:T(8,128)(2,1)S(1)}, bf16[2,160,384]{2,1,0:T(8,128)(2,1)S(1)}, u32[]{:S(2)}, u32[]{:S(2)}) collective-permute-start(bf16[2,160,384]{2,1,0:T(8,128)(2,1)S(1)} %collective-permute-done.2.refs_1_), channel_id=1, source_target_pairs={{0,16},{16,32},{32,48},{48,64},{64,80},{80,96},{96,112},{112,0},{1... | collective-permute-start | bytes 737288 | tf_op jit(solution)/shard_map/ppermute | solution.py:130
  96.2 8.7 %collective-permute-start.6 = (f32[768]{0:T(1024)S(1)}, f32[768]{0:T(1024)S(1)}, u32[]{:S(2)}, u32[]{:S(2)}) collective-permute-start(f32[768]{0:T(1024)S(1)} %fusion), channel_id=1, source_target_pairs={{0,1},{1,0},{2,3},{3,2},{4,5},{5,4},{6,7},{7,6},{8,9},{9,8},{10,11... | collective-permute-start | bytes 9224 | tf_op jit(solution)/shard_map/ppermute | solution.py:107
  98.3 10.6 %collective-permute-start.7 = (bf16[2,160,384]{2,1,0:T(8,128)(2,1)S(1)}, bf16[2,160,384]{2,1,0:T(8,128)(2,1)S(1)}, u32[]{:S(2)}, u32[]{:S(2)}) collective-permute-start(bf16[2,160,384]{2,1,0:T(8,128)(2,1)S(1)} %collective-permute-done.3.refs_2_), channel_id=1, source_target_pairs={{0,16},{16,32},{32,48},{48,64},{64,80},{80,96},{96,112},{112,0},{1... | collective-permute-start | bytes 737288 | tf_op jit(solution)/shard_map/ppermute | solution.py:130
  100.2 10.7 %collective-permute-start.9 = (bf16[2,160,384]{2,1,0:T(8,128)(2,1)S(1)}, bf16[2,160,384]{2,1,0:T(8,128)(2,1)S(1)}, u32[]{:S(2)}, u32[]{:S(2)}) collective-permute-start(bf16[2,160,384]{2,1,0:T(8,128)(2,1)S(1)} %collective-permute-done.5.refs_6_), channel_id=1, source_target_pairs={{0,112},{16,0},{32,16},{48,32},{64,48},{80,64},{96,80},{112,96},{1... | collective-permute-start | bytes 737288 | tf_op jit(solution)/shard_map/ppermute | solution.py:130
  108.9 8.1 %collective-permute-start.8 = (bf16[2,160,384]{2,1,0:T(8,128)(2,1)S(1)}, bf16[2,160,384]{2,1,0:T(8,128)(2,1)S(1)}, u32[]{:S(2)}, u32[]{:S(2)}) collective-permute-start(bf16[2,160,384]{2,1,0:T(8,128)(2,1)S(1)} %collective-permute-done.7.refs_3_), channel_id=1, source_target_pairs={{0,16},{16,32},{32,48},{48,64},{64,80},{80,96},{96,112},{112,0},{1... | collective-permute-start | bytes 737288 | tf_op jit(solution)/shard_map/ppermute | solution.py:130
  110.9 0.7 copy-start.3
  117.1 0.7 copy-start.5
  117.8 0.9 copy-start.4
  118.7 0.9 copy-start.6
  120.4 9.8 %collective-permute-start.10 = (bf16[1280,768]{1,0:T(8,128)(2,1)S(1)}, bf16[1280,768]{1,0:T(8,128)(2,1)}, u32[]{:S(2)}, u32[]{:S(2)}) collective-permute-start(bf16[1280,768]{1,0:T(8,128)(2,1)S(1)} %assemble.1), channel_id=1, source_target_pairs={{0,128},{128,0},{1,129},{129,1},{2,130},{130,2},{3,131},{131,3},{4... | collective-permute-start | bytes 5898248 | tf_op jit(solution)/shard_map/ppermute | solution.py:107
  135.4 1.4 copy-start.8
  136.9 22.8 %collective-permute-start.11 = (bf16[768,512]{1,0:T(8,128)(2,1)S(1)}, bf16[768,512]{1,0:T(8,128)(2,1)S(1)}, u32[]{:S(2)}, u32[]{:S(2)}) collective-permute-start(bf16[768,512]{1,0:T(8,128)(2,1)S(1)} %pad_maximum_fusion.1), channel_id=1, source_target_pairs={{0,1},{1,0},{2,3},{3,2},{4,5},{5,4},{6,7},{7,6},{8,9},{9,8},{10,11... | collective-permute-start | bytes 2359304 | tf_op jit(solution)/shard_map/ppermute | solution.py:107
  143.9 15.7 %copy-start.1 = (f32[768,128]{1,0:T(8,128)S(1)}, f32[768,128]{1,0:T(8,128)}, u32[]{:S(2)}) copy-start(f32[768,128]{1,0:T(8,128)} %constant.72.clone.sin_ref) | copy-start | bytes 1179652
  143.9 15.7 %copy-start.2 = (f32[768,128]{1,0:T(8,128)S(1)}, f32[768,128]{1,0:T(8,128)}, u32[]{:S(2)}) copy-start(f32[768,128]{1,0:T(8,128)} %constant.71.clone.cos_ref) | copy-start | bytes 1179652
  143.9 15.7 %copy-start.7 = (f32[2,128]{1,0:T(2,128)S(1)}, f32[2,128]{1,0:T(2,128)}, u32[]{:S(2)}) copy-start(f32[2,128]{1,0:T(2,128)} %query_gain_ref.1) | copy-start | bytes 3076
Sparse Core Ops, SparseCore 0:
  9.4 66.8 all-gather.1

commit v3 on v2

v3 whole, which is shorter than its diff:
```python
import functools

import jax
import jax.numpy as jnp
import numpy as np
from jax import lax
from jax.experimental import pallas as pl
from jax.experimental.pallas import tpu as pltpu
from jax.sharding import Mesh, PartitionSpec as P

STEP_SCALE = 0.5
BETA_ONE = 0.9
BETA_TWO = 0.95
ROPE_BASE = 500000.0
AXES = ("xl", "core", "y", "z", "xh")
SIZES = (2, 2, 8, 8, 2)


def rope_tables(length, head_size):
    exponent = np.arange(head_size // 2, dtype=np.float32) * np.float32(2.0) / head_size
    inverse = np.power(np.float64(ROPE_BASE), -exponent.astype(np.float64)).astype(np.float32)
    angles = np.arange(length, dtype=np.float32)[:, None] * inverse[None, :]
    cosine = np.cos(angles.astype(np.float64)).astype(np.float32)
    sine = np.sin(angles.astype(np.float64)).astype(np.float32)
    return np.concatenate([cosine, cosine], axis=1), np.concatenate([-sine, sine], axis=1)


def rms_rotated(inputs, gain, cosine, sine):
    scale = lax.rsqrt(jnp.mean(inputs * inputs, axis=-1, keepdims=True) + 1e-06)
    scaled = inputs * scale * gain
    return scaled * cosine + pltpu.roll(scaled, scaled.shape[-1] // 2, 1) * sine


VMEM = pl.BlockSpec(memory_space=pltpu.VMEM)
SMEM = pl.BlockSpec(memory_space=pltpu.SMEM)


def local_call(kernel, name, out_shape, in_specs, out_specs):
    params = pltpu.CompilerParams(vmem_limit_bytes=40 << 20)
    return pl.pallas_call(
        kernel, out_shape=out_shape, in_specs=in_specs, out_specs=out_specs, compiler_params=params, name=name
    )


def assemble_kernel(place_ref, *refs):
    *blocks, out_ref = refs
    rows, cols = blocks[0].shape[1:]
    half = out_ref.shape[0] // 2
    head = out_ref.shape[1] // 6
    wide = cols - head
    for step, block in enumerate(blocks):
        row = pl.multiple_of(place_ref[0, step] * rows, 32)
        query_col = pl.multiple_of(place_ref[1, step] * wide, 128)
        pair_col = pl.multiple_of(2 * wide + place_ref[2, step] * head, 128)
        for near in range(2):
            span = pl.ds(near * half + row, rows)
            out_ref[span, pl.ds(query_col, wide)] = block[near, :, :wide]
            out_ref[span, pl.ds(pair_col, head)] = block[near, :, wide:]


def assemble(place, blocks):
    rows, cols = blocks[0].shape[1:]
    shape = jax.ShapeDtypeStruct((len(blocks) * rows, 2 * cols), blocks[0].dtype)
    call = local_call(assemble_kernel, "assemble", shape, [SMEM] + [VMEM] * len(blocks), VMEM)
    return call(place, *blocks)


def squares_kernel(*refs):
    *blocks, out_ref = refs
    total = None
    for block in blocks:
        wide = block[...].astype(jnp.float32)
        square = jnp.sum(wide * wide, axis=0, keepdims=True)
        total = square if total is None else total + square
    out_ref[...] = total


def squares(blocks):
    shape = jax.ShapeDtypeStruct((1, blocks[0].shape[1]), jnp.float32)
    return local_call(squares_kernel, "squares", shape, [VMEM] * len(blocks), VMEM)(*blocks)


def normalise_kernel(width_all, place_ref, square_ref, other_ref, gain_ref, *refs):
    *blocks, out_ref = refs
    rows = blocks[0].shape[0]
    scale = lax.rsqrt((square_ref[...] + other_ref[...]) / width_all + 1e-06)
    for step, block in enumerate(blocks):
        row = pl.multiple_of(place_ref[step] * rows, 64)
        gain = gain_ref[step * rows : (step + 1) * rows, :]
        out_ref[pl.ds(row, rows), :] = (block[...].astype(jnp.float32) * scale * gain).astype(out_ref.dtype)


def normalise(width_all, place, square, other, gain, blocks):
    rows, cols = blocks[0].shape
    shape = jax.ShapeDtypeStruct((len(blocks) * rows, cols), jnp.bfloat16)
    kernel = functools.partial(normalise_kernel, width_all)
    call = local_call(kernel, "normalise", shape, [SMEM] + [VMEM] * (3 + len(blocks)), VMEM)
    return call(place, square, other, gain, *blocks)


def attend_kernel(tile, first, length, limit_ref, own_ref, got_ref, query_gain_ref, key_gain_ref, cos_ref, sin_ref, *refs):
    before, out_ref, keys_ref, values_ref = refs[:-3], *refs[-3:]
    heads, head = query_gain_ref.shape
    wide = heads * head
    limit = limit_ref[0]
    rows = own_ref.shape[0]
    if before:
        out_ref[:first, :] = before[0][...]
        keys_ref[:first, :] = before[1][...]
        values_ref[:first, :] = before[2][...]

    def summed(start, size, own_col, got_col):
        got = got_ref[start : start + size, got_col : got_col + head].astype(jnp.float32)
        return own_ref[start : start + size, own_col : own_col + head] + got

    cosine, sine = cos_ref[...], sin_ref[...]
    keys = rms_rotated(summed(0, rows, 2 * wide, wide), key_gain_ref[...], cosine, sine)
    keys_ref[first:, :] = keys.astype(jnp.bfloat16)
    values_ref[first:, :] = summed(0, rows, 2 * wide + head, wide + head).astype(jnp.bfloat16)
    for start in range(0, rows, tile):
        seen = first + start + tile
        row = first + start + lax.broadcasted_iota(jnp.int32, (tile, seen), 0)
        col = lax.broadcasted_iota(jnp.int32, (tile, seen), 1)
        allowed = (col <= row) & (col < limit)
        cosine, sine = cos_ref[start : start + tile, :], sin_ref[start : start + tile, :]
        for j in range(heads):
            projected = summed(start, tile, j * head, j * head)
            query = rms_rotated(projected, query_gain_ref[j : j + 1, :], cosine, sine)
            query = (query * head**-0.5).astype(jnp.bfloat16)
            scores = lax.dot_general(
                query, keys_ref[:seen, :], (((1,), (1,)), ((), ())), preferred_element_type=jnp.float32
            )
            scores = jnp.where(allowed, scores, -1e30)
            weights = jnp.exp(scores - jnp.max(scores, axis=-1, keepdims=True))
            weights = weights / jnp.sum(weights, axis=-1, keepdims=True)
            output = jnp.dot(weights.astype(jnp.bfloat16), values_ref[:seen, :], preferred_element_type=jnp.float32)
            out_ref[first + start : seen, j * head : (j + 1) * head] = output.astype(out_ref.dtype)


def attend(limit, own, got, query_gain, key_gain, tables, before):
    rows = own.shape[0]
    heads, head = query_gain.shape
    first = before[0].shape[0] if before else 0
    cosine, sine = (table[first : first + rows] for table in tables)
    shape = [jax.ShapeDtypeStruct((first + rows, n), jnp.bfloat16) for n in (heads * head, head, head)]
    kernel = functools.partial(attend_kernel, rows // 2, first, first + rows)
    call = local_call(kernel, "attend", shape, [SMEM] + [VMEM] * (6 + len(before)), [VMEM] * 3)
    return call(limit, own, got, query_gain, key_gain, cosine, sine, *before)


def swap(array, axis):
    return lax.ppermute(array, axis, [(0, 1), (1, 0)])


def global_sum(value):
    count = 1
    for size in SIZES:
        count *= size
    spread = jnp.broadcast_to(value, (count, 128))
    return jnp.sum(lax.all_to_all(spread, AXES, 0, 0, tiled=True)[:, 0])


def to_column(block, other):
    pairs = []
    for xl in range(2):
        for y in range(8):
            for slab in range(2):
                target = ((xl ^ other) * 8 + (y + 2 * slab) % 8) * 2 + (y >> 1) % 2
                pairs.append(((xl * 8 + y) * 2 + slab, target))
    return lax.ppermute(block, ("xl", "y", "xh"), pairs)


def along(array, axis, step):
    size = lax.axis_size(axis)
    return lax.ppermute(array, axis, [(i, (i + step) % size) for i in range(size)])


def shards(
    activations, norm_gain, master_weight, grad, moment, variance, query_gain, key_gain, prompt_len
):
    xl, core, y, z, xh = (lax.axis_index(a) for a in AXES)
    width_all = norm_gain.shape[0]
    seq_rows, width_part = activations.shape
    slab_rows, _, slab_heads, head_size = grad.shape
    steps = jnp.arange(8)

    features = {0: activations.T}
    features[1] = along(features[0], "z", 1)
    features[7] = along(features[0], "z", -1)

    grad_local = grad.astype(jnp.float32)
    sumsq = global_sum(jnp.sum(grad_local * grad_local))
    sumsq, features[1], features[7] = lax.optimization_barrier((sumsq, features[1], features[7]))
    clip_factor = 1.0 / jnp.sqrt(sumsq + 1e-12)
    clipped = grad_local * clip_factor
    moment_new = BETA_ONE * moment + (1.0 - BETA_ONE) * clipped
    variance_new = BETA_TWO * variance + (1.0 - BETA_TWO) * clipped * clipped
    step_size = STEP_SCALE * width_all ** (-0.5)
    updated = (master_weight - step_size * moment_new / (jnp.sqrt(variance_new) + 1e-08)).astype(
        jnp.bfloat16
    )
    updated = updated.reshape(slab_rows, slab_heads * head_size)

    home = jnp.stack([to_column(updated, 0), to_column(updated, 1)])
    features[2] = along(features[1], "z", 1)
    features[6] = along(features[7], "z", -1)
    home, features[2], features[6] = lax.optimization_barrier((home, features[2], features[6]))

    arrived = {0: home}
    arrived[1] = along(home, "y", 1)
    arrived[7] = along(home, "y", -1)
    features[3] = along(features[2], "z", 1)
    features[5] = along(features[6], "z", -1)
    arrived[1], arrived[7], features[3] = lax.optimization_barrier((arrived[1], arrived[7], features[3]))

    arrived[2] = along(arrived[1], "y", 1)
    arrived[6] = along(arrived[7], "y", -1)
    features[4] = along(features[3], "z", 1)
    arrived[2], arrived[6], features[4], features[5] = lax.optimization_barrier(
        (arrived[2], arrived[6], features[4], features[5])
    )

    arrived[3] = along(arrived[2], "y", 1)
    arrived[5] = along(arrived[6], "y", -1)
    blocks = [features[step] for step in range(8)]
    square = squares(blocks)
    arrived[3], square = lax.optimization_barrier((arrived[3], square))
    arrived[4] = along(arrived[3], "y", 1)

    other_square = swap(square, "xh")
    origin = (z - steps) & 7
    gain = norm_gain.reshape(8, 2, width_part)[origin, xh].reshape(-1, 1)
    place = ((((origin >> 1) & 1) ^ core) * 2 + ((origin >> 2) ^ xl)) * 2 + (origin & 1)
    normed = normalise(float(width_all), place.astype(jnp.int32), square, other_square, gain, blocks)

    source = (y - steps) & 7
    native = ((source >> 1) & 1) == xh
    origin = jnp.where(native, source, (source - 2) & 7)
    slab = jnp.where(native, 0, 1)
    place = jnp.stack([(origin >> 2) * 2 + (origin & 1), slab ^ xh, slab]).astype(jnp.int32)
    own_weight = assemble(place, [arrived[step] for step in range(8)])
    other_weight = swap(own_weight, "core")

    tables = rope_tables(seq_rows, head_size)
    gain_row = lax.dynamic_slice_in_dim(key_gain, z, 1, 0)
    half = normed.shape[0] // 2
    query_cols = (slab_heads - 1) * head_size
    part = seq_rows // 2

    def product(rows, weight):
        return lax.dot_general(rows, weight, (((0,), (0,)), ((), ())), preferred_element_type=jnp.float32)

    result = ()
    for start in range(0, seq_rows, part):
        tokens = normed[:, start : start + part]
        partial = product(tokens[:half], own_weight) + product(tokens[half:], other_weight)
        got = swap(partial[:, query_cols:].astype(jnp.bfloat16), "xh")
        result = attend(prompt_len, partial, got, query_gain, gain_row, tables, tuple(result))
    return result[0]


def solution(mesh):
    fine = Mesh(mesh.devices.reshape(SIZES), AXES)
    rows, cols = ("xl", "core", "y"), ("z", "xh")
    slab = P(rows, cols, None, None)
    in_specs = (P(rows, cols), P(), slab, slab, slab, slab, P(cols, None), P(), P(rows))
    return jax.shard_map(
        shards, mesh=fine, in_specs=in_specs, out_specs=P(rows, cols), check_vma=False
    )
```

time: 172 us -> 182 us (1.058)
  starting transfers between devices: 48.2 us -> 103 us
  blocking collectives: 38.9 us -> 0 us
  between operations: 15.1 us -> 2.04 us
  local copies, waits for them, and re-layouts: 10.5 us -> 21.9 us
  other arithmetic: 13.2 us -> 6.1 us
  waiting for transfers between devices: 34.8 us -> 32.1 us
  Pallas kernels: 5.6 us -> 8.12 us
  matrix products: 5.13 us -> 6.97 us
    all_to_all x1 -> x0, blocking collectives: 38.9 us -> none  [global_sum(): return jnp.sum(lax.all_to_all(spread, AXES, 0, 0, tiled=True)[:, 0])]
    ppermute x7 -> x14, starting transfers between devices: 31.9 us -> 58.1 us  [along(): lax.ppermute(array, axis, [(i, (i + step) % size) for i in range(size)])]
    all_to_all x0 -> x1, starting transfers between devices: none -> 22.2 us  [global_sum(): return jnp.sum(lax.all_to_all(spread, AXES, 0, 0, tiled=True)[:, 0])]
    unnamed x21 -> x69, local copies, waits for them, and re-layouts: 4.61 us -> 17 us
    ppermute x3 -> x4, waiting for transfers between devices: 15.5 us -> 5.11 us  [swap(): return lax.ppermute(array, axis, [(0, 1), (1, 0)])]
    all_to_all x0 -> x1, waiting for transfers between devices: none -> 6.76 us  [global_sum(): return jnp.sum(lax.all_to_all(spread, AXES, 0, 0, tiled=True)[:, 0])]
    ppermute x3 -> x4, starting transfers between devices: 13.4 us -> 18.7 us  [swap(): return lax.ppermute(array, axis, [(0, 1), (1, 0)])]
    convert_element_type x1 -> x0, other arithmetic: 4.08 us -> none  [shards(): normed = (widened * row_scale[:, None] * gain).astype(jnp.bfloat16)]
  transfers between devices with their start and end apart: 13 -> 21, of which waited for: 7 -> 8; matrix products, arithmetic and copies ran while one was open for 9% -> 6% of each run, Pallas kernels for 0% -> 2%
where the time goes in v3:
time: 182 us; the launch traced here: 180 us
  starting transfers between devices  103 us (57%)
  waiting for transfers between devices  32.1 us (18%)
  local copies, waits for them, and re-layouts  21.9 us (12%)
  Pallas kernels  8.12 us (4%)
  matrix products  6.97 us (4%)
  other arithmetic  6.1 us (3%)
  between operations  2.04 us (1%)
    ppermute x14, starting transfers between devices, along(): lax.ppermute(array, axis, [(i, (i + step) % size) for i in range(size)])  58.1 us
    all_to_all x1, starting transfers between devices, global_sum(): return jnp.sum(lax.all_to_all(spread, AXES, 0, 0, tiled=True)[:, 0])  22.2 us
    ppermute x4, starting transfers between devices, swap(): return lax.ppermute(array, axis, [(0, 1), (1, 0)])  18.7 us
    ppermute x14, waiting for transfers between devices, along(): lax.ppermute(array, axis, [(i, (i + step) % size) for i in range(size)])  17.5 us
    unnamed x69, local copies, waits for them, and re-layouts  17 us
    dot_general x4, matrix products, product(): lax.dot_general(rows, weight, (((0,), (0,)), ((), ())), preferred_element...  6.97 us
    all_to_all x1, waiting for transfers between devices, global_sum(): return jnp.sum(lax.all_to_all(spread, AXES, 0, 0, tiled=True)[:, 0])  6.76 us
    pallas_call x2, Pallas kernels, attend(): return call(limit, own, got, query_gain, key_gain, cosine, sine, *before)  5.19 us
  transfers between devices with their start and end apart: 21, of which 8 were waited for; matrix products, arithmetic and copies ran while one was open for 6% of the time, Pallas kernels for 2%

profile of v3, /device:TPU:1, one launch (start us, length us, event | category | flops | bytes accessed | tf_op | source)
XLA Modules:
  0.0 180.1 jit_solution(12943236238691649631)
XLA Ops:
  0.0 2.1 %multiply_reduce_fusion = f32[]{:T(128)} fusion(bf16[160,1,3,128]{3,0,2,1:T(8,128)(2,1)} %param.16), kind=kLoop, calls=%fused_computation.17 | loop fusion | flops 184319 | bytes 122884 | tf_op jit(solution)/shard_map/reduce_sum | solution.py:192
  2.1 1.5 broadcast_in_dim.4
  3.6 22.2 %all-to-all-start = ((f32[512,1,128]{2,1,0:T(1,128)}), f32[512,1,128]{2,1,0:T(1,128)S(1)}, u32[]{:S(2)}, u32[]{:S(2)}) async-start(f32[512,1,128]{2,1,0:T(1,128)} %broadcast_in_dim.4), calls=%async_computation | async-start | bytes 524288 | tf_op jit(solution)/shard_map/all_to_all | solution.py:160
  25.8 3.7 %collective-permute-start = (bf16[320,768]{1,0:T(8,128)(2,1)}, bf16[320,768]{1,0:T(8,128)(2,1)S(1)}, u32[]{:S(2)}, u32[]{:S(2)}) collective-permute-start(bf16[320,768]{1,0:T(8,128)(2,1)} %bitcast.14), channel_id=1, source_target_pairs={{0,2},{2,4},{4,6},{6,8},{8,10},{10,12},{12,14},{14,0},{1,3},{3,5},... | collective-permute-start | bytes 1474568 | tf_op jit(solution)/shard_map/ppermute | solution.py:175
  29.5 6.4 %collective-permute-start.1 = (bf16[320,768]{1,0:T(8,128)(2,1)}, bf16[320,768]{1,0:T(8,128)(2,1)S(1)}, u32[]{:S(2)}, u32[]{:S(2)}) collective-permute-start(bf16[320,768]{1,0:T(8,128)(2,1)} %bitcast.15), channel_id=1, source_target_pairs={{0,14},{2,0},{4,2},{6,4},{8,6},{10,8},{12,10},{14,12},{1,15},{3,1}... | collective-permute-start | bytes 1474568 | tf_op jit(solution)/shard_map/ppermute | solution.py:175
  35.8 6.8 %all-to-all-done = f32[512,1,128]{2,1,0:T(1,128)S(1)} async-done(((f32[512,1,128]{2,1,0:T(1,128)}), f32[512,1,128]{2,1,0:T(1,128)S(1)}, u32[]{:S(2)}, u32[]{:S(2)}) %all-to-all-start) | async-done | bytes 262176 | tf_op jit(solution)/shard_map/all_to_all | solution.py:160
  43.3 4.9 %collective-permute-done.refs_1_ = bf16[320,768]{1,0:T(8,128)(2,1)S(1)} collective-permute-done((bf16[320,768]{1,0:T(8,128)(2,1)}, bf16[320,768]{1,0:T(8,128)(2,1)S(1)}, u32[]{:S(2)}, u32[]{:S(2)}) %collective-permute-start) | collective-permute-done | bytes 491552 | tf_op jit(solution)/shard_map/ppermute | solution.py:175
  48.9 1.9 %collective-permute-start.4 = (bf16[320,768]{1,0:T(8,128)(2,1)S(1)}, bf16[320,768]{1,0:T(8,128)(2,1)S(1)}, u32[]{:S(2)}, u32[]{:S(2)}) collective-permute-start(bf16[320,768]{1,0:T(8,128)(2,1)S(1)} %collective-permute-done.refs_1_), channel_id=1, source_target_pairs={{0,2},{2,4},{4,6},{6,8},{8,10},{10,12},{12,14},{14,0},{1,3},{3,5},... | collective-permute-start | bytes 1474568 | tf_op jit(solution)/shard_map/ppermute | solution.py:175
  50.8 4.6 %collective-permute-start.5 = (bf16[320,768]{1,0:T(8,128)(2,1)S(1)}, bf16[320,768]{1,0:T(8,128)(2,1)S(1)}, u32[]{:S(2)}, u32[]{:S(2)}) collective-permute-start(bf16[320,768]{1,0:T(8,128)(2,1)S(1)} %collective-permute-done.1.refs_7_), channel_id=1, source_target_pairs={{0,14},{2,0},{4,2},{6,4},{8,6},{10,8},{12,10},{14,12},{1,15},{3,1}... | collective-permute-start | bytes 1474568 | tf_op jit(solution)/shard_map/ppermute | solution.py:175
  55.4 3.2 %convert_reduce_fusion = bf16[160,3,128]{2,1,0:T(4,128)(2,1)S(1)} fusion(f32[160,1,3,128]{3,1,2,0:T(1,128)} %param.15, f32[160,1,3,128]{3,1,2,0:T(1,128)} %param.18, f32[160,1,3,128]{3,1,2,0:T(1,128)} %param.17, bf16[160,1,3,128]{3,0,2,1:T(8,128)(2,1)} %param.16, f32[]{:T(128)S(6)} %sqrt.6), kind=kLoop, calls=%fused_computation.16 | loop fusion | flops 860160 | bytes 983044 | tf_op jit(solution)/shard_map/convert_element_type | solution.py:199
  59.4 3.2 %collective-permute-start.3 = (bf16[160,384]{1,0:T(8,128)(2,1)S(1)}, bf16[160,384]{1,0:T(8,128)(2,1)S(1)}, u32[]{:S(2)}, u32[]{:S(2)}) collective-permute-start(bf16[160,384]{1,0:T(8,128)(2,1)S(1)} %bitcast.21), channel_id=1, source_target_pairs={{0,256},{1,288},{16,272},{17,304},{32,289},{33,321},{48,305},{49,3... | collective-permute-start | bytes 368648 | tf_op jit(solution)/shard_map/ppermute | solution.py:170
  62.5 2.7 %collective-permute-done.3 = bf16[160,384]{1,0:T(8,128)(2,1)S(1)} collective-permute-done((bf16[160,384]{1,0:T(8,128)(2,1)S(1)}, bf16[160,384]{1,0:T(8,128)(2,1)S(1)}, u32[]{:S(2)}, u32[]{:S(2)}) %collective-permute-start.3) | collective-permute-done | bytes 122912 | tf_op jit(solution)/shard_map/ppermute | solution.py:170
  65.3 2.4 %collective-permute-start.8 = (bf16[320,768]{1,0:T(8,128)(2,1)S(1)}, bf16[320,768]{1,0:T(8,128)(2,1)S(1)}, u32[]{:S(2)}, u32[]{:S(2)}) collective-permute-start(bf16[320,768]{1,0:T(8,128)(2,1)S(1)} %collective-permute-done.4.refs_2_), channel_id=1, source_target_pairs={{0,2},{2,4},{4,6},{6,8},{8,10},{10,12},{12,14},{14,0},{1,3},{3,5},... | collective-permute-start | bytes 1474568 | tf_op jit(solution)/shard_map/ppermute | solution.py:175
  67.8 2.9 %collective-permute-start.6 = (bf16[2,160,384]{2,1,0:T(8,128)(2,1)S(1)}, bf16[2,160,384]{2,1,0:T(8,128)(2,1)S(1)}, u32[]{:S(2)}, u32[]{:S(2)}) collective-permute-start(bf16[2,160,384]{2,1,0:T(8,128)(2,1)S(1)} %pad_maximum_fusion.refs_0_), channel_id=1, source_target_pairs={{0,16},{16,32},{32,48},{48,64},{64,80},{80,96},{96,112},{112,0},{1... | collective-permute-start | bytes 737288 | tf_op jit(solution)/shard_map/ppermute | solution.py:175
  70.7 13.8 %collective-permute-start.7 = (bf16[2,160,384]{2,1,0:T(8,128)(2,1)S(1)}, bf16[2,160,384]{2,1,0:T(8,128)(2,1)S(1)}, u32[]{:S(2)}, u32[]{:S(2)}) collective-permute-start(bf16[2,160,384]{2,1,0:T(8,128)(2,1)S(1)} %pad_maximum_fusion.refs_0_), channel_id=1, source_target_pairs={{0,112},{16,0},{32,16},{48,32},{64,48},{80,64},{96,80},{112,96},{1... | collective-permute-start | bytes 737288 | tf_op jit(solution)/shard_map/ppermute | solution.py:175
  85.3 4.6 %collective-permute-start.12 = (bf16[320,768]{1,0:T(8,128)(2,1)S(1)}, bf16[320,768]{1,0:T(8,128)(2,1)S(1)}, u32[]{:S(2)}, u32[]{:S(2)}) collective-permute-start(bf16[320,768]{1,0:T(8,128)(2,1)S(1)} %collective-permute-done.5.refs_6_), channel_id=1, source_target_pairs={{0,14},{2,0},{4,2},{6,4},{8,6},{10,8},{12,10},{14,12},{1,15},{3,1}... | collective-permute-start | bytes 1474568 | tf_op jit(solution)/shard_map/ppermute | solution.py:175
  89.9 1.9 %collective-permute-start.11 = (bf16[320,768]{1,0:T(8,128)(2,1)S(1)}, bf16[320,768]{1,0:T(8,128)(2,1)S(1)}, u32[]{:S(2)}, u32[]{:S(2)}) collective-permute-start(bf16[320,768]{1,0:T(8,128)(2,1)S(1)} %collective-permute-done.8.refs_3_), channel_id=1, source_target_pairs={{0,2},{2,4},{4,6},{6,8},{8,10},{10,12},{12,14},{14,0},{1,3},{3,5},... | collective-permute-start | bytes 1474568 | tf_op jit(solution)/shard_map/ppermute | solution.py:175
  91.8 5.6 %collective-permute-start.10 = (bf16[2,160,384]{2,1,0:T(8,128)(2,1)S(1)}, bf16[2,160,384]{2,1,0:T(8,128)(2,1)S(1)}, u32[]{:S(2)}, u32[]{:S(2)}) collective-permute-start(bf16[2,160,384]{2,1,0:T(8,128)(2,1)S(1)} %collective-permute-done.7.refs_7_), channel_id=1, source_target_pairs={{0,112},{16,0},{32,16},{48,32},{64,48},{80,64},{96,80},{112,96},{1... | collective-permute-start | bytes 737288 | tf_op jit(solution)/shard_map/ppermute | solution.py:175
  98.1 1.9 %collective-permute-start.9 = (bf16[2,160,384]{2,1,0:T(8,128)(2,1)S(1)}, bf16[2,160,384]{2,1,0:T(8,128)(2,1)}, u32[]{:S(2)}, u32[]{:S(2)}) collective-permute-start(bf16[2,160,384]{2,1,0:T(8,128)(2,1)S(1)} %collective-permute-done.6.refs_1_), channel_id=1, source_target_pairs={{0,16},{16,32},{32,48},{48,64},{64,80},{80,96},{96,112},{112,0},{1... | collective-permute-start | bytes 737288 | tf_op jit(solution)/shard_map/ppermute | solution.py:175
  100.8 5.6 %collective-permute-done.9.refs_2_ = bf16[2,160,384]{2,1,0:T(8,128)(2,1)} collective-permute-done((bf16[2,160,384]{2,1,0:T(8,128)(2,1)S(1)}, bf16[2,160,384]{2,1,0:T(8,128)(2,1)}, u32[]{:S(2)}, u32[]{:S(2)}) %collective-permute-start.9) | collective-permute-done | bytes 245792 | tf_op jit(solution)/shard_map/ppermute | solution.py:175
  107.2 1.9 %collective-permute-start.13 = (bf16[2,160,384]{2,1,0:T(8,128)(2,1)}, bf16[2,160,384]{2,1,0:T(8,128)(2,1)}, u32[]{:S(2)}, u32[]{:S(2)}) collective-permute-start(bf16[2,160,384]{2,1,0:T(8,128)(2,1)} %collective-permute-done.9.refs_2_), channel_id=1, source_target_pairs={{0,16},{16,32},{32,48},{48,64},{64,80},{80,96},{96,112},{112,0},{1... | collective-permute-start | bytes 737288 | tf_op jit(solution)/shard_map/ppermute | solution.py:175
  109.1 4.6 %collective-permute-start.16 = (bf16[2,160,384]{2,1,0:T(8,128)(2,1)}, bf16[2,160,384]{2,1,0:T(8,128)(2,1)S(1)}, u32[]{:S(2)}, u32[]{:S(2)}) collective-permute-start(bf16[2,160,384]{2,1,0:T(8,128)(2,1)} %copy-done.26), channel_id=1, source_target_pairs={{0,112},{16,0},{32,16},{48,32},{64,48},{80,64},{96,80},{112,96},{1... | collective-permute-start | bytes 737288 | tf_op jit(solution)/shard_map/ppermute | solution.py:175
  113.7 1.0 copy-done.18
  115.6 1.9 %collective-permute-start.15 = (bf16[2,160,384]{2,1,0:T(8,128)(2,1)}, bf16[2,160,384]{2,1,0:T(8,128)(2,1)S(1)}, u32[]{:S(2)}, u32[]{:S(2)}) collective-permute-start(bf16[2,160,384]{2,1,0:T(8,128)(2,1)} %collective-permute-done.13.refs_3_), channel_id=1, source_target_pairs={{0,16},{16,32},{32,48},{48,64},{64,80},{80,96},{96,112},{112,0},{1... | collective-permute-start | bytes 737288 | tf_op jit(solution)/shard_map/ppermute | solution.py:175
  117.6 6.4 %collective-permute-done.15.refs_4_ = bf16[2,160,384]{2,1,0:T(8,128)(2,1)S(1)} collective-permute-done((bf16[2,160,384]{2,1,0:T(8,128)(2,1)}, bf16[2,160,384]{2,1,0:T(8,128)(2,1)S(1)}, u32[]{:S(2)}, u32[]{:S(2)}) %collective-permute-start.15) | collective-permute-done | bytes 245792 | tf_op jit(solution)/shard_map/ppermute | solution.py:175
  124.0 1.3 assemble.1
  125.3 7.6 %collective-permute-start.17 = (bf16[1280,768]{1,0:T(8,128)(2,1)S(1)}, bf16[1280,768]{1,0:T(8,128)(2,1)}, u32[]{:S(2)}, u32[]{:S(2)}) collective-permute-start(bf16[1280,768]{1,0:T(8,128)(2,1)S(1)} %assemble.1), channel_id=1, source_target_pairs={{0,128},{128,0},{1,129},{129,1},{2,130},{130,2},{3,131},{131,3},{4... | collective-permute-start | bytes 5898248 | tf_op jit(solution)/shard_map/ppermute | solution.py:152
  132.9 4.1 %collective-permute-start.14 = (f32[1,768]{1,0:T(1,128)S(1)}, f32[1,768]{1,0:T(1,128)S(1)}, u32[]{:S(2)}, u32[]{:S(2)}) collective-permute-start(f32[1,768]{1,0:T(1,128)S(1)} %squares.1.square_ref), channel_id=1, source_target_pairs={{0,1},{1,0},{2,3},{3,2},{4,5},{5,4},{6,7},{7,6},{8,9},{9,8},{10,11... | collective-permute-start | bytes 9224 | tf_op jit(solution)/shard_map/ppermute | solution.py:152
  137.8 1.1 reshape.87.gain_ref
  138.9 1.0 copy-done.4
  140.0 1.0 copy-done.6
  141.0 1.0 copy-done.8
  142.0 1.0 copy-done.10
  143.1 1.0 copy-done.12
  144.1 1.0 copy-done.14
  145.1 1.0 copy-done.16
  146.1 1.0 copy-done.19
  147.2 1.5 normalise.1
  148.7 2.5 %fusion = f32[384,768]{1,0:T(8,128)S(1)} fusion(bf16[1280,768]{1,0:T(8,128)(2,1)} %collective-permute-done.17, bf16[2560,768]{1,0:T(8,128)(2,1)S(1)} %normalise.1), kind=kOutput, calls=%fused_computation.3 | convolution fusion | flops 754974720 | bytes 4128768 | tf_op jit(solution)/shard_map/dot_general | solution.py:251
  151.2 1.0 convolution_add_fusion.own_ref
  152.9 4.1 %collective-permute-start.19 = (bf16[384,512]{1,0:T(8,128)(2,1)}, bf16[384,512]{1,0:T(8,128)(2,1)S(1)}, u32[]{:S(2)}, u32[]{:S(2)}) collective-permute-start(bf16[384,512]{1,0:T(8,128)(2,1)} %slice.56), channel_id=1, source_target_pairs={{0,1},{1,0},{2,3},{3,2},{4,5},{5,4},{6,7},{7,6},{8,9},{9,8},{10,11... | collective-permute-start | bytes 1179656 | tf_op jit(solution)/shard_map/ppermute | solution.py:152
  157.1 2.5 %fusion.3 = f32[384,768]{1,0:T(8,128)S(1)} fusion(bf16[1280,768]{1,0:T(8,128)(2,1)} %collective-permute-done.17, bf16[2560,768]{1,0:T(8,128)(2,1)S(1)} %normalise.1), kind=kOutput, calls=%fused_computation.6 | convolution fusion | flops 754974720 | bytes 4128768 | tf_op jit(solution)/shard_map/dot_general | solution.py:251
  159.6 1.0 convolution_add_fusion.1.own_ref
  161.4 1.1 copy-done.1
  162.5 2.8 %collective-permute-start.18 = (bf16[384,512]{1,0:T(8,128)(2,1)}, bf16[384,512]{1,0:T(8,128)(2,1)S(1)}, u32[]{:S(2)}, u32[]{:S(2)}) collective-permute-start(bf16[384,512]{1,0:T(8,128)(2,1)} %slice.57), channel_id=1, source_target_pairs={{0,1},{1,0},{2,3},{3,2},{4,5},{5,4},{6,7},{7,6},{8,9},{9,8},{10,11... | collective-permute-start | bytes 1179656 | tf_op jit(solution)/shard_map/ppermute | solution.py:152
  168.0 2.2 %attend.2 = (bf16[384,256]{1,0:T(8,128)(2,1)S(1)}, bf16[384,128]{1,0:T(8,128)(2,1)S(1)}, bf16[384,128]{1,0:T(8,128)(2,1)S(1)}) custom-call(s32[1]{0:T(128)S(6)} %copy.31.limit_ref, f32[384,768]{1,0:T(8,128)S(1)} %convolution_add_fusion.own_ref, bf16[384,512]{1,0:T(8,128)(2,1)S(1)} %collective-permute-done.19.got_ref, f32[2,128]{1,0:T(2,128)S(1)} %copy-done.32, ...), custom_call_target="tpu_custom_call" | custom-call | tf_op jit(solution)/shard_map/attend/pallas_call | solution.py:148
  170.2 5.0 %collective-permute-done.18.got_ref = bf16[384,512]{1,0:T(8,128)(2,1)S(1)} collective-permute-done((bf16[384,512]{1,0:T(8,128)(2,1)}, bf16[384,512]{1,0:T(8,128)(2,1)S(1)}, u32[]{:S(2)}, u32[]{:S(2)}) %collective-permute-start.18) | collective-permute-done | bytes 393248 | tf_op jit(solution)/shard_map/ppermute | solution.py:152
  177.1 3.0 %attend.3 = (bf16[768,256]{1,0:T(8,128)(2,1)}, bf16[768,128]{1,0:T(8,128)(2,1)}, bf16[768,128]{1,0:T(8,128)(2,1)}) custom-call(s32[1]{0:T(128)S(6)} %copy.31.limit_ref, f32[384,768]{1,0:T(8,128)S(1)} %copy-done.2, bf16[384,512]{1,0:T(8,128)(2,1)S(1)} %collective-permute-done.18.got_ref, f32[2,128]{1,0:T(2,128)S(1)} %copy-done.32, ...), custom_call_target="tpu_custom_call" | custom-call | tf_op jit(solution)/shard_map/attend/pallas_call | solution.py:148
  (88 shorter events, 11.4 us)
Async XLA Ops:
  0.0 166.0 %copy-start = (f32[8,128]{1,0:T(8,128)S(1)}, f32[8,128]{1,0:T(8,128)}, u32[]{:S(2)}) copy-start(f32[8,128]{1,0:T(8,128)} %param.20) | copy-start | bytes 12292
  0.0 113.7 %copy-start.3 = (bf16[768,320]{0,1:T(8,128)(2,1)S(1)}, bf16[768,320]{0,1:T(8,128)(2,1)}, u32[]{:S(2)}) copy-start(bf16[768,320]{0,1:T(8,128)(2,1)} %param.13) | copy-start | bytes 1474564
  3.6 39.0 %all-to-all-start = ((f32[512,1,128]{2,1,0:T(1,128)}), f32[512,1,128]{2,1,0:T(1,128)S(1)}, u32[]{:S(2)}, u32[]{:S(2)}) async-start(f32[512,1,128]{2,1,0:T(1,128)} %broadcast_in_dim.4), calls=%async_computation | async-start | bytes 524288 | tf_op jit(solution)/shard_map/all_to_all | solution.py:160
  25.8 22.4 %collective-permute-start = (bf16[320,768]{1,0:T(8,128)(2,1)}, bf16[320,768]{1,0:T(8,128)(2,1)S(1)}, u32[]{:S(2)}, u32[]{:S(2)}) collective-permute-start(bf16[320,768]{1,0:T(8,128)(2,1)} %bitcast.14), channel_id=1, source_target_pairs={{0,2},{2,4},{4,6},{6,8},{8,10},{10,12},{12,14},{14,0},{1,3},{3,5},... | collective-permute-start | bytes 1474568 | tf_op jit(solution)/shard_map/ppermute | solution.py:175
  29.5 18.7 %collective-permute-start.1 = (bf16[320,768]{1,0:T(8,128)(2,1)}, bf16[320,768]{1,0:T(8,128)(2,1)S(1)}, u32[]{:S(2)}, u32[]{:S(2)}) collective-permute-start(bf16[320,768]{1,0:T(8,128)(2,1)} %bitcast.15), channel_id=1, source_target_pairs={{0,14},{2,0},{4,2},{6,4},{8,6},{10,8},{12,10},{14,12},{1,15},{3,1}... | collective-permute-start | bytes 1474568 | tf_op jit(solution)/shard_map/ppermute | solution.py:175
  48.2 66.7 %copy-start.5 = (bf16[320,768]{1,0:T(8,128)(2,1)}, bf16[320,768]{1,0:T(8,128)(2,1)S(1)}, u32[]{:S(2)}) copy-start(bf16[320,768]{1,0:T(8,128)(2,1)S(1)} %collective-permute-done.refs_1_) | copy-start | bytes 1474564
  48.2 66.7 %copy-start.7 = (bf16[320,768]{1,0:T(8,128)(2,1)}, bf16[320,768]{1,0:T(8,128)(2,1)S(1)}, u32[]{:S(2)}) copy-start(bf16[320,768]{1,0:T(8,128)(2,1)S(1)} %collective-permute-done.1.refs_7_) | copy-start | bytes 1474564
  48.9 16.4 %collective-permute-start.4 = (bf16[320,768]{1,0:T(8,128)(2,1)S(1)}, bf16[320,768]{1,0:T(8,128)(2,1)S(1)}, u32[]{:S(2)}, u32[]{:S(2)}) collective-permute-start(bf16[320,768]{1,0:T(8,128)(2,1)S(1)} %collective-permute-done.refs_1_), channel_id=1, source_target_pairs={{0,2},{2,4},{4,6},{6,8},{8,10},{10,12},{12,14},{14,0},{1,3},{3,5},... | collective-permute-start | bytes 1474568 | tf_op jit(solution)/shard_map/ppermute | solution.py:175
  50.8 14.5 %collective-permute-start.5 = (bf16[320,768]{1,0:T(8,128)(2,1)S(1)}, bf16[320,768]{1,0:T(8,128)(2,1)S(1)}, u32[]{:S(2)}, u32[]{:S(2)}) collective-permute-start(bf16[320,768]{1,0:T(8,128)(2,1)S(1)} %collective-permute-done.1.refs_7_), channel_id=1, source_target_pairs={{0,14},{2,0},{4,2},{6,4},{8,6},{10,8},{12,10},{14,12},{1,15},{3,1}... | collective-permute-start | bytes 1474568 | tf_op jit(solution)/shard_map/ppermute | solution.py:175
  58.7 3.9 %collective-permute-start.2 = (bf16[160,384]{1,0:T(8,128)(2,1)S(1)}, bf16[160,384]{1,0:T(8,128)(2,1)S(1)}, u32[]{:S(2)}, u32[]{:S(2)}) collective-permute-start(bf16[160,384]{1,0:T(8,128)(2,1)S(1)} %bitcast.20), channel_id=1, source_target_pairs={{0,0},{1,32},{16,16},{17,48},{32,33},{33,65},{48,49},{49,81},{64,6... | collective-permute-start | bytes 368648 | tf_op jit(solution)/shard_map/ppermute | solution.py:170
  59.4 5.9 %collective-permute-start.3 = (bf16[160,384]{1,0:T(8,128)(2,1)S(1)}, bf16[160,384]{1,0:T(8,128)(2,1)S(1)}, u32[]{:S(2)}, u32[]{:S(2)}) collective-permute-start(bf16[160,384]{1,0:T(8,128)(2,1)S(1)} %bitcast.21), channel_id=1, source_target_pairs={{0,256},{1,288},{16,272},{17,304},{32,289},{33,321},{48,305},{49,3... | collective-permute-start | bytes 368648 | tf_op jit(solution)/shard_map/ppermute | solution.py:170
  65.3 49.6 %copy-start.9 = (bf16[320,768]{1,0:T(8,128)(2,1)}, bf16[320,768]{1,0:T(8,128)(2,1)S(1)}, u32[]{:S(2)}) copy-start(bf16[320,768]{1,0:T(8,128)(2,1)S(1)} %collective-permute-done.4.refs_2_) | copy-start | bytes 1474564
  65.3 49.6 %copy-start.11 = (bf16[320,768]{1,0:T(8,128)(2,1)}, bf16[320,768]{1,0:T(8,128)(2,1)S(1)}, u32[]{:S(2)}) copy-start(bf16[320,768]{1,0:T(8,128)(2,1)S(1)} %collective-permute-done.5.refs_6_) | copy-start | bytes 1474564
  65.3 24.5 %collective-permute-start.8 = (bf16[320,768]{1,0:T(8,128)(2,1)S(1)}, bf16[320,768]{1,0:T(8,128)(2,1)S(1)}, u32[]{:S(2)}, u32[]{:S(2)}) collective-permute-start(bf16[320,768]{1,0:T(8,128)(2,1)S(1)} %collective-permute-done.4.refs_2_), channel_id=1, source_target_pairs={{0,2},{2,4},{4,6},{6,8},{8,10},{10,12},{12,14},{14,0},{1,3},{3,5},... | collective-permute-start | bytes 1474568 | tf_op jit(solution)/shard_map/ppermute | solution.py:175
  67.8 22.1 %collective-permute-start.6 = (bf16[2,160,384]{2,1,0:T(8,128)(2,1)S(1)}, bf16[2,160,384]{2,1,0:T(8,128)(2,1)S(1)}, u32[]{:S(2)}, u32[]{:S(2)}) collective-permute-start(bf16[2,160,384]{2,1,0:T(8,128)(2,1)S(1)} %pad_maximum_fusion.refs_0_), channel_id=1, source_target_pairs={{0,16},{16,32},{32,48},{48,64},{64,80},{80,96},{96,112},{112,0},{1... | collective-permute-start | bytes 737288 | tf_op jit(solution)/shard_map/ppermute | solution.py:175
  70.7 19.1 %collective-permute-start.7 = (bf16[2,160,384]{2,1,0:T(8,128)(2,1)S(1)}, bf16[2,160,384]{2,1,0:T(8,128)(2,1)S(1)}, u32[]{:S(2)}, u32[]{:S(2)}) collective-permute-start(bf16[2,160,384]{2,1,0:T(8,128)(2,1)S(1)} %pad_maximum_fusion.refs_0_), channel_id=1, source_target_pairs={{0,112},{16,0},{32,16},{48,32},{64,48},{80,64},{96,80},{112,96},{1... | collective-permute-start | bytes 737288 | tf_op jit(solution)/shard_map/ppermute | solution.py:175
  85.3 15.5 %collective-permute-start.12 = (bf16[320,768]{1,0:T(8,128)(2,1)S(1)}, bf16[320,768]{1,0:T(8,128)(2,1)S(1)}, u32[]{:S(2)}, u32[]{:S(2)}) collective-permute-start(bf16[320,768]{1,0:T(8,128)(2,1)S(1)} %collective-permute-done.5.refs_6_), channel_id=1, source_target_pairs={{0,14},{2,0},{4,2},{6,4},{8,6},{10,8},{12,10},{14,12},{1,15},{3,1}... | collective-permute-start | bytes 1474568 | tf_op jit(solution)/shard_map/ppermute | solution.py:175
  89.9 25.1 %copy-start.13 = (bf16[320,768]{1,0:T(8,128)(2,1)}, bf16[320,768]{1,0:T(8,128)(2,1)S(1)}, u32[]{:S(2)}) copy-start(bf16[320,768]{1,0:T(8,128)(2,1)S(1)} %collective-permute-done.8.refs_3_) | copy-start | bytes 1474564
  89.9 16.5 %collective-permute-start.11 = (bf16[320,768]{1,0:T(8,128)(2,1)S(1)}, bf16[320,768]{1,0:T(8,128)(2,1)S(1)}, u32[]{:S(2)}, u32[]{:S(2)}) collective-permute-start(bf16[320,768]{1,0:T(8,128)(2,1)S(1)} %collective-permute-done.8.refs_3_), channel_id=1, source_target_pairs={{0,2},{2,4},{4,6},{6,8},{8,10},{10,12},{12,14},{14,0},{1,3},{3,5},... | collective-permute-start | bytes 1474568 | tf_op jit(solution)/shard_map/ppermute | solution.py:175
  91.8 8.9 %collective-permute-start.10 = (bf16[2,160,384]{2,1,0:T(8,128)(2,1)S(1)}, bf16[2,160,384]{2,1,0:T(8,128)(2,1)S(1)}, u32[]{:S(2)}, u32[]{:S(2)}) collective-permute-start(bf16[2,160,384]{2,1,0:T(8,128)(2,1)S(1)} %collective-permute-done.7.refs_7_), channel_id=1, source_target_pairs={{0,112},{16,0},{32,16},{48,32},{64,48},{80,64},{96,80},{112,96},{1... | collective-permute-start | bytes 737288 | tf_op jit(solution)/shard_map/ppermute | solution.py:175
  98.1 8.2 %collective-permute-start.9 = (bf16[2,160,384]{2,1,0:T(8,128)(2,1)S(1)}, bf16[2,160,384]{2,1,0:T(8,128)(2,1)}, u32[]{:S(2)}, u32[]{:S(2)}) collective-permute-start(bf16[2,160,384]{2,1,0:T(8,128)(2,1)S(1)} %collective-permute-done.6.refs_1_), channel_id=1, source_target_pairs={{0,16},{16,32},{32,48},{48,64},{64,80},{80,96},{96,112},{112,0},{1... | collective-permute-start | bytes 737288 | tf_op jit(solution)/shard_map/ppermute | solution.py:175
  100.7 14.2 %copy-start.15 = (bf16[320,768]{1,0:T(8,128)(2,1)}, bf16[320,768]{1,0:T(8,128)(2,1)S(1)}, u32[]{:S(2)}) copy-start(bf16[320,768]{1,0:T(8,128)(2,1)S(1)} %collective-permute-done.12.refs_5_) | copy-start | bytes 1474564
  100.7 5.6 %copy-start.26 = (bf16[2,160,384]{2,1,0:T(8,128)(2,1)}, bf16[2,160,384]{2,1,0:T(8,128)(2,1)S(1)}, u32[]{:S(2)}) copy-start(bf16[2,160,384]{2,1,0:T(8,128)(2,1)S(1)} %collective-permute-done.10.refs_6_) | copy-start | bytes 737284
  107.2 8.5 %collective-permute-start.13 = (bf16[2,160,384]{2,1,0:T(8,128)(2,1)}, bf16[2,160,384]{2,1,0:T(8,128)(2,1)}, u32[]{:S(2)}, u32[]{:S(2)}) collective-permute-start(bf16[2,160,384]{2,1,0:T(8,128)(2,1)} %collective-permute-done.9.refs_2_), channel_id=1, source_target_pairs={{0,16},{16,32},{32,48},{48,64},{64,80},{80,96},{96,112},{112,0},{1... | collective-permute-start | bytes 737288 | tf_op jit(solution)/shard_map/ppermute | solution.py:175
  109.1 8.5 %collective-permute-start.16 = (bf16[2,160,384]{2,1,0:T(8,128)(2,1)}, bf16[2,160,384]{2,1,0:T(8,128)(2,1)S(1)}, u32[]{:S(2)}, u32[]{:S(2)}) collective-permute-start(bf16[2,160,384]{2,1,0:T(8,128)(2,1)} %copy-done.26), channel_id=1, source_target_pairs={{0,112},{16,0},{32,16},{48,32},{64,48},{80,64},{96,80},{112,96},{1... | collective-permute-start | bytes 737288 | tf_op jit(solution)/shard_map/ppermute | solution.py:175
  113.7 1.0 copy-start.18
  114.7 9.3 %copy-start.21 = (bf16[2,160,384]{2,1,0:T(8,128)(2,1)S(1)}, bf16[2,160,384]{2,1,0:T(8,128)(2,1)}, u32[]{:S(2)}) copy-start(bf16[2,160,384]{2,1,0:T(8,128)(2,1)} %copy-done.20) | copy-start | bytes 737284
  114.7 9.3 %copy-start.23 = (bf16[2,160,384]{2,1,0:T(8,128)(2,1)S(1)}, bf16[2,160,384]{2,1,0:T(8,128)(2,1)}, u32[]{:S(2)}) copy-start(bf16[2,160,384]{2,1,0:T(8,128)(2,1)} %copy-done.22) | copy-start | bytes 737284
  114.7 9.3 %copy-start.25 = (bf16[2,160,384]{2,1,0:T(8,128)(2,1)S(1)}, bf16[2,160,384]{2,1,0:T(8,128)(2,1)}, u32[]{:S(2)}) copy-start(bf16[2,160,384]{2,1,0:T(8,128)(2,1)} %copy-done.24) | copy-start | bytes 737284
  114.7 9.3 %copy-start.27 = (bf16[2,160,384]{2,1,0:T(8,128)(2,1)S(1)}, bf16[2,160,384]{2,1,0:T(8,128)(2,1)}, u32[]{:S(2)}) copy-start(bf16[2,160,384]{2,1,0:T(8,128)(2,1)} %copy-done.26) | copy-start | bytes 737284
  115.6 8.3 %collective-permute-start.15 = (bf16[2,160,384]{2,1,0:T(8,128)(2,1)}, bf16[2,160,384]{2,1,0:T(8,128)(2,1)S(1)}, u32[]{:S(2)}, u32[]{:S(2)}) collective-permute-start(bf16[2,160,384]{2,1,0:T(8,128)(2,1)} %collective-permute-done.13.refs_3_), channel_id=1, source_target_pairs={{0,16},{16,32},{32,48},{48,64},{64,80},{80,96},{96,112},{112,0},{1... | collective-permute-start | bytes 737288 | tf_op jit(solution)/shard_map/ppermute | solution.py:175
  117.6 19.5 %copy-start.33 = (f32[5120]{0:T(1024)S(1)}, f32[5120]{0:T(1024)}, u32[]{:S(2)}) copy-start(f32[5120]{0:T(1024)} %param.14) | copy-start | bytes 61444
  125.3 23.4 %collective-permute-start.17 = (bf16[1280,768]{1,0:T(8,128)(2,1)S(1)}, bf16[1280,768]{1,0:T(8,128)(2,1)}, u32[]{:S(2)}, u32[]{:S(2)}) collective-permute-start(bf16[1280,768]{1,0:T(8,128)(2,1)S(1)} %assemble.1), channel_id=1, source_target_pairs={{0,128},{128,0},{1,129},{129,1},{2,130},{130,2},{3,131},{131,3},{4... | collective-permute-start | bytes 5898248 | tf_op jit(solution)/shard_map/ppermute | solution.py:152
  132.9 6.0 %collective-permute-start.14 = (f32[1,768]{1,0:T(1,128)S(1)}, f32[1,768]{1,0:T(1,128)S(1)}, u32[]{:S(2)}, u32[]{:S(2)}) collective-permute-start(f32[1,768]{1,0:T(1,128)S(1)} %squares.1.square_ref), channel_id=1, source_target_pairs={{0,1},{1,0},{2,3},{3,2},{4,5},{5,4},{6,7},{7,6},{8,9},{9,8},{10,11... | collective-permute-start | bytes 9224 | tf_op jit(solution)/shard_map/ppermute | solution.py:152
  138.9 1.0 copy-start.4
  140.0 1.0 copy-start.6
  141.0 1.0 copy-start.8
  142.0 1.0 copy-start.10
  143.1 1.0 copy-start.12
  144.1 1.0 copy-start.14
  145.1 1.0 copy-start.16
  146.1 1.0 copy-start.19
  152.9 13.2 %collective-permute-start.19 = (bf16[384,512]{1,0:T(8,128)(2,1)}, bf16[384,512]{1,0:T(8,128)(2,1)S(1)}, u32[]{:S(2)}, u32[]{:S(2)}) collective-permute-start(bf16[384,512]{1,0:T(8,128)(2,1)} %slice.56), channel_id=1, source_target_pairs={{0,1},{1,0},{2,3},{3,2},{4,5},{5,4},{6,7},{7,6},{8,9},{9,8},{10,11... | collective-permute-start | bytes 1179656 | tf_op jit(solution)/shard_map/ppermute | solution.py:152
  159.6 6.5 %copy-start.32 = (f32[2,128]{1,0:T(2,128)S(1)}, f32[2,128]{1,0:T(2,128)}, u32[]{:S(2)}) copy-start(f32[2,128]{1,0:T(2,128)} %query_gain_ref.3) | copy-start | bytes 3076
  161.4 1.1 copy-start.1
  162.5 12.8 %collective-permute-start.18 = (bf16[384,512]{1,0:T(8,128)(2,1)}, bf16[384,512]{1,0:T(8,128)(2,1)S(1)}, u32[]{:S(2)}, u32[]{:S(2)}) collective-permute-start(bf16[384,512]{1,0:T(8,128)(2,1)} %slice.57), channel_id=1, source_target_pairs={{0,1},{1,0},{2,3},{3,2},{4,5},{5,4},{6,7},{7,6},{8,9},{9,8},{10,11... | collective-permute-start | bytes 1179656 | tf_op jit(solution)/shard_map/ppermute | solution.py:152
  165.3 10.0 %copy-start.2 = (f32[384,768]{1,0:T(8,128)S(1)}, f32[384,768]{1,0:T(8,128)}, u32[]{:S(2)}) copy-start(f32[384,768]{1,0:T(8,128)} %copy-done.1) | copy-start | bytes 3538948
  175.2 0.9 copy-start.30
  (7 other events, 5.7 us)

commit v4 on v3

--- a/solution.py
+++ b/solution.py
@@ -36,66 +36,75 @@
 
 
 def local_call(kernel, name, out_shape, in_specs, out_specs):
-    params = pltpu.CompilerParams(vmem_limit_bytes=40 << 20)
+    params = pltpu.CompilerParams(vmem_limit_bytes=8 << 20)
     return pl.pallas_call(
         kernel, out_shape=out_shape, in_specs=in_specs, out_specs=out_specs, compiler_params=params, name=name
     )
 
 
-def assemble_kernel(place_ref, *refs):
-    *blocks, out_ref = refs
-    rows, cols = blocks[0].shape[1:]
-    half = out_ref.shape[0] // 2
+def assemble_kernel(place_ref, home_ref, *refs):
+    *step_refs, last_ref, early_ref, late_ref, out_ref = refs
+    _, _, rows, cols = home_ref.shape
     head = out_ref.shape[1] // 6
     wide = cols - head
-    for step, block in enumerate(blocks):
+
+    def put(step, lane, block_ref, *index):
         row = pl.multiple_of(place_ref[0, step] * rows, 32)
         query_col = pl.multiple_of(place_ref[1, step] * wide, 128)
         pair_col = pl.multiple_of(2 * wide + place_ref[2, step] * head, 128)
         for near in range(2):
-            span = pl.ds(near * half + row, rows)
-            out_ref[span, pl.ds(query_col, wide)] = block[near, :, :wide]
-            out_ref[span, pl.ds(pair_col, head)] = block[near, :, wide:]
-
-
-def assemble(place, blocks):
-    rows, cols = blocks[0].shape[1:]
-    shape = jax.ShapeDtypeStruct((len(blocks) * rows, 2 * cols), blocks[0].dtype)
-    call = local_call(assemble_kernel, "assemble", shape, [SMEM] + [VMEM] * len(blocks), VMEM)
-    return call(place, *blocks)
-
-
-def squares_kernel(*refs):
-    *blocks, out_ref = refs
+            span = pl.ds((lane * 2 + near) * 4 * rows + row, rows)
+            out_ref[span, pl.ds(query_col, wide)] = block_ref[*index, near, :, :wide]
+            out_ref[span, pl.ds(pair_col, head)] = block_ref[*index, near, :, wide:]
+
+    for lane in range(2):
+        put(0, lane, home_ref, lane)
+        for step in range(3):
+            put(1 + step, lane, step_refs[step], lane)
+        for step in range(2):
+            put(5 + step, 1 - lane, early_ref, step, lane)
+        put(7, 1 - lane, late_ref, lane)
+    put(4, 0, last_ref)
+    put(4, 1, late_ref, 2)
+
+
+def assemble(place, home, *rest):
+    _, _, rows, cols = home.shape
+    shape = jax.ShapeDtypeStruct((16 * rows, 2 * cols), home.dtype)
+    call = local_call(assemble_kernel, "assemble", shape, [SMEM] + [VMEM] * (1 + len(rest)), VMEM)
+    return call(place, home, *rest)
+
+
+def squares_kernel(parts, features_ref, out_ref):
+    rows = features_ref.shape[0] // parts
     total = None
-    for block in blocks:
-        wide = block[...].astype(jnp.float32)
+    for step in range(parts):
+        wide = features_ref[step * rows : (step + 1) * rows, :].astype(jnp.float32)
         square = jnp.sum(wide * wide, axis=0, keepdims=True)
         total = square if total is None else total + square
     out_ref[...] = total
 
 
-def squares(blocks):
-    shape = jax.ShapeDtypeStruct((1, blocks[0].shape[1]), jnp.float32)
-    return local_call(squares_kernel, "squares", shape, [VMEM] * len(blocks), VMEM)(*blocks)
-
-
-def normalise_kernel(width_all, place_ref, square_ref, other_ref, gain_ref, *refs):
-    *blocks, out_ref = refs
-    rows = blocks[0].shape[0]
+def squares(parts, features):
+    shape = jax.ShapeDtypeStruct((1, features.shape[1]), jnp.float32)
+    return local_call(functools.partial(squares_kernel, parts), "squares", shape, [VMEM], VMEM)(features)
+
+
+def normalise_kernel(width_all, parts, place_ref, square_ref, other_ref, gain_ref, features_ref, out_ref):
+    rows = features_ref.shape[0] // parts
     scale = lax.rsqrt((square_ref[...] + other_ref[...]) / width_all + 1e-06)
-    for step, block in enumerate(blocks):
+    for step in range(parts):
+        span = slice(step * rows, (step + 1) * rows)
         row = pl.multiple_of(place_ref[step] * rows, 64)
-        gain = gain_ref[step * rows : (step + 1) * rows, :]
-        out_ref[pl.ds(row, rows), :] = (block[...].astype(jnp.float32) * scale * gain).astype(out_ref.dtype)
-
-
-def normalise(width_all, place, square, other, gain, blocks):
-    rows, cols = blocks[0].shape
-    shape = jax.ShapeDtypeStruct((len(blocks) * rows, cols), jnp.bfloat16)
-    kernel = functools.partial(normalise_kernel, width_all)
-    call = local_call(kernel, "normalise", shape, [SMEM] + [VMEM] * (3 + len(blocks)), VMEM)
-    return call(place, square, other, gain, *blocks)
+        scaled = features_ref[span, :].astype(jnp.float32) * scale * gain_ref[span, :]
+        out_ref[pl.ds(row, rows), :] = scaled.astype(out_ref.dtype)
+
+
+def normalise(width_all, parts, place, square, other, gain, features):
+    shape = jax.ShapeDtypeStruct(features.shape, jnp.bfloat16)
+    kernel = functools.partial(normalise_kernel, width_all, parts)
+    call = local_call(kernel, "normalise", shape, [SMEM] + [VMEM] * 4, VMEM)
+    return call(place, square, other, gain, features)
 
 
 def attend_kernel(tile, first, length, limit_ref, own_ref, got_ref, query_gain_ref, key_gain_ref, cos_ref, sin_ref, *refs):
@@ -165,14 +174,15 @@
     for xl in range(2):
         for y in range(8):
             for slab in range(2):
-                target = ((xl ^ other) * 8 + (y + 2 * slab) % 8) * 2 + (y >> 1) % 2
-                pairs.append(((xl * 8 + y) * 2 + slab, target))
+                column = (y >> 1) % 2
+                target = y if slab == column else (y + (1 if y % 2 else -1)) % 8
+                pairs.append(((xl * 8 + y) * 2 + slab, ((xl ^ other) * 8 + target) * 2 + column))
     return lax.ppermute(block, ("xl", "y", "xh"), pairs)
 
 
-def along(array, axis, step):
-    size = lax.axis_size(axis)
-    return lax.ppermute(array, axis, [(i, (i + step) % size) for i in range(size)])
+def onward(block):
+    pairs = [(y, (y + 1) % 8) for y in range(8)] + [(8 + y, 8 + (y - 1) % 8) for y in range(8)]
+    return lax.ppermute(block, ("core", "y"), pairs)
 
 
 def shards(
@@ -184,13 +194,10 @@
     slab_rows, _, slab_heads, head_size = grad.shape
     steps = jnp.arange(8)
 
-    features = {0: activations.T}
-    features[1] = along(features[0], "z", 1)
-    features[7] = along(features[0], "z", -1)
+    gathered = lax.all_gather(activations.T, "z", axis=0, tiled=True)
 
     grad_local = grad.astype(jnp.float32)
     sumsq = global_sum(jnp.sum(grad_local * grad_local))
-    sumsq, features[1], features[7] = lax.optimization_barrier((sumsq, features[1], features[7]))
     clip_factor = 1.0 / jnp.sqrt(sumsq + 1e-12)
     clipped = grad_local * clip_factor
     moment_new = BETA_ONE * moment + (1.0 - BETA_ONE) * clipped
@@ -200,50 +207,34 @@
         jnp.bfloat16
     )
     updated = updated.reshape(slab_rows, slab_heads * head_size)
-
     home = jnp.stack([to_column(updated, 0), to_column(updated, 1)])
-    features[2] = along(features[1], "z", 1)
-    features[6] = along(features[7], "z", -1)
-    home, features[2], features[6] = lax.optimization_barrier((home, features[2], features[6]))
-
-    arrived = {0: home}
-    arrived[1] = along(home, "y", 1)
-    arrived[7] = along(home, "y", -1)
-    features[3] = along(features[2], "z", 1)
-    features[5] = along(features[6], "z", -1)
-    arrived[1], arrived[7], features[3] = lax.optimization_barrier((arrived[1], arrived[7], features[3]))
-
-    arrived[2] = along(arrived[1], "y", 1)
-    arrived[6] = along(arrived[7], "y", -1)
-    features[4] = along(features[3], "z", 1)
-    arrived[2], arrived[6], features[4], features[5] = lax.optimization_barrier(
-        (arrived[2], arrived[6], features[4], features[5])
-    )
-
-    arrived[3] = along(arrived[2], "y", 1)
-    arrived[5] = along(arrived[6], "y", -1)
-    blocks = [features[step] for step in range(8)]
-    square = squares(blocks)
-    arrived[3], square = lax.optimization_barrier((arrived[3], square))
-    arrived[4] = along(arrived[3], "y", 1)
-
+    home = jnp.stack([home, swap(home, "core")])
+    first = onward(home)
+    first, gathered = lax.optimization_barrier((first, gathered))
+
+    square = squares(8, gathered)
     other_square = swap(square, "xh")
-    origin = (z - steps) & 7
-    gain = norm_gain.reshape(8, 2, width_part)[origin, xh].reshape(-1, 1)
-    place = ((((origin >> 1) & 1) ^ core) * 2 + ((origin >> 2) ^ xl)) * 2 + (origin & 1)
-    normed = normalise(float(width_all), place.astype(jnp.int32), square, other_square, gain, blocks)
-
-    source = (y - steps) & 7
+    gain = lax.dynamic_index_in_dim(norm_gain.reshape(8, 2, width_part), xh, 1, False).reshape(-1, 1)
+    place = (((((steps >> 1) & 1) ^ core) * 2 + ((steps >> 2) ^ xl)) * 2 + (steps & 1)).astype(jnp.int32)
+    normed = normalise(float(width_all), 8, place, square, other_square, gain, gathered)
+
+    second = onward(first)
+    third = onward(second)
+    early = swap(jnp.stack([first, second]), "core")
+    last = onward(third[0])
+    last, normed = lax.optimization_barrier((last, normed))
+    late = swap(jnp.concatenate([third, last[None]]), "core")
+
+    up = 1 - 2 * core
+    source = (y - up * jnp.where(steps < 5, steps, 4 - steps)) & 7
     native = ((source >> 1) & 1) == xh
-    origin = jnp.where(native, source, (source - 2) & 7)
-    slab = jnp.where(native, 0, 1)
+    origin = jnp.where(native, source, (source + 2 * (source & 1) - 1) & 7)
+    slab = jnp.where(native, xh, 1 - xh)
     place = jnp.stack([(origin >> 2) * 2 + (origin & 1), slab ^ xh, slab]).astype(jnp.int32)
-    own_weight = assemble(place, [arrived[step] for step in range(8)])
-    other_weight = swap(own_weight, "core")
+    weight = assemble(place, home, first, second, third, last, early, late)
 
     tables = rope_tables(seq_rows, head_size)
     gain_row = lax.dynamic_slice_in_dim(key_gain, z, 1, 0)
-    half = normed.shape[0] // 2
     query_cols = (slab_heads - 1) * head_size
     part = seq_rows // 2
 
@@ -252,8 +243,7 @@
 
     result = ()
     for start in range(0, seq_rows, part):
-        tokens = normed[:, start : start + part]
-        partial = product(tokens[:half], own_weight) + product(tokens[half:], other_weight)
+        partial = product(normed[:, start : start + part], weight)
         got = swap(partial[:, query_cols:].astype(jnp.bfloat16), "xh")
         result = attend(prompt_len, partial, got, query_gain, gain_row, tables, tuple(result))
     return result[0]

time: 182 us -> 171 us (0.940)
  starting transfers between devices: 103 us -> 48.2 us
  blocking collectives: 0 us -> 38.9 us
  between operations: 2.04 us -> 15 us
  local copies, waits for them, and re-layouts: 21.9 us -> 12.3 us
  waiting for transfers between devices: 32.1 us -> 35.6 us
  matrix products: 6.97 us -> 3.49 us
  other arithmetic: 6.1 us -> 8.11 us
    all_to_all x0 -> x1, blocking collectives: none -> 38.9 us  [global_sum(): return jnp.sum(lax.all_to_all(spread, AXES, 0, 0, tiled=True)[:, 0])]
    ppermute x14 -> x4, starting transfers between devices: 58.1 us -> 22.2 us  [onward(): return lax.ppermute(block, ('core', 'y'), pairs)]
    all_to_all x1 -> x0, starting transfers between devices: 22.2 us -> none  [global_sum(): return jnp.sum(lax.all_to_all(spread, AXES, 0, 0, tiled=True)[:, 0])]
    unnamed x69 -> x23, local copies, waits for them, and re-layouts: 17 us -> 7.96 us
    ppermute x4 -> x6, waiting for transfers between devices: 5.11 us -> 13.8 us  [swap(): return lax.ppermute(array, axis, [(0, 1), (1, 0)])]
    all_to_all x1 -> x0, waiting for transfers between devices: 6.76 us -> none  [global_sum(): return jnp.sum(lax.all_to_all(spread, AXES, 0, 0, tiled=True)[:, 0])]
    ppermute x4 -> x6, starting transfers between devices: 18.7 us -> 23.1 us  [swap(): return lax.ppermute(array, axis, [(0, 1), (1, 0)])]
    dot_general x4 -> x2, matrix products: 6.97 us -> 3.49 us  [product(): lax.dot_general(rows, weight, (((0,), (0,)), ((), ())), preferred_element...]
  transfers between devices with their start and end apart: 21 -> 13, of which waited for: 8 -> 9; matrix products, arithmetic and copies ran while one was open for 6% -> 7% of each run, Pallas kernels for 2% -> 2%
where the time goes in v4:
time: 171 us; the launch traced here: 170 us
  starting transfers between devices  48.2 us (28%)
  blocking collectives  38.9 us (23%)
  waiting for transfers between devices  35.6 us (21%)
  between operations  15 us (9%)
  local copies, waits for them, and re-layouts  12.3 us (7%)
  Pallas kernels  8.45 us (5%)
  other arithmetic  8.11 us (5%)
  matrix products  3.49 us (2%)
    all_to_all x1, blocking collectives, global_sum(): return jnp.sum(lax.all_to_all(spread, AXES, 0, 0, tiled=True)[:, 0])  38.9 us
    ppermute x6, starting transfers between devices, swap(): return lax.ppermute(array, axis, [(0, 1), (1, 0)])  23.1 us
    ppermute x4, starting transfers between devices, onward(): return lax.ppermute(block, ('core', 'y'), pairs)  22.2 us
    ppermute x4, waiting for transfers between devices, onward(): return lax.ppermute(block, ('core', 'y'), pairs)  17.3 us
    ppermute x6, waiting for transfers between devices, swap(): return lax.ppermute(array, axis, [(0, 1), (1, 0)])  13.8 us
    unnamed x23, local copies, waits for them, and re-layouts  7.96 us
    pallas_call x2, Pallas kernels, attend(): return call(limit, own, got, query_gain, key_gain, cosine, sine, *before)  5.19 us
    ppermute x2, waiting for transfers between devices, to_column(): return lax.ppermute(block, ('xl', 'y', 'xh'), pairs)  3.8 us
  transfers between devices with their start and end apart: 13, of which 9 were waited for; matrix products, arithmetic and copies ran while one was open for 7% of the time, Pallas kernels for 2%

profile of v4, /device:TPU:1, one launch (start us, length us, event | category | flops | bytes accessed | tf_op | source)
XLA Modules:
  0.0 170.1 jit_solution(17317138032485220865)
XLA Ops:
  6.5 0.7 all-gather.2.cloned.1.call-update
  7.3 2.0 %multiply_reduce_fusion = f32[]{:T(128)} fusion(bf16[160,1,3,128]{3,0,2,1:T(8,128)(2,1)} %param.16), kind=kLoop, calls=%fused_computation.16 | loop fusion | flops 184319 | bytes 122884 | tf_op jit(solution)/shard_map/reduce_sum | solution.py:200
  9.3 0.8 broadcast_in_dim.12
  10.1 38.9 %all_to_all.9 = f32[512,1,128]{2,1,0:T(1,128)S(1)} all-to-all(f32[512,1,128]{2,1,0:T(1,128)S(1)} %broadcast_in_dim.12), channel_id=1, replica_groups=mesh['xl'=2,'core'=2,'y'=8,'z'=8,'xh'=2] {'xl','core','y','z','xh'}, dimensions={0} | all-to-all | bytes 524288 | tf_op jit(solution)/shard_map/all_to_all | solution.py:169
  48.9 0.7 slice_reduce_fusion
  50.3 3.2 %convert_reduce_fusion = bf16[160,3,128]{2,1,0:T(4,128)(2,1)S(1)} fusion(f32[160,1,3,128]{3,1,2,0:T(1,128)} %param.15, f32[160,1,3,128]{3,1,2,0:T(1,128)} %param.18, f32[160,1,3,128]{3,1,2,0:T(1,128)} %param.17, bf16[160,1,3,128]{3,0,2,1:T(8,128)(2,1)} %param.16, f32[]{:T(128)S(6)} %sqrt.6), kind=kLoop, calls=%fused_computation.15 | loop fusion | flops 860160 | bytes 983044 | tf_op jit(solution)/shard_map/convert_element_type | solution.py:206
  53.6 0.7 collective-permute-start
  54.2 2.2 %collective-permute-start.1 = (bf16[160,384]{1,0:T(8,128)(2,1)S(1)}, bf16[160,384]{1,0:T(8,128)(2,1)S(1)}, u32[]{:S(2)}, u32[]{:S(2)}) collective-permute-start(bf16[160,384]{1,0:T(8,128)(2,1)S(1)} %bitcast.27), channel_id=1, source_target_pairs={{0,256},{1,368},{16,272},{17,288},{32,273},{33,289},{48,321},{49,3... | collective-permute-start | bytes 368648 | tf_op jit(solution)/shard_map/ppermute | solution.py:180
  56.4 0.0 collective-permute-done
  56.5 3.8 %collective-permute-done.1 = bf16[160,384]{1,0:T(8,128)(2,1)S(1)} collective-permute-done((bf16[160,384]{1,0:T(8,128)(2,1)S(1)}, bf16[160,384]{1,0:T(8,128)(2,1)S(1)}, u32[]{:S(2)}, u32[]{:S(2)}) %collective-permute-start.1) | collective-permute-done | bytes 122912 | tf_op jit(solution)/shard_map/ppermute | solution.py:180
  60.3 6.4 %collective-permute-start.2 = (bf16[2,160,384]{2,1,0:T(8,128)(2,1)S(1)}, bf16[2,160,384]{2,1,0:T(8,128)(2,1)S(1)}, u32[]{:S(2)}, u32[]{:S(2)}) collective-permute-start(bf16[2,160,384]{2,1,0:T(8,128)(2,1)S(1)} %get-tuple-element.24), channel_id=1, source_target_pairs={{0,128},{128,0},{1,129},{129,1},{2,130},{130,2},{3,131},{131,3},{4... | collective-permute-start | bytes 737288 | tf_op jit(solution)/shard_map/ppermute | solution.py:161
  66.8 1.1 collective-permute-done.2
  67.9 0.1 pad_maximum_fusion.2.home_ref
  67.9 7.2 %collective-permute-start.3 = (bf16[2,2,160,384]{3,2,1,0:T(8,128)(2,1)S(1)}, bf16[2,2,160,384]{3,2,1,0:T(8,128)(2,1)S(1)}, u32[]{:S(2)}, u32[]{:S(2)}) collective-permute-start(bf16[2,2,160,384]{3,2,1,0:T(8,128)(2,1)S(1)} %pad_maximum_fusion.2.home_ref), channel_id=1, source_target_pairs={{0,16},{16,32},{32,48},{48,64},{64,80},{80,96},{96,112},{112,0},{1... | collective-permute-start | bytes 1474568 | tf_op jit(solution)/shard_map/ppermute | solution.py:185
  75.2 5.8 %collective-permute-done.3.refs_0_ = bf16[2,2,160,384]{3,2,1,0:T(8,128)(2,1)S(1)} collective-permute-done((bf16[2,2,160,384]{3,2,1,0:T(8,128)(2,1)S(1)}, bf16[2,2,160,384]{3,2,1,0:T(8,128)(2,1)S(1)}, u32[]{:S(2)}, u32[]{:S(2)}) %collective-permute-start.3) | collective-permute-done | bytes 491552 | tf_op jit(solution)/shard_map/ppermute | solution.py:185
  80.9 5.0 %collective-permute-start.4 = (bf16[2,2,160,384]{3,2,1,0:T(8,128)(2,1)S(1)}, bf16[2,2,160,384]{3,2,1,0:T(8,128)(2,1)S(1)}, u32[]{:S(2)}, u32[]{:S(2)}) collective-permute-start(bf16[2,2,160,384]{3,2,1,0:T(8,128)(2,1)S(1)} %collective-permute-done.3.refs_0_), channel_id=1, source_target_pairs={{0,16},{16,32},{32,48},{48,64},{64,80},{80,96},{96,112},{112,0},{1... | collective-permute-start | bytes 1474568 | tf_op jit(solution)/shard_map/ppermute | solution.py:185
  85.9 5.8 %collective-permute-done.4.refs_1_ = bf16[2,2,160,384]{3,2,1,0:T(8,128)(2,1)S(1)} collective-permute-done((bf16[2,2,160,384]{3,2,1,0:T(8,128)(2,1)S(1)}, bf16[2,2,160,384]{3,2,1,0:T(8,128)(2,1)S(1)}, u32[]{:S(2)}, u32[]{:S(2)}) %collective-permute-start.4) | collective-permute-done | bytes 491552 | tf_op jit(solution)/shard_map/ppermute | solution.py:185
  91.7 5.0 %collective-permute-start.5 = (bf16[2,2,160,384]{3,2,1,0:T(8,128)(2,1)S(1)}, bf16[2,2,160,384]{3,2,1,0:T(8,128)(2,1)S(1)}, u32[]{:S(2)}, u32[]{:S(2)}) collective-permute-start(bf16[2,2,160,384]{3,2,1,0:T(8,128)(2,1)S(1)} %collective-permute-done.4.refs_1_), channel_id=1, source_target_pairs={{0,16},{16,32},{32,48},{48,64},{64,80},{80,96},{96,112},{112,0},{1... | collective-permute-start | bytes 1474568 | tf_op jit(solution)/shard_map/ppermute | solution.py:185
  96.7 5.8 %collective-permute-done.5.refs_2_ = bf16[2,2,160,384]{3,2,1,0:T(8,128)(2,1)S(1)} collective-permute-done((bf16[2,2,160,384]{3,2,1,0:T(8,128)(2,1)S(1)}, bf16[2,2,160,384]{3,2,1,0:T(8,128)(2,1)S(1)}, u32[]{:S(2)}, u32[]{:S(2)}) %collective-permute-start.5) | collective-permute-done | bytes 491552 | tf_op jit(solution)/shard_map/ppermute | solution.py:185
  102.5 0.7 slice_bitcast_fusion
  103.2 5.0 %collective-permute-start.6 = (bf16[2,160,384]{2,1,0:T(8,128)(2,1)}, bf16[2,160,384]{2,1,0:T(8,128)(2,1)S(1)}, u32[]{:S(2)}, u32[]{:S(2)}) collective-permute-start(bf16[2,160,384]{2,1,0:T(8,128)(2,1)} %slice_bitcast_fusion), channel_id=1, source_target_pairs={{0,16},{16,32},{32,48},{48,64},{64,80},{80,96},{96,112},{112,0},{1... | collective-permute-start | bytes 737288 | tf_op jit(solution)/shard_map/ppermute | solution.py:185
  108.2 1.1 pad_maximum_fusion
  109.3 2.8 %collective-permute-start.8 = (bf16[2,2,2,160,384]{4,3,2,1,0:T(8,128)(2,1)}, bf16[2,2,2,160,384]{4,3,2,1,0:T(8,128)(2,1)}, u32[]{:S(2)}, u32[]{:S(2)}) collective-permute-start(bf16[2,2,2,160,384]{4,3,2,1,0:T(8,128)(2,1)} %pad_maximum_fusion), channel_id=1, source_target_pairs={{0,128},{128,0},{1,129},{129,1},{2,130},{130,2},{3,131},{131,3},{4... | collective-permute-start | bytes 2949128 | tf_op jit(solution)/shard_map/ppermute | solution.py:161
  112.1 2.1 %copy-done.1 = bf16[2560,768]{1,0:T(8,128)(2,1)S(1)} copy-done((bf16[2560,768]{1,0:T(8,128)(2,1)S(1)}, bf16[2560,768]{1,0:T(8,128)(2,1)}, u32[]{:S(2)}) %copy-start.1) | copy-done | bytes 3932184
  114.2 0.2 squares.1.square_ref
  114.4 3.7 %collective-permute-start.7 = (f32[1,768]{1,0:T(1,128)S(1)}, f32[1,768]{1,0:T(1,128)S(1)}, u32[]{:S(2)}, u32[]{:S(2)}) collective-permute-start(f32[1,768]{1,0:T(1,128)S(1)} %squares.1.square_ref), channel_id=1, source_target_pairs={{0,1},{1,0},{2,3},{3,2},{4,5},{5,4},{6,7},{7,6},{8,9},{9,8},{10,11... | collective-permute-start | bytes 9224 | tf_op jit(solution)/shard_map/ppermute | solution.py:161
  118.2 0.1 reshape.88
  118.3 1.1 reshape.90.gain_ref
  119.4 0.8 collective-permute-done.7.other_ref
  120.3 2.1 %copy-done.2 = bf16[2560,768]{1,0:T(8,128)(2,1)S(1)} copy-done((bf16[2560,768]{1,0:T(8,128)(2,1)S(1)}, bf16[2560,768]{1,0:T(8,128)(2,1)}, u32[]{:S(2)}) %copy-start.2) | copy-done | bytes 3932184
  122.4 1.5 normalise.1
  123.8 1.8 %copy-done.3 = bf16[2560,768]{1,0:T(8,128)(2,1)} copy-done((bf16[2560,768]{1,0:T(8,128)(2,1)}, bf16[2560,768]{1,0:T(8,128)(2,1)S(1)}, u32[]{:S(2)}) %copy-start.3) | copy-done | bytes 3932184
  125.7 1.0 pad_maximum_fusion.1
  126.7 3.1 %collective-permute-start.9 = (bf16[3,2,160,384]{3,2,1,0:T(8,128)(2,1)}, bf16[3,2,160,384]{3,2,1,0:T(8,128)(2,1)S(1)}, u32[]{:S(2)}, u32[]{:S(2)}) collective-permute-start(bf16[3,2,160,384]{3,2,1,0:T(8,128)(2,1)} %pad_maximum_fusion.1), channel_id=1, source_target_pairs={{0,128},{128,0},{1,129},{129,1},{2,130},{130,2},{3,131},{131,3},{4... | collective-permute-start | bytes 2211848 | tf_op jit(solution)/shard_map/ppermute | solution.py:161
  129.8 1.9 %collective-permute-done.9.refs_5_ = bf16[3,2,160,384]{3,2,1,0:T(8,128)(2,1)S(1)} collective-permute-done((bf16[3,2,160,384]{3,2,1,0:T(8,128)(2,1)}, bf16[3,2,160,384]{3,2,1,0:T(8,128)(2,1)S(1)}, u32[]{:S(2)}, u32[]{:S(2)}) %collective-permute-start.9) | collective-permute-done | bytes 737312 | tf_op jit(solution)/shard_map/ppermute | solution.py:161
  131.8 1.6 assemble.1
  133.4 1.7 %fusion.own_ref = f32[384,768]{1,0:T(8,128)S(1)} fusion(bf16[2560,768]{1,0:T(8,128)(2,1)S(1)} %assemble.1, bf16[2560,768]{1,0:T(8,128)(2,1)S(1)} %copy-done.4), kind=kOutput, calls=%fused_computation | convolution fusion | flops 1509949440 | bytes 7077888 | tf_op jit(solution)/shard_map/dot_general | solution.py:242
  135.1 0.8 slice.38
  135.9 4.0 %collective-permute-start.11 = (bf16[384,512]{1,0:T(8,128)(2,1)}, bf16[384,512]{1,0:T(8,128)(2,1)S(1)}, u32[]{:S(2)}, u32[]{:S(2)}) collective-permute-start(bf16[384,512]{1,0:T(8,128)(2,1)} %slice.38), channel_id=1, source_target_pairs={{0,1},{1,0},{2,3},{3,2},{4,5},{5,4},{6,7},{7,6},{8,9},{9,8},{10,11... | collective-permute-start | bytes 1179656 | tf_op jit(solution)/shard_map/ppermute | solution.py:161
  139.9 1.7 %fusion.2.own_ref = f32[384,768]{1,0:T(8,128)S(1)} fusion(bf16[2560,768]{1,0:T(8,128)(2,1)S(1)} %assemble.1, bf16[2560,768]{1,0:T(8,128)(2,1)S(1)} %copy-done.4), kind=kOutput, calls=%fused_computation.2 | convolution fusion | flops 1509949440 | bytes 7077888 | tf_op jit(solution)/shard_map/dot_general | solution.py:242
  141.7 0.8 slice.39
  142.5 3.1 %collective-permute-start.10 = (bf16[384,512]{1,0:T(8,128)(2,1)}, bf16[384,512]{1,0:T(8,128)(2,1)S(1)}, u32[]{:S(2)}, u32[]{:S(2)}) collective-permute-start(bf16[384,512]{1,0:T(8,128)(2,1)} %slice.39), channel_id=1, source_target_pairs={{0,1},{1,0},{2,3},{3,2},{4,5},{5,4},{6,7},{7,6},{8,9},{9,8},{10,11... | collective-permute-start | bytes 1179656 | tf_op jit(solution)/shard_map/ppermute | solution.py:161
  146.2 3.8 %collective-permute-done.11.got_ref = bf16[384,512]{1,0:T(8,128)(2,1)S(1)} collective-permute-done((bf16[384,512]{1,0:T(8,128)(2,1)}, bf16[384,512]{1,0:T(8,128)(2,1)S(1)}, u32[]{:S(2)}, u32[]{:S(2)}) %collective-permute-start.11) | collective-permute-done | bytes 393248 | tf_op jit(solution)/shard_map/ppermute | solution.py:161
  150.0 2.2 %attend.2 = (bf16[384,256]{1,0:T(8,128)(2,1)S(1)}, bf16[384,128]{1,0:T(8,128)(2,1)S(1)}, bf16[384,128]{1,0:T(8,128)(2,1)S(1)}) custom-call(s32[1]{0:T(128)S(6)} %copy.31.limit_ref, f32[384,768]{1,0:T(8,128)S(1)} %fusion.own_ref, bf16[384,512]{1,0:T(8,128)(2,1)S(1)} %collective-permute-done.11.got_ref, f32[2,128]{1,0:T(2,128)S(1)} %copy-done.9, ...), custom_call_target="tpu_custom_call" | custom-call | tf_op jit(solution)/shard_map/attend/pallas_call | solution.py:157
  152.2 6.2 %collective-permute-done.10.got_ref = bf16[384,512]{1,0:T(8,128)(2,1)S(1)} collective-permute-done((bf16[384,512]{1,0:T(8,128)(2,1)}, bf16[384,512]{1,0:T(8,128)(2,1)S(1)}, u32[]{:S(2)}, u32[]{:S(2)}) %collective-permute-start.10) | collective-permute-done | bytes 393248 | tf_op jit(solution)/shard_map/ppermute | solution.py:161
  158.4 0.9 copy-done.7
  159.3 0.9 copy-done.8
  160.3 3.0 %attend.3 = (bf16[768,256]{1,0:T(8,128)(2,1)}, bf16[768,128]{1,0:T(8,128)(2,1)}, bf16[768,128]{1,0:T(8,128)(2,1)}) custom-call(s32[1]{0:T(128)S(6)} %copy.31.limit_ref, f32[384,768]{1,0:T(8,128)S(1)} %fusion.2.own_ref, bf16[384,512]{1,0:T(8,128)(2,1)S(1)} %collective-permute-done.10.got_ref, f32[2,128]{1,0:T(2,128)S(1)} %copy-done.9, ...), custom_call_target="tpu_custom_call" | custom-call | tf_op jit(solution)/shard_map/attend/pallas_call | solution.py:157
  (29 shorter events, 0.2 us)
Async XLA Ops:
  6.5 139.7 %copy-start = (f32[8,128]{1,0:T(8,128)S(1)}, f32[8,128]{1,0:T(8,128)}, u32[]{:S(2)}) copy-start(f32[8,128]{1,0:T(8,128)} %param.20) | copy-start | bytes 12292
  6.5 74.4 %all-gather.2.cloned.1.call-start = ((), (), s32[]{:S(2)}) async-start(), calls=%async_computation.1 | async-start | bytes 4423680 | tf_op jit(solution)/shard_map/all_gather | solution.py:197
  53.6 2.9 %collective-permute-start = (bf16[160,384]{1,0:T(8,128)(2,1)S(1)}, bf16[160,384]{1,0:T(8,128)(2,1)S(1)}, u32[]{:S(2)}, u32[]{:S(2)}) collective-permute-start(bf16[160,384]{1,0:T(8,128)(2,1)S(1)} %bitcast.26), channel_id=1, source_target_pairs={{0,0},{1,112},{16,16},{17,32},{32,17},{33,33},{48,65},{49,49},{64,... | collective-permute-start | bytes 368648 | tf_op jit(solution)/shard_map/ppermute | solution.py:180
  54.2 6.0 %collective-permute-start.1 = (bf16[160,384]{1,0:T(8,128)(2,1)S(1)}, bf16[160,384]{1,0:T(8,128)(2,1)S(1)}, u32[]{:S(2)}, u32[]{:S(2)}) collective-permute-start(bf16[160,384]{1,0:T(8,128)(2,1)S(1)} %bitcast.27), channel_id=1, source_target_pairs={{0,256},{1,368},{16,272},{17,288},{32,273},{33,289},{48,321},{49,3... | collective-permute-start | bytes 368648 | tf_op jit(solution)/shard_map/ppermute | solution.py:180
  60.3 57.9 %copy-start.10 = (f32[5120]{0:T(1024)S(1)}, f32[5120]{0:T(1024)}, u32[]{:S(2)}) copy-start(f32[5120]{0:T(1024)} %param.14) | copy-start | bytes 61444
  60.3 7.6 %collective-permute-start.2 = (bf16[2,160,384]{2,1,0:T(8,128)(2,1)S(1)}, bf16[2,160,384]{2,1,0:T(8,128)(2,1)S(1)}, u32[]{:S(2)}, u32[]{:S(2)}) collective-permute-start(bf16[2,160,384]{2,1,0:T(8,128)(2,1)S(1)} %get-tuple-element.24), channel_id=1, source_target_pairs={{0,128},{128,0},{1,129},{129,1},{2,130},{130,2},{3,131},{131,3},{4... | collective-permute-start | bytes 737288 | tf_op jit(solution)/shard_map/ppermute | solution.py:161
  67.9 13.0 %collective-permute-start.3 = (bf16[2,2,160,384]{3,2,1,0:T(8,128)(2,1)S(1)}, bf16[2,2,160,384]{3,2,1,0:T(8,128)(2,1)S(1)}, u32[]{:S(2)}, u32[]{:S(2)}) collective-permute-start(bf16[2,2,160,384]{3,2,1,0:T(8,128)(2,1)S(1)} %pad_maximum_fusion.2.home_ref), channel_id=1, source_target_pairs={{0,16},{16,32},{32,48},{48,64},{64,80},{80,96},{96,112},{112,0},{1... | collective-permute-start | bytes 1474568 | tf_op jit(solution)/shard_map/ppermute | solution.py:185
  80.9 10.8 %collective-permute-start.4 = (bf16[2,2,160,384]{3,2,1,0:T(8,128)(2,1)S(1)}, bf16[2,2,160,384]{3,2,1,0:T(8,128)(2,1)S(1)}, u32[]{:S(2)}, u32[]{:S(2)}) collective-permute-start(bf16[2,2,160,384]{3,2,1,0:T(8,128)(2,1)S(1)} %collective-permute-done.3.refs_0_), channel_id=1, source_target_pairs={{0,16},{16,32},{32,48},{48,64},{64,80},{80,96},{96,112},{112,0},{1... | collective-permute-start | bytes 1474568 | tf_op jit(solution)/shard_map/ppermute | solution.py:185
  91.7 10.8 %collective-permute-start.5 = (bf16[2,2,160,384]{3,2,1,0:T(8,128)(2,1)S(1)}, bf16[2,2,160,384]{3,2,1,0:T(8,128)(2,1)S(1)}, u32[]{:S(2)}, u32[]{:S(2)}) collective-permute-start(bf16[2,2,160,384]{3,2,1,0:T(8,128)(2,1)S(1)} %collective-permute-done.4.refs_1_), channel_id=1, source_target_pairs={{0,16},{16,32},{32,48},{48,64},{64,80},{80,96},{96,112},{112,0},{1... | collective-permute-start | bytes 1474568 | tf_op jit(solution)/shard_map/ppermute | solution.py:185
  103.2 22.5 %collective-permute-start.6 = (bf16[2,160,384]{2,1,0:T(8,128)(2,1)}, bf16[2,160,384]{2,1,0:T(8,128)(2,1)S(1)}, u32[]{:S(2)}, u32[]{:S(2)}) collective-permute-start(bf16[2,160,384]{2,1,0:T(8,128)(2,1)} %slice_bitcast_fusion), channel_id=1, source_target_pairs={{0,16},{16,32},{32,48},{48,64},{64,80},{80,96},{96,112},{112,0},{1... | collective-permute-start | bytes 737288 | tf_op jit(solution)/shard_map/ppermute | solution.py:185
  109.3 20.5 %collective-permute-start.8 = (bf16[2,2,2,160,384]{4,3,2,1,0:T(8,128)(2,1)}, bf16[2,2,2,160,384]{4,3,2,1,0:T(8,128)(2,1)}, u32[]{:S(2)}, u32[]{:S(2)}) collective-permute-start(bf16[2,2,2,160,384]{4,3,2,1,0:T(8,128)(2,1)} %pad_maximum_fusion), channel_id=1, source_target_pairs={{0,128},{128,0},{1,129},{129,1},{2,130},{130,2},{3,131},{131,3},{4... | collective-permute-start | bytes 2949128 | tf_op jit(solution)/shard_map/ppermute | solution.py:161
  112.1 2.1 %copy-start.1 = (bf16[2560,768]{1,0:T(8,128)(2,1)S(1)}, bf16[2560,768]{1,0:T(8,128)(2,1)}, u32[]{:S(2)}) copy-start(bf16[2560,768]{1,0:T(8,128)(2,1)} %all-gather.2.cloned.1.call-done.features_ref) | copy-start | bytes 11796484
  114.4 5.8 %collective-permute-start.7 = (f32[1,768]{1,0:T(1,128)S(1)}, f32[1,768]{1,0:T(1,128)S(1)}, u32[]{:S(2)}, u32[]{:S(2)}) collective-permute-start(f32[1,768]{1,0:T(1,128)S(1)} %squares.1.square_ref), channel_id=1, source_target_pairs={{0,1},{1,0},{2,3},{3,2},{4,5},{5,4},{6,7},{7,6},{8,9},{9,8},{10,11... | collective-permute-start | bytes 9224 | tf_op jit(solution)/shard_map/ppermute | solution.py:161
  120.3 2.1 %copy-start.2 = (bf16[2560,768]{1,0:T(8,128)(2,1)S(1)}, bf16[2560,768]{1,0:T(8,128)(2,1)}, u32[]{:S(2)}) copy-start(bf16[2560,768]{1,0:T(8,128)(2,1)} %all-gather.2.cloned.1.call-done.features_ref) | copy-start | bytes 11796484
  123.8 1.9 %copy-start.3 = (bf16[2560,768]{1,0:T(8,128)(2,1)}, bf16[2560,768]{1,0:T(8,128)(2,1)S(1)}, u32[]{:S(2)}) copy-start(bf16[2560,768]{1,0:T(8,128)(2,1)S(1)} %normalise.1) | copy-start | bytes 11796484
  126.7 5.1 %collective-permute-start.9 = (bf16[3,2,160,384]{3,2,1,0:T(8,128)(2,1)}, bf16[3,2,160,384]{3,2,1,0:T(8,128)(2,1)S(1)}, u32[]{:S(2)}, u32[]{:S(2)}) collective-permute-start(bf16[3,2,160,384]{3,2,1,0:T(8,128)(2,1)} %pad_maximum_fusion.1), channel_id=1, source_target_pairs={{0,128},{128,0},{1,129},{129,1},{2,130},{130,2},{3,131},{131,3},{4... | collective-permute-start | bytes 2211848 | tf_op jit(solution)/shard_map/ppermute | solution.py:161
  129.8 3.6 %copy-start.4 = (bf16[2560,768]{1,0:T(8,128)(2,1)S(1)}, bf16[2560,768]{1,0:T(8,128)(2,1)}, u32[]{:S(2)}) copy-start(bf16[2560,768]{1,0:T(8,128)(2,1)} %copy-done.3) | copy-start | bytes 11796484
  135.9 14.1 %copy-start.5 = (f32[384,128]{1,0:T(8,128)S(1)}, f32[384,128]{1,0:T(8,128)}, u32[]{:S(2)}) copy-start(f32[384,128]{1,0:T(8,128)} %constant.66.clone.cos_ref) | copy-start | bytes 589828
  135.9 14.1 %copy-start.6 = (f32[384,128]{1,0:T(8,128)S(1)}, f32[384,128]{1,0:T(8,128)}, u32[]{:S(2)}) copy-start(f32[384,128]{1,0:T(8,128)} %constant.67.clone.sin_ref) | copy-start | bytes 589828
  135.9 14.1 %copy-start.9 = (f32[2,128]{1,0:T(2,128)S(1)}, f32[2,128]{1,0:T(2,128)}, u32[]{:S(2)}) copy-start(f32[2,128]{1,0:T(2,128)} %query_gain_ref.3) | copy-start | bytes 3076
  135.9 14.1 %collective-permute-start.11 = (bf16[384,512]{1,0:T(8,128)(2,1)}, bf16[384,512]{1,0:T(8,128)(2,1)S(1)}, u32[]{:S(2)}, u32[]{:S(2)}) collective-permute-start(bf16[384,512]{1,0:T(8,128)(2,1)} %slice.38), channel_id=1, source_target_pairs={{0,1},{1,0},{2,3},{3,2},{4,5},{5,4},{6,7},{7,6},{8,9},{9,8},{10,11... | collective-permute-start | bytes 1179656 | tf_op jit(solution)/shard_map/ppermute | solution.py:161
  142.5 15.9 %collective-permute-start.10 = (bf16[384,512]{1,0:T(8,128)(2,1)}, bf16[384,512]{1,0:T(8,128)(2,1)S(1)}, u32[]{:S(2)}, u32[]{:S(2)}) collective-permute-start(bf16[384,512]{1,0:T(8,128)(2,1)} %slice.39), channel_id=1, source_target_pairs={{0,1},{1,0},{2,3},{3,2},{4,5},{5,4},{6,7},{7,6},{8,9},{9,8},{10,11... | collective-permute-start | bytes 1179656 | tf_op jit(solution)/shard_map/ppermute | solution.py:161
  158.4 0.9 copy-start.7
  159.3 0.9 copy-start.8
Sparse Core Ops, SparseCore 0:
  9.4 66.8 all-gather.1

commit v5 on v4

--- a/solution.py
+++ b/solution.py
@@ -43,19 +43,26 @@
 
 
 def assemble_kernel(place_ref, home_ref, *refs):
-    *step_refs, last_ref, early_ref, late_ref, out_ref = refs
+    *step_refs, last_ref, early_ref, late_ref, own_ref, sent_ref = refs
     _, _, rows, cols = home_ref.shape
-    head = out_ref.shape[1] // 6
+    head = own_ref.shape[1] // 4
     wide = cols - head
 
     def put(step, lane, block_ref, *index):
         row = pl.multiple_of(place_ref[0, step] * rows, 32)
-        query_col = pl.multiple_of(place_ref[1, step] * wide, 128)
-        pair_col = pl.multiple_of(2 * wide + place_ref[2, step] * head, 128)
-        for near in range(2):
-            span = pl.ds((lane * 2 + near) * 4 * rows + row, rows)
-            out_ref[span, pl.ds(query_col, wide)] = block_ref[*index, near, :, :wide]
-            out_ref[span, pl.ds(pair_col, head)] = block_ref[*index, near, :, wide:]
+        pair_col = pl.multiple_of(wide + place_ref[2, step] * head, 128)
+        spans = [pl.ds((lane * 2 + near) * 4 * rows + row, rows) for near in range(2)]
+
+        def put_queries(out_ref):
+            for near, span in enumerate(spans):
+                out_ref[span, :wide] = block_ref[*index, near, :, :wide]
+
+        pl.when(place_ref[1, step] == 0)(lambda: put_queries(own_ref))
+        pl.when(place_ref[1, step] == 1)(lambda: put_queries(sent_ref))
+        for near, span in enumerate(spans):
+            pair = block_ref[*index, near, :, wide:]
+            own_ref[span, pl.ds(pair_col, head)] = pair
+            sent_ref[span, pl.ds(pair_col, head)] = pair
 
     for lane in range(2):
         put(0, lane, home_ref, lane)
@@ -70,8 +77,8 @@
 
 def assemble(place, home, *rest):
     _, _, rows, cols = home.shape
-    shape = jax.ShapeDtypeStruct((16 * rows, 2 * cols), home.dtype)
-    call = local_call(assemble_kernel, "assemble", shape, [SMEM] + [VMEM] * (1 + len(rest)), VMEM)
+    shape = [jax.ShapeDtypeStruct((16 * rows, 4 * cols // 3), home.dtype)] * 2
+    call = local_call(assemble_kernel, "assemble", shape, [SMEM] + [VMEM] * (1 + len(rest)), [VMEM] * 2)
     return call(place, home, *rest)
 
 
@@ -107,7 +114,7 @@
     return call(place, square, other, gain, features)
 
 
-def attend_kernel(tile, first, length, limit_ref, own_ref, got_ref, query_gain_ref, key_gain_ref, cos_ref, sin_ref, *refs):
+def attend_kernel(tile, first, limit_ref, own_ref, got_ref, query_gain_ref, key_gain_ref, cos_ref, sin_ref, *refs):
     before, out_ref, keys_ref, values_ref = refs[:-3], *refs[-3:]
     heads, head = query_gain_ref.shape
     wide = heads * head
@@ -118,22 +125,22 @@
         keys_ref[:first, :] = before[1][...]
         values_ref[:first, :] = before[2][...]
 
-    def summed(start, size, own_col, got_col):
-        got = got_ref[start : start + size, got_col : got_col + head].astype(jnp.float32)
-        return own_ref[start : start + size, own_col : own_col + head] + got
-
-    cosine, sine = cos_ref[...], sin_ref[...]
-    keys = rms_rotated(summed(0, rows, 2 * wide, wide), key_gain_ref[...], cosine, sine)
+    def summed(start, size, col):
+        got = got_ref[start : start + size, col : col + head].astype(jnp.float32)
+        return own_ref[start : start + size, col : col + head] + got
+
+    cosine, sine = cos_ref[first : first + rows, :], sin_ref[first : first + rows, :]
+    keys = rms_rotated(summed(0, rows, wide), key_gain_ref[...], cosine, sine)
     keys_ref[first:, :] = keys.astype(jnp.bfloat16)
-    values_ref[first:, :] = summed(0, rows, 2 * wide + head, wide + head).astype(jnp.bfloat16)
+    values_ref[first:, :] = summed(0, rows, wide + head).astype(jnp.bfloat16)
     for start in range(0, rows, tile):
         seen = first + start + tile
         row = first + start + lax.broadcasted_iota(jnp.int32, (tile, seen), 0)
         col = lax.broadcasted_iota(jnp.int32, (tile, seen), 1)
         allowed = (col <= row) & (col < limit)
-        cosine, sine = cos_ref[start : start + tile, :], sin_ref[start : start + tile, :]
+        cosine, sine = cos_ref[first + start : seen, :], sin_ref[first + start : seen, :]
         for j in range(heads):
-            projected = summed(start, tile, j * head, j * head)
+            projected = summed(start, tile, j * head)
             query = rms_rotated(projected, query_gain_ref[j : j + 1, :], cosine, sine)
             query = (query * head**-0.5).astype(jnp.bfloat16)
             scores = lax.dot_general(
@@ -150,11 +157,10 @@
     rows = own.shape[0]
     heads, head = query_gain.shape
     first = before[0].shape[0] if before else 0
-    cosine, sine = (table[first : first + rows] for table in tables)
     shape = [jax.ShapeDtypeStruct((first + rows, n), jnp.bfloat16) for n in (heads * head, head, head)]
-    kernel = functools.partial(attend_kernel, rows // 2, first, first + rows)
+    kernel = functools.partial(attend_kernel, rows // 2, first)
     call = local_call(kernel, "attend", shape, [SMEM] + [VMEM] * (6 + len(before)), [VMEM] * 3)
-    return call(limit, own, got, query_gain, key_gain, cosine, sine, *before)
+    return call(limit, own, got, query_gain, key_gain, *tables, *before)
 
 
 def swap(array, axis):
@@ -213,16 +219,17 @@
     first, gathered = lax.optimization_barrier((first, gathered))
 
     square = squares(8, gathered)
+    second = onward(first)
+    second, square = lax.optimization_barrier((second, square))
     other_square = swap(square, "xh")
     gain = lax.dynamic_index_in_dim(norm_gain.reshape(8, 2, width_part), xh, 1, False).reshape(-1, 1)
     place = (((((steps >> 1) & 1) ^ core) * 2 + ((steps >> 2) ^ xl)) * 2 + (steps & 1)).astype(jnp.int32)
     normed = normalise(float(width_all), 8, place, square, other_square, gain, gathered)
 
-    second = onward(first)
     third = onward(second)
+    third, normed = lax.optimization_barrier((third, normed))
     early = swap(jnp.stack([first, second]), "core")
     last = onward(third[0])
-    last, normed = lax.optimization_barrier((last, normed))
     late = swap(jnp.concatenate([third, last[None]]), "core")
 
     up = 1 - 2 * core
@@ -231,21 +238,22 @@
     origin = jnp.where(native, source, (source + 2 * (source & 1) - 1) & 7)
     slab = jnp.where(native, xh, 1 - xh)
     place = jnp.stack([(origin >> 2) * 2 + (origin & 1), slab ^ xh, slab]).astype(jnp.int32)
-    weight = assemble(place, home, first, second, third, last, early, late)
+    own_weight, sent_weight = assemble(place, home, first, second, third, last, early, late)
 
     tables = rope_tables(seq_rows, head_size)
     gain_row = lax.dynamic_slice_in_dim(key_gain, z, 1, 0)
-    query_cols = (slab_heads - 1) * head_size
     part = seq_rows // 2
 
-    def product(rows, weight):
+    def product(start, weight):
+        rows = normed[:, start : start + part]
         return lax.dot_general(rows, weight, (((0,), (0,)), ((), ())), preferred_element_type=jnp.float32)
 
+    starts = range(0, seq_rows, part)
+    got = [swap(product(start, sent_weight).astype(jnp.bfloat16), "xh") for start in starts]
     result = ()
-    for start in range(0, seq_rows, part):
-        partial = product(normed[:, start : start + part], weight)
-        got = swap(partial[:, query_cols:].astype(jnp.bfloat16), "xh")
-        result = attend(prompt_len, partial, got, query_gain, gain_row, tables, tuple(result))
+    for start, other in zip(starts, got):
+        own = product(start, own_weight)
+        result = attend(prompt_len, own, other, query_gain, gain_row, tables, tuple(result))
     return result[0]
 
 

time: 171 us -> 160 us (0.936)
  waiting for transfers between devices: 35.6 us -> 30.6 us
  local copies, waits for them, and re-layouts: 12.3 us -> 8.21 us
  starting transfers between devices: 48.2 us -> 45.1 us
    ppermute x4, waiting for transfers between devices: 17.3 us -> 10.6 us  [onward(): return lax.ppermute(block, ('core', 'y'), pairs)]
    ppermute x4, starting transfers between devices: 22.2 us -> 19.2 us  [onward(): return lax.ppermute(block, ('core', 'y'), pairs)]
    unnamed x23 -> x19, local copies, waits for them, and re-layouts: 7.96 us -> 6.12 us
    dot_general x2 -> x4, matrix products: 3.49 us -> 4.8 us  [product(): lax.dot_general(rows, weight, (((0,), (0,)), ((), ())), preferred_element...]
  transfers between devices with their start and end apart: 13 -> 13, of which waited for: 9 -> 9; matrix products, arithmetic and copies ran while one was open for 7% -> 8% of each run, Pallas kernels for 2% -> 2%
where the time goes in v5:
time: 160 us; the launch traced here: 159 us
  starting transfers between devices  45.1 us (28%)
  blocking collectives  38.9 us (24%)
  waiting for transfers between devices  30.6 us (19%)
  between operations  15.1 us (9%)
  Pallas kernels  8.66 us (5%)
  local copies, waits for them, and re-layouts  8.21 us (5%)
  other arithmetic  8.11 us (5%)
  matrix products  4.8 us (3%)
    all_to_all x1, blocking collectives, global_sum(): return jnp.sum(lax.all_to_all(spread, AXES, 0, 0, tiled=True)[:, 0])  38.9 us
    ppermute x6, starting transfers between devices, swap(): return lax.ppermute(array, axis, [(0, 1), (1, 0)])  23.1 us
    ppermute x4, starting transfers between devices, onward(): return lax.ppermute(block, ('core', 'y'), pairs)  19.2 us
    ppermute x6, waiting for transfers between devices, swap(): return lax.ppermute(array, axis, [(0, 1), (1, 0)])  15.5 us
    ppermute x4, waiting for transfers between devices, onward(): return lax.ppermute(block, ('core', 'y'), pairs)  10.6 us
    unnamed x19, local copies, waits for them, and re-layouts  6.12 us
    pallas_call x2, Pallas kernels, attend(): return call(limit, own, got, query_gain, key_gain, *tables, *before)  5.19 us
    dot_general x4, matrix products, product(): lax.dot_general(rows, weight, (((0,), (0,)), ((), ())), preferred_element...  4.8 us
  transfers between devices with their start and end apart: 13, of which 9 were waited for; matrix products, arithmetic and copies ran while one was open for 8% of the time, Pallas kernels for 2%

profile of v5, /device:TPU:1, one launch (start us, length us, event | category | flops | bytes accessed | tf_op | source)
XLA Modules:
  0.0 159.5 jit_solution(2880368076021997202)
XLA Ops:
  6.5 0.7 all-gather.2.cloned.1.call-update
  7.3 2.0 %multiply_reduce_fusion = f32[]{:T(128)} fusion(bf16[160,1,3,128]{3,0,2,1:T(8,128)(2,1)} %param.14), kind=kLoop, calls=%fused_computation.20 | loop fusion | flops 184319 | bytes 122884 | tf_op jit(solution)/shard_map/reduce_sum | solution.py:206
  9.3 0.8 broadcast_in_dim.12
  10.1 38.9 %all_to_all.9 = f32[512,1,128]{2,1,0:T(1,128)S(1)} all-to-all(f32[512,1,128]{2,1,0:T(1,128)S(1)} %broadcast_in_dim.12), channel_id=1, replica_groups=mesh['xl'=2,'core'=2,'y'=8,'z'=8,'xh'=2] {'xl','core','y','z','xh'}, dimensions={0} | all-to-all | bytes 524288 | tf_op jit(solution)/shard_map/all_to_all | solution.py:175
  48.9 0.7 slice_reduce_fusion
  50.3 3.2 %convert_reduce_fusion = bf16[160,3,128]{2,1,0:T(4,128)(2,1)S(1)} fusion(f32[160,1,3,128]{3,1,2,0:T(1,128)} %param.13, f32[160,1,3,128]{3,1,2,0:T(1,128)} %param.16, f32[160,1,3,128]{3,1,2,0:T(1,128)} %param.15, bf16[160,1,3,128]{3,0,2,1:T(8,128)(2,1)} %param.14, f32[]{:T(128)S(6)} %sqrt.6), kind=kLoop, calls=%fused_computation.19 | loop fusion | flops 860160 | bytes 983044 | tf_op jit(solution)/shard_map/convert_element_type | solution.py:212
  53.6 0.7 collective-permute-start
  54.2 2.2 %collective-permute-start.1 = (bf16[160,384]{1,0:T(8,128)(2,1)S(1)}, bf16[160,384]{1,0:T(8,128)(2,1)S(1)}, u32[]{:S(2)}, u32[]{:S(2)}) collective-permute-start(bf16[160,384]{1,0:T(8,128)(2,1)S(1)} %bitcast.29), channel_id=1, source_target_pairs={{0,256},{1,368},{16,272},{17,288},{32,273},{33,289},{48,321},{49,3... | collective-permute-start | bytes 368648 | tf_op jit(solution)/shard_map/ppermute | solution.py:186
  56.5 3.8 %collective-permute-done.1 = bf16[160,384]{1,0:T(8,128)(2,1)S(1)} collective-permute-done((bf16[160,384]{1,0:T(8,128)(2,1)S(1)}, bf16[160,384]{1,0:T(8,128)(2,1)S(1)}, u32[]{:S(2)}, u32[]{:S(2)}) %collective-permute-start.1) | collective-permute-done | bytes 122912 | tf_op jit(solution)/shard_map/ppermute | solution.py:186
  60.3 0.0 copy-start.8
  60.3 6.4 %collective-permute-start.2 = (bf16[2,160,384]{2,1,0:T(8,128)(2,1)S(1)}, bf16[2,160,384]{2,1,0:T(8,128)(2,1)S(1)}, u32[]{:S(2)}, u32[]{:S(2)}) collective-permute-start(bf16[2,160,384]{2,1,0:T(8,128)(2,1)S(1)} %get-tuple-element.32), channel_id=1, source_target_pairs={{0,128},{128,0},{1,129},{129,1},{2,130},{130,2},{3,131},{131,3},{4... | collective-permute-start | bytes 737288 | tf_op jit(solution)/shard_map/ppermute | solution.py:167
  66.8 1.1 collective-permute-done.2
  67.9 0.1 pad_maximum_fusion.2.home_ref
  68.0 7.2 %collective-permute-start.3 = (bf16[2,2,160,384]{3,2,1,0:T(8,128)(2,1)S(1)}, bf16[2,2,160,384]{3,2,1,0:T(8,128)(2,1)S(1)}, u32[]{:S(2)}, u32[]{:S(2)}) collective-permute-start(bf16[2,2,160,384]{3,2,1,0:T(8,128)(2,1)S(1)} %pad_maximum_fusion.2.home_ref), channel_id=1, source_target_pairs={{0,16},{16,32},{32,48},{48,64},{64,80},{80,96},{96,112},{112,0},{1... | collective-permute-start | bytes 1474568 | tf_op jit(solution)/shard_map/ppermute | solution.py:191
  75.2 5.8 %collective-permute-done.3.refs_0_ = bf16[2,2,160,384]{3,2,1,0:T(8,128)(2,1)S(1)} collective-permute-done((bf16[2,2,160,384]{3,2,1,0:T(8,128)(2,1)S(1)}, bf16[2,2,160,384]{3,2,1,0:T(8,128)(2,1)S(1)}, u32[]{:S(2)}, u32[]{:S(2)}) %collective-permute-start.3) | collective-permute-done | bytes 491552 | tf_op jit(solution)/shard_map/ppermute | solution.py:191
  80.9 5.0 %collective-permute-start.4 = (bf16[2,2,160,384]{3,2,1,0:T(8,128)(2,1)S(1)}, bf16[2,2,160,384]{3,2,1,0:T(8,128)(2,1)S(1)}, u32[]{:S(2)}, u32[]{:S(2)}) collective-permute-start(bf16[2,2,160,384]{3,2,1,0:T(8,128)(2,1)S(1)} %collective-permute-done.3.refs_0_), channel_id=1, source_target_pairs={{0,16},{16,32},{32,48},{48,64},{64,80},{80,96},{96,112},{112,0},{1... | collective-permute-start | bytes 1474568 | tf_op jit(solution)/shard_map/ppermute | solution.py:191
  86.0 2.1 %copy-done.1 = bf16[2560,768]{1,0:T(8,128)(2,1)S(1)} copy-done((bf16[2560,768]{1,0:T(8,128)(2,1)S(1)}, bf16[2560,768]{1,0:T(8,128)(2,1)}, u32[]{:S(2)}) %copy-start.1) | copy-done | bytes 3932184
  88.1 0.2 squares.1.square_ref
  88.3 3.4 %collective-permute-done.4.refs_1_ = bf16[2,2,160,384]{3,2,1,0:T(8,128)(2,1)S(1)} collective-permute-done((bf16[2,2,160,384]{3,2,1,0:T(8,128)(2,1)S(1)}, bf16[2,2,160,384]{3,2,1,0:T(8,128)(2,1)S(1)}, u32[]{:S(2)}, u32[]{:S(2)}) %collective-permute-start.4) | collective-permute-done | bytes 491552 | tf_op jit(solution)/shard_map/ppermute | solution.py:191
  91.7 5.0 %collective-permute-start.5 = (bf16[2,2,160,384]{3,2,1,0:T(8,128)(2,1)S(1)}, bf16[2,2,160,384]{3,2,1,0:T(8,128)(2,1)S(1)}, u32[]{:S(2)}, u32[]{:S(2)}) collective-permute-start(bf16[2,2,160,384]{3,2,1,0:T(8,128)(2,1)S(1)} %collective-permute-done.4.refs_1_), channel_id=1, source_target_pairs={{0,16},{16,32},{32,48},{48,64},{64,80},{80,96},{96,112},{112,0},{1... | collective-permute-start | bytes 1474568 | tf_op jit(solution)/shard_map/ppermute | solution.py:191
  96.7 1.9 %collective-permute-start.6 = (f32[1,768]{1,0:T(1,128)S(1)}, f32[1,768]{1,0:T(1,128)S(1)}, u32[]{:S(2)}, u32[]{:S(2)}) collective-permute-start(f32[1,768]{1,0:T(1,128)S(1)} %squares.1.square_ref), channel_id=1, source_target_pairs={{0,1},{1,0},{2,3},{3,2},{4,5},{5,4},{6,7},{7,6},{8,9},{9,8},{10,11... | collective-permute-start | bytes 9224 | tf_op jit(solution)/shard_map/ppermute | solution.py:167
  98.7 0.1 reshape.88
  98.8 1.1 reshape.90.gain_ref
  100.0 2.6 %collective-permute-done.6.other_ref = f32[1,768]{1,0:T(1,128)S(1)} collective-permute-done((f32[1,768]{1,0:T(1,128)S(1)}, f32[1,768]{1,0:T(1,128)S(1)}, u32[]{:S(2)}, u32[]{:S(2)}) %collective-permute-start.6) | collective-permute-done | bytes 3104 | tf_op jit(solution)/shard_map/ppermute | solution.py:167
  102.6 2.1 %copy-done.2 = bf16[2560,768]{1,0:T(8,128)(2,1)S(1)} copy-done((bf16[2560,768]{1,0:T(8,128)(2,1)S(1)}, bf16[2560,768]{1,0:T(8,128)(2,1)}, u32[]{:S(2)}) %copy-start.2) | copy-done | bytes 3932184
  104.7 1.5 normalise.1
  106.2 1.8 %copy-done.3 = bf16[2560,768]{1,0:T(8,128)(2,1)} copy-done((bf16[2560,768]{1,0:T(8,128)(2,1)}, bf16[2560,768]{1,0:T(8,128)(2,1)S(1)}, u32[]{:S(2)}) %copy-start.3) | copy-done | bytes 3932184
  108.0 1.9 %collective-permute-start.7 = (bf16[2,160,384]{2,1,0:T(8,128)(2,1)S(1)}, bf16[2,160,384]{2,1,0:T(8,128)(2,1)S(1)}, u32[]{:S(2)}, u32[]{:S(2)}) collective-permute-start(bf16[2,160,384]{2,1,0:T(8,128)(2,1)S(1)} %slice_bitcast_fusion), channel_id=1, source_target_pairs={{0,16},{16,32},{32,48},{48,64},{64,80},{80,96},{96,112},{112,0},{1... | collective-permute-start | bytes 737288 | tf_op jit(solution)/shard_map/ppermute | solution.py:191
  110.0 1.1 pad_maximum_fusion
  111.0 2.8 %collective-permute-start.8 = (bf16[2,2,2,160,384]{4,3,2,1,0:T(8,128)(2,1)}, bf16[2,2,2,160,384]{4,3,2,1,0:T(8,128)(2,1)S(1)}, u32[]{:S(2)}, u32[]{:S(2)}) collective-permute-start(bf16[2,2,2,160,384]{4,3,2,1,0:T(8,128)(2,1)} %pad_maximum_fusion), channel_id=1, source_target_pairs={{0,128},{128,0},{1,129},{129,1},{2,130},{130,2},{3,131},{131,3},{4... | collective-permute-start | bytes 2949128 | tf_op jit(solution)/shard_map/ppermute | solution.py:167
  113.8 1.5 collective-permute-done.7.refs_3_
  115.3 1.0 pad_maximum_fusion.1
  116.3 4.9 %collective-permute-start.9 = (bf16[3,2,160,384]{3,2,1,0:T(8,128)(2,1)}, bf16[3,2,160,384]{3,2,1,0:T(8,128)(2,1)}, u32[]{:S(2)}, u32[]{:S(2)}) collective-permute-start(bf16[3,2,160,384]{3,2,1,0:T(8,128)(2,1)} %pad_maximum_fusion.1), channel_id=1, source_target_pairs={{0,128},{128,0},{1,129},{129,1},{2,130},{130,2},{3,131},{131,3},{4... | collective-permute-start | bytes 2211848 | tf_op jit(solution)/shard_map/ppermute | solution.py:167
  121.9 1.4 collective-permute-done.9.refs_5_
  123.3 1.8 %assemble.1 = (bf16[2560,512]{1,0:T(8,128)(2,1)S(1)}, bf16[2560,512]{1,0:T(8,128)(2,1)S(1)}) custom-call(s32[3,8]{1,0:T(4,128)S(1)} %pad_add_fusion.place_ref, bf16[2,2,160,384]{3,2,1,0:T(8,128)(2,1)S(1)} %pad_maximum_fusion.2.home_ref, bf16[2,2,160,384]{3,2,1,0:T(8,128)(2,1)S(1)} %collective-permute-done.3.refs_0_, ...), custom_call_target="tpu_custom_call" | custom-call | tf_op jit(solution)/shard_map/assemble/pallas_call | solution.py:82
  125.1 1.2 fusion.11
  126.3 1.2 fusion.8
  127.5 3.9 %collective-permute-start.11 = (bf16[384,512]{1,0:T(8,128)(2,1)S(1)}, bf16[384,512]{1,0:T(8,128)(2,1)S(1)}, u32[]{:S(2)}, u32[]{:S(2)}) collective-permute-start(bf16[384,512]{1,0:T(8,128)(2,1)S(1)} %fusion.11), channel_id=1, source_target_pairs={{0,1},{1,0},{2,3},{3,2},{4,5},{5,4},{6,7},{7,6},{8,9},{9,8},{10,11... | collective-permute-start | bytes 1179656 | tf_op jit(solution)/shard_map/ppermute | solution.py:167
  131.4 1.2 fusion.2.own_ref
  132.6 0.0 copy-start.5
  132.6 0.0 copy-start.6
  132.7 0.0 copy-start.7
  132.7 3.2 %collective-permute-start.10 = (bf16[384,512]{1,0:T(8,128)(2,1)S(1)}, bf16[384,512]{1,0:T(8,128)(2,1)S(1)}, u32[]{:S(2)}, u32[]{:S(2)}) collective-permute-start(bf16[384,512]{1,0:T(8,128)(2,1)S(1)} %fusion.8), channel_id=1, source_target_pairs={{0,1},{1,0},{2,3},{3,2},{4,5},{5,4},{6,7},{7,6},{8,9},{9,8},{10,11... | collective-permute-start | bytes 1179656 | tf_op jit(solution)/shard_map/ppermute | solution.py:167
  135.9 1.2 fusion.6.own_ref
  137.1 4.2 %collective-permute-done.11.got_ref = bf16[384,512]{1,0:T(8,128)(2,1)S(1)} collective-permute-done((bf16[384,512]{1,0:T(8,128)(2,1)S(1)}, bf16[384,512]{1,0:T(8,128)(2,1)S(1)}, u32[]{:S(2)}, u32[]{:S(2)}) %collective-permute-start.11) | collective-permute-done | bytes 393248 | tf_op jit(solution)/shard_map/ppermute | solution.py:167
  141.3 2.2 %attend.2 = (bf16[384,256]{1,0:T(8,128)(2,1)S(1)}, bf16[384,128]{1,0:T(8,128)(2,1)S(1)}, bf16[384,128]{1,0:T(8,128)(2,1)S(1)}) custom-call(s32[1]{0:T(128)S(6)} %copy.29.limit_ref, f32[384,512]{1,0:T(8,128)S(1)} %fusion.2.own_ref, bf16[384,512]{1,0:T(8,128)(2,1)S(1)} %collective-permute-done.11.got_ref, f32[2,128]{1,0:T(2,128)S(1)} %copy-done.7, ...), custom_call_target="tpu_custom_call" | custom-call | tf_op jit(solution)/shard_map/attend/pallas_call | solution.py:163
  143.5 6.2 %collective-permute-done.10.got_ref = bf16[384,512]{1,0:T(8,128)(2,1)S(1)} collective-permute-done((bf16[384,512]{1,0:T(8,128)(2,1)S(1)}, bf16[384,512]{1,0:T(8,128)(2,1)S(1)}, u32[]{:S(2)}, u32[]{:S(2)}) %collective-permute-start.10) | collective-permute-done | bytes 393248 | tf_op jit(solution)/shard_map/ppermute | solution.py:167
  149.7 3.0 %attend.3 = (bf16[768,256]{1,0:T(8,128)(2,1)}, bf16[768,128]{1,0:T(8,128)(2,1)}, bf16[768,128]{1,0:T(8,128)(2,1)}) custom-call(s32[1]{0:T(128)S(6)} %copy.29.limit_ref, f32[384,512]{1,0:T(8,128)S(1)} %fusion.6.own_ref, bf16[384,512]{1,0:T(8,128)(2,1)S(1)} %collective-permute-done.10.got_ref, f32[2,128]{1,0:T(2,128)S(1)} %copy-done.7, ...), custom_call_target="tpu_custom_call" | custom-call | tf_op jit(solution)/shard_map/attend/pallas_call | solution.py:163
  (25 shorter events, 0.2 us)
Async XLA Ops:
  6.5 115.3 %copy-start = (f32[8,128]{1,0:T(8,128)S(1)}, f32[8,128]{1,0:T(8,128)}, u32[]{:S(2)}) copy-start(f32[8,128]{1,0:T(8,128)} %param.18) | copy-start | bytes 12292
  6.5 74.4 %all-gather.2.cloned.1.call-start = ((), (), s32[]{:S(2)}) async-start(), calls=%async_computation.1 | async-start | bytes 4423680 | tf_op jit(solution)/shard_map/all_gather | solution.py:203
  53.6 2.9 %collective-permute-start = (bf16[160,384]{1,0:T(8,128)(2,1)S(1)}, bf16[160,384]{1,0:T(8,128)(2,1)S(1)}, u32[]{:S(2)}, u32[]{:S(2)}) collective-permute-start(bf16[160,384]{1,0:T(8,128)(2,1)S(1)} %bitcast.28), channel_id=1, source_target_pairs={{0,0},{1,112},{16,16},{17,32},{32,17},{33,33},{48,65},{49,49},{64,... | collective-permute-start | bytes 368648 | tf_op jit(solution)/shard_map/ppermute | solution.py:186
  54.2 6.0 %collective-permute-start.1 = (bf16[160,384]{1,0:T(8,128)(2,1)S(1)}, bf16[160,384]{1,0:T(8,128)(2,1)S(1)}, u32[]{:S(2)}, u32[]{:S(2)}) collective-permute-start(bf16[160,384]{1,0:T(8,128)(2,1)S(1)} %bitcast.29), channel_id=1, source_target_pairs={{0,256},{1,368},{16,272},{17,288},{32,273},{33,289},{48,321},{49,3... | collective-permute-start | bytes 368648 | tf_op jit(solution)/shard_map/ppermute | solution.py:186
  60.3 38.4 %copy-start.8 = (f32[5120]{0:T(1024)S(1)}, f32[5120]{0:T(1024)}, u32[]{:S(2)}) copy-start(f32[5120]{0:T(1024)} %param.12) | copy-start | bytes 61444
  60.3 7.6 %collective-permute-start.2 = (bf16[2,160,384]{2,1,0:T(8,128)(2,1)S(1)}, bf16[2,160,384]{2,1,0:T(8,128)(2,1)S(1)}, u32[]{:S(2)}, u32[]{:S(2)}) collective-permute-start(bf16[2,160,384]{2,1,0:T(8,128)(2,1)S(1)} %get-tuple-element.32), channel_id=1, source_target_pairs={{0,128},{128,0},{1,129},{129,1},{2,130},{130,2},{3,131},{131,3},{4... | collective-permute-start | bytes 737288 | tf_op jit(solution)/shard_map/ppermute | solution.py:167
  68.0 13.0 %collective-permute-start.3 = (bf16[2,2,160,384]{3,2,1,0:T(8,128)(2,1)S(1)}, bf16[2,2,160,384]{3,2,1,0:T(8,128)(2,1)S(1)}, u32[]{:S(2)}, u32[]{:S(2)}) collective-permute-start(bf16[2,2,160,384]{3,2,1,0:T(8,128)(2,1)S(1)} %pad_maximum_fusion.2.home_ref), channel_id=1, source_target_pairs={{0,16},{16,32},{32,48},{48,64},{64,80},{80,96},{96,112},{112,0},{1... | collective-permute-start | bytes 1474568 | tf_op jit(solution)/shard_map/ppermute | solution.py:191
  80.9 10.8 %collective-permute-start.4 = (bf16[2,2,160,384]{3,2,1,0:T(8,128)(2,1)S(1)}, bf16[2,2,160,384]{3,2,1,0:T(8,128)(2,1)S(1)}, u32[]{:S(2)}, u32[]{:S(2)}) collective-permute-start(bf16[2,2,160,384]{3,2,1,0:T(8,128)(2,1)S(1)} %collective-permute-done.3.refs_0_), channel_id=1, source_target_pairs={{0,16},{16,32},{32,48},{48,64},{64,80},{80,96},{96,112},{112,0},{1... | collective-permute-start | bytes 1474568 | tf_op jit(solution)/shard_map/ppermute | solution.py:191
  85.9 2.1 %copy-start.1 = (bf16[2560,768]{1,0:T(8,128)(2,1)S(1)}, bf16[2560,768]{1,0:T(8,128)(2,1)}, u32[]{:S(2)}) copy-start(bf16[2560,768]{1,0:T(8,128)(2,1)} %all-gather.2.cloned.1.call-done.features_ref) | copy-start | bytes 11796484
  91.7 16.3 %collective-permute-start.5 = (bf16[2,2,160,384]{3,2,1,0:T(8,128)(2,1)S(1)}, bf16[2,2,160,384]{3,2,1,0:T(8,128)(2,1)S(1)}, u32[]{:S(2)}, u32[]{:S(2)}) collective-permute-start(bf16[2,2,160,384]{3,2,1,0:T(8,128)(2,1)S(1)} %collective-permute-done.4.refs_1_), channel_id=1, source_target_pairs={{0,16},{16,32},{32,48},{48,64},{64,80},{80,96},{96,112},{112,0},{1... | collective-permute-start | bytes 1474568 | tf_op jit(solution)/shard_map/ppermute | solution.py:191
  96.7 5.8 %collective-permute-start.6 = (f32[1,768]{1,0:T(1,128)S(1)}, f32[1,768]{1,0:T(1,128)S(1)}, u32[]{:S(2)}, u32[]{:S(2)}) collective-permute-start(f32[1,768]{1,0:T(1,128)S(1)} %squares.1.square_ref), channel_id=1, source_target_pairs={{0,1},{1,0},{2,3},{3,2},{4,5},{5,4},{6,7},{7,6},{8,9},{9,8},{10,11... | collective-permute-start | bytes 9224 | tf_op jit(solution)/shard_map/ppermute | solution.py:167
  102.6 2.1 %copy-start.2 = (bf16[2560,768]{1,0:T(8,128)(2,1)S(1)}, bf16[2560,768]{1,0:T(8,128)(2,1)}, u32[]{:S(2)}) copy-start(bf16[2560,768]{1,0:T(8,128)(2,1)} %all-gather.2.cloned.1.call-done.features_ref) | copy-start | bytes 11796484
  106.2 1.9 %copy-start.3 = (bf16[2560,768]{1,0:T(8,128)(2,1)}, bf16[2560,768]{1,0:T(8,128)(2,1)S(1)}, u32[]{:S(2)}) copy-start(bf16[2560,768]{1,0:T(8,128)(2,1)S(1)} %normalise.1) | copy-start | bytes 11796484
  108.0 7.2 %collective-permute-start.7 = (bf16[2,160,384]{2,1,0:T(8,128)(2,1)S(1)}, bf16[2,160,384]{2,1,0:T(8,128)(2,1)S(1)}, u32[]{:S(2)}, u32[]{:S(2)}) collective-permute-start(bf16[2,160,384]{2,1,0:T(8,128)(2,1)S(1)} %slice_bitcast_fusion), channel_id=1, source_target_pairs={{0,16},{16,32},{32,48},{48,64},{64,80},{80,96},{96,112},{112,0},{1... | collective-permute-start | bytes 737288 | tf_op jit(solution)/shard_map/ppermute | solution.py:191
  111.0 10.8 %collective-permute-start.8 = (bf16[2,2,2,160,384]{4,3,2,1,0:T(8,128)(2,1)}, bf16[2,2,2,160,384]{4,3,2,1,0:T(8,128)(2,1)S(1)}, u32[]{:S(2)}, u32[]{:S(2)}) collective-permute-start(bf16[2,2,2,160,384]{4,3,2,1,0:T(8,128)(2,1)} %pad_maximum_fusion), channel_id=1, source_target_pairs={{0,128},{128,0},{1,129},{129,1},{2,130},{130,2},{3,131},{131,3},{4... | collective-permute-start | bytes 2949128 | tf_op jit(solution)/shard_map/ppermute | solution.py:167
  116.3 7.0 %collective-permute-start.9 = (bf16[3,2,160,384]{3,2,1,0:T(8,128)(2,1)}, bf16[3,2,160,384]{3,2,1,0:T(8,128)(2,1)}, u32[]{:S(2)}, u32[]{:S(2)}) collective-permute-start(bf16[3,2,160,384]{3,2,1,0:T(8,128)(2,1)} %pad_maximum_fusion.1), channel_id=1, source_target_pairs={{0,128},{128,0},{1,129},{129,1},{2,130},{130,2},{3,131},{131,3},{4... | collective-permute-start | bytes 2211848 | tf_op jit(solution)/shard_map/ppermute | solution.py:167
  121.8 3.3 %copy-start.4 = (bf16[2560,768]{1,0:T(8,128)(2,1)S(1)}, bf16[2560,768]{1,0:T(8,128)(2,1)}, u32[]{:S(2)}) copy-start(bf16[2560,768]{1,0:T(8,128)(2,1)} %copy-done.3) | copy-start | bytes 11796484
  127.5 13.7 %collective-permute-start.11 = (bf16[384,512]{1,0:T(8,128)(2,1)S(1)}, bf16[384,512]{1,0:T(8,128)(2,1)S(1)}, u32[]{:S(2)}, u32[]{:S(2)}) collective-permute-start(bf16[384,512]{1,0:T(8,128)(2,1)S(1)} %fusion.11), channel_id=1, source_target_pairs={{0,1},{1,0},{2,3},{3,2},{4,5},{5,4},{6,7},{7,6},{8,9},{9,8},{10,11... | collective-permute-start | bytes 1179656 | tf_op jit(solution)/shard_map/ppermute | solution.py:167
  132.6 8.6 %copy-start.5 = (f32[768,128]{1,0:T(8,128)S(1)}, f32[768,128]{1,0:T(8,128)}, u32[]{:S(2)}) copy-start(f32[768,128]{1,0:T(8,128)} %constant.62.clone.cos_ref) | copy-start | bytes 1179652
  132.6 8.6 %copy-start.6 = (f32[768,128]{1,0:T(8,128)S(1)}, f32[768,128]{1,0:T(8,128)}, u32[]{:S(2)}) copy-start(f32[768,128]{1,0:T(8,128)} %constant.63.clone.sin_ref) | copy-start | bytes 1179652
  132.7 8.6 %copy-start.7 = (f32[2,128]{1,0:T(2,128)S(1)}, f32[2,128]{1,0:T(2,128)}, u32[]{:S(2)}) copy-start(f32[2,128]{1,0:T(2,128)} %query_gain_ref.3) | copy-start | bytes 3076
  132.7 17.0 %collective-permute-start.10 = (bf16[384,512]{1,0:T(8,128)(2,1)S(1)}, bf16[384,512]{1,0:T(8,128)(2,1)S(1)}, u32[]{:S(2)}, u32[]{:S(2)}) collective-permute-start(bf16[384,512]{1,0:T(8,128)(2,1)S(1)} %fusion.8), channel_id=1, source_target_pairs={{0,1},{1,0},{2,3},{3,2},{4,5},{5,4},{6,7},{7,6},{8,9},{9,8},{10,11... | collective-permute-start | bytes 1179656 | tf_op jit(solution)/shard_map/ppermute | solution.py:167
Sparse Core Ops, SparseCore 0:
  9.4 66.8 all-gather.1

commit v6 on v5

--- a/solution.py
+++ b/solution.py
@@ -42,44 +42,45 @@
     )
 
 
-def assemble_kernel(place_ref, home_ref, *refs):
+def assemble_kernel(place_ref, ring_place_ref, gathered_ref, swapped_ref, home_ref, *refs):
     *step_refs, last_ref, early_ref, late_ref, own_ref, sent_ref = refs
-    _, _, rows, cols = home_ref.shape
+    parts, rows, cols = gathered_ref.shape
     head = own_ref.shape[1] // 4
     wide = cols - head
 
-    def put(step, lane, block_ref, *index):
-        row = pl.multiple_of(place_ref[0, step] * rows, 32)
-        pair_col = pl.multiple_of(wide + place_ref[2, step] * head, 128)
-        spans = [pl.ds((lane * 2 + near) * 4 * rows + row, rows) for near in range(2)]
+    def put(table_ref, step, lane, near, block_ref, *index):
+        row = pl.multiple_of(table_ref[0, step] * rows, 32)
+        pair_col = pl.multiple_of(wide + table_ref[2, step] * head, 128)
+        span = pl.ds((lane * 2 + near) * 4 * rows + row, rows)
 
         def put_queries(out_ref):
-            for near, span in enumerate(spans):
-                out_ref[span, :wide] = block_ref[*index, near, :, :wide]
-
-        pl.when(place_ref[1, step] == 0)(lambda: put_queries(own_ref))
-        pl.when(place_ref[1, step] == 1)(lambda: put_queries(sent_ref))
-        for near, span in enumerate(spans):
-            pair = block_ref[*index, near, :, wide:]
-            own_ref[span, pl.ds(pair_col, head)] = pair
-            sent_ref[span, pl.ds(pair_col, head)] = pair
-
+            out_ref[span, :wide] = block_ref[*index, :, :wide]
+
+        pl.when(table_ref[1, step] == 0)(lambda: put_queries(own_ref))
+        pl.when(table_ref[1, step] == 1)(lambda: put_queries(sent_ref))
+        pair = block_ref[*index, :, wide:]
+        own_ref[span, pl.ds(pair_col, head)] = pair
+        sent_ref[span, pl.ds(pair_col, head)] = pair
+
+    for step in range(parts):
+        put(place_ref, step, 0, 0, gathered_ref, step)
+        put(place_ref, step, 1, 0, swapped_ref, step)
     for lane in range(2):
-        put(0, lane, home_ref, lane)
+        put(ring_place_ref, 0, lane, 1, home_ref, lane)
         for step in range(3):
-            put(1 + step, lane, step_refs[step], lane)
+            put(ring_place_ref, 1 + step, lane, 1, step_refs[step], lane)
         for step in range(2):
-            put(5 + step, 1 - lane, early_ref, step, lane)
-        put(7, 1 - lane, late_ref, lane)
-    put(4, 0, last_ref)
-    put(4, 1, late_ref, 2)
-
-
-def assemble(place, home, *rest):
-    _, _, rows, cols = home.shape
-    shape = [jax.ShapeDtypeStruct((16 * rows, 4 * cols // 3), home.dtype)] * 2
-    call = local_call(assemble_kernel, "assemble", shape, [SMEM] + [VMEM] * (1 + len(rest)), [VMEM] * 2)
-    return call(place, home, *rest)
+            put(ring_place_ref, 5 + step, 1 - lane, 1, early_ref, step, lane)
+        put(ring_place_ref, 7, 1 - lane, 1, late_ref, lane)
+    put(ring_place_ref, 4, 0, 1, last_ref)
+    put(ring_place_ref, 4, 1, 1, late_ref, 2)
+
+
+def assemble(place, ring_place, gathered, *rest):
+    parts, rows, cols = gathered.shape
+    shape = [jax.ShapeDtypeStruct((4 * parts // 2 * rows, 4 * cols // 3), gathered.dtype)] * 2
+    call = local_call(assemble_kernel, "assemble", shape, [SMEM] * 2 + [VMEM] * (1 + len(rest)), [VMEM] * 2)
+    return call(place, ring_place, gathered, *rest)
 
 
 def squares_kernel(parts, features_ref, out_ref):
@@ -213,7 +214,8 @@
         jnp.bfloat16
     )
     updated = updated.reshape(slab_rows, slab_heads * head_size)
-    home = jnp.stack([to_column(updated, 0), to_column(updated, 1)])
+    arrived = lax.all_gather(to_column(updated, 0), "y", axis=0)
+    home = to_column(updated, 1)
     home = jnp.stack([home, swap(home, "core")])
     first = onward(home)
     first, gathered = lax.optimization_barrier((first, gathered))
@@ -230,15 +232,19 @@
     third, normed = lax.optimization_barrier((third, normed))
     early = swap(jnp.stack([first, second]), "core")
     last = onward(third[0])
+    last, arrived = lax.optimization_barrier((last, arrived))
     late = swap(jnp.concatenate([third, last[None]]), "core")
 
-    up = 1 - 2 * core
-    source = (y - up * jnp.where(steps < 5, steps, 4 - steps)) & 7
-    native = ((source >> 1) & 1) == xh
-    origin = jnp.where(native, source, (source + 2 * (source & 1) - 1) & 7)
-    slab = jnp.where(native, xh, 1 - xh)
-    place = jnp.stack([(origin >> 2) * 2 + (origin & 1), slab ^ xh, slab]).astype(jnp.int32)
-    own_weight, sent_weight = assemble(place, home, first, second, third, last, early, late)
+    def place_of(source):
+        native = ((source >> 1) & 1) == xh
+        origin = jnp.where(native, source, (source + 2 * (source & 1) - 1) & 7)
+        slab = jnp.where(native, xh, 1 - xh)
+        return jnp.stack([(origin >> 2) * 2 + (origin & 1), slab ^ xh, slab]).astype(jnp.int32)
+
+    ring_source = (y - (1 - 2 * core) * jnp.where(steps < 5, steps, 4 - steps)) & 7
+    own_weight, sent_weight = assemble(
+        place_of(steps), place_of(ring_source), arrived, swap(arrived, "core"), home, first, second, third, last, early, late
+    )
 
     tables = rope_tables(seq_rows, head_size)
     gain_row = lax.dynamic_slice_in_dim(key_gain, z, 1, 0)

time: 160 us -> 180 us (1.12)
  blocking collectives: 38.9 us -> 60.3 us
  starting transfers between devices: 45.1 us -> 53.3 us
  waiting for transfers between devices: 30.6 us -> 23.5 us
  other arithmetic: 8.11 us -> 6.12 us
    all_gather x0 -> x1, blocking collectives: none -> 21.4 us  [shards(): arrived = lax.all_gather(to_column(updated, 0), 'y', axis=0)]
    ppermute x4, waiting for transfers between devices: 10.6 us -> 3.92 us  [onward(): return lax.ppermute(block, ('core', 'y'), pairs)]
    ppermute x6 -> x7, starting transfers between devices: 23.1 us -> 29.2 us  [swap(): return lax.ppermute(array, axis, [(0, 1), (1, 0)])]
    ppermute x6 -> x7, waiting for transfers between devices: 15.5 us -> 12.2 us  [swap(): return lax.ppermute(array, axis, [(0, 1), (1, 0)])]
    all_gather x1, waiting for transfers between devices: 0.01 us -> 2.88 us  [shards(): gathered = lax.all_gather(activations.T, 'z', axis=0, tiled=True)]
    ppermute x4, starting transfers between devices: 19.2 us -> 21.2 us  [onward(): return lax.ppermute(block, ('core', 'y'), pairs)]
  transfers between devices with their start and end apart: 13 -> 14, of which waited for: 9 -> 8; matrix products, arithmetic and copies ran while one was open for 8% -> 6% of each run, Pallas kernels for 2% -> 2%
where the time goes in v6:
time: 180 us
  blocking collectives  60.3 us (34%)
  starting transfers between devices  53.3 us (30%)
  waiting for transfers between devices  23.5 us (13%)
  between operations  15.1 us (8%)
  Pallas kernels  8.29 us (5%)
  local copies, waits for them, and re-layouts  8.2 us (5%)
  other arithmetic  6.12 us (3%)
  matrix products  4.8 us (3%)
    all_to_all x1, blocking collectives, global_sum(): return jnp.sum(lax.all_to_all(spread, AXES, 0, 0, tiled=True)[:, 0])  38.9 us
    ppermute x7, starting transfers between devices, swap(): return lax.ppermute(array, axis, [(0, 1), (1, 0)])  29.2 us
    all_gather x1, blocking collectives, shards(): arrived = lax.all_gather(to_column(updated, 0), 'y', axis=0)  21.4 us
    ppermute x4, starting transfers between devices, onward(): return lax.ppermute(block, ('core', 'y'), pairs)  21.2 us
    ppermute x7, waiting for transfers between devices, swap(): return lax.ppermute(array, axis, [(0, 1), (1, 0)])  12.2 us
    unnamed x19, local copies, waits for them, and re-layouts  6.12 us
    pallas_call x2, Pallas kernels, attend(): return call(limit, own, got, query_gain, key_gain, *tables, *before)  5.19 us
    dot_general x4, matrix products, product(): lax.dot_general(rows, weight, (((0,), (0,)), ((), ())), preferred_element...  4.8 us
  transfers between devices with their start and end apart: 14, of which 8 were waited for; matrix products, arithmetic and copies ran while one was open for 6% of the time, Pallas kernels for 2%

profile of v6, /device:TPU:1, one launch (start us, length us, event | category | flops | bytes accessed | tf_op | source)
XLA Modules:
  0.0 179.6 jit_solution(16370723360184854572)
XLA Ops:
  6.5 0.7 all-gather.3.cloned.1.call-update
  7.3 2.0 %multiply_reduce_fusion = f32[]{:T(128)} fusion(bf16[160,1,3,128]{3,0,2,1:T(8,128)(2,1)} %param.14), kind=kLoop, calls=%fused_computation.18 | loop fusion | flops 184319 | bytes 122884 | tf_op jit(solution)/shard_map/reduce_sum | solution.py:207
  9.3 0.8 broadcast_in_dim.14
  10.1 38.9 %all_to_all.9 = f32[512,1,128]{2,1,0:T(1,128)S(1)} all-to-all(f32[512,1,128]{2,1,0:T(1,128)S(1)} %broadcast_in_dim.14), channel_id=1, replica_groups=mesh['xl'=2,'core'=2,'y'=8,'z'=8,'xh'=2] {'xl','core','y','z','xh'}, dimensions={0} | all-to-all | bytes 524288 | tf_op jit(solution)/shard_map/all_to_all | solution.py:176
  48.9 0.7 slice_reduce_fusion
  50.3 3.2 %convert_reduce_fusion = bf16[160,3,128]{2,1,0:T(4,128)(2,1)S(1)} fusion(f32[160,1,3,128]{3,1,2,0:T(1,128)} %param.13, f32[160,1,3,128]{3,1,2,0:T(1,128)} %param.16, f32[160,1,3,128]{3,1,2,0:T(1,128)} %param.15, bf16[160,1,3,128]{3,0,2,1:T(8,128)(2,1)} %param.14, f32[]{:T(128)S(6)} %sqrt.6), kind=kLoop, calls=%fused_computation.17 | loop fusion | flops 860160 | bytes 983044 | tf_op jit(solution)/shard_map/convert_element_type | solution.py:213
  53.5 0.0 copy-start.8
  53.6 2.2 %collective-permute-start = (bf16[160,384]{1,0:T(8,128)(2,1)S(1)}, bf16[160,384]{1,0:T(8,128)(2,1)S(1)}, u32[]{:S(2)}, u32[]{:S(2)}) collective-permute-start(bf16[160,384]{1,0:T(8,128)(2,1)S(1)} %bitcast.26), channel_id=1, source_target_pairs={{0,256},{1,368},{16,272},{17,288},{32,273},{33,289},{48,321},{49,3... | collective-permute-start | bytes 368648 | tf_op jit(solution)/shard_map/ppermute | solution.py:187
  55.8 3.8 %collective-permute-done = bf16[160,384]{1,0:T(8,128)(2,1)S(1)} collective-permute-done((bf16[160,384]{1,0:T(8,128)(2,1)S(1)}, bf16[160,384]{1,0:T(8,128)(2,1)S(1)}, u32[]{:S(2)}, u32[]{:S(2)}) %collective-permute-start) | collective-permute-done | bytes 122912 | tf_op jit(solution)/shard_map/ppermute | solution.py:187
  59.6 3.8 %collective-permute-start.1 = (bf16[160,384]{1,0:T(8,128)(2,1)S(1)}, bf16[160,384]{1,0:T(8,128)(2,1)S(1)}, u32[]{:S(2)}, u32[]{:S(2)}) collective-permute-start(bf16[160,384]{1,0:T(8,128)(2,1)S(1)} %collective-permute-done), channel_id=1, source_target_pairs={{0,128},{128,0},{1,129},{129,1},{2,130},{130,2},{3,131},{131,3},{4... | collective-permute-start | bytes 368648 | tf_op jit(solution)/shard_map/ppermute | solution.py:168
  63.4 1.0 collective-permute-done.1
  64.4 5.9 %collective-permute-start.2 = (bf16[2,160,384]{2,1,0:T(8,128)(2,1)S(1)}, bf16[2,160,384]{2,1,0:T(8,128)(2,1)S(1)}, u32[]{:S(2)}, u32[]{:S(2)}) collective-permute-start(bf16[2,160,384]{2,1,0:T(8,128)(2,1)S(1)} %pad_maximum_fusion.2.home_ref), channel_id=1, source_target_pairs={{0,16},{16,32},{32,48},{48,64},{64,80},{80,96},{96,112},{112,0},{1... | collective-permute-start | bytes 737288 | tf_op jit(solution)/shard_map/ppermute | solution.py:192
  70.4 3.1 %collective-permute-done.2.refs_0_ = bf16[2,160,384]{2,1,0:T(8,128)(2,1)S(1)} collective-permute-done((bf16[2,160,384]{2,1,0:T(8,128)(2,1)S(1)}, bf16[2,160,384]{2,1,0:T(8,128)(2,1)S(1)}, u32[]{:S(2)}, u32[]{:S(2)}) %collective-permute-start.2) | collective-permute-done | bytes 245792 | tf_op jit(solution)/shard_map/ppermute | solution.py:192
  73.5 2.9 %all-gather.3.cloned.1.call-done.features_ref = bf16[2560,768]{1,0:T(8,128)(2,1)} async-done(((bf16[320,768]{1,0:T(8,128)(2,1)}), bf16[2560,768]{1,0:T(8,128)(2,1)}) %all-gather.3.cloned.1.call-update) | async-done | bytes 3932176 | tf_op jit(solution)/shard_map/all_gather | solution.py:204
  76.4 4.4 %collective-permute-start.3 = (bf16[2,160,384]{2,1,0:T(8,128)(2,1)S(1)}, bf16[2,160,384]{2,1,0:T(8,128)(2,1)S(1)}, u32[]{:S(2)}, u32[]{:S(2)}) collective-permute-start(bf16[2,160,384]{2,1,0:T(8,128)(2,1)S(1)} %collective-permute-done.2.refs_0_), channel_id=1, source_target_pairs={{0,16},{16,32},{32,48},{48,64},{64,80},{80,96},{96,112},{112,0},{1... | collective-permute-start | bytes 737288 | tf_op jit(solution)/shard_map/ppermute | solution.py:192
  80.8 2.1 %copy-done.1 = bf16[2560,768]{1,0:T(8,128)(2,1)S(1)} copy-done((bf16[2560,768]{1,0:T(8,128)(2,1)S(1)}, bf16[2560,768]{1,0:T(8,128)(2,1)}, u32[]{:S(2)}) %copy-start.1) | copy-done | bytes 3932184
  82.9 0.2 squares.1.square_ref
  83.2 0.8 collective-permute-done.3.refs_1_
  84.0 5.0 %collective-permute-start.4 = (bf16[2,160,384]{2,1,0:T(8,128)(2,1)S(1)}, bf16[2,160,384]{2,1,0:T(8,128)(2,1)S(1)}, u32[]{:S(2)}, u32[]{:S(2)}) collective-permute-start(bf16[2,160,384]{2,1,0:T(8,128)(2,1)S(1)} %collective-permute-done.3.refs_1_), channel_id=1, source_target_pairs={{0,16},{16,32},{32,48},{48,64},{64,80},{80,96},{96,112},{112,0},{1... | collective-permute-start | bytes 737288 | tf_op jit(solution)/shard_map/ppermute | solution.py:192
  89.0 4.6 %collective-permute-start.5 = (f32[1,768]{1,0:T(1,128)S(1)}, f32[1,768]{1,0:T(1,128)S(1)}, u32[]{:S(2)}, u32[]{:S(2)}) collective-permute-start(f32[1,768]{1,0:T(1,128)S(1)} %squares.1.square_ref), channel_id=1, source_target_pairs={{0,1},{1,0},{2,3},{3,2},{4,5},{5,4},{6,7},{7,6},{8,9},{9,8},{10,11... | collective-permute-start | bytes 9224 | tf_op jit(solution)/shard_map/ppermute | solution.py:168
  93.6 0.1 reshape.148
  93.8 1.1 reshape.151.gain_ref
  94.9 0.7 collective-permute-start.7
  95.6 2.1 %copy-done.2 = bf16[2560,768]{1,0:T(8,128)(2,1)S(1)} copy-done((bf16[2560,768]{1,0:T(8,128)(2,1)S(1)}, bf16[2560,768]{1,0:T(8,128)(2,1)}, u32[]{:S(2)}) %copy-start.2) | copy-done | bytes 3932184
  97.7 1.5 normalise.1
  99.2 1.9 %copy-done.3 = bf16[2560,768]{1,0:T(8,128)(2,1)} copy-done((bf16[2560,768]{1,0:T(8,128)(2,1)}, bf16[2560,768]{1,0:T(8,128)(2,1)S(1)}, u32[]{:S(2)}) %copy-start.3) | copy-done | bytes 3932184
  101.1 5.8 %collective-permute-start.6 = (bf16[160,384]{1,0:T(8,128)(2,1)S(1)}, bf16[160,384]{1,0:T(8,128)(2,1)S(1)}, u32[]{:S(2)}, u32[]{:S(2)}) collective-permute-start(bf16[160,384]{1,0:T(8,128)(2,1)S(1)} %slice_bitcast_fusion), channel_id=1, source_target_pairs={{0,16},{16,32},{32,48},{48,64},{64,80},{80,96},{96,112},{112,0},{1... | collective-permute-start | bytes 368648 | tf_op jit(solution)/shard_map/ppermute | solution.py:192
  106.9 0.0 collective-permute-done.7
  106.9 21.4 %all-gather = bf16[1280,384]{1,0:T(8,128)(2,1)S(1)} all-gather(bf16[160,384]{1,0:T(8,128)(2,1)S(1)} %collective-permute-done.7), channel_id=2, replica_groups=mesh['xl'=2,'core'=2,'y'=8,'z'=8,'xh'=2] {'y'}, dimensions={0}, use_global_device_ids=true | all-gather | bytes 1105920 | tf_op jit(solution)/shard_map/all_gather | solution.py:217
  128.3 7.7 %collective-permute-start.8 = (bf16[8,160,384]{2,1,0:T(8,128)(2,1)S(1)}, bf16[8,160,384]{2,1,0:T(8,128)(2,1)S(1)}, u32[]{:S(2)}, u32[]{:S(2)}) collective-permute-start(bf16[8,160,384]{2,1,0:T(8,128)(2,1)S(1)} %bitcast.18), channel_id=1, source_target_pairs={{0,128},{128,0},{1,129},{129,1},{2,130},{130,2},{3,131},{131,3},{4... | collective-permute-start | bytes 2949128 | tf_op jit(solution)/shard_map/ppermute | solution.py:168
  136.0 0.1 pad_maximum_fusion
  136.1 2.2 %collective-permute-start.9 = (bf16[2,2,160,384]{3,2,1,0:T(8,128)(2,1)S(1)}, bf16[2,2,160,384]{3,2,1,0:T(8,128)(2,1)S(1)}, u32[]{:S(2)}, u32[]{:S(2)}) collective-permute-start(bf16[2,2,160,384]{3,2,1,0:T(8,128)(2,1)S(1)} %pad_maximum_fusion), channel_id=1, source_target_pairs={{0,128},{128,0},{1,129},{129,1},{2,130},{130,2},{3,131},{131,3},{4... | collective-permute-start | bytes 1474568 | tf_op jit(solution)/shard_map/ppermute | solution.py:168
  138.3 2.4 %collective-permute-start.10 = (bf16[3,160,384]{2,1,0:T(8,128)(2,1)S(1)}, bf16[3,160,384]{2,1,0:T(8,128)(2,1)S(1)}, u32[]{:S(2)}, u32[]{:S(2)}) collective-permute-start(bf16[3,160,384]{2,1,0:T(8,128)(2,1)S(1)} %pad_maximum_fusion.1), channel_id=1, source_target_pairs={{0,128},{128,0},{1,129},{129,1},{2,130},{130,2},{3,131},{131,3},{4... | collective-permute-start | bytes 1105928 | tf_op jit(solution)/shard_map/ppermute | solution.py:168
  141.5 0.6 collective-permute-done.10.refs_5_
  142.0 1.4 assemble.1
  143.5 1.2 fusion.11
  144.7 1.2 fusion.8
  145.9 6.4 %collective-permute-start.12 = (bf16[384,512]{1,0:T(8,128)(2,1)S(1)}, bf16[384,512]{1,0:T(8,128)(2,1)S(1)}, u32[]{:S(2)}, u32[]{:S(2)}) collective-permute-start(bf16[384,512]{1,0:T(8,128)(2,1)S(1)} %fusion.11), channel_id=1, source_target_pairs={{0,1},{1,0},{2,3},{3,2},{4,5},{5,4},{6,7},{7,6},{8,9},{9,8},{10,11... | collective-permute-start | bytes 1179656 | tf_op jit(solution)/shard_map/ppermute | solution.py:168
  152.4 1.2 fusion.2.own_ref
  153.6 0.0 copy-start.5
  153.6 0.0 copy-start.6
  153.6 0.0 copy-start.7
  153.6 2.1 %collective-permute-start.11 = (bf16[384,512]{1,0:T(8,128)(2,1)S(1)}, bf16[384,512]{1,0:T(8,128)(2,1)S(1)}, u32[]{:S(2)}, u32[]{:S(2)}) collective-permute-start(bf16[384,512]{1,0:T(8,128)(2,1)S(1)} %fusion.8), channel_id=1, source_target_pairs={{0,1},{1,0},{2,3},{3,2},{4,5},{5,4},{6,7},{7,6},{8,9},{9,8},{10,11... | collective-permute-start | bytes 1179656 | tf_op jit(solution)/shard_map/ppermute | solution.py:168
  155.7 1.2 fusion.6.own_ref
  156.9 4.5 %collective-permute-done.12.got_ref = bf16[384,512]{1,0:T(8,128)(2,1)S(1)} collective-permute-done((bf16[384,512]{1,0:T(8,128)(2,1)S(1)}, bf16[384,512]{1,0:T(8,128)(2,1)S(1)}, u32[]{:S(2)}, u32[]{:S(2)}) %collective-permute-start.12) | collective-permute-done | bytes 393248 | tf_op jit(solution)/shard_map/ppermute | solution.py:168
  161.3 2.2 %attend.2 = (bf16[384,256]{1,0:T(8,128)(2,1)S(1)}, bf16[384,128]{1,0:T(8,128)(2,1)S(1)}, bf16[384,128]{1,0:T(8,128)(2,1)S(1)}) custom-call(s32[1]{0:T(128)S(6)} %copy.29.limit_ref, f32[384,512]{1,0:T(8,128)S(1)} %fusion.2.own_ref, bf16[384,512]{1,0:T(8,128)(2,1)S(1)} %collective-permute-done.12.got_ref, f32[2,128]{1,0:T(2,128)S(1)} %copy-done.7, ...), custom_call_target="tpu_custom_call" | custom-call | tf_op jit(solution)/shard_map/attend/pallas_call | solution.py:164
  163.6 6.2 %collective-permute-done.11.got_ref = bf16[384,512]{1,0:T(8,128)(2,1)S(1)} collective-permute-done((bf16[384,512]{1,0:T(8,128)(2,1)S(1)}, bf16[384,512]{1,0:T(8,128)(2,1)S(1)}, u32[]{:S(2)}, u32[]{:S(2)}) %collective-permute-start.11) | collective-permute-done | bytes 393248 | tf_op jit(solution)/shard_map/ppermute | solution.py:168
  169.8 3.0 %attend.3 = (bf16[768,256]{1,0:T(8,128)(2,1)}, bf16[768,128]{1,0:T(8,128)(2,1)}, bf16[768,128]{1,0:T(8,128)(2,1)}) custom-call(s32[1]{0:T(128)S(6)} %copy.29.limit_ref, f32[384,512]{1,0:T(8,128)S(1)} %fusion.6.own_ref, bf16[384,512]{1,0:T(8,128)(2,1)S(1)} %collective-permute-done.11.got_ref, f32[2,128]{1,0:T(2,128)S(1)} %copy-done.7, ...), custom_call_target="tpu_custom_call" | custom-call | tf_op jit(solution)/shard_map/attend/pallas_call | solution.py:164
  (29 shorter events, 0.3 us)
Async XLA Ops:
  6.5 134.2 %copy-start = (f32[8,128]{1,0:T(8,128)S(1)}, f32[8,128]{1,0:T(8,128)}, u32[]{:S(2)}) copy-start(f32[8,128]{1,0:T(8,128)} %param.18) | copy-start | bytes 12292
  6.5 69.8 %all-gather.3.cloned.1.call-start = ((), (), s32[]{:S(2)}) async-start(), calls=%async_computation.1 | async-start | bytes 4423680 | tf_op jit(solution)/shard_map/all_gather | solution.py:204
  53.5 40.1 %copy-start.8 = (f32[5120]{0:T(1024)S(1)}, f32[5120]{0:T(1024)}, u32[]{:S(2)}) copy-start(f32[5120]{0:T(1024)} %param.12) | copy-start | bytes 61444
  53.6 6.0 %collective-permute-start = (bf16[160,384]{1,0:T(8,128)(2,1)S(1)}, bf16[160,384]{1,0:T(8,128)(2,1)S(1)}, u32[]{:S(2)}, u32[]{:S(2)}) collective-permute-start(bf16[160,384]{1,0:T(8,128)(2,1)S(1)} %bitcast.26), channel_id=1, source_target_pairs={{0,256},{1,368},{16,272},{17,288},{32,273},{33,289},{48,321},{49,3... | collective-permute-start | bytes 368648 | tf_op jit(solution)/shard_map/ppermute | solution.py:187
  59.6 4.8 %collective-permute-start.1 = (bf16[160,384]{1,0:T(8,128)(2,1)S(1)}, bf16[160,384]{1,0:T(8,128)(2,1)S(1)}, u32[]{:S(2)}, u32[]{:S(2)}) collective-permute-start(bf16[160,384]{1,0:T(8,128)(2,1)S(1)} %collective-permute-done), channel_id=1, source_target_pairs={{0,128},{128,0},{1,129},{129,1},{2,130},{130,2},{3,131},{131,3},{4... | collective-permute-start | bytes 368648 | tf_op jit(solution)/shard_map/ppermute | solution.py:168
  64.4 9.1 %collective-permute-start.2 = (bf16[2,160,384]{2,1,0:T(8,128)(2,1)S(1)}, bf16[2,160,384]{2,1,0:T(8,128)(2,1)S(1)}, u32[]{:S(2)}, u32[]{:S(2)}) collective-permute-start(bf16[2,160,384]{2,1,0:T(8,128)(2,1)S(1)} %pad_maximum_fusion.2.home_ref), channel_id=1, source_target_pairs={{0,16},{16,32},{32,48},{48,64},{64,80},{80,96},{96,112},{112,0},{1... | collective-permute-start | bytes 737288 | tf_op jit(solution)/shard_map/ppermute | solution.py:192
  76.4 7.6 %collective-permute-start.3 = (bf16[2,160,384]{2,1,0:T(8,128)(2,1)S(1)}, bf16[2,160,384]{2,1,0:T(8,128)(2,1)S(1)}, u32[]{:S(2)}, u32[]{:S(2)}) collective-permute-start(bf16[2,160,384]{2,1,0:T(8,128)(2,1)S(1)} %collective-permute-done.2.refs_0_), channel_id=1, source_target_pairs={{0,16},{16,32},{32,48},{48,64},{64,80},{80,96},{96,112},{112,0},{1... | collective-permute-start | bytes 737288 | tf_op jit(solution)/shard_map/ppermute | solution.py:192
  80.8 2.1 %copy-start.1 = (bf16[2560,768]{1,0:T(8,128)(2,1)S(1)}, bf16[2560,768]{1,0:T(8,128)(2,1)}, u32[]{:S(2)}) copy-start(bf16[2560,768]{1,0:T(8,128)(2,1)} %all-gather.3.cloned.1.call-done.features_ref) | copy-start | bytes 11796484
  84.0 17.1 %collective-permute-start.4 = (bf16[2,160,384]{2,1,0:T(8,128)(2,1)S(1)}, bf16[2,160,384]{2,1,0:T(8,128)(2,1)S(1)}, u32[]{:S(2)}, u32[]{:S(2)}) collective-permute-start(bf16[2,160,384]{2,1,0:T(8,128)(2,1)S(1)} %collective-permute-done.3.refs_1_), channel_id=1, source_target_pairs={{0,16},{16,32},{32,48},{48,64},{64,80},{80,96},{96,112},{112,0},{1... | collective-permute-start | bytes 737288 | tf_op jit(solution)/shard_map/ppermute | solution.py:192
  89.0 6.6 %collective-permute-start.5 = (f32[1,768]{1,0:T(1,128)S(1)}, f32[1,768]{1,0:T(1,128)S(1)}, u32[]{:S(2)}, u32[]{:S(2)}) collective-permute-start(f32[1,768]{1,0:T(1,128)S(1)} %squares.1.square_ref), channel_id=1, source_target_pairs={{0,1},{1,0},{2,3},{3,2},{4,5},{5,4},{6,7},{7,6},{8,9},{9,8},{10,11... | collective-permute-start | bytes 9224 | tf_op jit(solution)/shard_map/ppermute | solution.py:168
  94.9 12.0 %collective-permute-start.7 = (bf16[160,384]{1,0:T(8,128)(2,1)S(1)}, bf16[160,384]{1,0:T(8,128)(2,1)S(1)}, u32[]{:S(2)}, u32[]{:S(2)}) collective-permute-start(bf16[160,384]{1,0:T(8,128)(2,1)S(1)} %bitcast.27), channel_id=1, source_target_pairs={{0,0},{1,112},{16,16},{17,32},{32,17},{33,33},{48,65},{49,49},{64,... | collective-permute-start | bytes 368648 | tf_op jit(solution)/shard_map/ppermute | solution.py:187
  95.6 2.1 %copy-start.2 = (bf16[2560,768]{1,0:T(8,128)(2,1)S(1)}, bf16[2560,768]{1,0:T(8,128)(2,1)}, u32[]{:S(2)}) copy-start(bf16[2560,768]{1,0:T(8,128)(2,1)} %all-gather.3.cloned.1.call-done.features_ref) | copy-start | bytes 11796484
  99.2 1.9 %copy-start.3 = (bf16[2560,768]{1,0:T(8,128)(2,1)}, bf16[2560,768]{1,0:T(8,128)(2,1)S(1)}, u32[]{:S(2)}) copy-start(bf16[2560,768]{1,0:T(8,128)(2,1)S(1)} %normalise.1) | copy-start | bytes 11796484
  101.1 27.2 %collective-permute-start.6 = (bf16[160,384]{1,0:T(8,128)(2,1)S(1)}, bf16[160,384]{1,0:T(8,128)(2,1)S(1)}, u32[]{:S(2)}, u32[]{:S(2)}) collective-permute-start(bf16[160,384]{1,0:T(8,128)(2,1)S(1)} %slice_bitcast_fusion), channel_id=1, source_target_pairs={{0,16},{16,32},{32,48},{48,64},{64,80},{80,96},{96,112},{112,0},{1... | collective-permute-start | bytes 368648 | tf_op jit(solution)/shard_map/ppermute | solution.py:192
  128.3 13.8 %collective-permute-start.8 = (bf16[8,160,384]{2,1,0:T(8,128)(2,1)S(1)}, bf16[8,160,384]{2,1,0:T(8,128)(2,1)S(1)}, u32[]{:S(2)}, u32[]{:S(2)}) collective-permute-start(bf16[8,160,384]{2,1,0:T(8,128)(2,1)S(1)} %bitcast.18), channel_id=1, source_target_pairs={{0,128},{128,0},{1,129},{129,1},{2,130},{130,2},{3,131},{131,3},{4... | collective-permute-start | bytes 2949128 | tf_op jit(solution)/shard_map/ppermute | solution.py:168
  136.0 7.5 %copy-start.4 = (bf16[2560,768]{1,0:T(8,128)(2,1)S(1)}, bf16[2560,768]{1,0:T(8,128)(2,1)}, u32[]{:S(2)}) copy-start(bf16[2560,768]{1,0:T(8,128)(2,1)} %copy-done.3) | copy-start | bytes 11796484
  136.1 5.4 %collective-permute-start.9 = (bf16[2,2,160,384]{3,2,1,0:T(8,128)(2,1)S(1)}, bf16[2,2,160,384]{3,2,1,0:T(8,128)(2,1)S(1)}, u32[]{:S(2)}, u32[]{:S(2)}) collective-permute-start(bf16[2,2,160,384]{3,2,1,0:T(8,128)(2,1)S(1)} %pad_maximum_fusion), channel_id=1, source_target_pairs={{0,128},{128,0},{1,129},{129,1},{2,130},{130,2},{3,131},{131,3},{4... | collective-permute-start | bytes 1474568 | tf_op jit(solution)/shard_map/ppermute | solution.py:168
  138.3 3.7 %collective-permute-start.10 = (bf16[3,160,384]{2,1,0:T(8,128)(2,1)S(1)}, bf16[3,160,384]{2,1,0:T(8,128)(2,1)S(1)}, u32[]{:S(2)}, u32[]{:S(2)}) collective-permute-start(bf16[3,160,384]{2,1,0:T(8,128)(2,1)S(1)} %pad_maximum_fusion.1), channel_id=1, source_target_pairs={{0,128},{128,0},{1,129},{129,1},{2,130},{130,2},{3,131},{131,3},{4... | collective-permute-start | bytes 1105928 | tf_op jit(solution)/shard_map/ppermute | solution.py:168
  145.9 15.4 %collective-permute-start.12 = (bf16[384,512]{1,0:T(8,128)(2,1)S(1)}, bf16[384,512]{1,0:T(8,128)(2,1)S(1)}, u32[]{:S(2)}, u32[]{:S(2)}) collective-permute-start(bf16[384,512]{1,0:T(8,128)(2,1)S(1)} %fusion.11), channel_id=1, source_target_pairs={{0,1},{1,0},{2,3},{3,2},{4,5},{5,4},{6,7},{7,6},{8,9},{9,8},{10,11... | collective-permute-start | bytes 1179656 | tf_op jit(solution)/shard_map/ppermute | solution.py:168
  153.6 7.8 %copy-start.5 = (f32[768,128]{1,0:T(8,128)S(1)}, f32[768,128]{1,0:T(8,128)}, u32[]{:S(2)}) copy-start(f32[768,128]{1,0:T(8,128)} %constant.63.clone.cos_ref) | copy-start | bytes 1179652
  153.6 7.8 %copy-start.6 = (f32[768,128]{1,0:T(8,128)S(1)}, f32[768,128]{1,0:T(8,128)}, u32[]{:S(2)}) copy-start(f32[768,128]{1,0:T(8,128)} %constant.64.clone.sin_ref) | copy-start | bytes 1179652
  153.6 7.8 %copy-start.7 = (f32[2,128]{1,0:T(2,128)S(1)}, f32[2,128]{1,0:T(2,128)}, u32[]{:S(2)}) copy-start(f32[2,128]{1,0:T(2,128)} %query_gain_ref.3) | copy-start | bytes 3076
  153.6 16.2 %collective-permute-start.11 = (bf16[384,512]{1,0:T(8,128)(2,1)S(1)}, bf16[384,512]{1,0:T(8,128)(2,1)S(1)}, u32[]{:S(2)}, u32[]{:S(2)}) collective-permute-start(bf16[384,512]{1,0:T(8,128)(2,1)S(1)} %fusion.8), channel_id=1, source_target_pairs={{0,1},{1,0},{2,3},{3,2},{4,5},{5,4},{6,7},{7,6},{8,9},{9,8},{10,11... | collective-permute-start | bytes 1179656 | tf_op jit(solution)/shard_map/ppermute | solution.py:168
Sparse Core Ops, SparseCore 0:
  9.4 66.8 all-gather.2

commit v7 on v5

--- a/solution.py
+++ b/solution.py
@@ -36,43 +36,44 @@
 
 
 def local_call(kernel, name, out_shape, in_specs, out_specs):
-    params = pltpu.CompilerParams(vmem_limit_bytes=8 << 20)
     return pl.pallas_call(
-        kernel, out_shape=out_shape, in_specs=in_specs, out_specs=out_specs, compiler_params=params, name=name
+        kernel,
+        out_shape=out_shape,
+        in_specs=in_specs,
+        out_specs=out_specs,
+        compiler_params=pltpu.CompilerParams(vmem_limit_bytes=8 << 20),
+        name=name,
     )
 
 
-def assemble_kernel(place_ref, home_ref, *refs):
-    *step_refs, last_ref, early_ref, late_ref, own_ref, sent_ref = refs
-    _, _, rows, cols = home_ref.shape
+def put_block(place_ref, step, lane, block_ref, index, own_ref, sent_ref):
+    rows, cols = block_ref.shape[-2:]
     head = own_ref.shape[1] // 4
     wide = cols - head
-
-    def put(step, lane, block_ref, *index):
-        row = pl.multiple_of(place_ref[0, step] * rows, 32)
-        pair_col = pl.multiple_of(wide + place_ref[2, step] * head, 128)
-        spans = [pl.ds((lane * 2 + near) * 4 * rows + row, rows) for near in range(2)]
-
-        def put_queries(out_ref):
-            for near, span in enumerate(spans):
-                out_ref[span, :wide] = block_ref[*index, near, :, :wide]
-
-        pl.when(place_ref[1, step] == 0)(lambda: put_queries(own_ref))
-        pl.when(place_ref[1, step] == 1)(lambda: put_queries(sent_ref))
+    row = pl.multiple_of(place_ref[0, step] * rows, 32)
+    pair_col = pl.multiple_of(wide + place_ref[2, step] * head, 128)
+    spans = [pl.ds((lane * 2 + near) * 4 * rows + row, rows) for near in range(2)]
+
+    def put_queries(out_ref):
         for near, span in enumerate(spans):
-            pair = block_ref[*index, near, :, wide:]
-            own_ref[span, pl.ds(pair_col, head)] = pair
-            sent_ref[span, pl.ds(pair_col, head)] = pair
-
+            out_ref[span, :wide] = block_ref[*index, near, :, :wide]
+
+    pl.when(place_ref[1, step] == 0)(lambda: put_queries(own_ref))
+    pl.when(place_ref[1, step] == 1)(lambda: put_queries(sent_ref))
+    for near, span in enumerate(spans):
+        pair = block_ref[*index, near, :, wide:]
+        own_ref[span, pl.ds(pair_col, head)] = pair
+        sent_ref[span, pl.ds(pair_col, head)] = pair
+
+
+def assemble_kernel(place_ref, home_ref, first_ref, second_ref, third_ref, early_ref, last_ref, final_ref, *outs):
     for lane in range(2):
-        put(0, lane, home_ref, lane)
+        for step, block_ref in enumerate((home_ref, first_ref, second_ref, third_ref)):
+            put_block(place_ref, step, lane, block_ref, (lane,), *outs)
         for step in range(3):
-            put(1 + step, lane, step_refs[step], lane)
-        for step in range(2):
-            put(5 + step, 1 - lane, early_ref, step, lane)
-        put(7, 1 - lane, late_ref, lane)
-    put(4, 0, last_ref)
-    put(4, 1, late_ref, 2)
+            put_block(place_ref, 5 + step, 1 - lane, early_ref, (step, lane), *outs)
+    put_block(place_ref, 4, 0, last_ref, (), *outs)
+    put_block(place_ref, 4, 1, final_ref, (), *outs)
 
 
 def assemble(place, home, *rest):
@@ -148,7 +149,7 @@
             )
             scores = jnp.where(allowed, scores, -1e30)
             weights = jnp.exp(scores - jnp.max(scores, axis=-1, keepdims=True))
-            weights = weights / jnp.sum(weights, axis=-1, keepdims=True)
+            weights = weights * (1.0 / jnp.sum(weights, axis=-1, keepdims=True))
             output = jnp.dot(weights.astype(jnp.bfloat16), values_ref[:seen, :], preferred_element_type=jnp.float32)
             out_ref[first + start : seen, j * head : (j + 1) * head] = output.astype(out_ref.dtype)
 
@@ -158,7 +159,7 @@
     heads, head = query_gain.shape
     first = before[0].shape[0] if before else 0
     shape = [jax.ShapeDtypeStruct((first + rows, n), jnp.bfloat16) for n in (heads * head, head, head)]
-    kernel = functools.partial(attend_kernel, rows // 2, first)
+    kernel = functools.partial(attend_kernel, min(rows, 256), first)
     call = local_call(kernel, "attend", shape, [SMEM] + [VMEM] * (6 + len(before)), [VMEM] * 3)
     return call(limit, own, got, query_gain, key_gain, *tables, *before)
 
@@ -204,33 +205,30 @@
 
     grad_local = grad.astype(jnp.float32)
     sumsq = global_sum(jnp.sum(grad_local * grad_local))
+    flat = (slab_rows, slab_heads * head_size)
+    flats = [array.reshape(flat) for array in (master_weight, moment, variance, grad)]
+    gain = lax.dynamic_index_in_dim(norm_gain.reshape(8, 2, width_part), xh, 1, False).reshape(-1, 1)
+    sumsq, gain, *flats = lax.optimization_barrier((sumsq, gain, *flats))
+    master_flat, moment_flat, variance_flat, grad_flat = flats
     clip_factor = 1.0 / jnp.sqrt(sumsq + 1e-12)
-    clipped = grad_local * clip_factor
-    moment_new = BETA_ONE * moment + (1.0 - BETA_ONE) * clipped
-    variance_new = BETA_TWO * variance + (1.0 - BETA_TWO) * clipped * clipped
+    clipped = grad_flat.astype(jnp.float32) * clip_factor
+    moment_new = BETA_ONE * moment_flat + (1.0 - BETA_ONE) * clipped
+    variance_new = BETA_TWO * variance_flat + (1.0 - BETA_TWO) * clipped * clipped
     step_size = STEP_SCALE * width_all ** (-0.5)
-    updated = (master_weight - step_size * moment_new / (jnp.sqrt(variance_new) + 1e-08)).astype(
+    updated = (master_flat - step_size * moment_new / (jnp.sqrt(variance_new) + 1e-08)).astype(
         jnp.bfloat16
     )
-    updated = updated.reshape(slab_rows, slab_heads * head_size)
     home = jnp.stack([to_column(updated, 0), to_column(updated, 1)])
     home = jnp.stack([home, swap(home, "core")])
     first = onward(home)
     first, gathered = lax.optimization_barrier((first, gathered))
 
     square = squares(8, gathered)
+    other_square = swap(square, "xh")
     second = onward(first)
-    second, square = lax.optimization_barrier((second, square))
-    other_square = swap(square, "xh")
-    gain = lax.dynamic_index_in_dim(norm_gain.reshape(8, 2, width_part), xh, 1, False).reshape(-1, 1)
+    second, other_square = lax.optimization_barrier((second, other_square))
     place = (((((steps >> 1) & 1) ^ core) * 2 + ((steps >> 2) ^ xl)) * 2 + (steps & 1)).astype(jnp.int32)
     normed = normalise(float(width_all), 8, place, square, other_square, gain, gathered)
-
-    third = onward(second)
-    third, normed = lax.optimization_barrier((third, normed))
-    early = swap(jnp.stack([first, second]), "core")
-    last = onward(third[0])
-    late = swap(jnp.concatenate([third, last[None]]), "core")
 
     up = 1 - 2 * core
     source = (y - up * jnp.where(steps < 5, steps, 4 - steps)) & 7
@@ -238,21 +236,32 @@
     origin = jnp.where(native, source, (source + 2 * (source & 1) - 1) & 7)
     slab = jnp.where(native, xh, 1 - xh)
     place = jnp.stack([(origin >> 2) * 2 + (origin & 1), slab ^ xh, slab]).astype(jnp.int32)
-    own_weight, sent_weight = assemble(place, home, first, second, third, last, early, late)
+
+    third = onward(second)
+    third, normed = lax.optimization_barrier((third, normed))
+    last = onward(third[0])
+    early = swap(jnp.stack([first, second, third]), "core")
+
+    up = 1 - 2 * core
+    source = (y - up * jnp.where(steps < 5, steps, 4 - steps)) & 7
+    native = ((source >> 1) & 1) == xh
+    origin = jnp.where(native, source, (source + 2 * (source & 1) - 1) & 7)
+    slab = jnp.where(native, xh, 1 - xh)
+    place = jnp.stack([(origin >> 2) * 2 + (origin & 1), slab ^ xh, slab]).astype(jnp.int32)
+    own_weight, sent_weight = assemble(place, home, first, second, third, early, last, swap(last, "core"))
 
     tables = rope_tables(seq_rows, head_size)
     gain_row = lax.dynamic_slice_in_dim(key_gain, z, 1, 0)
-    part = seq_rows // 2
-
-    def product(start, weight):
-        rows = normed[:, start : start + part]
+    cut = seq_rows // 3 * 2
+
+    def product(rows, weight):
         return lax.dot_general(rows, weight, (((0,), (0,)), ((), ())), preferred_element_type=jnp.float32)
 
-    starts = range(0, seq_rows, part)
-    got = [swap(product(start, sent_weight).astype(jnp.bfloat16), "xh") for start in starts]
+    tokens = [normed[:, :cut], normed[:, cut:]]
+    got = [swap(product(rows, sent_weight).astype(jnp.bfloat16), "xh") for rows in tokens]
     result = ()
-    for start, other in zip(starts, got):
-        own = product(start, own_weight)
+    for rows, other in zip(tokens, got):
+        own = product(rows, own_weight)
         result = attend(prompt_len, own, other, query_gain, gain_row, tables, tuple(result))
     return result[0]
 

time: 160 us -> 155 us (0.969)
  blocking collectives: 38.9 us -> 0 us
  starting transfers between devices: 45.1 us -> 67 us
  waiting for transfers between devices: 30.6 us -> 40.7 us
  local copies, waits for them, and re-layouts: 8.21 us -> 9.98 us
    all_to_all x1 -> x0, blocking collectives: 38.9 us -> none  [global_sum(): return jnp.sum(lax.all_to_all(spread, AXES, 0, 0, tiled=True)[:, 0])]
    all_to_all x0 -> x1, starting transfers between devices: none -> 22.2 us  [global_sum(): return jnp.sum(lax.all_to_all(spread, AXES, 0, 0, tiled=True)[:, 0])]
    all_to_all x0 -> x1, waiting for transfers between devices: none -> 10.8 us  [global_sum(): return jnp.sum(lax.all_to_all(spread, AXES, 0, 0, tiled=True)[:, 0])]
    unnamed x0 -> x3, other arithmetic: none -> 3.93 us
    convert_element_type x1, other arithmetic: 3.22 us -> 0.19 us  [shards(): (master_flat - step_size * moment_new / (jnp.sqrt(variance_new) + 1e-08))...]
    unnamed x19 -> x21, local copies, waits for them, and re-layouts: 6.12 us -> 7.13 us
  transfers between devices with their start and end apart: 13 -> 14, of which waited for: 9 -> 10; matrix products, arithmetic and copies ran while one was open for 8% -> 9% of each run, Pallas kernels for 2% -> 3%
where the time goes in v7:
time: 155 us; the launch traced here: 154 us
  starting transfers between devices  67 us (43%)
  waiting for transfers between devices  40.7 us (26%)
  between operations  15.3 us (10%)
  local copies, waits for them, and re-layouts  9.98 us (6%)
  Pallas kernels  8.92 us (6%)
  other arithmetic  7.85 us (5%)
  matrix products  4.79 us (3%)
    ppermute x6, starting transfers between devices, swap(): return lax.ppermute(array, axis, [(0, 1), (1, 0)])  24.2 us
    all_to_all x1, starting transfers between devices, global_sum(): return jnp.sum(lax.all_to_all(spread, AXES, 0, 0, tiled=True)[:, 0])  22.2 us
    ppermute x4, starting transfers between devices, onward(): return lax.ppermute(block, ('core', 'y'), pairs)  17.8 us
    ppermute x6, waiting for transfers between devices, swap(): return lax.ppermute(array, axis, [(0, 1), (1, 0)])  14 us
    ppermute x4, waiting for transfers between devices, onward(): return lax.ppermute(block, ('core', 'y'), pairs)  11.3 us
    all_to_all x1, waiting for transfers between devices, global_sum(): return jnp.sum(lax.all_to_all(spread, AXES, 0, 0, tiled=True)[:, 0])  10.8 us
    unnamed x21, local copies, waits for them, and re-layouts  7.13 us
    pallas_call x2, Pallas kernels, attend(): return call(limit, own, got, query_gain, key_gain, *tables, *before)  5.08 us
  transfers between devices with their start and end apart: 14, of which 10 were waited for; matrix products, arithmetic and copies ran while one was open for 9% of the time, Pallas kernels for 3%

profile of v7, /device:TPU:1, one launch (start us, length us, event | category | flops | bytes accessed | tf_op | source)
XLA Modules:
  0.0 154.5 jit_solution(17177084619241909268)
XLA Ops:
  6.5 0.7 all-gather.2.cloned.1.call-update
  7.3 1.6 %multiply_reduce_fusion = f32[]{:T(128)} fusion(bf16[160,1,3,128]{3,0,2,1:T(8,128)(2,1)} %param.14), kind=kLoop, calls=%fused_computation.23 | loop fusion | flops 184319 | bytes 122884 | tf_op jit(solution)/shard_map/reduce_sum | solution.py:207
  8.8 1.4 broadcast_in_dim.9
  10.2 22.2 %all-to-all-start = ((f32[512,1,128]{2,1,0:T(1,128)}), f32[512,1,128]{2,1,0:T(1,128)S(1)}, u32[]{:S(2)}, u32[]{:S(2)}) async-start(f32[512,1,128]{2,1,0:T(1,128)} %broadcast_in_dim.9), calls=%async_computation | async-start | bytes 524288 | tf_op jit(solution)/shard_map/all_to_all | solution.py:176
  32.4 1.0 copy.18
  33.4 0.8 reshape.96
  34.3 0.1 reshape.97
  34.4 1.6 %reduce.3 = f32[160,3,128]{2,1,0:T(4,128)S(1)} reduce(f32[160,1,3,128]{3,1,2,0:T(1,128)} %param.15, f32[]{:T(128)} %constant.70), dimensions={1}, to_apply=%param.15.reduce_sub_computation | reduce | bytes 491524 | tf_op args[4]
  36.0 1.6 %reduce.4 = f32[160,3,128]{2,1,0:T(4,128)S(1)} reduce(f32[160,1,3,128]{3,1,2,0:T(1,128)} %param.16, f32[]{:T(128)} %constant.70), dimensions={1}, to_apply=%param.16.reduce_sub_computation | reduce | bytes 491524 | tf_op args[5]
  37.6 0.7 reduce.2
  38.4 10.8 %all-to-all-done = f32[512,1,128]{2,1,0:T(1,128)S(1)} async-done(((f32[512,1,128]{2,1,0:T(1,128)}), f32[512,1,128]{2,1,0:T(1,128)S(1)}, u32[]{:S(2)}, u32[]{:S(2)}) %all-to-all-start) | async-done | bytes 262176 | tf_op jit(solution)/shard_map/all_to_all | solution.py:176
  49.2 0.7 slice_reduce_fusion
  50.6 0.2 fusion.15
  50.8 0.7 collective-permute-start
  51.5 2.2 %collective-permute-start.1 = (bf16[160,384]{1,0:T(8,128)(2,1)S(1)}, bf16[160,384]{1,0:T(8,128)(2,1)S(1)}, u32[]{:S(2)}, u32[]{:S(2)}) collective-permute-start(bf16[160,384]{1,0:T(8,128)(2,1)S(1)} %fusion.15), channel_id=1, source_target_pairs={{0,256},{1,368},{16,272},{17,288},{32,273},{33,289},{48,321},{49,3... | collective-permute-start | bytes 368648 | tf_op jit(solution)/shard_map/ppermute | solution.py:187
  53.7 3.8 %collective-permute-done.1 = bf16[160,384]{1,0:T(8,128)(2,1)S(1)} collective-permute-done((bf16[160,384]{1,0:T(8,128)(2,1)S(1)}, bf16[160,384]{1,0:T(8,128)(2,1)S(1)}, u32[]{:S(2)}, u32[]{:S(2)}) %collective-permute-start.1) | collective-permute-done | bytes 122912 | tf_op jit(solution)/shard_map/ppermute | solution.py:187
  57.5 6.4 %collective-permute-start.2 = (bf16[2,160,384]{2,1,0:T(8,128)(2,1)S(1)}, bf16[2,160,384]{2,1,0:T(8,128)(2,1)S(1)}, u32[]{:S(2)}, u32[]{:S(2)}) collective-permute-start(bf16[2,160,384]{2,1,0:T(8,128)(2,1)S(1)} %get-tuple-element.44), channel_id=1, source_target_pairs={{0,128},{128,0},{1,129},{129,1},{2,130},{130,2},{3,131},{131,3},{4... | collective-permute-start | bytes 737288 | tf_op jit(solution)/shard_map/ppermute | solution.py:168
  64.0 1.1 collective-permute-done.2
  65.2 7.2 %collective-permute-start.3 = (bf16[2,2,160,384]{3,2,1,0:T(8,128)(2,1)S(1)}, bf16[2,2,160,384]{3,2,1,0:T(8,128)(2,1)S(1)}, u32[]{:S(2)}, u32[]{:S(2)}) collective-permute-start(bf16[2,2,160,384]{3,2,1,0:T(8,128)(2,1)S(1)} %pad_maximum_fusion.1.home_ref), channel_id=1, source_target_pairs={{0,16},{16,32},{32,48},{48,64},{64,80},{80,96},{96,112},{112,0},{1... | collective-permute-start | bytes 1474568 | tf_op jit(solution)/shard_map/ppermute | solution.py:192
  72.4 5.8 %collective-permute-done.3.first_ref = bf16[2,2,160,384]{3,2,1,0:T(8,128)(2,1)S(1)} collective-permute-done((bf16[2,2,160,384]{3,2,1,0:T(8,128)(2,1)S(1)}, bf16[2,2,160,384]{3,2,1,0:T(8,128)(2,1)S(1)}, u32[]{:S(2)}, u32[]{:S(2)}) %collective-permute-start.3) | collective-permute-done | bytes 491552 | tf_op jit(solution)/shard_map/ppermute | solution.py:192
  78.1 5.0 %collective-permute-start.4 = (bf16[2,2,160,384]{3,2,1,0:T(8,128)(2,1)S(1)}, bf16[2,2,160,384]{3,2,1,0:T(8,128)(2,1)S(1)}, u32[]{:S(2)}, u32[]{:S(2)}) collective-permute-start(bf16[2,2,160,384]{3,2,1,0:T(8,128)(2,1)S(1)} %collective-permute-done.3.first_ref), channel_id=1, source_target_pairs={{0,16},{16,32},{32,48},{48,64},{64,80},{80,96},{96,112},{112,0},{1... | collective-permute-start | bytes 1474568 | tf_op jit(solution)/shard_map/ppermute | solution.py:192
  83.2 2.1 %copy-done.1 = bf16[2560,768]{1,0:T(8,128)(2,1)S(1)} copy-done((bf16[2560,768]{1,0:T(8,128)(2,1)S(1)}, bf16[2560,768]{1,0:T(8,128)(2,1)}, u32[]{:S(2)}) %copy-start.1) | copy-done | bytes 3932184
  85.3 0.2 squares.1.square_ref
  85.5 2.3 %collective-permute-start.5 = (f32[1,768]{1,0:T(1,128)S(1)}, f32[1,768]{1,0:T(1,128)S(1)}, u32[]{:S(2)}, u32[]{:S(2)}) collective-permute-start(f32[1,768]{1,0:T(1,128)S(1)} %squares.1.square_ref), channel_id=1, source_target_pairs={{0,1},{1,0},{2,3},{3,2},{4,5},{5,4},{6,7},{7,6},{8,9},{9,8},{10,11... | collective-permute-start | bytes 9224 | tf_op jit(solution)/shard_map/ppermute | solution.py:168
  87.8 3.5 %collective-permute-done.5.other_ref = f32[1,768]{1,0:T(1,128)S(1)} collective-permute-done((f32[1,768]{1,0:T(1,128)S(1)}, f32[1,768]{1,0:T(1,128)S(1)}, u32[]{:S(2)}, u32[]{:S(2)}) %collective-permute-start.5) | collective-permute-done | bytes 3104 | tf_op jit(solution)/shard_map/ppermute | solution.py:168
  91.3 2.6 %collective-permute-start.6 = (bf16[2,2,160,384]{3,2,1,0:T(8,128)(2,1)S(1)}, bf16[2,2,160,384]{3,2,1,0:T(8,128)(2,1)S(1)}, u32[]{:S(2)}, u32[]{:S(2)}) collective-permute-start(bf16[2,2,160,384]{3,2,1,0:T(8,128)(2,1)S(1)} %collective-permute-done.4.second_ref), channel_id=1, source_target_pairs={{0,16},{16,32},{32,48},{48,64},{64,80},{80,96},{96,112},{112,0},{1... | collective-permute-start | bytes 1474568 | tf_op jit(solution)/shard_map/ppermute | solution.py:192
  93.9 0.4 copy.19.gain_ref
  94.4 2.1 %copy-done.2 = bf16[2560,768]{1,0:T(8,128)(2,1)S(1)} copy-done((bf16[2560,768]{1,0:T(8,128)(2,1)S(1)}, bf16[2560,768]{1,0:T(8,128)(2,1)}, u32[]{:S(2)}) %copy-start.2) | copy-done | bytes 3932184
  96.5 1.5 normalise.1
  98.0 1.8 %copy-done.3 = bf16[2560,768]{1,0:T(8,128)(2,1)} copy-done((bf16[2560,768]{1,0:T(8,128)(2,1)}, bf16[2560,768]{1,0:T(8,128)(2,1)S(1)}, u32[]{:S(2)}) %copy-start.3) | copy-done | bytes 3932184
  99.8 1.4 collective-permute-done.6.third_ref
  101.2 1.3 pad_maximum_fusion
  102.5 4.4 %collective-permute-start.7 = (bf16[3,2,2,160,384]{4,3,2,1,0:T(8,128)(2,1)}, bf16[3,2,2,160,384]{4,3,2,1,0:T(8,128)(2,1)}, u32[]{:S(2)}, u32[]{:S(2)}) collective-permute-start(bf16[3,2,2,160,384]{4,3,2,1,0:T(8,128)(2,1)} %pad_maximum_fusion), channel_id=1, source_target_pairs={{0,128},{128,0},{1,129},{129,1},{2,130},{130,2},{3,131},{131,3},{4... | collective-permute-start | bytes 4423688 | tf_op jit(solution)/shard_map/ppermute | solution.py:168
  106.9 3.0 %collective-permute-start.8 = (bf16[2,160,384]{2,1,0:T(8,128)(2,1)S(1)}, bf16[2,160,384]{2,1,0:T(8,128)(2,1)S(1)}, u32[]{:S(2)}, u32[]{:S(2)}) collective-permute-start(bf16[2,160,384]{2,1,0:T(8,128)(2,1)S(1)} %slice_bitcast_fusion), channel_id=1, source_target_pairs={{0,16},{16,32},{32,48},{48,64},{64,80},{80,96},{96,112},{112,0},{1... | collective-permute-start | bytes 737288 | tf_op jit(solution)/shard_map/ppermute | solution.py:192
  109.9 4.2 %collective-permute-done.8.last_ref = bf16[2,160,384]{2,1,0:T(8,128)(2,1)S(1)} collective-permute-done((bf16[2,160,384]{2,1,0:T(8,128)(2,1)S(1)}, bf16[2,160,384]{2,1,0:T(8,128)(2,1)S(1)}, u32[]{:S(2)}, u32[]{:S(2)}) %collective-permute-start.8) | collective-permute-done | bytes 245792 | tf_op jit(solution)/shard_map/ppermute | solution.py:192
  114.2 4.0 %collective-permute-start.9 = (bf16[2,160,384]{2,1,0:T(8,128)(2,1)S(1)}, bf16[2,160,384]{2,1,0:T(8,128)(2,1)S(1)}, u32[]{:S(2)}, u32[]{:S(2)}) collective-permute-start(bf16[2,160,384]{2,1,0:T(8,128)(2,1)S(1)} %collective-permute-done.8.last_ref), channel_id=1, source_target_pairs={{0,128},{128,0},{1,129},{129,1},{2,130},{130,2},{3,131},{131,3},{4... | collective-permute-start | bytes 737288 | tf_op jit(solution)/shard_map/ppermute | solution.py:168
  119.0 0.2 collective-permute-done.9.final_ref
  119.3 2.2 %assemble.1 = (bf16[2560,512]{1,0:T(8,128)(2,1)S(1)}, bf16[2560,512]{1,0:T(8,128)(2,1)S(1)}) custom-call(s32[3,8]{1,0:T(4,128)S(1)} %pad_add_fusion.place_ref, bf16[2,2,160,384]{3,2,1,0:T(8,128)(2,1)S(1)} %pad_maximum_fusion.1.home_ref, bf16[2,2,160,384]{3,2,1,0:T(8,128)(2,1)S(1)} %collective-permute-done.3.first_ref, ...), custom_call_target="tpu_custom_call" | custom-call | tf_op jit(solution)/shard_map/assemble/pallas_call | solution.py:83
  121.5 1.5 fusion.4
  123.0 3.7 %collective-permute-start.11 = (bf16[512,512]{1,0:T(8,128)(2,1)S(1)}, bf16[512,512]{1,0:T(8,128)(2,1)S(1)}, u32[]{:S(2)}, u32[]{:S(2)}) collective-permute-start(bf16[512,512]{1,0:T(8,128)(2,1)S(1)} %fusion.4), channel_id=1, source_target_pairs={{0,1},{1,0},{2,3},{3,2},{4,5},{5,4},{6,7},{7,6},{8,9},{9,8},{10,11... | collective-permute-start | bytes 1572872 | tf_op jit(solution)/shard_map/ppermute | solution.py:168
  126.7 1.5 fusion.2.own_ref
  128.3 0.9 convolution_convert_fusion
  129.2 3.4 %collective-permute-start.10 = (bf16[256,512]{1,0:T(8,128)(2,1)S(1)}, bf16[256,512]{1,0:T(8,128)(2,1)S(1)}, u32[]{:S(2)}, u32[]{:S(2)}) collective-permute-start(bf16[256,512]{1,0:T(8,128)(2,1)S(1)} %convolution_convert_fusion), channel_id=1, source_target_pairs={{0,1},{1,0},{2,3},{3,2},{4,5},{5,4},{6,7},{7,6},{8,9},{9,8},{10,11... | collective-permute-start | bytes 786440 | tf_op jit(solution)/shard_map/ppermute | solution.py:168
  132.6 0.9 fusion.8.own_ref
  133.4 6.2 %collective-permute-done.11.got_ref = bf16[512,512]{1,0:T(8,128)(2,1)S(1)} collective-permute-done((bf16[512,512]{1,0:T(8,128)(2,1)S(1)}, bf16[512,512]{1,0:T(8,128)(2,1)S(1)}, u32[]{:S(2)}, u32[]{:S(2)}) %collective-permute-start.11) | collective-permute-done | bytes 524320 | tf_op jit(solution)/shard_map/ppermute | solution.py:168
  139.7 2.7 %attend.2 = (bf16[512,256]{1,0:T(8,128)(2,1)S(1)}, bf16[512,128]{1,0:T(8,128)(2,1)S(1)}, bf16[512,128]{1,0:T(8,128)(2,1)S(1)}) custom-call(s32[1]{0:T(128)S(6)} %copy.31.limit_ref, f32[512,512]{1,0:T(8,128)S(1)} %fusion.2.own_ref, bf16[512,512]{1,0:T(8,128)(2,1)S(1)} %collective-permute-done.11.got_ref, f32[2,128]{1,0:T(2,128)S(1)} %copy-done.7, ...), custom_call_target="tpu_custom_call" | custom-call | tf_op jit(solution)/shard_map/attend/pallas_call | solution.py:164
  142.4 2.9 %collective-permute-done.10.got_ref = bf16[256,512]{1,0:T(8,128)(2,1)S(1)} collective-permute-done((bf16[256,512]{1,0:T(8,128)(2,1)S(1)}, bf16[256,512]{1,0:T(8,128)(2,1)S(1)}, u32[]{:S(2)}, u32[]{:S(2)}) %collective-permute-start.10) | collective-permute-done | bytes 262176 | tf_op jit(solution)/shard_map/ppermute | solution.py:168
  145.3 2.3 %attend.3 = (bf16[768,256]{1,0:T(8,128)(2,1)}, bf16[768,128]{1,0:T(8,128)(2,1)}, bf16[768,128]{1,0:T(8,128)(2,1)}) custom-call(s32[1]{0:T(128)S(6)} %copy.31.limit_ref, f32[256,512]{1,0:T(8,128)S(1)} %fusion.8.own_ref, bf16[256,512]{1,0:T(8,128)(2,1)S(1)} %collective-permute-done.10.got_ref, f32[2,128]{1,0:T(2,128)S(1)} %copy-done.7, ...), custom_call_target="tpu_custom_call" | custom-call | tf_op jit(solution)/shard_map/attend/pallas_call | solution.py:164
  (32 shorter events, 0.4 us)
Async XLA Ops:
  6.5 111.6 %copy-start = (f32[8,128]{1,0:T(8,128)S(1)}, f32[8,128]{1,0:T(8,128)}, u32[]{:S(2)}) copy-start(f32[8,128]{1,0:T(8,128)} %param.18) | copy-start | bytes 12292
  6.5 31.0 %copy-start.8 = (f32[160,1,3,128]{3,1,2,0:T(1,128)S(1)}, f32[160,1,3,128]{3,1,2,0:T(1,128)}, u32[]{:S(2)}) copy-start(f32[160,1,3,128]{3,1,2,0:T(1,128)} %param.13) | copy-start | bytes 737284
  6.5 71.6 %all-gather.2.cloned.1.call-start = ((), (), s32[]{:S(2)}) async-start(), calls=%async_computation.1 | async-start | bytes 4423680 | tf_op jit(solution)/shard_map/all_gather | solution.py:204
  10.2 39.0 %all-to-all-start = ((f32[512,1,128]{2,1,0:T(1,128)}), f32[512,1,128]{2,1,0:T(1,128)S(1)}, u32[]{:S(2)}, u32[]{:S(2)}) async-start(f32[512,1,128]{2,1,0:T(1,128)} %broadcast_in_dim.9), calls=%async_computation | async-start | bytes 524288 | tf_op jit(solution)/shard_map/all_to_all | solution.py:176
  50.8 2.9 %collective-permute-start = (bf16[160,384]{1,0:T(8,128)(2,1)S(1)}, bf16[160,384]{1,0:T(8,128)(2,1)S(1)}, u32[]{:S(2)}, u32[]{:S(2)}) collective-permute-start(bf16[160,384]{1,0:T(8,128)(2,1)S(1)} %fusion.15), channel_id=1, source_target_pairs={{0,0},{1,112},{16,16},{17,32},{32,17},{33,33},{48,65},{49,49},{64,... | collective-permute-start | bytes 368648 | tf_op jit(solution)/shard_map/ppermute | solution.py:187
  51.5 6.0 %collective-permute-start.1 = (bf16[160,384]{1,0:T(8,128)(2,1)S(1)}, bf16[160,384]{1,0:T(8,128)(2,1)S(1)}, u32[]{:S(2)}, u32[]{:S(2)}) collective-permute-start(bf16[160,384]{1,0:T(8,128)(2,1)S(1)} %fusion.15), channel_id=1, source_target_pairs={{0,256},{1,368},{16,272},{17,288},{32,273},{33,289},{48,321},{49,3... | collective-permute-start | bytes 368648 | tf_op jit(solution)/shard_map/ppermute | solution.py:187
  57.5 7.6 %collective-permute-start.2 = (bf16[2,160,384]{2,1,0:T(8,128)(2,1)S(1)}, bf16[2,160,384]{2,1,0:T(8,128)(2,1)S(1)}, u32[]{:S(2)}, u32[]{:S(2)}) collective-permute-start(bf16[2,160,384]{2,1,0:T(8,128)(2,1)S(1)} %get-tuple-element.44), channel_id=1, source_target_pairs={{0,128},{128,0},{1,129},{129,1},{2,130},{130,2},{3,131},{131,3},{4... | collective-permute-start | bytes 737288 | tf_op jit(solution)/shard_map/ppermute | solution.py:168
  65.2 13.0 %collective-permute-start.3 = (bf16[2,2,160,384]{3,2,1,0:T(8,128)(2,1)S(1)}, bf16[2,2,160,384]{3,2,1,0:T(8,128)(2,1)S(1)}, u32[]{:S(2)}, u32[]{:S(2)}) collective-permute-start(bf16[2,2,160,384]{3,2,1,0:T(8,128)(2,1)S(1)} %pad_maximum_fusion.1.home_ref), channel_id=1, source_target_pairs={{0,16},{16,32},{32,48},{48,64},{64,80},{80,96},{96,112},{112,0},{1... | collective-permute-start | bytes 1474568 | tf_op jit(solution)/shard_map/ppermute | solution.py:192
  78.1 13.2 %collective-permute-start.4 = (bf16[2,2,160,384]{3,2,1,0:T(8,128)(2,1)S(1)}, bf16[2,2,160,384]{3,2,1,0:T(8,128)(2,1)S(1)}, u32[]{:S(2)}, u32[]{:S(2)}) collective-permute-start(bf16[2,2,160,384]{3,2,1,0:T(8,128)(2,1)S(1)} %collective-permute-done.3.first_ref), channel_id=1, source_target_pairs={{0,16},{16,32},{32,48},{48,64},{64,80},{80,96},{96,112},{112,0},{1... | collective-permute-start | bytes 1474568 | tf_op jit(solution)/shard_map/ppermute | solution.py:192
  83.2 2.1 %copy-start.1 = (bf16[2560,768]{1,0:T(8,128)(2,1)S(1)}, bf16[2560,768]{1,0:T(8,128)(2,1)}, u32[]{:S(2)}) copy-start(bf16[2560,768]{1,0:T(8,128)(2,1)} %all-gather.2.cloned.1.call-done.features_ref) | copy-start | bytes 11796484
  85.5 5.8 %collective-permute-start.5 = (f32[1,768]{1,0:T(1,128)S(1)}, f32[1,768]{1,0:T(1,128)S(1)}, u32[]{:S(2)}, u32[]{:S(2)}) collective-permute-start(f32[1,768]{1,0:T(1,128)S(1)} %squares.1.square_ref), channel_id=1, source_target_pairs={{0,1},{1,0},{2,3},{3,2},{4,5},{5,4},{6,7},{7,6},{8,9},{9,8},{10,11... | collective-permute-start | bytes 9224 | tf_op jit(solution)/shard_map/ppermute | solution.py:168
  91.3 9.9 %collective-permute-start.6 = (bf16[2,2,160,384]{3,2,1,0:T(8,128)(2,1)S(1)}, bf16[2,2,160,384]{3,2,1,0:T(8,128)(2,1)S(1)}, u32[]{:S(2)}, u32[]{:S(2)}) collective-permute-start(bf16[2,2,160,384]{3,2,1,0:T(8,128)(2,1)S(1)} %collective-permute-done.4.second_ref), channel_id=1, source_target_pairs={{0,16},{16,32},{32,48},{48,64},{64,80},{80,96},{96,112},{112,0},{1... | collective-permute-start | bytes 1474568 | tf_op jit(solution)/shard_map/ppermute | solution.py:192
  94.4 2.1 %copy-start.2 = (bf16[2560,768]{1,0:T(8,128)(2,1)S(1)}, bf16[2560,768]{1,0:T(8,128)(2,1)}, u32[]{:S(2)}) copy-start(bf16[2560,768]{1,0:T(8,128)(2,1)} %all-gather.2.cloned.1.call-done.features_ref) | copy-start | bytes 11796484
  98.0 1.9 %copy-start.3 = (bf16[2560,768]{1,0:T(8,128)(2,1)}, bf16[2560,768]{1,0:T(8,128)(2,1)S(1)}, u32[]{:S(2)}) copy-start(bf16[2560,768]{1,0:T(8,128)(2,1)S(1)} %normalise.1) | copy-start | bytes 11796484
  102.5 16.8 %collective-permute-start.7 = (bf16[3,2,2,160,384]{4,3,2,1,0:T(8,128)(2,1)}, bf16[3,2,2,160,384]{4,3,2,1,0:T(8,128)(2,1)}, u32[]{:S(2)}, u32[]{:S(2)}) collective-permute-start(bf16[3,2,2,160,384]{4,3,2,1,0:T(8,128)(2,1)} %pad_maximum_fusion), channel_id=1, source_target_pairs={{0,128},{128,0},{1,129},{129,1},{2,130},{130,2},{3,131},{131,3},{4... | collective-permute-start | bytes 4423688 | tf_op jit(solution)/shard_map/ppermute | solution.py:168
  106.9 7.2 %collective-permute-start.8 = (bf16[2,160,384]{2,1,0:T(8,128)(2,1)S(1)}, bf16[2,160,384]{2,1,0:T(8,128)(2,1)S(1)}, u32[]{:S(2)}, u32[]{:S(2)}) collective-permute-start(bf16[2,160,384]{2,1,0:T(8,128)(2,1)S(1)} %slice_bitcast_fusion), channel_id=1, source_target_pairs={{0,16},{16,32},{32,48},{48,64},{64,80},{80,96},{96,112},{112,0},{1... | collective-permute-start | bytes 737288 | tf_op jit(solution)/shard_map/ppermute | solution.py:192
  114.2 5.1 %collective-permute-start.9 = (bf16[2,160,384]{2,1,0:T(8,128)(2,1)S(1)}, bf16[2,160,384]{2,1,0:T(8,128)(2,1)S(1)}, u32[]{:S(2)}, u32[]{:S(2)}) collective-permute-start(bf16[2,160,384]{2,1,0:T(8,128)(2,1)S(1)} %collective-permute-done.8.last_ref), channel_id=1, source_target_pairs={{0,128},{128,0},{1,129},{129,1},{2,130},{130,2},{3,131},{131,3},{4... | collective-permute-start | bytes 737288 | tf_op jit(solution)/shard_map/ppermute | solution.py:168
  118.2 3.3 %copy-start.4 = (bf16[2560,768]{1,0:T(8,128)(2,1)S(1)}, bf16[2560,768]{1,0:T(8,128)(2,1)}, u32[]{:S(2)}) copy-start(bf16[2560,768]{1,0:T(8,128)(2,1)} %copy-done.3) | copy-start | bytes 11796484
  123.0 16.7 %collective-permute-start.11 = (bf16[512,512]{1,0:T(8,128)(2,1)S(1)}, bf16[512,512]{1,0:T(8,128)(2,1)S(1)}, u32[]{:S(2)}, u32[]{:S(2)}) collective-permute-start(bf16[512,512]{1,0:T(8,128)(2,1)S(1)} %fusion.4), channel_id=1, source_target_pairs={{0,1},{1,0},{2,3},{3,2},{4,5},{5,4},{6,7},{7,6},{8,9},{9,8},{10,11... | collective-permute-start | bytes 1572872 | tf_op jit(solution)/shard_map/ppermute | solution.py:168
  129.1 10.6 %copy-start.5 = (f32[768,128]{1,0:T(8,128)S(1)}, f32[768,128]{1,0:T(8,128)}, u32[]{:S(2)}) copy-start(f32[768,128]{1,0:T(8,128)} %constant.62.clone.cos_ref) | copy-start | bytes 1179652
  129.1 10.5 %copy-start.6 = (f32[768,128]{1,0:T(8,128)S(1)}, f32[768,128]{1,0:T(8,128)}, u32[]{:S(2)}) copy-start(f32[768,128]{1,0:T(8,128)} %constant.63.clone.sin_ref) | copy-start | bytes 1179652
  129.2 10.5 %copy-start.7 = (f32[2,128]{1,0:T(2,128)S(1)}, f32[2,128]{1,0:T(2,128)}, u32[]{:S(2)}) copy-start(f32[2,128]{1,0:T(2,128)} %query_gain_ref.3) | copy-start | bytes 3076
  129.2 16.1 %collective-permute-start.10 = (bf16[256,512]{1,0:T(8,128)(2,1)S(1)}, bf16[256,512]{1,0:T(8,128)(2,1)S(1)}, u32[]{:S(2)}, u32[]{:S(2)}) collective-permute-start(bf16[256,512]{1,0:T(8,128)(2,1)S(1)} %convolution_convert_fusion), channel_id=1, source_target_pairs={{0,1},{1,0},{2,3},{3,2},{4,5},{5,4},{6,7},{7,6},{8,9},{9,8},{10,11... | collective-permute-start | bytes 786440 | tf_op jit(solution)/shard_map/ppermute | solution.py:168
Sparse Core Ops, SparseCore 0:
  9.4 66.8 all-gather.1

commit v8 on v7

--- a/solution.py
+++ b/solution.py
@@ -66,12 +66,14 @@
         sent_ref[span, pl.ds(pair_col, head)] = pair
 
 
-def assemble_kernel(place_ref, home_ref, first_ref, second_ref, third_ref, early_ref, last_ref, final_ref, *outs):
+def assemble_kernel(place_ref, *refs):
+    *block_refs, last_ref, final_ref, own_ref, sent_ref = refs
+    outs = (own_ref, sent_ref)
     for lane in range(2):
-        for step, block_ref in enumerate((home_ref, first_ref, second_ref, third_ref)):
-            put_block(place_ref, step, lane, block_ref, (lane,), *outs)
+        for step in range(4):
+            put_block(place_ref, step, lane, block_refs[step], (lane,), *outs)
         for step in range(3):
-            put_block(place_ref, 5 + step, 1 - lane, early_ref, (step, lane), *outs)
+            put_block(place_ref, 5 + step, 1 - lane, block_refs[4 + step], (lane,), *outs)
     put_block(place_ref, 4, 0, last_ref, (), *outs)
     put_block(place_ref, 4, 1, final_ref, (), *outs)
 
@@ -187,8 +189,8 @@
     return lax.ppermute(block, ("xl", "y", "xh"), pairs)
 
 
-def onward(block):
-    pairs = [(y, (y + 1) % 8) for y in range(8)] + [(8 + y, 8 + (y - 1) % 8) for y in range(8)]
+def onward(block, steps):
+    pairs = [(y, (y + steps) % 8) for y in range(8)] + [(8 + y, 8 + (y - steps) % 8) for y in range(8)]
     return lax.ppermute(block, ("core", "y"), pairs)
 
 
@@ -220,15 +222,19 @@
     )
     home = jnp.stack([to_column(updated, 0), to_column(updated, 1)])
     home = jnp.stack([home, swap(home, "core")])
-    first = onward(home)
+    first, second = onward(home, 1), onward(home, 2)
     first, gathered = lax.optimization_barrier((first, gathered))
+    exchanged = [swap(first, "core")]
 
     square = squares(8, gathered)
+    second, square, exchanged[0] = lax.optimization_barrier((second, square, exchanged[0]))
     other_square = swap(square, "xh")
-    second = onward(first)
-    second, other_square = lax.optimization_barrier((second, other_square))
     place = (((((steps >> 1) & 1) ^ core) * 2 + ((steps >> 2) ^ xl)) * 2 + (steps & 1)).astype(jnp.int32)
     normed = normalise(float(width_all), 8, place, square, other_square, gain, gathered)
+
+    third, last = onward(second, 1), onward(second[0], 2)
+    third, normed = lax.optimization_barrier((third, normed))
+    exchanged += [swap(second, "core"), swap(third, "core")]
 
     up = 1 - 2 * core
     source = (y - up * jnp.where(steps < 5, steps, 4 - steps)) & 7
@@ -236,19 +242,9 @@
     origin = jnp.where(native, source, (source + 2 * (source & 1) - 1) & 7)
     slab = jnp.where(native, xh, 1 - xh)
     place = jnp.stack([(origin >> 2) * 2 + (origin & 1), slab ^ xh, slab]).astype(jnp.int32)
-
-    third = onward(second)
-    third, normed = lax.optimization_barrier((third, normed))
-    last = onward(third[0])
-    early = swap(jnp.stack([first, second, third]), "core")
-
-    up = 1 - 2 * core
-    source = (y - up * jnp.where(steps < 5, steps, 4 - steps)) & 7
-    native = ((source >> 1) & 1) == xh
-    origin = jnp.where(native, source, (source + 2 * (source & 1) - 1) & 7)
-    slab = jnp.where(native, xh, 1 - xh)
-    place = jnp.stack([(origin >> 2) * 2 + (origin & 1), slab ^ xh, slab]).astype(jnp.int32)
-    own_weight, sent_weight = assemble(place, home, first, second, third, early, last, swap(last, "core"))
+    own_weight, sent_weight = assemble(
+        place, home, first, second, third, *exchanged, last, swap(last, "core")
+    )
 
     tables = rope_tables(seq_rows, head_size)
     gain_row = lax.dynamic_slice_in_dim(key_gain, z, 1, 0)

time: 155 us -> 150 us (0.968)
  waiting for transfers between devices: 40.7 us -> 35.9 us
    ppermute x6 -> x8, waiting for transfers between devices: 14 us -> 10.4 us  [swap(): return lax.ppermute(array, axis, [(0, 1), (1, 0)])]
    ppermute x6 -> x8, starting transfers between devices: 24.2 us -> 26.6 us  [swap(): return lax.ppermute(array, axis, [(0, 1), (1, 0)])]
    ppermute x4, starting transfers between devices: 17.8 us -> 15.9 us  [onward(): return lax.ppermute(block, ('core', 'y'), pairs)]
  transfers between devices with their start and end apart: 14 -> 16, of which waited for: 10 -> 8; matrix products, arithmetic and copies ran while one was open for 9% -> 10% of each run, Pallas kernels for 3% -> 3%
where the time goes in v8:
time: 150 us
  starting transfers between devices  67.6 us (45%)
  waiting for transfers between devices  35.9 us (24%)
  between operations  15.3 us (10%)
  local copies, waits for them, and re-layouts  10.7 us (7%)
  Pallas kernels  8.72 us (6%)
  other arithmetic  6.54 us (4%)
  matrix products  4.79 us (3%)
    ppermute x8, starting transfers between devices, swap(): return lax.ppermute(array, axis, [(0, 1), (1, 0)])  26.6 us
    all_to_all x1, starting transfers between devices, global_sum(): return jnp.sum(lax.all_to_all(spread, AXES, 0, 0, tiled=True)[:, 0])  22.2 us
    ppermute x4, starting transfers between devices, onward(): return lax.ppermute(block, ('core', 'y'), pairs)  15.9 us
    all_to_all x1, waiting for transfers between devices, global_sum(): return jnp.sum(lax.all_to_all(spread, AXES, 0, 0, tiled=True)[:, 0])  10.8 us
    ppermute x8, waiting for transfers between devices, swap(): return lax.ppermute(array, axis, [(0, 1), (1, 0)])  10.4 us
    ppermute x4, waiting for transfers between devices, onward(): return lax.ppermute(block, ('core', 'y'), pairs)  10.1 us
    unnamed x21, local copies, waits for them, and re-layouts  7.13 us
    pallas_call x2, Pallas kernels, attend(): return call(limit, own, got, query_gain, key_gain, *tables, *before)  5.08 us
  transfers between devices with their start and end apart: 16, of which 8 were waited for; matrix products, arithmetic and copies ran while one was open for 10% of the time, Pallas kernels for 3%

profile of v8, /device:TPU:1, one launch (start us, length us, event | category | flops | bytes accessed | tf_op | source)
XLA Modules:
  0.0 149.5 jit_solution(4967043594574384470)
XLA Ops:
  6.5 0.7 all-gather.2.cloned.1.call-update
  7.3 1.6 %multiply_reduce_fusion = f32[]{:T(128)} fusion(bf16[160,1,3,128]{3,0,2,1:T(8,128)(2,1)} %param.14), kind=kLoop, calls=%fused_computation.22 | loop fusion | flops 184319 | bytes 122884 | tf_op jit(solution)/shard_map/reduce_sum | solution.py:209
  8.9 1.4 broadcast_in_dim.9
  10.3 22.2 %all-to-all-start = ((f32[512,1,128]{2,1,0:T(1,128)}), f32[512,1,128]{2,1,0:T(1,128)S(1)}, u32[]{:S(2)}, u32[]{:S(2)}) async-start(f32[512,1,128]{2,1,0:T(1,128)} %broadcast_in_dim.9), calls=%async_computation | async-start | bytes 524288 | tf_op jit(solution)/shard_map/all_to_all | solution.py:178
  32.5 1.0 copy.18
  33.5 0.8 reshape.96
  34.3 0.1 reshape.97
  34.4 1.6 %reduce.4 = f32[160,3,128]{2,1,0:T(4,128)S(1)} reduce(f32[160,1,3,128]{3,1,2,0:T(1,128)} %param.16, f32[]{:T(128)} %constant.70), dimensions={1}, to_apply=%param.16.reduce_sub_computation | reduce | bytes 491524 | tf_op args[5]
  36.0 1.6 %reduce.3 = f32[160,3,128]{2,1,0:T(4,128)S(1)} reduce(f32[160,1,3,128]{3,1,2,0:T(1,128)} %param.15, f32[]{:T(128)} %constant.70), dimensions={1}, to_apply=%param.15.reduce_sub_computation | reduce | bytes 491524 | tf_op args[4]
  37.7 0.7 reduce.2
  38.5 10.8 %all-to-all-done = f32[512,1,128]{2,1,0:T(1,128)S(1)} async-done(((f32[512,1,128]{2,1,0:T(1,128)}), f32[512,1,128]{2,1,0:T(1,128)S(1)}, u32[]{:S(2)}, u32[]{:S(2)}) %all-to-all-start) | async-done | bytes 262176 | tf_op jit(solution)/shard_map/all_to_all | solution.py:178
  49.3 0.7 slice_reduce_fusion
  50.7 0.2 fusion.15
  50.9 0.7 collective-permute-start
  51.5 2.2 %collective-permute-start.1 = (bf16[160,384]{1,0:T(8,128)(2,1)S(1)}, bf16[160,384]{1,0:T(8,128)(2,1)S(1)}, u32[]{:S(2)}, u32[]{:S(2)}) collective-permute-start(bf16[160,384]{1,0:T(8,128)(2,1)S(1)} %fusion.15), channel_id=1, source_target_pairs={{0,256},{1,368},{16,272},{17,288},{32,273},{33,289},{48,321},{49,3... | collective-permute-start | bytes 368648 | tf_op jit(solution)/shard_map/ppermute | solution.py:189
  53.8 3.8 %collective-permute-done.1 = bf16[160,384]{1,0:T(8,128)(2,1)S(1)} collective-permute-done((bf16[160,384]{1,0:T(8,128)(2,1)S(1)}, bf16[160,384]{1,0:T(8,128)(2,1)S(1)}, u32[]{:S(2)}, u32[]{:S(2)}) %collective-permute-start.1) | collective-permute-done | bytes 122912 | tf_op jit(solution)/shard_map/ppermute | solution.py:189
  57.6 6.5 %collective-permute-start.2 = (bf16[2,160,384]{2,1,0:T(8,128)(2,1)S(1)}, bf16[2,160,384]{2,1,0:T(8,128)(2,1)S(1)}, u32[]{:S(2)}, u32[]{:S(2)}) collective-permute-start(bf16[2,160,384]{2,1,0:T(8,128)(2,1)S(1)} %get-tuple-element.46), channel_id=1, source_target_pairs={{0,128},{128,0},{1,129},{129,1},{2,130},{130,2},{3,131},{131,3},{4... | collective-permute-start | bytes 737288 | tf_op jit(solution)/shard_map/ppermute | solution.py:170
  64.1 1.1 collective-permute-done.2
  65.2 7.2 %collective-permute-start.4 = (bf16[2,2,160,384]{3,2,1,0:T(8,128)(2,1)S(1)}, bf16[2,2,160,384]{3,2,1,0:T(8,128)(2,1)S(1)}, u32[]{:S(2)}, u32[]{:S(2)}) collective-permute-start(bf16[2,2,160,384]{3,2,1,0:T(8,128)(2,1)S(1)} %pad_maximum_fusion.refs_0_), channel_id=1, source_target_pairs={{0,16},{16,32},{32,48},{48,64},{64,80},{80,96},{96,112},{112,0},{1... | collective-permute-start | bytes 1474568 | tf_op jit(solution)/shard_map/ppermute | solution.py:194
  72.5 1.9 %collective-permute-start.3 = (bf16[2,2,160,384]{3,2,1,0:T(8,128)(2,1)S(1)}, bf16[2,2,160,384]{3,2,1,0:T(8,128)(2,1)S(1)}, u32[]{:S(2)}, u32[]{:S(2)}) collective-permute-start(bf16[2,2,160,384]{3,2,1,0:T(8,128)(2,1)S(1)} %pad_maximum_fusion.refs_0_), channel_id=1, source_target_pairs={{0,32},{16,48},{32,64},{48,80},{64,96},{80,112},{96,0},{112,16},{1... | collective-permute-start | bytes 1474568 | tf_op jit(solution)/shard_map/ppermute | solution.py:194
  74.4 9.1 %collective-permute-done.4.refs_1_ = bf16[2,2,160,384]{3,2,1,0:T(8,128)(2,1)S(1)} collective-permute-done((bf16[2,2,160,384]{3,2,1,0:T(8,128)(2,1)S(1)}, bf16[2,2,160,384]{3,2,1,0:T(8,128)(2,1)S(1)}, u32[]{:S(2)}, u32[]{:S(2)}) %collective-permute-start.4) | collective-permute-done | bytes 491552 | tf_op jit(solution)/shard_map/ppermute | solution.py:194
  83.5 1.9 %collective-permute-start.5 = (bf16[2,2,160,384]{3,2,1,0:T(8,128)(2,1)S(1)}, bf16[2,2,160,384]{3,2,1,0:T(8,128)(2,1)S(1)}, u32[]{:S(2)}, u32[]{:S(2)}) collective-permute-start(bf16[2,2,160,384]{3,2,1,0:T(8,128)(2,1)S(1)} %collective-permute-done.4.refs_1_), channel_id=1, source_target_pairs={{0,128},{128,0},{1,129},{129,1},{2,130},{130,2},{3,131},{131,3},{4... | collective-permute-start | bytes 1474568 | tf_op jit(solution)/shard_map/ppermute | solution.py:170
  85.4 2.1 %copy-done.1 = bf16[2560,768]{1,0:T(8,128)(2,1)S(1)} copy-done((bf16[2560,768]{1,0:T(8,128)(2,1)S(1)}, bf16[2560,768]{1,0:T(8,128)(2,1)}, u32[]{:S(2)}) %copy-start.1) | copy-done | bytes 3932184
  87.5 0.2 squares.1.square_ref
  87.7 1.0 collective-permute-done.3.refs_2_
  88.7 4.2 %collective-permute-start.6 = (bf16[2,2,160,384]{3,2,1,0:T(8,128)(2,1)S(1)}, bf16[2,2,160,384]{3,2,1,0:T(8,128)(2,1)}, u32[]{:S(2)}, u32[]{:S(2)}) collective-permute-start(bf16[2,2,160,384]{3,2,1,0:T(8,128)(2,1)S(1)} %collective-permute-done.3.refs_2_), channel_id=1, source_target_pairs={{0,16},{16,32},{32,48},{48,64},{64,80},{80,96},{96,112},{112,0},{1... | collective-permute-start | bytes 1474568 | tf_op jit(solution)/shard_map/ppermute | solution.py:194
  92.9 2.9 %collective-permute-start.7 = (f32[1,768]{1,0:T(1,128)S(1)}, f32[1,768]{1,0:T(1,128)S(1)}, u32[]{:S(2)}, u32[]{:S(2)}) collective-permute-start(f32[1,768]{1,0:T(1,128)S(1)} %squares.1.square_ref), channel_id=1, source_target_pairs={{0,1},{1,0},{2,3},{3,2},{4,5},{5,4},{6,7},{7,6},{8,9},{9,8},{10,11... | collective-permute-start | bytes 9224 | tf_op jit(solution)/shard_map/ppermute | solution.py:170
  95.8 0.7 slice_bitcast_fusion
  96.6 2.7 %collective-permute-start.10 = (bf16[2,160,384]{2,1,0:T(8,128)(2,1)}, bf16[2,160,384]{2,1,0:T(8,128)(2,1)S(1)}, u32[]{:S(2)}, u32[]{:S(2)}) collective-permute-start(bf16[2,160,384]{2,1,0:T(8,128)(2,1)} %slice_bitcast_fusion), channel_id=1, source_target_pairs={{0,32},{16,48},{32,64},{48,80},{64,96},{80,112},{96,0},{112,16},{1... | collective-permute-start | bytes 737288 | tf_op jit(solution)/shard_map/ppermute | solution.py:194
  99.2 0.4 copy.19.gain_ref
  99.7 3.1 %collective-permute-start.8 = (bf16[2,2,160,384]{3,2,1,0:T(8,128)(2,1)S(1)}, bf16[2,2,160,384]{3,2,1,0:T(8,128)(2,1)}, u32[]{:S(2)}, u32[]{:S(2)}) collective-permute-start(bf16[2,2,160,384]{3,2,1,0:T(8,128)(2,1)S(1)} %collective-permute-done.3.refs_2_), channel_id=1, source_target_pairs={{0,128},{128,0},{1,129},{129,1},{2,130},{130,2},{3,131},{131,3},{4... | collective-permute-start | bytes 1474568 | tf_op jit(solution)/shard_map/ppermute | solution.py:170
  102.8 2.1 %copy-done.2 = bf16[2560,768]{1,0:T(8,128)(2,1)S(1)} copy-done((bf16[2560,768]{1,0:T(8,128)(2,1)S(1)}, bf16[2560,768]{1,0:T(8,128)(2,1)}, u32[]{:S(2)}) %copy-start.2) | copy-done | bytes 3932184
  104.9 1.5 normalise.1
  106.4 1.9 %copy-done.3 = bf16[2560,768]{1,0:T(8,128)(2,1)} copy-done((bf16[2560,768]{1,0:T(8,128)(2,1)}, bf16[2560,768]{1,0:T(8,128)(2,1)S(1)}, u32[]{:S(2)}) %copy-start.3) | copy-done | bytes 3932184
  108.3 1.9 %collective-permute-start.9 = (bf16[2,2,160,384]{3,2,1,0:T(8,128)(2,1)}, bf16[2,2,160,384]{3,2,1,0:T(8,128)(2,1)S(1)}, u32[]{:S(2)}, u32[]{:S(2)}) collective-permute-start(bf16[2,2,160,384]{3,2,1,0:T(8,128)(2,1)} %collective-permute-done.6.refs_3_), channel_id=1, source_target_pairs={{0,128},{128,0},{1,129},{129,1},{2,130},{130,2},{3,131},{131,3},{4... | collective-permute-start | bytes 1474568 | tf_op jit(solution)/shard_map/ppermute | solution.py:170
  110.2 3.2 %collective-permute-start.11 = (bf16[2,160,384]{2,1,0:T(8,128)(2,1)S(1)}, bf16[2,160,384]{2,1,0:T(8,128)(2,1)S(1)}, u32[]{:S(2)}, u32[]{:S(2)}) collective-permute-start(bf16[2,160,384]{2,1,0:T(8,128)(2,1)S(1)} %collective-permute-done.10.refs_7_), channel_id=1, source_target_pairs={{0,128},{128,0},{1,129},{129,1},{2,130},{130,2},{3,131},{131,3},{4... | collective-permute-start | bytes 737288 | tf_op jit(solution)/shard_map/ppermute | solution.py:170
  114.3 0.2 collective-permute-done.11.refs_8_
  114.5 2.0 %assemble.1 = (bf16[2560,512]{1,0:T(8,128)(2,1)S(1)}, bf16[2560,512]{1,0:T(8,128)(2,1)S(1)}) custom-call(s32[3,8]{1,0:T(4,128)S(1)} %pad_add_fusion.place_ref, bf16[2,2,160,384]{3,2,1,0:T(8,128)(2,1)S(1)} %pad_maximum_fusion.refs_0_, bf16[2,2,160,384]{3,2,1,0:T(8,128)(2,1)S(1)} %collective-permute-done.4.refs_1_, ...), custom_call_target="tpu_custom_call" | custom-call | tf_op jit(solution)/shard_map/assemble/pallas_call | solution.py:85
  116.5 1.5 %fusion.4 = bf16[512,512]{1,0:T(8,128)(2,1)S(1)} fusion(bf16[2560,512]{1,0:T(8,128)(2,1)S(1)} %get-tuple-element.38, bf16[2560,768]{1,0:T(8,128)(2,1)S(1)} %copy-done.4), kind=kOutput, calls=%fused_computation.4 | convolution fusion | flops 1342439424 | bytes 5767168 | tf_op jit(solution)/shard_map/dot_general | solution.py:254
  118.1 3.2 %collective-permute-start.13 = (bf16[512,512]{1,0:T(8,128)(2,1)S(1)}, bf16[512,512]{1,0:T(8,128)(2,1)S(1)}, u32[]{:S(2)}, u32[]{:S(2)}) collective-permute-start(bf16[512,512]{1,0:T(8,128)(2,1)S(1)} %fusion.4), channel_id=1, source_target_pairs={{0,1},{1,0},{2,3},{3,2},{4,5},{5,4},{6,7},{7,6},{8,9},{9,8},{10,11... | collective-permute-start | bytes 1572872 | tf_op jit(solution)/shard_map/ppermute | solution.py:170
  121.2 1.5 %fusion.2.own_ref = f32[512,512]{1,0:T(8,128)S(1)} fusion(bf16[2560,512]{1,0:T(8,128)(2,1)S(1)} %get-tuple-element.37, bf16[2560,768]{1,0:T(8,128)(2,1)S(1)} %copy-done.4), kind=kOutput, calls=%fused_computation.2 | convolution fusion | flops 1342177280 | bytes 6291456 | tf_op jit(solution)/shard_map/dot_general | solution.py:254
  122.8 0.9 convolution_convert_fusion
  123.7 3.9 %collective-permute-start.12 = (bf16[256,512]{1,0:T(8,128)(2,1)S(1)}, bf16[256,512]{1,0:T(8,128)(2,1)S(1)}, u32[]{:S(2)}, u32[]{:S(2)}) collective-permute-start(bf16[256,512]{1,0:T(8,128)(2,1)S(1)} %convolution_convert_fusion), channel_id=1, source_target_pairs={{0,1},{1,0},{2,3},{3,2},{4,5},{5,4},{6,7},{7,6},{8,9},{9,8},{10,11... | collective-permute-start | bytes 786440 | tf_op jit(solution)/shard_map/ppermute | solution.py:170
  127.6 0.9 fusion.8.own_ref
  128.5 6.2 %collective-permute-done.13.got_ref = bf16[512,512]{1,0:T(8,128)(2,1)S(1)} collective-permute-done((bf16[512,512]{1,0:T(8,128)(2,1)S(1)}, bf16[512,512]{1,0:T(8,128)(2,1)S(1)}, u32[]{:S(2)}, u32[]{:S(2)}) %collective-permute-start.13) | collective-permute-done | bytes 524320 | tf_op jit(solution)/shard_map/ppermute | solution.py:170
  134.7 2.7 %attend.2 = (bf16[512,256]{1,0:T(8,128)(2,1)S(1)}, bf16[512,128]{1,0:T(8,128)(2,1)S(1)}, bf16[512,128]{1,0:T(8,128)(2,1)S(1)}) custom-call(s32[1]{0:T(128)S(6)} %copy.31.limit_ref, f32[512,512]{1,0:T(8,128)S(1)} %fusion.2.own_ref, bf16[512,512]{1,0:T(8,128)(2,1)S(1)} %collective-permute-done.13.got_ref, f32[2,128]{1,0:T(2,128)S(1)} %copy-done.7, ...), custom_call_target="tpu_custom_call" | custom-call | tf_op jit(solution)/shard_map/attend/pallas_call | solution.py:166
  137.5 2.9 %collective-permute-done.12.got_ref = bf16[256,512]{1,0:T(8,128)(2,1)S(1)} collective-permute-done((bf16[256,512]{1,0:T(8,128)(2,1)S(1)}, bf16[256,512]{1,0:T(8,128)(2,1)S(1)}, u32[]{:S(2)}, u32[]{:S(2)}) %collective-permute-start.12) | collective-permute-done | bytes 262176 | tf_op jit(solution)/shard_map/ppermute | solution.py:170
  140.3 2.3 %attend.3 = (bf16[768,256]{1,0:T(8,128)(2,1)}, bf16[768,128]{1,0:T(8,128)(2,1)}, bf16[768,128]{1,0:T(8,128)(2,1)}) custom-call(s32[1]{0:T(128)S(6)} %copy.31.limit_ref, f32[256,512]{1,0:T(8,128)S(1)} %fusion.8.own_ref, bf16[256,512]{1,0:T(8,128)(2,1)S(1)} %collective-permute-done.12.got_ref, f32[2,128]{1,0:T(2,128)S(1)} %copy-done.7, ...), custom_call_target="tpu_custom_call" | custom-call | tf_op jit(solution)/shard_map/attend/pallas_call | solution.py:166
  (35 shorter events, 0.4 us)
Async XLA Ops:
  6.5 106.9 %copy-start = (f32[8,128]{1,0:T(8,128)S(1)}, f32[8,128]{1,0:T(8,128)}, u32[]{:S(2)}) copy-start(f32[8,128]{1,0:T(8,128)} %param.18) | copy-start | bytes 12292
  6.5 31.1 %copy-start.8 = (f32[160,1,3,128]{3,1,2,0:T(1,128)S(1)}, f32[160,1,3,128]{3,1,2,0:T(1,128)}, u32[]{:S(2)}) copy-start(f32[160,1,3,128]{3,1,2,0:T(1,128)} %param.13) | copy-start | bytes 737284
  6.5 76.9 %all-gather.2.cloned.1.call-start = ((), (), s32[]{:S(2)}) async-start(), calls=%async_computation.1 | async-start | bytes 4423680 | tf_op jit(solution)/shard_map/all_gather | solution.py:206
  10.3 39.0 %all-to-all-start = ((f32[512,1,128]{2,1,0:T(1,128)}), f32[512,1,128]{2,1,0:T(1,128)S(1)}, u32[]{:S(2)}, u32[]{:S(2)}) async-start(f32[512,1,128]{2,1,0:T(1,128)} %broadcast_in_dim.9), calls=%async_computation | async-start | bytes 524288 | tf_op jit(solution)/shard_map/all_to_all | solution.py:178
  50.9 2.9 %collective-permute-start = (bf16[160,384]{1,0:T(8,128)(2,1)S(1)}, bf16[160,384]{1,0:T(8,128)(2,1)S(1)}, u32[]{:S(2)}, u32[]{:S(2)}) collective-permute-start(bf16[160,384]{1,0:T(8,128)(2,1)S(1)} %fusion.15), channel_id=1, source_target_pairs={{0,0},{1,112},{16,16},{17,32},{32,17},{33,33},{48,65},{49,49},{64,... | collective-permute-start | bytes 368648 | tf_op jit(solution)/shard_map/ppermute | solution.py:189
  51.5 6.0 %collective-permute-start.1 = (bf16[160,384]{1,0:T(8,128)(2,1)S(1)}, bf16[160,384]{1,0:T(8,128)(2,1)S(1)}, u32[]{:S(2)}, u32[]{:S(2)}) collective-permute-start(bf16[160,384]{1,0:T(8,128)(2,1)S(1)} %fusion.15), channel_id=1, source_target_pairs={{0,256},{1,368},{16,272},{17,288},{32,273},{33,289},{48,321},{49,3... | collective-permute-start | bytes 368648 | tf_op jit(solution)/shard_map/ppermute | solution.py:189
  57.6 7.6 %collective-permute-start.2 = (bf16[2,160,384]{2,1,0:T(8,128)(2,1)S(1)}, bf16[2,160,384]{2,1,0:T(8,128)(2,1)S(1)}, u32[]{:S(2)}, u32[]{:S(2)}) collective-permute-start(bf16[2,160,384]{2,1,0:T(8,128)(2,1)S(1)} %get-tuple-element.46), channel_id=1, source_target_pairs={{0,128},{128,0},{1,129},{129,1},{2,130},{130,2},{3,131},{131,3},{4... | collective-permute-start | bytes 737288 | tf_op jit(solution)/shard_map/ppermute | solution.py:170
  65.2 18.2 %collective-permute-start.4 = (bf16[2,2,160,384]{3,2,1,0:T(8,128)(2,1)S(1)}, bf16[2,2,160,384]{3,2,1,0:T(8,128)(2,1)S(1)}, u32[]{:S(2)}, u32[]{:S(2)}) collective-permute-start(bf16[2,2,160,384]{3,2,1,0:T(8,128)(2,1)S(1)} %pad_maximum_fusion.refs_0_), channel_id=1, source_target_pairs={{0,16},{16,32},{32,48},{48,64},{64,80},{80,96},{96,112},{112,0},{1... | collective-permute-start | bytes 1474568 | tf_op jit(solution)/shard_map/ppermute | solution.py:194
  72.5 16.3 %collective-permute-start.3 = (bf16[2,2,160,384]{3,2,1,0:T(8,128)(2,1)S(1)}, bf16[2,2,160,384]{3,2,1,0:T(8,128)(2,1)S(1)}, u32[]{:S(2)}, u32[]{:S(2)}) collective-permute-start(bf16[2,2,160,384]{3,2,1,0:T(8,128)(2,1)S(1)} %pad_maximum_fusion.refs_0_), channel_id=1, source_target_pairs={{0,32},{16,48},{32,64},{48,80},{64,96},{80,112},{96,0},{112,16},{1... | collective-permute-start | bytes 1474568 | tf_op jit(solution)/shard_map/ppermute | solution.py:194
  83.5 5.3 %collective-permute-start.5 = (bf16[2,2,160,384]{3,2,1,0:T(8,128)(2,1)S(1)}, bf16[2,2,160,384]{3,2,1,0:T(8,128)(2,1)S(1)}, u32[]{:S(2)}, u32[]{:S(2)}) collective-permute-start(bf16[2,2,160,384]{3,2,1,0:T(8,128)(2,1)S(1)} %collective-permute-done.4.refs_1_), channel_id=1, source_target_pairs={{0,128},{128,0},{1,129},{129,1},{2,130},{130,2},{3,131},{131,3},{4... | collective-permute-start | bytes 1474568 | tf_op jit(solution)/shard_map/ppermute | solution.py:170
  85.4 2.1 %copy-start.1 = (bf16[2560,768]{1,0:T(8,128)(2,1)S(1)}, bf16[2560,768]{1,0:T(8,128)(2,1)}, u32[]{:S(2)}) copy-start(bf16[2560,768]{1,0:T(8,128)(2,1)} %all-gather.2.cloned.1.call-done.features_ref) | copy-start | bytes 11796484
  88.7 19.5 %collective-permute-start.6 = (bf16[2,2,160,384]{3,2,1,0:T(8,128)(2,1)S(1)}, bf16[2,2,160,384]{3,2,1,0:T(8,128)(2,1)}, u32[]{:S(2)}, u32[]{:S(2)}) collective-permute-start(bf16[2,2,160,384]{3,2,1,0:T(8,128)(2,1)S(1)} %collective-permute-done.3.refs_2_), channel_id=1, source_target_pairs={{0,16},{16,32},{32,48},{48,64},{64,80},{80,96},{96,112},{112,0},{1... | collective-permute-start | bytes 1474568 | tf_op jit(solution)/shard_map/ppermute | solution.py:194
  92.9 9.9 %collective-permute-start.7 = (f32[1,768]{1,0:T(1,128)S(1)}, f32[1,768]{1,0:T(1,128)S(1)}, u32[]{:S(2)}, u32[]{:S(2)}) collective-permute-start(f32[1,768]{1,0:T(1,128)S(1)} %squares.1.square_ref), channel_id=1, source_target_pairs={{0,1},{1,0},{2,3},{3,2},{4,5},{5,4},{6,7},{7,6},{8,9},{9,8},{10,11... | collective-permute-start | bytes 9224 | tf_op jit(solution)/shard_map/ppermute | solution.py:170
  96.6 13.7 %collective-permute-start.10 = (bf16[2,160,384]{2,1,0:T(8,128)(2,1)}, bf16[2,160,384]{2,1,0:T(8,128)(2,1)S(1)}, u32[]{:S(2)}, u32[]{:S(2)}) collective-permute-start(bf16[2,160,384]{2,1,0:T(8,128)(2,1)} %slice_bitcast_fusion), channel_id=1, source_target_pairs={{0,32},{16,48},{32,64},{48,80},{64,96},{80,112},{96,0},{112,16},{1... | collective-permute-start | bytes 737288 | tf_op jit(solution)/shard_map/ppermute | solution.py:194
  99.7 14.6 %collective-permute-start.8 = (bf16[2,2,160,384]{3,2,1,0:T(8,128)(2,1)S(1)}, bf16[2,2,160,384]{3,2,1,0:T(8,128)(2,1)}, u32[]{:S(2)}, u32[]{:S(2)}) collective-permute-start(bf16[2,2,160,384]{3,2,1,0:T(8,128)(2,1)S(1)} %collective-permute-done.3.refs_2_), channel_id=1, source_target_pairs={{0,128},{128,0},{1,129},{129,1},{2,130},{130,2},{3,131},{131,3},{4... | collective-permute-start | bytes 1474568 | tf_op jit(solution)/shard_map/ppermute | solution.py:170
  102.8 2.1 %copy-start.2 = (bf16[2560,768]{1,0:T(8,128)(2,1)S(1)}, bf16[2560,768]{1,0:T(8,128)(2,1)}, u32[]{:S(2)}) copy-start(bf16[2560,768]{1,0:T(8,128)(2,1)} %all-gather.2.cloned.1.call-done.features_ref) | copy-start | bytes 11796484
  106.4 1.9 %copy-start.3 = (bf16[2560,768]{1,0:T(8,128)(2,1)}, bf16[2560,768]{1,0:T(8,128)(2,1)S(1)}, u32[]{:S(2)}) copy-start(bf16[2560,768]{1,0:T(8,128)(2,1)S(1)} %normalise.1) | copy-start | bytes 11796484
  108.3 6.3 %collective-permute-start.9 = (bf16[2,2,160,384]{3,2,1,0:T(8,128)(2,1)}, bf16[2,2,160,384]{3,2,1,0:T(8,128)(2,1)S(1)}, u32[]{:S(2)}, u32[]{:S(2)}) collective-permute-start(bf16[2,2,160,384]{3,2,1,0:T(8,128)(2,1)} %collective-permute-done.6.refs_3_), channel_id=1, source_target_pairs={{0,128},{128,0},{1,129},{129,1},{2,130},{130,2},{3,131},{131,3},{4... | collective-permute-start | bytes 1474568 | tf_op jit(solution)/shard_map/ppermute | solution.py:170
  110.2 4.3 %collective-permute-start.11 = (bf16[2,160,384]{2,1,0:T(8,128)(2,1)S(1)}, bf16[2,160,384]{2,1,0:T(8,128)(2,1)S(1)}, u32[]{:S(2)}, u32[]{:S(2)}) collective-permute-start(bf16[2,160,384]{2,1,0:T(8,128)(2,1)S(1)} %collective-permute-done.10.refs_7_), channel_id=1, source_target_pairs={{0,128},{128,0},{1,129},{129,1},{2,130},{130,2},{3,131},{131,3},{4... | collective-permute-start | bytes 737288 | tf_op jit(solution)/shard_map/ppermute | solution.py:170
  113.4 3.1 %copy-start.4 = (bf16[2560,768]{1,0:T(8,128)(2,1)S(1)}, bf16[2560,768]{1,0:T(8,128)(2,1)}, u32[]{:S(2)}) copy-start(bf16[2560,768]{1,0:T(8,128)(2,1)} %copy-done.3) | copy-start | bytes 11796484
  118.1 16.7 %collective-permute-start.13 = (bf16[512,512]{1,0:T(8,128)(2,1)S(1)}, bf16[512,512]{1,0:T(8,128)(2,1)S(1)}, u32[]{:S(2)}, u32[]{:S(2)}) collective-permute-start(bf16[512,512]{1,0:T(8,128)(2,1)S(1)} %fusion.4), channel_id=1, source_target_pairs={{0,1},{1,0},{2,3},{3,2},{4,5},{5,4},{6,7},{7,6},{8,9},{9,8},{10,11... | collective-permute-start | bytes 1572872 | tf_op jit(solution)/shard_map/ppermute | solution.py:170
  123.6 11.1 %copy-start.5 = (f32[768,128]{1,0:T(8,128)S(1)}, f32[768,128]{1,0:T(8,128)}, u32[]{:S(2)}) copy-start(f32[768,128]{1,0:T(8,128)} %constant.62.clone.cos_ref) | copy-start | bytes 1179652
  123.7 11.1 %copy-start.6 = (f32[768,128]{1,0:T(8,128)S(1)}, f32[768,128]{1,0:T(8,128)}, u32[]{:S(2)}) copy-start(f32[768,128]{1,0:T(8,128)} %constant.63.clone.sin_ref) | copy-start | bytes 1179652
  123.7 11.1 %copy-start.7 = (f32[2,128]{1,0:T(2,128)S(1)}, f32[2,128]{1,0:T(2,128)}, u32[]{:S(2)}) copy-start(f32[2,128]{1,0:T(2,128)} %query_gain_ref.3) | copy-start | bytes 3076
  123.7 16.6 %collective-permute-start.12 = (bf16[256,512]{1,0:T(8,128)(2,1)S(1)}, bf16[256,512]{1,0:T(8,128)(2,1)S(1)}, u32[]{:S(2)}, u32[]{:S(2)}) collective-permute-start(bf16[256,512]{1,0:T(8,128)(2,1)S(1)} %convolution_convert_fusion), channel_id=1, source_target_pairs={{0,1},{1,0},{2,3},{3,2},{4,5},{5,4},{6,7},{7,6},{8,9},{9,8},{10,11... | collective-permute-start | bytes 786440 | tf_op jit(solution)/shard_map/ppermute | solution.py:170
Sparse Core Ops, SparseCore 0:
  9.4 66.8 all-gather.1

commit v9 on v8

--- a/solution.py
+++ b/solution.py
@@ -224,17 +224,15 @@
     home = jnp.stack([home, swap(home, "core")])
     first, second = onward(home, 1), onward(home, 2)
     first, gathered = lax.optimization_barrier((first, gathered))
-    exchanged = [swap(first, "core")]
-
     square = squares(8, gathered)
-    second, square, exchanged[0] = lax.optimization_barrier((second, square, exchanged[0]))
     other_square = swap(square, "xh")
+    second, other_square = lax.optimization_barrier((second, other_square))
     place = (((((steps >> 1) & 1) ^ core) * 2 + ((steps >> 2) ^ xl)) * 2 + (steps & 1)).astype(jnp.int32)
     normed = normalise(float(width_all), 8, place, square, other_square, gain, gathered)
 
     third, last = onward(second, 1), onward(second[0], 2)
     third, normed = lax.optimization_barrier((third, normed))
-    exchanged += [swap(second, "core"), swap(third, "core")]
+    exchanged = [swap(block, "core") for block in (first, second, third)]
 
     up = 1 - 2 * core
     source = (y - up * jnp.where(steps < 5, steps, 4 - steps)) & 7

time: 150 us -> 152 us (1.013)
  waiting for transfers between devices: 35.9 us -> 38.8 us
  starting transfers between devices: 67.6 us -> 65.3 us
    ppermute x8, waiting for transfers between devices: 10.4 us -> 13.3 us  [swap(): return lax.ppermute(array, axis, [(0, 1), (1, 0)])]
    ppermute x8, starting transfers between devices: 26.6 us -> 24.1 us  [swap(): return lax.ppermute(array, axis, [(0, 1), (1, 0)])]
  transfers between devices with their start and end apart: 16 -> 16, of which waited for: 8 -> 9; matrix products, arithmetic and copies ran while one was open for 10% -> 10% of each run, Pallas kernels for 3% -> 3%
where the time goes in v9:
time: 152 us; the launch traced here: 150 us
  starting transfers between devices  65.3 us (43%)
  waiting for transfers between devices  38.8 us (26%)
  between operations  15.3 us (10%)
  local copies, waits for them, and re-layouts  10.7 us (7%)
  Pallas kernels  8.72 us (6%)
  other arithmetic  6.54 us (4%)
  matrix products  4.79 us (3%)
    ppermute x8, starting transfers between devices, swap(): return lax.ppermute(array, axis, [(0, 1), (1, 0)])  24.1 us
    all_to_all x1, starting transfers between devices, global_sum(): return jnp.sum(lax.all_to_all(spread, AXES, 0, 0, tiled=True)[:, 0])  22.2 us
    ppermute x4, starting transfers between devices, onward(): return lax.ppermute(block, ('core', 'y'), pairs)  16.2 us
    ppermute x8, waiting for transfers between devices, swap(): return lax.ppermute(array, axis, [(0, 1), (1, 0)])  13.3 us
    all_to_all x1, waiting for transfers between devices, global_sum(): return jnp.sum(lax.all_to_all(spread, AXES, 0, 0, tiled=True)[:, 0])  10.8 us
    ppermute x4, waiting for transfers between devices, onward(): return lax.ppermute(block, ('core', 'y'), pairs)  10.1 us
    unnamed x21, local copies, waits for them, and re-layouts  7.14 us
    pallas_call x2, Pallas kernels, attend(): return call(limit, own, got, query_gain, key_gain, *tables, *before)  5.08 us
  transfers between devices with their start and end apart: 16, of which 9 were waited for; matrix products, arithmetic and copies ran while one was open for 10% of the time, Pallas kernels for 3%

profile of v9, /device:TPU:1, one launch (start us, length us, event | category | flops | bytes accessed | tf_op | source)
XLA Modules:
  0.0 150.2 jit_solution(5328125485346385645)
XLA Ops:
  6.5 0.7 all-gather.2.cloned.1.call-update
  7.3 1.6 %multiply_reduce_fusion = f32[]{:T(128)} fusion(bf16[160,1,3,128]{3,0,2,1:T(8,128)(2,1)} %param.14), kind=kLoop, calls=%fused_computation.22 | loop fusion | flops 184319 | bytes 122884 | tf_op jit(solution)/shard_map/reduce_sum | solution.py:209
  8.9 1.4 broadcast_in_dim.9
  10.3 22.2 %all-to-all-start = ((f32[512,1,128]{2,1,0:T(1,128)}), f32[512,1,128]{2,1,0:T(1,128)S(1)}, u32[]{:S(2)}, u32[]{:S(2)}) async-start(f32[512,1,128]{2,1,0:T(1,128)} %broadcast_in_dim.9), calls=%async_computation | async-start | bytes 524288 | tf_op jit(solution)/shard_map/all_to_all | solution.py:178
  32.5 1.0 copy.18
  33.5 0.8 reshape.96
  34.4 1.6 %reduce.4 = f32[160,3,128]{2,1,0:T(4,128)S(1)} reduce(f32[160,1,3,128]{3,1,2,0:T(1,128)} %param.16, f32[]{:T(128)} %constant.70), dimensions={1}, to_apply=%param.16.reduce_sub_computation | reduce | bytes 491524 | tf_op args[5]
  36.0 1.6 %reduce.3 = f32[160,3,128]{2,1,0:T(4,128)S(1)} reduce(f32[160,1,3,128]{3,1,2,0:T(1,128)} %param.15, f32[]{:T(128)} %constant.70), dimensions={1}, to_apply=%param.15.reduce_sub_computation | reduce | bytes 491524 | tf_op args[4]
  37.7 0.7 reduce.2
  38.5 10.8 %all-to-all-done = f32[512,1,128]{2,1,0:T(1,128)S(1)} async-done(((f32[512,1,128]{2,1,0:T(1,128)}), f32[512,1,128]{2,1,0:T(1,128)S(1)}, u32[]{:S(2)}, u32[]{:S(2)}) %all-to-all-start) | async-done | bytes 262176 | tf_op jit(solution)/shard_map/all_to_all | solution.py:178
  49.3 0.7 slice_reduce_fusion
  50.7 0.2 fusion.15
  50.9 0.7 collective-permute-start
  51.5 2.2 %collective-permute-start.1 = (bf16[160,384]{1,0:T(8,128)(2,1)S(1)}, bf16[160,384]{1,0:T(8,128)(2,1)S(1)}, u32[]{:S(2)}, u32[]{:S(2)}) collective-permute-start(bf16[160,384]{1,0:T(8,128)(2,1)S(1)} %fusion.15), channel_id=1, source_target_pairs={{0,256},{1,368},{16,272},{17,288},{32,273},{33,289},{48,321},{49,3... | collective-permute-start | bytes 368648 | tf_op jit(solution)/shard_map/ppermute | solution.py:189
  53.8 3.8 %collective-permute-done.1 = bf16[160,384]{1,0:T(8,128)(2,1)S(1)} collective-permute-done((bf16[160,384]{1,0:T(8,128)(2,1)S(1)}, bf16[160,384]{1,0:T(8,128)(2,1)S(1)}, u32[]{:S(2)}, u32[]{:S(2)}) %collective-permute-start.1) | collective-permute-done | bytes 122912 | tf_op jit(solution)/shard_map/ppermute | solution.py:189
  57.6 6.5 %collective-permute-start.2 = (bf16[2,160,384]{2,1,0:T(8,128)(2,1)S(1)}, bf16[2,160,384]{2,1,0:T(8,128)(2,1)S(1)}, u32[]{:S(2)}, u32[]{:S(2)}) collective-permute-start(bf16[2,160,384]{2,1,0:T(8,128)(2,1)S(1)} %get-tuple-element.44), channel_id=1, source_target_pairs={{0,128},{128,0},{1,129},{129,1},{2,130},{130,2},{3,131},{131,3},{4... | collective-permute-start | bytes 737288 | tf_op jit(solution)/shard_map/ppermute | solution.py:170
  64.1 1.1 collective-permute-done.2
  65.2 7.2 %collective-permute-start.4 = (bf16[2,2,160,384]{3,2,1,0:T(8,128)(2,1)S(1)}, bf16[2,2,160,384]{3,2,1,0:T(8,128)(2,1)S(1)}, u32[]{:S(2)}, u32[]{:S(2)}) collective-permute-start(bf16[2,2,160,384]{3,2,1,0:T(8,128)(2,1)S(1)} %pad_maximum_fusion.refs_0_), channel_id=1, source_target_pairs={{0,16},{16,32},{32,48},{48,64},{64,80},{80,96},{96,112},{112,0},{1... | collective-permute-start | bytes 1474568 | tf_op jit(solution)/shard_map/ppermute | solution.py:194
  72.5 1.9 %collective-permute-start.3 = (bf16[2,2,160,384]{3,2,1,0:T(8,128)(2,1)S(1)}, bf16[2,2,160,384]{3,2,1,0:T(8,128)(2,1)S(1)}, u32[]{:S(2)}, u32[]{:S(2)}) collective-permute-start(bf16[2,2,160,384]{3,2,1,0:T(8,128)(2,1)S(1)} %pad_maximum_fusion.refs_0_), channel_id=1, source_target_pairs={{0,32},{16,48},{32,64},{48,80},{64,96},{80,112},{96,0},{112,16},{1... | collective-permute-start | bytes 1474568 | tf_op jit(solution)/shard_map/ppermute | solution.py:194
  74.4 9.1 %collective-permute-done.4.refs_1_ = bf16[2,2,160,384]{3,2,1,0:T(8,128)(2,1)S(1)} collective-permute-done((bf16[2,2,160,384]{3,2,1,0:T(8,128)(2,1)S(1)}, bf16[2,2,160,384]{3,2,1,0:T(8,128)(2,1)S(1)}, u32[]{:S(2)}, u32[]{:S(2)}) %collective-permute-start.4) | collective-permute-done | bytes 491552 | tf_op jit(solution)/shard_map/ppermute | solution.py:194
  83.5 2.1 %copy-done.1 = bf16[2560,768]{1,0:T(8,128)(2,1)S(1)} copy-done((bf16[2560,768]{1,0:T(8,128)(2,1)S(1)}, bf16[2560,768]{1,0:T(8,128)(2,1)}, u32[]{:S(2)}) %copy-start.1) | copy-done | bytes 3932184
  85.6 0.2 squares.1.square_ref
  85.8 1.9 %collective-permute-start.5 = (f32[1,768]{1,0:T(1,128)S(1)}, f32[1,768]{1,0:T(1,128)S(1)}, u32[]{:S(2)}, u32[]{:S(2)}) collective-permute-start(f32[1,768]{1,0:T(1,128)S(1)} %squares.1.square_ref), channel_id=1, source_target_pairs={{0,1},{1,0},{2,3},{3,2},{4,5},{5,4},{6,7},{7,6},{8,9},{9,8},{10,11... | collective-permute-start | bytes 9224 | tf_op jit(solution)/shard_map/ppermute | solution.py:170
  87.7 1.0 collective-permute-done.3.refs_2_
  88.7 2.9 %collective-permute-done.5.other_ref = f32[1,768]{1,0:T(1,128)S(1)} collective-permute-done((f32[1,768]{1,0:T(1,128)S(1)}, f32[1,768]{1,0:T(1,128)S(1)}, u32[]{:S(2)}, u32[]{:S(2)}) %collective-permute-start.5) | collective-permute-done | bytes 3104 | tf_op jit(solution)/shard_map/ppermute | solution.py:170
  91.6 5.2 %collective-permute-start.6 = (bf16[2,2,160,384]{3,2,1,0:T(8,128)(2,1)S(1)}, bf16[2,2,160,384]{3,2,1,0:T(8,128)(2,1)S(1)}, u32[]{:S(2)}, u32[]{:S(2)}) collective-permute-start(bf16[2,2,160,384]{3,2,1,0:T(8,128)(2,1)S(1)} %collective-permute-done.3.refs_2_), channel_id=1, source_target_pairs={{0,16},{16,32},{32,48},{48,64},{64,80},{80,96},{96,112},{112,0},{1... | collective-permute-start | bytes 1474568 | tf_op jit(solution)/shard_map/ppermute | solution.py:194
  96.8 0.7 slice_bitcast_fusion
  97.5 1.9 %collective-permute-start.10 = (bf16[2,160,384]{2,1,0:T(8,128)(2,1)}, bf16[2,160,384]{2,1,0:T(8,128)(2,1)S(1)}, u32[]{:S(2)}, u32[]{:S(2)}) collective-permute-start(bf16[2,160,384]{2,1,0:T(8,128)(2,1)} %slice_bitcast_fusion), channel_id=1, source_target_pairs={{0,32},{16,48},{32,64},{48,80},{64,96},{80,112},{96,0},{112,16},{1... | collective-permute-start | bytes 737288 | tf_op jit(solution)/shard_map/ppermute | solution.py:194
  99.5 0.4 copy.19.gain_ref
  99.9 1.9 %collective-permute-start.7 = (bf16[2,2,160,384]{3,2,1,0:T(8,128)(2,1)S(1)}, bf16[2,2,160,384]{3,2,1,0:T(8,128)(2,1)}, u32[]{:S(2)}, u32[]{:S(2)}) collective-permute-start(bf16[2,2,160,384]{3,2,1,0:T(8,128)(2,1)S(1)} %collective-permute-done.4.refs_1_), channel_id=1, source_target_pairs={{0,128},{128,0},{1,129},{129,1},{2,130},{130,2},{3,131},{131,3},{4... | collective-permute-start | bytes 1474568 | tf_op jit(solution)/shard_map/ppermute | solution.py:170
  101.8 2.4 %collective-permute-start.8 = (bf16[2,2,160,384]{3,2,1,0:T(8,128)(2,1)S(1)}, bf16[2,2,160,384]{3,2,1,0:T(8,128)(2,1)}, u32[]{:S(2)}, u32[]{:S(2)}) collective-permute-start(bf16[2,2,160,384]{3,2,1,0:T(8,128)(2,1)S(1)} %collective-permute-done.3.refs_2_), channel_id=1, source_target_pairs={{0,128},{128,0},{1,129},{129,1},{2,130},{130,2},{3,131},{131,3},{4... | collective-permute-start | bytes 1474568 | tf_op jit(solution)/shard_map/ppermute | solution.py:170
  104.3 2.1 %copy-done.2 = bf16[2560,768]{1,0:T(8,128)(2,1)S(1)} copy-done((bf16[2560,768]{1,0:T(8,128)(2,1)S(1)}, bf16[2560,768]{1,0:T(8,128)(2,1)}, u32[]{:S(2)}) %copy-start.2) | copy-done | bytes 3932184
  106.4 1.5 normalise.1
  107.8 1.9 %copy-done.3 = bf16[2560,768]{1,0:T(8,128)(2,1)} copy-done((bf16[2560,768]{1,0:T(8,128)(2,1)}, bf16[2560,768]{1,0:T(8,128)(2,1)S(1)}, u32[]{:S(2)}) %copy-start.3) | copy-done | bytes 3932184
  109.7 1.9 %collective-permute-start.9 = (bf16[2,2,160,384]{3,2,1,0:T(8,128)(2,1)S(1)}, bf16[2,2,160,384]{3,2,1,0:T(8,128)(2,1)S(1)}, u32[]{:S(2)}, u32[]{:S(2)}) collective-permute-start(bf16[2,2,160,384]{3,2,1,0:T(8,128)(2,1)S(1)} %collective-permute-done.6.refs_3_), channel_id=1, source_target_pairs={{0,128},{128,0},{1,129},{129,1},{2,130},{130,2},{3,131},{131,3},{4... | collective-permute-start | bytes 1474568 | tf_op jit(solution)/shard_map/ppermute | solution.py:170
  111.7 2.4 %collective-permute-start.11 = (bf16[2,160,384]{2,1,0:T(8,128)(2,1)S(1)}, bf16[2,160,384]{2,1,0:T(8,128)(2,1)S(1)}, u32[]{:S(2)}, u32[]{:S(2)}) collective-permute-start(bf16[2,160,384]{2,1,0:T(8,128)(2,1)S(1)} %collective-permute-done.10.refs_7_), channel_id=1, source_target_pairs={{0,128},{128,0},{1,129},{129,1},{2,130},{130,2},{3,131},{131,3},{4... | collective-permute-start | bytes 737288 | tf_op jit(solution)/shard_map/ppermute | solution.py:170
  115.0 0.2 collective-permute-done.11.refs_8_
  115.2 2.0 %assemble.1 = (bf16[2560,512]{1,0:T(8,128)(2,1)S(1)}, bf16[2560,512]{1,0:T(8,128)(2,1)S(1)}) custom-call(s32[3,8]{1,0:T(4,128)S(1)} %pad_add_fusion.place_ref, bf16[2,2,160,384]{3,2,1,0:T(8,128)(2,1)S(1)} %pad_maximum_fusion.refs_0_, bf16[2,2,160,384]{3,2,1,0:T(8,128)(2,1)S(1)} %collective-permute-done.4.refs_1_, ...), custom_call_target="tpu_custom_call" | custom-call | tf_op jit(solution)/shard_map/assemble/pallas_call | solution.py:85
  117.2 1.5 %fusion.4 = bf16[512,512]{1,0:T(8,128)(2,1)S(1)} fusion(bf16[2560,512]{1,0:T(8,128)(2,1)S(1)} %get-tuple-element.36, bf16[2560,768]{1,0:T(8,128)(2,1)S(1)} %copy-done.4), kind=kOutput, calls=%fused_computation.4 | convolution fusion | flops 1342439424 | bytes 5767168 | tf_op jit(solution)/shard_map/dot_general | solution.py:252
  118.7 3.1 %collective-permute-start.13 = (bf16[512,512]{1,0:T(8,128)(2,1)S(1)}, bf16[512,512]{1,0:T(8,128)(2,1)S(1)}, u32[]{:S(2)}, u32[]{:S(2)}) collective-permute-start(bf16[512,512]{1,0:T(8,128)(2,1)S(1)} %fusion.4), channel_id=1, source_target_pairs={{0,1},{1,0},{2,3},{3,2},{4,5},{5,4},{6,7},{7,6},{8,9},{9,8},{10,11... | collective-permute-start | bytes 1572872 | tf_op jit(solution)/shard_map/ppermute | solution.py:170
  121.9 1.5 %fusion.2.own_ref = f32[512,512]{1,0:T(8,128)S(1)} fusion(bf16[2560,512]{1,0:T(8,128)(2,1)S(1)} %get-tuple-element.35, bf16[2560,768]{1,0:T(8,128)(2,1)S(1)} %copy-done.4), kind=kOutput, calls=%fused_computation.2 | convolution fusion | flops 1342177280 | bytes 6291456 | tf_op jit(solution)/shard_map/dot_general | solution.py:252
  123.4 0.9 convolution_convert_fusion
  124.3 4.0 %collective-permute-start.12 = (bf16[256,512]{1,0:T(8,128)(2,1)S(1)}, bf16[256,512]{1,0:T(8,128)(2,1)S(1)}, u32[]{:S(2)}, u32[]{:S(2)}) collective-permute-start(bf16[256,512]{1,0:T(8,128)(2,1)S(1)} %convolution_convert_fusion), channel_id=1, source_target_pairs={{0,1},{1,0},{2,3},{3,2},{4,5},{5,4},{6,7},{7,6},{8,9},{9,8},{10,11... | collective-permute-start | bytes 786440 | tf_op jit(solution)/shard_map/ppermute | solution.py:170
  128.3 0.9 fusion.8.own_ref
  129.1 6.2 %collective-permute-done.13.got_ref = bf16[512,512]{1,0:T(8,128)(2,1)S(1)} collective-permute-done((bf16[512,512]{1,0:T(8,128)(2,1)S(1)}, bf16[512,512]{1,0:T(8,128)(2,1)S(1)}, u32[]{:S(2)}, u32[]{:S(2)}) %collective-permute-start.13) | collective-permute-done | bytes 524320 | tf_op jit(solution)/shard_map/ppermute | solution.py:170
  135.4 2.7 %attend.2 = (bf16[512,256]{1,0:T(8,128)(2,1)S(1)}, bf16[512,128]{1,0:T(8,128)(2,1)S(1)}, bf16[512,128]{1,0:T(8,128)(2,1)S(1)}) custom-call(s32[1]{0:T(128)S(6)} %copy.31.limit_ref, f32[512,512]{1,0:T(8,128)S(1)} %fusion.2.own_ref, bf16[512,512]{1,0:T(8,128)(2,1)S(1)} %collective-permute-done.13.got_ref, f32[2,128]{1,0:T(2,128)S(1)} %copy-done.7, ...), custom_call_target="tpu_custom_call" | custom-call | tf_op jit(solution)/shard_map/attend/pallas_call | solution.py:166
  138.1 2.9 %collective-permute-done.12.got_ref = bf16[256,512]{1,0:T(8,128)(2,1)S(1)} collective-permute-done((bf16[256,512]{1,0:T(8,128)(2,1)S(1)}, bf16[256,512]{1,0:T(8,128)(2,1)S(1)}, u32[]{:S(2)}, u32[]{:S(2)}) %collective-permute-start.12) | collective-permute-done | bytes 262176 | tf_op jit(solution)/shard_map/ppermute | solution.py:170
  141.0 2.3 %attend.3 = (bf16[768,256]{1,0:T(8,128)(2,1)}, bf16[768,128]{1,0:T(8,128)(2,1)}, bf16[768,128]{1,0:T(8,128)(2,1)}) custom-call(s32[1]{0:T(128)S(6)} %copy.31.limit_ref, f32[256,512]{1,0:T(8,128)S(1)} %fusion.8.own_ref, bf16[256,512]{1,0:T(8,128)(2,1)S(1)} %collective-permute-done.12.got_ref, f32[2,128]{1,0:T(2,128)S(1)} %copy-done.7, ...), custom_call_target="tpu_custom_call" | custom-call | tf_op jit(solution)/shard_map/attend/pallas_call | solution.py:166
  (35 shorter events, 0.4 us)
Async XLA Ops:
  6.5 107.5 %copy-start = (f32[8,128]{1,0:T(8,128)S(1)}, f32[8,128]{1,0:T(8,128)}, u32[]{:S(2)}) copy-start(f32[8,128]{1,0:T(8,128)} %param.18) | copy-start | bytes 12292
  6.5 31.1 %copy-start.8 = (f32[160,1,3,128]{3,1,2,0:T(1,128)S(1)}, f32[160,1,3,128]{3,1,2,0:T(1,128)}, u32[]{:S(2)}) copy-start(f32[160,1,3,128]{3,1,2,0:T(1,128)} %param.13) | copy-start | bytes 737284
  6.5 76.9 %all-gather.2.cloned.1.call-start = ((), (), s32[]{:S(2)}) async-start(), calls=%async_computation.1 | async-start | bytes 4423680 | tf_op jit(solution)/shard_map/all_gather | solution.py:206
  10.3 39.0 %all-to-all-start = ((f32[512,1,128]{2,1,0:T(1,128)}), f32[512,1,128]{2,1,0:T(1,128)S(1)}, u32[]{:S(2)}, u32[]{:S(2)}) async-start(f32[512,1,128]{2,1,0:T(1,128)} %broadcast_in_dim.9), calls=%async_computation | async-start | bytes 524288 | tf_op jit(solution)/shard_map/all_to_all | solution.py:178
  50.9 2.9 %collective-permute-start = (bf16[160,384]{1,0:T(8,128)(2,1)S(1)}, bf16[160,384]{1,0:T(8,128)(2,1)S(1)}, u32[]{:S(2)}, u32[]{:S(2)}) collective-permute-start(bf16[160,384]{1,0:T(8,128)(2,1)S(1)} %fusion.15), channel_id=1, source_target_pairs={{0,0},{1,112},{16,16},{17,32},{32,17},{33,33},{48,65},{49,49},{64,... | collective-permute-start | bytes 368648 | tf_op jit(solution)/shard_map/ppermute | solution.py:189
  51.5 6.0 %collective-permute-start.1 = (bf16[160,384]{1,0:T(8,128)(2,1)S(1)}, bf16[160,384]{1,0:T(8,128)(2,1)S(1)}, u32[]{:S(2)}, u32[]{:S(2)}) collective-permute-start(bf16[160,384]{1,0:T(8,128)(2,1)S(1)} %fusion.15), channel_id=1, source_target_pairs={{0,256},{1,368},{16,272},{17,288},{32,273},{33,289},{48,321},{49,3... | collective-permute-start | bytes 368648 | tf_op jit(solution)/shard_map/ppermute | solution.py:189
  57.6 7.6 %collective-permute-start.2 = (bf16[2,160,384]{2,1,0:T(8,128)(2,1)S(1)}, bf16[2,160,384]{2,1,0:T(8,128)(2,1)S(1)}, u32[]{:S(2)}, u32[]{:S(2)}) collective-permute-start(bf16[2,160,384]{2,1,0:T(8,128)(2,1)S(1)} %get-tuple-element.44), channel_id=1, source_target_pairs={{0,128},{128,0},{1,129},{129,1},{2,130},{130,2},{3,131},{131,3},{4... | collective-permute-start | bytes 737288 | tf_op jit(solution)/shard_map/ppermute | solution.py:170
  65.2 18.2 %collective-permute-start.4 = (bf16[2,2,160,384]{3,2,1,0:T(8,128)(2,1)S(1)}, bf16[2,2,160,384]{3,2,1,0:T(8,128)(2,1)S(1)}, u32[]{:S(2)}, u32[]{:S(2)}) collective-permute-start(bf16[2,2,160,384]{3,2,1,0:T(8,128)(2,1)S(1)} %pad_maximum_fusion.refs_0_), channel_id=1, source_target_pairs={{0,16},{16,32},{32,48},{48,64},{64,80},{80,96},{96,112},{112,0},{1... | collective-permute-start | bytes 1474568 | tf_op jit(solution)/shard_map/ppermute | solution.py:194
  72.5 16.3 %collective-permute-start.3 = (bf16[2,2,160,384]{3,2,1,0:T(8,128)(2,1)S(1)}, bf16[2,2,160,384]{3,2,1,0:T(8,128)(2,1)S(1)}, u32[]{:S(2)}, u32[]{:S(2)}) collective-permute-start(bf16[2,2,160,384]{3,2,1,0:T(8,128)(2,1)S(1)} %pad_maximum_fusion.refs_0_), channel_id=1, source_target_pairs={{0,32},{16,48},{32,64},{48,80},{64,96},{80,112},{96,0},{112,16},{1... | collective-permute-start | bytes 1474568 | tf_op jit(solution)/shard_map/ppermute | solution.py:194
  83.5 2.1 %copy-start.1 = (bf16[2560,768]{1,0:T(8,128)(2,1)S(1)}, bf16[2560,768]{1,0:T(8,128)(2,1)}, u32[]{:S(2)}) copy-start(bf16[2560,768]{1,0:T(8,128)(2,1)} %all-gather.2.cloned.1.call-done.features_ref) | copy-start | bytes 11796484
  85.8 5.8 %collective-permute-start.5 = (f32[1,768]{1,0:T(1,128)S(1)}, f32[1,768]{1,0:T(1,128)S(1)}, u32[]{:S(2)}, u32[]{:S(2)}) collective-permute-start(f32[1,768]{1,0:T(1,128)S(1)} %squares.1.square_ref), channel_id=1, source_target_pairs={{0,1},{1,0},{2,3},{3,2},{4,5},{5,4},{6,7},{7,6},{8,9},{9,8},{10,11... | collective-permute-start | bytes 9224 | tf_op jit(solution)/shard_map/ppermute | solution.py:170
  91.6 18.1 %collective-permute-start.6 = (bf16[2,2,160,384]{3,2,1,0:T(8,128)(2,1)S(1)}, bf16[2,2,160,384]{3,2,1,0:T(8,128)(2,1)S(1)}, u32[]{:S(2)}, u32[]{:S(2)}) collective-permute-start(bf16[2,2,160,384]{3,2,1,0:T(8,128)(2,1)S(1)} %collective-permute-done.3.refs_2_), channel_id=1, source_target_pairs={{0,16},{16,32},{32,48},{48,64},{64,80},{80,96},{96,112},{112,0},{1... | collective-permute-start | bytes 1474568 | tf_op jit(solution)/shard_map/ppermute | solution.py:194
  97.5 14.1 %collective-permute-start.10 = (bf16[2,160,384]{2,1,0:T(8,128)(2,1)}, bf16[2,160,384]{2,1,0:T(8,128)(2,1)S(1)}, u32[]{:S(2)}, u32[]{:S(2)}) collective-permute-start(bf16[2,160,384]{2,1,0:T(8,128)(2,1)} %slice_bitcast_fusion), channel_id=1, source_target_pairs={{0,32},{16,48},{32,64},{48,80},{64,96},{80,112},{96,0},{112,16},{1... | collective-permute-start | bytes 737288 | tf_op jit(solution)/shard_map/ppermute | solution.py:194
  99.9 15.0 %collective-permute-start.7 = (bf16[2,2,160,384]{3,2,1,0:T(8,128)(2,1)S(1)}, bf16[2,2,160,384]{3,2,1,0:T(8,128)(2,1)}, u32[]{:S(2)}, u32[]{:S(2)}) collective-permute-start(bf16[2,2,160,384]{3,2,1,0:T(8,128)(2,1)S(1)} %collective-permute-done.4.refs_1_), channel_id=1, source_target_pairs={{0,128},{128,0},{1,129},{129,1},{2,130},{130,2},{3,131},{131,3},{4... | collective-permute-start | bytes 1474568 | tf_op jit(solution)/shard_map/ppermute | solution.py:170
  101.8 13.1 %collective-permute-start.8 = (bf16[2,2,160,384]{3,2,1,0:T(8,128)(2,1)S(1)}, bf16[2,2,160,384]{3,2,1,0:T(8,128)(2,1)}, u32[]{:S(2)}, u32[]{:S(2)}) collective-permute-start(bf16[2,2,160,384]{3,2,1,0:T(8,128)(2,1)S(1)} %collective-permute-done.3.refs_2_), channel_id=1, source_target_pairs={{0,128},{128,0},{1,129},{129,1},{2,130},{130,2},{3,131},{131,3},{4... | collective-permute-start | bytes 1474568 | tf_op jit(solution)/shard_map/ppermute | solution.py:170
  104.2 2.1 %copy-start.2 = (bf16[2560,768]{1,0:T(8,128)(2,1)S(1)}, bf16[2560,768]{1,0:T(8,128)(2,1)}, u32[]{:S(2)}) copy-start(bf16[2560,768]{1,0:T(8,128)(2,1)} %all-gather.2.cloned.1.call-done.features_ref) | copy-start | bytes 11796484
  107.8 1.9 %copy-start.3 = (bf16[2560,768]{1,0:T(8,128)(2,1)}, bf16[2560,768]{1,0:T(8,128)(2,1)S(1)}, u32[]{:S(2)}) copy-start(bf16[2560,768]{1,0:T(8,128)(2,1)S(1)} %normalise.1) | copy-start | bytes 11796484
  109.7 5.5 %collective-permute-start.9 = (bf16[2,2,160,384]{3,2,1,0:T(8,128)(2,1)S(1)}, bf16[2,2,160,384]{3,2,1,0:T(8,128)(2,1)S(1)}, u32[]{:S(2)}, u32[]{:S(2)}) collective-permute-start(bf16[2,2,160,384]{3,2,1,0:T(8,128)(2,1)S(1)} %collective-permute-done.6.refs_3_), channel_id=1, source_target_pairs={{0,128},{128,0},{1,129},{129,1},{2,130},{130,2},{3,131},{131,3},{4... | collective-permute-start | bytes 1474568 | tf_op jit(solution)/shard_map/ppermute | solution.py:170
  111.7 3.5 %collective-permute-start.11 = (bf16[2,160,384]{2,1,0:T(8,128)(2,1)S(1)}, bf16[2,160,384]{2,1,0:T(8,128)(2,1)S(1)}, u32[]{:S(2)}, u32[]{:S(2)}) collective-permute-start(bf16[2,160,384]{2,1,0:T(8,128)(2,1)S(1)} %collective-permute-done.10.refs_7_), channel_id=1, source_target_pairs={{0,128},{128,0},{1,129},{129,1},{2,130},{130,2},{3,131},{131,3},{4... | collective-permute-start | bytes 737288 | tf_op jit(solution)/shard_map/ppermute | solution.py:170
  114.1 3.1 %copy-start.4 = (bf16[2560,768]{1,0:T(8,128)(2,1)S(1)}, bf16[2560,768]{1,0:T(8,128)(2,1)}, u32[]{:S(2)}) copy-start(bf16[2560,768]{1,0:T(8,128)(2,1)} %copy-done.3) | copy-start | bytes 11796484
  118.7 16.7 %collective-permute-start.13 = (bf16[512,512]{1,0:T(8,128)(2,1)S(1)}, bf16[512,512]{1,0:T(8,128)(2,1)S(1)}, u32[]{:S(2)}, u32[]{:S(2)}) collective-permute-start(bf16[512,512]{1,0:T(8,128)(2,1)S(1)} %fusion.4), channel_id=1, source_target_pairs={{0,1},{1,0},{2,3},{3,2},{4,5},{5,4},{6,7},{7,6},{8,9},{9,8},{10,11... | collective-permute-start | bytes 1572872 | tf_op jit(solution)/shard_map/ppermute | solution.py:170
  124.3 11.1 %copy-start.5 = (f32[768,128]{1,0:T(8,128)S(1)}, f32[768,128]{1,0:T(8,128)}, u32[]{:S(2)}) copy-start(f32[768,128]{1,0:T(8,128)} %constant.62.clone.cos_ref) | copy-start | bytes 1179652
  124.3 11.1 %copy-start.6 = (f32[768,128]{1,0:T(8,128)S(1)}, f32[768,128]{1,0:T(8,128)}, u32[]{:S(2)}) copy-start(f32[768,128]{1,0:T(8,128)} %constant.63.clone.sin_ref) | copy-start | bytes 1179652
  124.3 11.1 %copy-start.7 = (f32[2,128]{1,0:T(2,128)S(1)}, f32[2,128]{1,0:T(2,128)}, u32[]{:S(2)}) copy-start(f32[2,128]{1,0:T(2,128)} %query_gain_ref.3) | copy-start | bytes 3076
  124.3 16.7 %collective-permute-start.12 = (bf16[256,512]{1,0:T(8,128)(2,1)S(1)}, bf16[256,512]{1,0:T(8,128)(2,1)S(1)}, u32[]{:S(2)}, u32[]{:S(2)}) collective-permute-start(bf16[256,512]{1,0:T(8,128)(2,1)S(1)} %convolution_convert_fusion), channel_id=1, source_target_pairs={{0,1},{1,0},{2,3},{3,2},{4,5},{5,4},{6,7},{7,6},{8,9},{9,8},{10,11... | collective-permute-start | bytes 786440 | tf_op jit(solution)/shard_map/ppermute | solution.py:170
Sparse Core Ops, SparseCore 0:
  9.4 66.8 all-gather.1

commit v10 on v8

--- a/solution.py
+++ b/solution.py
@@ -85,36 +85,59 @@
     return call(place, home, *rest)
 
 
-def squares_kernel(parts, features_ref, out_ref):
-    rows = features_ref.shape[0] // parts
-    total = None
-    for step in range(parts):
-        wide = features_ref[step * rows : (step + 1) * rows, :].astype(jnp.float32)
-        square = jnp.sum(wide * wide, axis=0, keepdims=True)
-        total = square if total is None else total + square
-    out_ref[...] = total
+def squares_kernel(features_ref, out_ref):
+    wide = features_ref[...].astype(jnp.float32)
+    square = jnp.sum(wide * wide, axis=0, keepdims=True)
+
+    @pl.when(pl.program_id(0) == 0)
+    def _():
+        out_ref[...] = square
+
+    @pl.when(pl.program_id(0) > 0)
+    def _():
+        out_ref[...] += square
 
 
 def squares(parts, features):
-    shape = jax.ShapeDtypeStruct((1, features.shape[1]), jnp.float32)
-    return local_call(functools.partial(squares_kernel, parts), "squares", shape, [VMEM], VMEM)(features)
-
-
-def normalise_kernel(width_all, parts, place_ref, square_ref, other_ref, gain_ref, features_ref, out_ref):
-    rows = features_ref.shape[0] // parts
+    rows, cols = features.shape[0] // parts, features.shape[1]
+    return pl.pallas_call(
+        squares_kernel,
+        grid=(parts,),
+        out_shape=jax.ShapeDtypeStruct((1, cols), jnp.float32),
+        in_specs=[pl.BlockSpec((rows, cols), lambda i: (i, 0))],
+        out_specs=pl.BlockSpec((1, cols), lambda i: (0, 0)),
+        compiler_params=pltpu.CompilerParams(vmem_limit_bytes=8 << 20),
+        name="squares",
+    )(features)
+
+
+def normalise_kernel(width_all, place_ref, square_ref, other_ref, gain_ref, features_ref, out_ref):
     scale = lax.rsqrt((square_ref[...] + other_ref[...]) / width_all + 1e-06)
-    for step in range(parts):
-        span = slice(step * rows, (step + 1) * rows)
-        row = pl.multiple_of(place_ref[step] * rows, 64)
-        scaled = features_ref[span, :].astype(jnp.float32) * scale * gain_ref[span, :]
-        out_ref[pl.ds(row, rows), :] = scaled.astype(out_ref.dtype)
+    scaled = features_ref[...].astype(jnp.float32) * scale * gain_ref[...]
+    out_ref[...] = scaled.astype(out_ref.dtype)
 
 
 def normalise(width_all, parts, place, square, other, gain, features):
-    shape = jax.ShapeDtypeStruct(features.shape, jnp.bfloat16)
-    kernel = functools.partial(normalise_kernel, width_all, parts)
-    call = local_call(kernel, "normalise", shape, [SMEM] + [VMEM] * 4, VMEM)
-    return call(place, square, other, gain, features)
+    rows, cols = features.shape[0] // parts, features.shape[1]
+    whole = pl.BlockSpec((1, cols), lambda i, place: (0, 0))
+    grid_spec = pltpu.PrefetchScalarGridSpec(
+        num_scalar_prefetch=1,
+        grid=(parts,),
+        in_specs=[
+            whole,
+            whole,
+            pl.BlockSpec((rows, 1), lambda i, place: (i, 0)),
+            pl.BlockSpec((rows, cols), lambda i, place: (i, 0)),
+        ],
+        out_specs=pl.BlockSpec((rows, cols), lambda i, place: (place[i], 0)),
+    )
+    return pl.pallas_call(
+        functools.partial(normalise_kernel, width_all),
+        grid_spec=grid_spec,
+        out_shape=jax.ShapeDtypeStruct(features.shape, jnp.bfloat16),
+        compiler_params=pltpu.CompilerParams(vmem_limit_bytes=8 << 20),
+        name="normalise",
+    )(place, square, other, gain, features)
 
 
 def attend_kernel(tile, first, limit_ref, own_ref, got_ref, query_gain_ref, key_gain_ref, cos_ref, sin_ref, *refs):

time: 150 us -> 150 us (level)
  no operation moved by 1% of the time
where the time goes in v10:
time: 150 us
  starting transfers between devices  67.4 us (45%)
  waiting for transfers between devices  35.7 us (24%)
  between operations  15.3 us (10%)
  local copies, waits for them, and re-layouts  10.7 us (7%)
  Pallas kernels  9.11 us (6%)
  other arithmetic  6.54 us (4%)
  matrix products  4.79 us (3%)
    ppermute x8, starting transfers between devices, swap(): return lax.ppermute(array, axis, [(0, 1), (1, 0)])  26.2 us
    all_to_all x1, starting transfers between devices, global_sum(): return jnp.sum(lax.all_to_all(spread, AXES, 0, 0, tiled=True)[:, 0])  22.2 us
    ppermute x4, starting transfers between devices, onward(): return lax.ppermute(block, ('core', 'y'), pairs)  16.2 us
    all_to_all x1, waiting for transfers between devices, global_sum(): return jnp.sum(lax.all_to_all(spread, AXES, 0, 0, tiled=True)[:, 0])  10.8 us
    ppermute x8, waiting for transfers between devices, swap(): return lax.ppermute(array, axis, [(0, 1), (1, 0)])  10.4 us
    ppermute x4, waiting for transfers between devices, onward(): return lax.ppermute(block, ('core', 'y'), pairs)  9.91 us
    unnamed x21, local copies, waits for them, and re-layouts  7.13 us
    pallas_call x2, Pallas kernels, attend(): return call(limit, own, got, query_gain, key_gain, *tables, *before)  5.08 us
  transfers between devices with their start and end apart: 16, of which 8 were waited for; matrix products, arithmetic and copies ran while one was open for 10% of the time, Pallas kernels for 3%

profile of v10, /device:TPU:1, one launch (start us, length us, event | category | flops | bytes accessed | tf_op | source)
XLA Modules:
  0.0 149.5 jit_solution(16651948372185736034)
XLA Ops:
  6.5 0.7 all-gather.2.cloned.1.call-update
  7.3 1.6 %multiply_reduce_fusion = f32[]{:T(128)} fusion(bf16[160,1,3,128]{3,0,2,1:T(8,128)(2,1)} %param.14), kind=kLoop, calls=%fused_computation.22 | loop fusion | flops 184319 | bytes 122884 | tf_op jit(solution)/shard_map/reduce_sum | solution.py:232
  8.9 1.4 broadcast_in_dim.9
  10.3 22.2 %all-to-all-start = ((f32[512,1,128]{2,1,0:T(1,128)}), f32[512,1,128]{2,1,0:T(1,128)S(1)}, u32[]{:S(2)}, u32[]{:S(2)}) async-start(f32[512,1,128]{2,1,0:T(1,128)} %broadcast_in_dim.9), calls=%async_computation | async-start | bytes 524288 | tf_op jit(solution)/shard_map/all_to_all | solution.py:201
  32.5 1.0 copy.18
  33.5 0.8 reshape.96
  34.3 0.1 reshape.97
  34.4 1.6 %reduce.4 = f32[160,3,128]{2,1,0:T(4,128)S(1)} reduce(f32[160,1,3,128]{3,1,2,0:T(1,128)} %param.16, f32[]{:T(128)} %constant.70), dimensions={1}, to_apply=%param.16.reduce_sub_computation | reduce | bytes 491524 | tf_op args[5]
  36.0 1.6 %reduce.3 = f32[160,3,128]{2,1,0:T(4,128)S(1)} reduce(f32[160,1,3,128]{3,1,2,0:T(1,128)} %param.15, f32[]{:T(128)} %constant.70), dimensions={1}, to_apply=%param.15.reduce_sub_computation | reduce | bytes 491524 | tf_op args[4]
  37.7 0.7 reduce.2
  38.5 10.8 %all-to-all-done = f32[512,1,128]{2,1,0:T(1,128)S(1)} async-done(((f32[512,1,128]{2,1,0:T(1,128)}), f32[512,1,128]{2,1,0:T(1,128)S(1)}, u32[]{:S(2)}, u32[]{:S(2)}) %all-to-all-start) | async-done | bytes 262176 | tf_op jit(solution)/shard_map/all_to_all | solution.py:201
  49.3 0.7 slice_reduce_fusion
  50.7 0.2 fusion.15
  50.9 0.7 collective-permute-start
  51.5 2.2 %collective-permute-start.1 = (bf16[160,384]{1,0:T(8,128)(2,1)S(1)}, bf16[160,384]{1,0:T(8,128)(2,1)S(1)}, u32[]{:S(2)}, u32[]{:S(2)}) collective-permute-start(bf16[160,384]{1,0:T(8,128)(2,1)S(1)} %fusion.15), channel_id=1, source_target_pairs={{0,256},{1,368},{16,272},{17,288},{32,273},{33,289},{48,321},{49,3... | collective-permute-start | bytes 368648 | tf_op jit(solution)/shard_map/ppermute | solution.py:212
  53.8 3.8 %collective-permute-done.1 = bf16[160,384]{1,0:T(8,128)(2,1)S(1)} collective-permute-done((bf16[160,384]{1,0:T(8,128)(2,1)S(1)}, bf16[160,384]{1,0:T(8,128)(2,1)S(1)}, u32[]{:S(2)}, u32[]{:S(2)}) %collective-permute-start.1) | collective-permute-done | bytes 122912 | tf_op jit(solution)/shard_map/ppermute | solution.py:212
  57.6 6.5 %collective-permute-start.2 = (bf16[2,160,384]{2,1,0:T(8,128)(2,1)S(1)}, bf16[2,160,384]{2,1,0:T(8,128)(2,1)S(1)}, u32[]{:S(2)}, u32[]{:S(2)}) collective-permute-start(bf16[2,160,384]{2,1,0:T(8,128)(2,1)S(1)} %get-tuple-element.46), channel_id=1, source_target_pairs={{0,128},{128,0},{1,129},{129,1},{2,130},{130,2},{3,131},{131,3},{4... | collective-permute-start | bytes 737288 | tf_op jit(solution)/shard_map/ppermute | solution.py:193
  64.1 1.1 collective-permute-done.2
  65.2 7.2 %collective-permute-start.4 = (bf16[2,2,160,384]{3,2,1,0:T(8,128)(2,1)S(1)}, bf16[2,2,160,384]{3,2,1,0:T(8,128)(2,1)S(1)}, u32[]{:S(2)}, u32[]{:S(2)}) collective-permute-start(bf16[2,2,160,384]{3,2,1,0:T(8,128)(2,1)S(1)} %pad_maximum_fusion.refs_0_), channel_id=1, source_target_pairs={{0,16},{16,32},{32,48},{48,64},{64,80},{80,96},{96,112},{112,0},{1... | collective-permute-start | bytes 1474568 | tf_op jit(solution)/shard_map/ppermute | solution.py:217
  72.5 1.9 %collective-permute-start.3 = (bf16[2,2,160,384]{3,2,1,0:T(8,128)(2,1)S(1)}, bf16[2,2,160,384]{3,2,1,0:T(8,128)(2,1)S(1)}, u32[]{:S(2)}, u32[]{:S(2)}) collective-permute-start(bf16[2,2,160,384]{3,2,1,0:T(8,128)(2,1)S(1)} %pad_maximum_fusion.refs_0_), channel_id=1, source_target_pairs={{0,32},{16,48},{32,64},{48,80},{64,96},{80,112},{96,0},{112,16},{1... | collective-permute-start | bytes 1474568 | tf_op jit(solution)/shard_map/ppermute | solution.py:217
  74.4 9.1 %collective-permute-done.4.refs_1_ = bf16[2,2,160,384]{3,2,1,0:T(8,128)(2,1)S(1)} collective-permute-done((bf16[2,2,160,384]{3,2,1,0:T(8,128)(2,1)S(1)}, bf16[2,2,160,384]{3,2,1,0:T(8,128)(2,1)S(1)}, u32[]{:S(2)}, u32[]{:S(2)}) %collective-permute-start.4) | collective-permute-done | bytes 491552 | tf_op jit(solution)/shard_map/ppermute | solution.py:217
  83.5 1.9 %collective-permute-start.5 = (bf16[2,2,160,384]{3,2,1,0:T(8,128)(2,1)S(1)}, bf16[2,2,160,384]{3,2,1,0:T(8,128)(2,1)S(1)}, u32[]{:S(2)}, u32[]{:S(2)}) collective-permute-start(bf16[2,2,160,384]{3,2,1,0:T(8,128)(2,1)S(1)} %collective-permute-done.4.refs_1_), channel_id=1, source_target_pairs={{0,128},{128,0},{1,129},{129,1},{2,130},{130,2},{3,131},{131,3},{4... | collective-permute-start | bytes 1474568 | tf_op jit(solution)/shard_map/ppermute | solution.py:193
  85.4 2.1 %copy-done.1 = bf16[2560,768]{1,0:T(8,128)(2,1)S(1)} copy-done((bf16[2560,768]{1,0:T(8,128)(2,1)S(1)}, bf16[2560,768]{1,0:T(8,128)(2,1)}, u32[]{:S(2)}) %copy-start.1) | copy-done | bytes 3932184
  87.5 0.4 squares.1.square_ref
  87.9 0.8 collective-permute-done.3.refs_2_
  88.7 4.4 %collective-permute-start.6 = (bf16[2,2,160,384]{3,2,1,0:T(8,128)(2,1)S(1)}, bf16[2,2,160,384]{3,2,1,0:T(8,128)(2,1)}, u32[]{:S(2)}, u32[]{:S(2)}) collective-permute-start(bf16[2,2,160,384]{3,2,1,0:T(8,128)(2,1)S(1)} %collective-permute-done.3.refs_2_), channel_id=1, source_target_pairs={{0,16},{16,32},{32,48},{48,64},{64,80},{80,96},{96,112},{112,0},{1... | collective-permute-start | bytes 1474568 | tf_op jit(solution)/shard_map/ppermute | solution.py:217
  93.1 2.7 %collective-permute-start.7 = (f32[1,768]{1,0:T(1,128)S(1)}, f32[1,768]{1,0:T(1,128)S(1)}, u32[]{:S(2)}, u32[]{:S(2)}) collective-permute-start(f32[1,768]{1,0:T(1,128)S(1)} %squares.1.square_ref), channel_id=1, source_target_pairs={{0,1},{1,0},{2,3},{3,2},{4,5},{5,4},{6,7},{7,6},{8,9},{9,8},{10,11... | collective-permute-start | bytes 9224 | tf_op jit(solution)/shard_map/ppermute | solution.py:193
  95.8 0.7 slice_bitcast_fusion
  96.6 2.7 %collective-permute-start.10 = (bf16[2,160,384]{2,1,0:T(8,128)(2,1)}, bf16[2,160,384]{2,1,0:T(8,128)(2,1)S(1)}, u32[]{:S(2)}, u32[]{:S(2)}) collective-permute-start(bf16[2,160,384]{2,1,0:T(8,128)(2,1)} %slice_bitcast_fusion), channel_id=1, source_target_pairs={{0,32},{16,48},{32,64},{48,80},{64,96},{80,112},{96,0},{112,16},{1... | collective-permute-start | bytes 737288 | tf_op jit(solution)/shard_map/ppermute | solution.py:217
  99.2 0.4 copy.19.gain_ref
  99.7 3.1 %collective-permute-start.8 = (bf16[2,2,160,384]{3,2,1,0:T(8,128)(2,1)S(1)}, bf16[2,2,160,384]{3,2,1,0:T(8,128)(2,1)}, u32[]{:S(2)}, u32[]{:S(2)}) collective-permute-start(bf16[2,2,160,384]{3,2,1,0:T(8,128)(2,1)S(1)} %collective-permute-done.3.refs_2_), channel_id=1, source_target_pairs={{0,128},{128,0},{1,129},{129,1},{2,130},{130,2},{3,131},{131,3},{4... | collective-permute-start | bytes 1474568 | tf_op jit(solution)/shard_map/ppermute | solution.py:193
  102.8 2.1 %copy-done.2 = bf16[2560,768]{1,0:T(8,128)(2,1)S(1)} copy-done((bf16[2560,768]{1,0:T(8,128)(2,1)S(1)}, bf16[2560,768]{1,0:T(8,128)(2,1)}, u32[]{:S(2)}) %copy-start.2) | copy-done | bytes 3932184
  104.9 1.6 %normalise.1 = bf16[2560,768]{1,0:T(8,128)(2,1)S(1)} custom-call(s32[8]{0:T(128)S(1)} %and_add_fusion.1.place_ref, f32[1,768]{1,0:T(1,128)S(1)} %squares.1.square_ref, f32[1,768]{1,0:T(1,128)S(1)} %collective-permute-done.7.other_ref, f32[2560,1]{1,0:T(8,128)S(1)} %copy.19.gain_ref, bf16[2560,768]{1,0:T(8,128)(2,1)S(1)} %copy-done.2), custom_call_target="tpu_custom_call" | custom-call | tf_op jit(solution)/shard_map/normalise/pallas_call | solution.py:134
  106.6 1.9 %copy-done.3 = bf16[2560,768]{1,0:T(8,128)(2,1)} copy-done((bf16[2560,768]{1,0:T(8,128)(2,1)}, bf16[2560,768]{1,0:T(8,128)(2,1)S(1)}, u32[]{:S(2)}) %copy-start.3) | copy-done | bytes 3932184
  108.5 1.9 %collective-permute-start.9 = (bf16[2,2,160,384]{3,2,1,0:T(8,128)(2,1)}, bf16[2,2,160,384]{3,2,1,0:T(8,128)(2,1)S(1)}, u32[]{:S(2)}, u32[]{:S(2)}) collective-permute-start(bf16[2,2,160,384]{3,2,1,0:T(8,128)(2,1)} %collective-permute-done.6.refs_3_), channel_id=1, source_target_pairs={{0,128},{128,0},{1,129},{129,1},{2,130},{130,2},{3,131},{131,3},{4... | collective-permute-start | bytes 1474568 | tf_op jit(solution)/shard_map/ppermute | solution.py:193
  110.4 3.0 %collective-permute-start.11 = (bf16[2,160,384]{2,1,0:T(8,128)(2,1)S(1)}, bf16[2,160,384]{2,1,0:T(8,128)(2,1)S(1)}, u32[]{:S(2)}, u32[]{:S(2)}) collective-permute-start(bf16[2,160,384]{2,1,0:T(8,128)(2,1)S(1)} %collective-permute-done.10.refs_7_), channel_id=1, source_target_pairs={{0,128},{128,0},{1,129},{129,1},{2,130},{130,2},{3,131},{131,3},{4... | collective-permute-start | bytes 737288 | tf_op jit(solution)/shard_map/ppermute | solution.py:193
  114.3 0.2 collective-permute-done.11.refs_8_
  114.5 2.0 %assemble.1 = (bf16[2560,512]{1,0:T(8,128)(2,1)S(1)}, bf16[2560,512]{1,0:T(8,128)(2,1)S(1)}) custom-call(s32[3,8]{1,0:T(4,128)S(1)} %pad_add_fusion.place_ref, bf16[2,2,160,384]{3,2,1,0:T(8,128)(2,1)S(1)} %pad_maximum_fusion.refs_0_, bf16[2,2,160,384]{3,2,1,0:T(8,128)(2,1)S(1)} %collective-permute-done.4.refs_1_, ...), custom_call_target="tpu_custom_call" | custom-call | tf_op jit(solution)/shard_map/assemble/pallas_call | solution.py:85
  116.5 1.5 %fusion.4 = bf16[512,512]{1,0:T(8,128)(2,1)S(1)} fusion(bf16[2560,512]{1,0:T(8,128)(2,1)S(1)} %get-tuple-element.38, bf16[2560,768]{1,0:T(8,128)(2,1)S(1)} %copy-done.4), kind=kOutput, calls=%fused_computation.4 | convolution fusion | flops 1342439424 | bytes 5767168 | tf_op jit(solution)/shard_map/dot_general | solution.py:277
  118.1 3.4 %collective-permute-start.13 = (bf16[512,512]{1,0:T(8,128)(2,1)S(1)}, bf16[512,512]{1,0:T(8,128)(2,1)S(1)}, u32[]{:S(2)}, u32[]{:S(2)}) collective-permute-start(bf16[512,512]{1,0:T(8,128)(2,1)S(1)} %fusion.4), channel_id=1, source_target_pairs={{0,1},{1,0},{2,3},{3,2},{4,5},{5,4},{6,7},{7,6},{8,9},{9,8},{10,11... | collective-permute-start | bytes 1572872 | tf_op jit(solution)/shard_map/ppermute | solution.py:193
  121.4 1.5 %fusion.2.own_ref = f32[512,512]{1,0:T(8,128)S(1)} fusion(bf16[2560,512]{1,0:T(8,128)(2,1)S(1)} %get-tuple-element.37, bf16[2560,768]{1,0:T(8,128)(2,1)S(1)} %copy-done.4), kind=kOutput, calls=%fused_computation.2 | convolution fusion | flops 1342177280 | bytes 6291456 | tf_op jit(solution)/shard_map/dot_general | solution.py:277
  123.0 0.9 convolution_convert_fusion
  123.9 3.7 %collective-permute-start.12 = (bf16[256,512]{1,0:T(8,128)(2,1)S(1)}, bf16[256,512]{1,0:T(8,128)(2,1)S(1)}, u32[]{:S(2)}, u32[]{:S(2)}) collective-permute-start(bf16[256,512]{1,0:T(8,128)(2,1)S(1)} %convolution_convert_fusion), channel_id=1, source_target_pairs={{0,1},{1,0},{2,3},{3,2},{4,5},{5,4},{6,7},{7,6},{8,9},{9,8},{10,11... | collective-permute-start | bytes 786440 | tf_op jit(solution)/shard_map/ppermute | solution.py:193
  127.6 0.9 fusion.8.own_ref
  128.5 6.2 %collective-permute-done.13.got_ref = bf16[512,512]{1,0:T(8,128)(2,1)S(1)} collective-permute-done((bf16[512,512]{1,0:T(8,128)(2,1)S(1)}, bf16[512,512]{1,0:T(8,128)(2,1)S(1)}, u32[]{:S(2)}, u32[]{:S(2)}) %collective-permute-start.13) | collective-permute-done | bytes 524320 | tf_op jit(solution)/shard_map/ppermute | solution.py:193
  134.7 2.7 %attend.2 = (bf16[512,256]{1,0:T(8,128)(2,1)S(1)}, bf16[512,128]{1,0:T(8,128)(2,1)S(1)}, bf16[512,128]{1,0:T(8,128)(2,1)S(1)}) custom-call(s32[1]{0:T(128)S(6)} %copy.31.limit_ref, f32[512,512]{1,0:T(8,128)S(1)} %fusion.2.own_ref, bf16[512,512]{1,0:T(8,128)(2,1)S(1)} %collective-permute-done.13.got_ref, f32[2,128]{1,0:T(2,128)S(1)} %copy-done.7, ...), custom_call_target="tpu_custom_call" | custom-call | tf_op jit(solution)/shard_map/attend/pallas_call | solution.py:189
  137.5 2.9 %collective-permute-done.12.got_ref = bf16[256,512]{1,0:T(8,128)(2,1)S(1)} collective-permute-done((bf16[256,512]{1,0:T(8,128)(2,1)S(1)}, bf16[256,512]{1,0:T(8,128)(2,1)S(1)}, u32[]{:S(2)}, u32[]{:S(2)}) %collective-permute-start.12) | collective-permute-done | bytes 262176 | tf_op jit(solution)/shard_map/ppermute | solution.py:193
  140.3 2.3 %attend.3 = (bf16[768,256]{1,0:T(8,128)(2,1)}, bf16[768,128]{1,0:T(8,128)(2,1)}, bf16[768,128]{1,0:T(8,128)(2,1)}) custom-call(s32[1]{0:T(128)S(6)} %copy.31.limit_ref, f32[256,512]{1,0:T(8,128)S(1)} %fusion.8.own_ref, bf16[256,512]{1,0:T(8,128)(2,1)S(1)} %collective-permute-done.12.got_ref, f32[2,128]{1,0:T(2,128)S(1)} %copy-done.7, ...), custom_call_target="tpu_custom_call" | custom-call | tf_op jit(solution)/shard_map/attend/pallas_call | solution.py:189
  (35 shorter events, 0.4 us)
Async XLA Ops:
  6.5 106.9 %copy-start = (f32[8,128]{1,0:T(8,128)S(1)}, f32[8,128]{1,0:T(8,128)}, u32[]{:S(2)}) copy-start(f32[8,128]{1,0:T(8,128)} %param.18) | copy-start | bytes 12292
  6.5 31.1 %copy-start.8 = (f32[160,1,3,128]{3,1,2,0:T(1,128)S(1)}, f32[160,1,3,128]{3,1,2,0:T(1,128)}, u32[]{:S(2)}) copy-start(f32[160,1,3,128]{3,1,2,0:T(1,128)} %param.13) | copy-start | bytes 737284
  6.5 76.9 %all-gather.2.cloned.1.call-start = ((), (), s32[]{:S(2)}) async-start(), calls=%async_computation.1 | async-start | bytes 4423680 | tf_op jit(solution)/shard_map/all_gather | solution.py:229
  10.3 39.0 %all-to-all-start = ((f32[512,1,128]{2,1,0:T(1,128)}), f32[512,1,128]{2,1,0:T(1,128)S(1)}, u32[]{:S(2)}, u32[]{:S(2)}) async-start(f32[512,1,128]{2,1,0:T(1,128)} %broadcast_in_dim.9), calls=%async_computation | async-start | bytes 524288 | tf_op jit(solution)/shard_map/all_to_all | solution.py:201
  50.9 2.9 %collective-permute-start = (bf16[160,384]{1,0:T(8,128)(2,1)S(1)}, bf16[160,384]{1,0:T(8,128)(2,1)S(1)}, u32[]{:S(2)}, u32[]{:S(2)}) collective-permute-start(bf16[160,384]{1,0:T(8,128)(2,1)S(1)} %fusion.15), channel_id=1, source_target_pairs={{0,0},{1,112},{16,16},{17,32},{32,17},{33,33},{48,65},{49,49},{64,... | collective-permute-start | bytes 368648 | tf_op jit(solution)/shard_map/ppermute | solution.py:212
  51.5 6.0 %collective-permute-start.1 = (bf16[160,384]{1,0:T(8,128)(2,1)S(1)}, bf16[160,384]{1,0:T(8,128)(2,1)S(1)}, u32[]{:S(2)}, u32[]{:S(2)}) collective-permute-start(bf16[160,384]{1,0:T(8,128)(2,1)S(1)} %fusion.15), channel_id=1, source_target_pairs={{0,256},{1,368},{16,272},{17,288},{32,273},{33,289},{48,321},{49,3... | collective-permute-start | bytes 368648 | tf_op jit(solution)/shard_map/ppermute | solution.py:212
  57.6 7.6 %collective-permute-start.2 = (bf16[2,160,384]{2,1,0:T(8,128)(2,1)S(1)}, bf16[2,160,384]{2,1,0:T(8,128)(2,1)S(1)}, u32[]{:S(2)}, u32[]{:S(2)}) collective-permute-start(bf16[2,160,384]{2,1,0:T(8,128)(2,1)S(1)} %get-tuple-element.46), channel_id=1, source_target_pairs={{0,128},{128,0},{1,129},{129,1},{2,130},{130,2},{3,131},{131,3},{4... | collective-permute-start | bytes 737288 | tf_op jit(solution)/shard_map/ppermute | solution.py:193
  65.2 18.2 %collective-permute-start.4 = (bf16[2,2,160,384]{3,2,1,0:T(8,128)(2,1)S(1)}, bf16[2,2,160,384]{3,2,1,0:T(8,128)(2,1)S(1)}, u32[]{:S(2)}, u32[]{:S(2)}) collective-permute-start(bf16[2,2,160,384]{3,2,1,0:T(8,128)(2,1)S(1)} %pad_maximum_fusion.refs_0_), channel_id=1, source_target_pairs={{0,16},{16,32},{32,48},{48,64},{64,80},{80,96},{96,112},{112,0},{1... | collective-permute-start | bytes 1474568 | tf_op jit(solution)/shard_map/ppermute | solution.py:217
  72.5 16.3 %collective-permute-start.3 = (bf16[2,2,160,384]{3,2,1,0:T(8,128)(2,1)S(1)}, bf16[2,2,160,384]{3,2,1,0:T(8,128)(2,1)S(1)}, u32[]{:S(2)}, u32[]{:S(2)}) collective-permute-start(bf16[2,2,160,384]{3,2,1,0:T(8,128)(2,1)S(1)} %pad_maximum_fusion.refs_0_), channel_id=1, source_target_pairs={{0,32},{16,48},{32,64},{48,80},{64,96},{80,112},{96,0},{112,16},{1... | collective-permute-start | bytes 1474568 | tf_op jit(solution)/shard_map/ppermute | solution.py:217
  83.5 5.3 %collective-permute-start.5 = (bf16[2,2,160,384]{3,2,1,0:T(8,128)(2,1)S(1)}, bf16[2,2,160,384]{3,2,1,0:T(8,128)(2,1)S(1)}, u32[]{:S(2)}, u32[]{:S(2)}) collective-permute-start(bf16[2,2,160,384]{3,2,1,0:T(8,128)(2,1)S(1)} %collective-permute-done.4.refs_1_), channel_id=1, source_target_pairs={{0,128},{128,0},{1,129},{129,1},{2,130},{130,2},{3,131},{131,3},{4... | collective-permute-start | bytes 1474568 | tf_op jit(solution)/shard_map/ppermute | solution.py:193
  85.4 2.1 %copy-start.1 = (bf16[2560,768]{1,0:T(8,128)(2,1)S(1)}, bf16[2560,768]{1,0:T(8,128)(2,1)}, u32[]{:S(2)}) copy-start(bf16[2560,768]{1,0:T(8,128)(2,1)} %all-gather.2.cloned.1.call-done.features_ref) | copy-start | bytes 11796484
  88.7 19.7 %collective-permute-start.6 = (bf16[2,2,160,384]{3,2,1,0:T(8,128)(2,1)S(1)}, bf16[2,2,160,384]{3,2,1,0:T(8,128)(2,1)}, u32[]{:S(2)}, u32[]{:S(2)}) collective-permute-start(bf16[2,2,160,384]{3,2,1,0:T(8,128)(2,1)S(1)} %collective-permute-done.3.refs_2_), channel_id=1, source_target_pairs={{0,16},{16,32},{32,48},{48,64},{64,80},{80,96},{96,112},{112,0},{1... | collective-permute-start | bytes 1474568 | tf_op jit(solution)/shard_map/ppermute | solution.py:217
  93.1 9.7 %collective-permute-start.7 = (f32[1,768]{1,0:T(1,128)S(1)}, f32[1,768]{1,0:T(1,128)S(1)}, u32[]{:S(2)}, u32[]{:S(2)}) collective-permute-start(f32[1,768]{1,0:T(1,128)S(1)} %squares.1.square_ref), channel_id=1, source_target_pairs={{0,1},{1,0},{2,3},{3,2},{4,5},{5,4},{6,7},{7,6},{8,9},{9,8},{10,11... | collective-permute-start | bytes 9224 | tf_op jit(solution)/shard_map/ppermute | solution.py:193
  96.6 13.8 %collective-permute-start.10 = (bf16[2,160,384]{2,1,0:T(8,128)(2,1)}, bf16[2,160,384]{2,1,0:T(8,128)(2,1)S(1)}, u32[]{:S(2)}, u32[]{:S(2)}) collective-permute-start(bf16[2,160,384]{2,1,0:T(8,128)(2,1)} %slice_bitcast_fusion), channel_id=1, source_target_pairs={{0,32},{16,48},{32,64},{48,80},{64,96},{80,112},{96,0},{112,16},{1... | collective-permute-start | bytes 737288 | tf_op jit(solution)/shard_map/ppermute | solution.py:217
  99.7 14.6 %collective-permute-start.8 = (bf16[2,2,160,384]{3,2,1,0:T(8,128)(2,1)S(1)}, bf16[2,2,160,384]{3,2,1,0:T(8,128)(2,1)}, u32[]{:S(2)}, u32[]{:S(2)}) collective-permute-start(bf16[2,2,160,384]{3,2,1,0:T(8,128)(2,1)S(1)} %collective-permute-done.3.refs_2_), channel_id=1, source_target_pairs={{0,128},{128,0},{1,129},{129,1},{2,130},{130,2},{3,131},{131,3},{4... | collective-permute-start | bytes 1474568 | tf_op jit(solution)/shard_map/ppermute | solution.py:193
  102.8 2.1 %copy-start.2 = (bf16[2560,768]{1,0:T(8,128)(2,1)S(1)}, bf16[2560,768]{1,0:T(8,128)(2,1)}, u32[]{:S(2)}) copy-start(bf16[2560,768]{1,0:T(8,128)(2,1)} %all-gather.2.cloned.1.call-done.features_ref) | copy-start | bytes 11796484
  106.6 1.9 %copy-start.3 = (bf16[2560,768]{1,0:T(8,128)(2,1)}, bf16[2560,768]{1,0:T(8,128)(2,1)S(1)}, u32[]{:S(2)}) copy-start(bf16[2560,768]{1,0:T(8,128)(2,1)S(1)} %normalise.1) | copy-start | bytes 11796484
  108.5 6.1 %collective-permute-start.9 = (bf16[2,2,160,384]{3,2,1,0:T(8,128)(2,1)}, bf16[2,2,160,384]{3,2,1,0:T(8,128)(2,1)S(1)}, u32[]{:S(2)}, u32[]{:S(2)}) collective-permute-start(bf16[2,2,160,384]{3,2,1,0:T(8,128)(2,1)} %collective-permute-done.6.refs_3_), channel_id=1, source_target_pairs={{0,128},{128,0},{1,129},{129,1},{2,130},{130,2},{3,131},{131,3},{4... | collective-permute-start | bytes 1474568 | tf_op jit(solution)/shard_map/ppermute | solution.py:193
  110.4 4.1 %collective-permute-start.11 = (bf16[2,160,384]{2,1,0:T(8,128)(2,1)S(1)}, bf16[2,160,384]{2,1,0:T(8,128)(2,1)S(1)}, u32[]{:S(2)}, u32[]{:S(2)}) collective-permute-start(bf16[2,160,384]{2,1,0:T(8,128)(2,1)S(1)} %collective-permute-done.10.refs_7_), channel_id=1, source_target_pairs={{0,128},{128,0},{1,129},{129,1},{2,130},{130,2},{3,131},{131,3},{4... | collective-permute-start | bytes 737288 | tf_op jit(solution)/shard_map/ppermute | solution.py:193
  113.4 3.1 %copy-start.4 = (bf16[2560,768]{1,0:T(8,128)(2,1)S(1)}, bf16[2560,768]{1,0:T(8,128)(2,1)}, u32[]{:S(2)}) copy-start(bf16[2560,768]{1,0:T(8,128)(2,1)} %copy-done.3) | copy-start | bytes 11796484
  118.1 16.7 %collective-permute-start.13 = (bf16[512,512]{1,0:T(8,128)(2,1)S(1)}, bf16[512,512]{1,0:T(8,128)(2,1)S(1)}, u32[]{:S(2)}, u32[]{:S(2)}) collective-permute-start(bf16[512,512]{1,0:T(8,128)(2,1)S(1)} %fusion.4), channel_id=1, source_target_pairs={{0,1},{1,0},{2,3},{3,2},{4,5},{5,4},{6,7},{7,6},{8,9},{9,8},{10,11... | collective-permute-start | bytes 1572872 | tf_op jit(solution)/shard_map/ppermute | solution.py:193
  123.8 10.9 %copy-start.5 = (f32[768,128]{1,0:T(8,128)S(1)}, f32[768,128]{1,0:T(8,128)}, u32[]{:S(2)}) copy-start(f32[768,128]{1,0:T(8,128)} %constant.62.clone.cos_ref) | copy-start | bytes 1179652
  123.8 10.9 %copy-start.6 = (f32[768,128]{1,0:T(8,128)S(1)}, f32[768,128]{1,0:T(8,128)}, u32[]{:S(2)}) copy-start(f32[768,128]{1,0:T(8,128)} %constant.63.clone.sin_ref) | copy-start | bytes 1179652
  123.9 10.9 %copy-start.7 = (f32[2,128]{1,0:T(2,128)S(1)}, f32[2,128]{1,0:T(2,128)}, u32[]{:S(2)}) copy-start(f32[2,128]{1,0:T(2,128)} %query_gain_ref.3) | copy-start | bytes 3076
  123.9 16.5 %collective-permute-start.12 = (bf16[256,512]{1,0:T(8,128)(2,1)S(1)}, bf16[256,512]{1,0:T(8,128)(2,1)S(1)}, u32[]{:S(2)}, u32[]{:S(2)}) collective-permute-start(bf16[256,512]{1,0:T(8,128)(2,1)S(1)} %convolution_convert_fusion), channel_id=1, source_target_pairs={{0,1},{1,0},{2,3},{3,2},{4,5},{5,4},{6,7},{7,6},{8,9},{9,8},{10,11... | collective-permute-start | bytes 786440 | tf_op jit(solution)/shard_map/ppermute | solution.py:193
Sparse Core Ops, SparseCore 0:
  9.4 66.8 all-gather.1

commit v11 on v10

--- a/solution.py
+++ b/solution.py
@@ -134,7 +134,7 @@
     return pl.pallas_call(
         functools.partial(normalise_kernel, width_all),
         grid_spec=grid_spec,
-        out_shape=jax.ShapeDtypeStruct(features.shape, jnp.bfloat16),
+        out_shape=pltpu.HBM(features.shape, jnp.bfloat16),
         compiler_params=pltpu.CompilerParams(vmem_limit_bytes=8 << 20),
         name="normalise",
     )(place, square, other, gain, features)
@@ -249,9 +249,10 @@
     first, gathered = lax.optimization_barrier((first, gathered))
     exchanged = [swap(first, "core")]
 
+    gathered = pltpu.with_memory_space_constraint(gathered, pltpu.HBM)
     square = squares(8, gathered)
-    second, square, exchanged[0] = lax.optimization_barrier((second, square, exchanged[0]))
     other_square = swap(square, "xh")
+    second, other_square, exchanged[0] = lax.optimization_barrier((second, other_square, exchanged[0]))
     place = (((((steps >> 1) & 1) ^ core) * 2 + ((steps >> 2) ^ xl)) * 2 + (steps & 1)).astype(jnp.int32)
     normed = normalise(float(width_all), 8, place, square, other_square, gain, gathered)
 

time: 150 us -> 156 us (1.040)
  Pallas kernels: 9.11 us -> 19 us
  local copies, waits for them, and re-layouts: 10.7 us -> 4.68 us
    unnamed x21 -> x15, local copies, waits for them, and re-layouts: 7.13 us -> 1.07 us
    pallas_call x1, Pallas kernels: 1.65 us -> 7.41 us  [normalise(): pl.pallas_call(functools.partial(normalise_kernel, width_all), grid_spec=...]
    pallas_call x1, Pallas kernels: 0.41 us -> 4.57 us  [squares(): pl.pallas_call(squares_kernel, grid=(parts,), out_shape=jax.ShapeDtypeStr...]
  transfers between devices with their start and end apart: 16 -> 16, of which waited for: 8 -> 8; matrix products, arithmetic and copies ran while one was open for 10% -> 9% of each run, Pallas kernels for 3% -> 10%
where the time goes in v11:
time: 156 us; the launch traced here: 154 us
  starting transfers between devices  68.3 us (44%)
  waiting for transfers between devices  35.9 us (23%)
  Pallas kernels  19 us (12%)
  between operations  15.3 us (10%)
  other arithmetic  6.53 us (4%)
  matrix products  4.79 us (3%)
  local copies, waits for them, and re-layouts  4.68 us (3%)
    ppermute x8, starting transfers between devices, swap(): return lax.ppermute(array, axis, [(0, 1), (1, 0)])  27.6 us
    all_to_all x1, starting transfers between devices, global_sum(): return jnp.sum(lax.all_to_all(spread, AXES, 0, 0, tiled=True)[:, 0])  22.2 us
    ppermute x4, starting transfers between devices, onward(): return lax.ppermute(block, ('core', 'y'), pairs)  15.6 us
    ppermute x8, waiting for transfers between devices, swap(): return lax.ppermute(array, axis, [(0, 1), (1, 0)])  11.4 us
    all_to_all x1, waiting for transfers between devices, global_sum(): return jnp.sum(lax.all_to_all(spread, AXES, 0, 0, tiled=True)[:, 0])  10.8 us
    ppermute x4, waiting for transfers between devices, onward(): return lax.ppermute(block, ('core', 'y'), pairs)  9.1 us
    pallas_call x1, Pallas kernels, normalise(): pl.pallas_call(functools.partial(normalise_kernel, width_all), grid_spec=...  7.41 us
    pallas_call x2, Pallas kernels, attend(): return call(limit, own, got, query_gain, key_gain, *tables, *before)  5.08 us
  transfers between devices with their start and end apart: 16, of which 8 were waited for; matrix products, arithmetic and copies ran while one was open for 9% of the time, Pallas kernels for 10%

profile of v11, /device:TPU:1, one launch (start us, length us, event | category | flops | bytes accessed | tf_op | source)
XLA Modules:
  0.0 154.5 jit_solution(9091491911217509585)
XLA Ops:
  6.5 0.7 all-gather.2.cloned.1.call-update
  7.3 1.6 %multiply_reduce_fusion = f32[]{:T(128)} fusion(bf16[160,1,3,128]{3,0,2,1:T(8,128)(2,1)} %param.14), kind=kLoop, calls=%fused_computation.22 | loop fusion | flops 184319 | bytes 122884 | tf_op jit(solution)/shard_map/reduce_sum | solution.py:232
  8.9 1.5 broadcast_in_dim.9
  10.3 22.2 %all-to-all-start = ((f32[512,1,128]{2,1,0:T(1,128)}), f32[512,1,128]{2,1,0:T(1,128)S(1)}, u32[]{:S(2)}, u32[]{:S(2)}) async-start(f32[512,1,128]{2,1,0:T(1,128)} %broadcast_in_dim.9), calls=%async_computation | async-start | bytes 524288 | tf_op jit(solution)/shard_map/all_to_all | solution.py:201
  32.5 1.0 copy.18
  33.5 0.8 reshape.96
  34.4 0.1 reshape.97
  34.4 1.6 %reduce.4 = f32[160,3,128]{2,1,0:T(4,128)S(1)} reduce(f32[160,1,3,128]{3,1,2,0:T(1,128)} %param.16, f32[]{:T(128)} %constant.70), dimensions={1}, to_apply=%param.16.reduce_sub_computation | reduce | bytes 491524 | tf_op args[5]
  36.1 1.6 %reduce.3 = f32[160,3,128]{2,1,0:T(4,128)S(1)} reduce(f32[160,1,3,128]{3,1,2,0:T(1,128)} %param.15, f32[]{:T(128)} %constant.70), dimensions={1}, to_apply=%param.15.reduce_sub_computation | reduce | bytes 491524 | tf_op args[4]
  37.7 0.7 reduce.2
  38.5 10.8 %all-to-all-done = f32[512,1,128]{2,1,0:T(1,128)S(1)} async-done(((f32[512,1,128]{2,1,0:T(1,128)}), f32[512,1,128]{2,1,0:T(1,128)S(1)}, u32[]{:S(2)}, u32[]{:S(2)}) %all-to-all-start) | async-done | bytes 262176 | tf_op jit(solution)/shard_map/all_to_all | solution.py:201
  49.3 0.7 slice_reduce_fusion
  50.7 0.2 fusion.15
  50.9 0.7 collective-permute-start
  51.6 2.2 %collective-permute-start.1 = (bf16[160,384]{1,0:T(8,128)(2,1)S(1)}, bf16[160,384]{1,0:T(8,128)(2,1)S(1)}, u32[]{:S(2)}, u32[]{:S(2)}) collective-permute-start(bf16[160,384]{1,0:T(8,128)(2,1)S(1)} %fusion.15), channel_id=1, source_target_pairs={{0,256},{1,368},{16,272},{17,288},{32,273},{33,289},{48,321},{49,3... | collective-permute-start | bytes 368648 | tf_op jit(solution)/shard_map/ppermute | solution.py:212
  53.8 3.8 %collective-permute-done.1 = bf16[160,384]{1,0:T(8,128)(2,1)S(1)} collective-permute-done((bf16[160,384]{1,0:T(8,128)(2,1)S(1)}, bf16[160,384]{1,0:T(8,128)(2,1)S(1)}, u32[]{:S(2)}, u32[]{:S(2)}) %collective-permute-start.1) | collective-permute-done | bytes 122912 | tf_op jit(solution)/shard_map/ppermute | solution.py:212
  57.6 6.4 %collective-permute-start.2 = (bf16[2,160,384]{2,1,0:T(8,128)(2,1)S(1)}, bf16[2,160,384]{2,1,0:T(8,128)(2,1)S(1)}, u32[]{:S(2)}, u32[]{:S(2)}) collective-permute-start(bf16[2,160,384]{2,1,0:T(8,128)(2,1)S(1)} %get-tuple-element.46), channel_id=1, source_target_pairs={{0,128},{128,0},{1,129},{129,1},{2,130},{130,2},{3,131},{131,3},{4... | collective-permute-start | bytes 737288 | tf_op jit(solution)/shard_map/ppermute | solution.py:193
  64.1 1.1 collective-permute-done.2
  65.2 0.1 pad_maximum_fusion.refs_0_
  65.3 7.2 %collective-permute-start.4 = (bf16[2,2,160,384]{3,2,1,0:T(8,128)(2,1)S(1)}, bf16[2,2,160,384]{3,2,1,0:T(8,128)(2,1)S(1)}, u32[]{:S(2)}, u32[]{:S(2)}) collective-permute-start(bf16[2,2,160,384]{3,2,1,0:T(8,128)(2,1)S(1)} %pad_maximum_fusion.refs_0_), channel_id=1, source_target_pairs={{0,16},{16,32},{32,48},{48,64},{64,80},{80,96},{96,112},{112,0},{1... | collective-permute-start | bytes 1474568 | tf_op jit(solution)/shard_map/ppermute | solution.py:217
  72.5 1.9 %collective-permute-start.3 = (bf16[2,2,160,384]{3,2,1,0:T(8,128)(2,1)S(1)}, bf16[2,2,160,384]{3,2,1,0:T(8,128)(2,1)S(1)}, u32[]{:S(2)}, u32[]{:S(2)}) collective-permute-start(bf16[2,2,160,384]{3,2,1,0:T(8,128)(2,1)S(1)} %pad_maximum_fusion.refs_0_), channel_id=1, source_target_pairs={{0,32},{16,48},{32,64},{48,80},{64,96},{80,112},{96,0},{112,16},{1... | collective-permute-start | bytes 1474568 | tf_op jit(solution)/shard_map/ppermute | solution.py:217
  74.4 9.1 %collective-permute-done.4.refs_1_ = bf16[2,2,160,384]{3,2,1,0:T(8,128)(2,1)S(1)} collective-permute-done((bf16[2,2,160,384]{3,2,1,0:T(8,128)(2,1)S(1)}, bf16[2,2,160,384]{3,2,1,0:T(8,128)(2,1)S(1)}, u32[]{:S(2)}, u32[]{:S(2)}) %collective-permute-start.4) | collective-permute-done | bytes 491552 | tf_op jit(solution)/shard_map/ppermute | solution.py:217
  83.5 1.9 %collective-permute-start.6 = (bf16[2,2,160,384]{3,2,1,0:T(8,128)(2,1)S(1)}, bf16[2,2,160,384]{3,2,1,0:T(8,128)(2,1)S(1)}, u32[]{:S(2)}, u32[]{:S(2)}) collective-permute-start(bf16[2,2,160,384]{3,2,1,0:T(8,128)(2,1)S(1)} %collective-permute-done.4.refs_1_), channel_id=1, source_target_pairs={{0,128},{128,0},{1,129},{129,1},{2,130},{130,2},{3,131},{131,3},{4... | collective-permute-start | bytes 1474568 | tf_op jit(solution)/shard_map/ppermute | solution.py:193
  85.4 4.6 %squares.1.square_ref = f32[1,768]{1,0:T(1,128)S(1)} custom-call(bf16[2560,768]{1,0:T(8,128)(2,1)} %all-gather.2.cloned.1.call-done.features_ref), custom_call_target="tpu_custom_call" | custom-call | tf_op jit(solution)/shard_map/squares/pallas_call | solution.py:103
  90.0 5.4 %collective-permute-start.5 = (f32[1,768]{1,0:T(1,128)S(1)}, f32[1,768]{1,0:T(1,128)S(1)}, u32[]{:S(2)}, u32[]{:S(2)}) collective-permute-start(f32[1,768]{1,0:T(1,128)S(1)} %squares.1.square_ref), channel_id=1, source_target_pairs={{0,1},{1,0},{2,3},{3,2},{4,5},{5,4},{6,7},{7,6},{8,9},{9,8},{10,11... | collective-permute-start | bytes 9224 | tf_op jit(solution)/shard_map/ppermute | solution.py:193
  95.4 1.0 collective-permute-done.5.other_ref
  96.4 4.6 %collective-permute-start.7 = (bf16[2,2,160,384]{3,2,1,0:T(8,128)(2,1)S(1)}, bf16[2,2,160,384]{3,2,1,0:T(8,128)(2,1)}, u32[]{:S(2)}, u32[]{:S(2)}) collective-permute-start(bf16[2,2,160,384]{3,2,1,0:T(8,128)(2,1)S(1)} %collective-permute-done.3.refs_2_), channel_id=1, source_target_pairs={{0,16},{16,32},{32,48},{48,64},{64,80},{80,96},{96,112},{112,0},{1... | collective-permute-start | bytes 1474568 | tf_op jit(solution)/shard_map/ppermute | solution.py:217
  101.0 0.7 slice_bitcast_fusion
  101.7 1.9 %collective-permute-start.10 = (bf16[2,160,384]{2,1,0:T(8,128)(2,1)}, bf16[2,160,384]{2,1,0:T(8,128)(2,1)S(1)}, u32[]{:S(2)}, u32[]{:S(2)}) collective-permute-start(bf16[2,160,384]{2,1,0:T(8,128)(2,1)} %slice_bitcast_fusion), channel_id=1, source_target_pairs={{0,32},{16,48},{32,64},{48,80},{64,96},{80,112},{96,0},{112,16},{1... | collective-permute-start | bytes 737288 | tf_op jit(solution)/shard_map/ppermute | solution.py:217
  103.7 0.4 copy.19.gain_ref
  104.1 1.9 %collective-permute-start.8 = (bf16[2,2,160,384]{3,2,1,0:T(8,128)(2,1)S(1)}, bf16[2,2,160,384]{3,2,1,0:T(8,128)(2,1)}, u32[]{:S(2)}, u32[]{:S(2)}) collective-permute-start(bf16[2,2,160,384]{3,2,1,0:T(8,128)(2,1)S(1)} %collective-permute-done.3.refs_2_), channel_id=1, source_target_pairs={{0,128},{128,0},{1,129},{129,1},{2,130},{130,2},{3,131},{131,3},{4... | collective-permute-start | bytes 1474568 | tf_op jit(solution)/shard_map/ppermute | solution.py:193
  106.0 7.4 %normalise.1 = bf16[2560,768]{1,0:T(8,128)(2,1)} custom-call(s32[8]{0:T(128)S(1)} %and_add_fusion.1.place_ref, f32[1,768]{1,0:T(1,128)S(1)} %squares.1.square_ref, f32[1,768]{1,0:T(1,128)S(1)} %collective-permute-done.5.other_ref, f32[2560,1]{1,0:T(8,128)S(1)} %copy.19.gain_ref, bf16[2560,768]{1,0:T(8,128)(2,1)} %all-gather.2.cloned.1.call-done.features_ref), custom_call_target="tpu_custom_call" | custom-call | tf_op jit(solution)/shard_map/normalise/pallas_call | solution.py:134
  113.4 2.4 %collective-permute-start.9 = (bf16[2,2,160,384]{3,2,1,0:T(8,128)(2,1)}, bf16[2,2,160,384]{3,2,1,0:T(8,128)(2,1)S(1)}, u32[]{:S(2)}, u32[]{:S(2)}) collective-permute-start(bf16[2,2,160,384]{3,2,1,0:T(8,128)(2,1)} %collective-permute-done.7.refs_3_), channel_id=1, source_target_pairs={{0,128},{128,0},{1,129},{129,1},{2,130},{130,2},{3,131},{131,3},{4... | collective-permute-start | bytes 1474568 | tf_op jit(solution)/shard_map/ppermute | solution.py:193
  115.9 2.5 %collective-permute-start.11 = (bf16[2,160,384]{2,1,0:T(8,128)(2,1)S(1)}, bf16[2,160,384]{2,1,0:T(8,128)(2,1)S(1)}, u32[]{:S(2)}, u32[]{:S(2)}) collective-permute-start(bf16[2,160,384]{2,1,0:T(8,128)(2,1)S(1)} %collective-permute-done.10.refs_7_), channel_id=1, source_target_pairs={{0,128},{128,0},{1,129},{129,1},{2,130},{130,2},{3,131},{131,3},{4... | collective-permute-start | bytes 737288 | tf_op jit(solution)/shard_map/ppermute | solution.py:193
  119.2 0.2 collective-permute-done.11.refs_8_
  119.5 2.0 %assemble.1 = (bf16[2560,512]{1,0:T(8,128)(2,1)S(1)}, bf16[2560,512]{1,0:T(8,128)(2,1)S(1)}) custom-call(s32[3,8]{1,0:T(4,128)S(1)} %pad_add_fusion.place_ref, bf16[2,2,160,384]{3,2,1,0:T(8,128)(2,1)S(1)} %pad_maximum_fusion.refs_0_, bf16[2,2,160,384]{3,2,1,0:T(8,128)(2,1)S(1)} %collective-permute-done.4.refs_1_, ...), custom_call_target="tpu_custom_call" | custom-call | tf_op jit(solution)/shard_map/assemble/pallas_call | solution.py:85
  121.5 1.5 fusion.4
  123.0 2.8 %collective-permute-start.13 = (bf16[512,512]{1,0:T(8,128)(2,1)S(1)}, bf16[512,512]{1,0:T(8,128)(2,1)S(1)}, u32[]{:S(2)}, u32[]{:S(2)}) collective-permute-start(bf16[512,512]{1,0:T(8,128)(2,1)S(1)} %fusion.4), channel_id=1, source_target_pairs={{0,1},{1,0},{2,3},{3,2},{4,5},{5,4},{6,7},{7,6},{8,9},{9,8},{10,11... | collective-permute-start | bytes 1572872 | tf_op jit(solution)/shard_map/ppermute | solution.py:193
  125.9 1.5 fusion.2.own_ref
  127.4 0.9 convolution_convert_fusion
  128.3 0.0 copy-start.1
  128.3 0.0 copy-start.2
  128.3 4.2 %collective-permute-start.12 = (bf16[256,512]{1,0:T(8,128)(2,1)S(1)}, bf16[256,512]{1,0:T(8,128)(2,1)S(1)}, u32[]{:S(2)}, u32[]{:S(2)}) collective-permute-start(bf16[256,512]{1,0:T(8,128)(2,1)S(1)} %convolution_convert_fusion), channel_id=1, source_target_pairs={{0,1},{1,0},{2,3},{3,2},{4,5},{5,4},{6,7},{7,6},{8,9},{9,8},{10,11... | collective-permute-start | bytes 786440 | tf_op jit(solution)/shard_map/ppermute | solution.py:193
  132.6 0.9 fusion.8.own_ref
  133.4 6.2 %collective-permute-done.13.got_ref = bf16[512,512]{1,0:T(8,128)(2,1)S(1)} collective-permute-done((bf16[512,512]{1,0:T(8,128)(2,1)S(1)}, bf16[512,512]{1,0:T(8,128)(2,1)S(1)}, u32[]{:S(2)}, u32[]{:S(2)}) %collective-permute-start.13) | collective-permute-done | bytes 524320 | tf_op jit(solution)/shard_map/ppermute | solution.py:193
  139.7 2.7 %attend.2 = (bf16[512,256]{1,0:T(8,128)(2,1)S(1)}, bf16[512,128]{1,0:T(8,128)(2,1)S(1)}, bf16[512,128]{1,0:T(8,128)(2,1)S(1)}) custom-call(s32[1]{0:T(128)S(6)} %copy.31.limit_ref, f32[512,512]{1,0:T(8,128)S(1)} %fusion.2.own_ref, bf16[512,512]{1,0:T(8,128)(2,1)S(1)} %collective-permute-done.13.got_ref, f32[2,128]{1,0:T(2,128)S(1)} %copy-done.3, ...), custom_call_target="tpu_custom_call" | custom-call | tf_op jit(solution)/shard_map/attend/pallas_call | solution.py:189
  142.4 2.9 %collective-permute-done.12.got_ref = bf16[256,512]{1,0:T(8,128)(2,1)S(1)} collective-permute-done((bf16[256,512]{1,0:T(8,128)(2,1)S(1)}, bf16[256,512]{1,0:T(8,128)(2,1)S(1)}, u32[]{:S(2)}, u32[]{:S(2)}) %collective-permute-start.12) | collective-permute-done | bytes 262176 | tf_op jit(solution)/shard_map/ppermute | solution.py:193
  145.3 2.3 %attend.3 = (bf16[768,256]{1,0:T(8,128)(2,1)}, bf16[768,128]{1,0:T(8,128)(2,1)}, bf16[768,128]{1,0:T(8,128)(2,1)}) custom-call(s32[1]{0:T(128)S(6)} %copy.31.limit_ref, f32[256,512]{1,0:T(8,128)S(1)} %fusion.8.own_ref, bf16[256,512]{1,0:T(8,128)(2,1)S(1)} %collective-permute-done.12.got_ref, f32[2,128]{1,0:T(2,128)S(1)} %copy-done.3, ...), custom_call_target="tpu_custom_call" | custom-call | tf_op jit(solution)/shard_map/attend/pallas_call | solution.py:189
  (29 shorter events, 0.3 us)
Async XLA Ops:
  6.5 111.8 %copy-start = (f32[8,128]{1,0:T(8,128)S(1)}, f32[8,128]{1,0:T(8,128)}, u32[]{:S(2)}) copy-start(f32[8,128]{1,0:T(8,128)} %param.18) | copy-start | bytes 12292
  6.5 31.1 %copy-start.5 = (f32[160,1,3,128]{3,1,2,0:T(1,128)S(1)}, f32[160,1,3,128]{3,1,2,0:T(1,128)}, u32[]{:S(2)}) copy-start(f32[160,1,3,128]{3,1,2,0:T(1,128)} %param.13) | copy-start | bytes 737284
  6.5 77.0 %all-gather.2.cloned.1.call-start = ((), (), s32[]{:S(2)}) async-start(), calls=%async_computation.1 | async-start | bytes 4423680 | tf_op jit(solution)/shard_map/all_gather | solution.py:229
  10.3 39.0 %all-to-all-start = ((f32[512,1,128]{2,1,0:T(1,128)}), f32[512,1,128]{2,1,0:T(1,128)S(1)}, u32[]{:S(2)}, u32[]{:S(2)}) async-start(f32[512,1,128]{2,1,0:T(1,128)} %broadcast_in_dim.9), calls=%async_computation | async-start | bytes 524288 | tf_op jit(solution)/shard_map/all_to_all | solution.py:201
  50.9 2.9 %collective-permute-start = (bf16[160,384]{1,0:T(8,128)(2,1)S(1)}, bf16[160,384]{1,0:T(8,128)(2,1)S(1)}, u32[]{:S(2)}, u32[]{:S(2)}) collective-permute-start(bf16[160,384]{1,0:T(8,128)(2,1)S(1)} %fusion.15), channel_id=1, source_target_pairs={{0,0},{1,112},{16,16},{17,32},{32,17},{33,33},{48,65},{49,49},{64,... | collective-permute-start | bytes 368648 | tf_op jit(solution)/shard_map/ppermute | solution.py:212
  51.6 6.0 %collective-permute-start.1 = (bf16[160,384]{1,0:T(8,128)(2,1)S(1)}, bf16[160,384]{1,0:T(8,128)(2,1)S(1)}, u32[]{:S(2)}, u32[]{:S(2)}) collective-permute-start(bf16[160,384]{1,0:T(8,128)(2,1)S(1)} %fusion.15), channel_id=1, source_target_pairs={{0,256},{1,368},{16,272},{17,288},{32,273},{33,289},{48,321},{49,3... | collective-permute-start | bytes 368648 | tf_op jit(solution)/shard_map/ppermute | solution.py:212
  57.6 7.6 %collective-permute-start.2 = (bf16[2,160,384]{2,1,0:T(8,128)(2,1)S(1)}, bf16[2,160,384]{2,1,0:T(8,128)(2,1)S(1)}, u32[]{:S(2)}, u32[]{:S(2)}) collective-permute-start(bf16[2,160,384]{2,1,0:T(8,128)(2,1)S(1)} %get-tuple-element.46), channel_id=1, source_target_pairs={{0,128},{128,0},{1,129},{129,1},{2,130},{130,2},{3,131},{131,3},{4... | collective-permute-start | bytes 737288 | tf_op jit(solution)/shard_map/ppermute | solution.py:193
  65.3 18.2 %collective-permute-start.4 = (bf16[2,2,160,384]{3,2,1,0:T(8,128)(2,1)S(1)}, bf16[2,2,160,384]{3,2,1,0:T(8,128)(2,1)S(1)}, u32[]{:S(2)}, u32[]{:S(2)}) collective-permute-start(bf16[2,2,160,384]{3,2,1,0:T(8,128)(2,1)S(1)} %pad_maximum_fusion.refs_0_), channel_id=1, source_target_pairs={{0,16},{16,32},{32,48},{48,64},{64,80},{80,96},{96,112},{112,0},{1... | collective-permute-start | bytes 1474568 | tf_op jit(solution)/shard_map/ppermute | solution.py:217
  72.5 22.9 %collective-permute-start.3 = (bf16[2,2,160,384]{3,2,1,0:T(8,128)(2,1)S(1)}, bf16[2,2,160,384]{3,2,1,0:T(8,128)(2,1)S(1)}, u32[]{:S(2)}, u32[]{:S(2)}) collective-permute-start(bf16[2,2,160,384]{3,2,1,0:T(8,128)(2,1)S(1)} %pad_maximum_fusion.refs_0_), channel_id=1, source_target_pairs={{0,32},{16,48},{32,64},{48,80},{64,96},{80,112},{96,0},{112,16},{1... | collective-permute-start | bytes 1474568 | tf_op jit(solution)/shard_map/ppermute | solution.py:217
  83.5 12.9 %collective-permute-start.6 = (bf16[2,2,160,384]{3,2,1,0:T(8,128)(2,1)S(1)}, bf16[2,2,160,384]{3,2,1,0:T(8,128)(2,1)S(1)}, u32[]{:S(2)}, u32[]{:S(2)}) collective-permute-start(bf16[2,2,160,384]{3,2,1,0:T(8,128)(2,1)S(1)} %collective-permute-done.4.refs_1_), channel_id=1, source_target_pairs={{0,128},{128,0},{1,129},{129,1},{2,130},{130,2},{3,131},{131,3},{4... | collective-permute-start | bytes 1474568 | tf_op jit(solution)/shard_map/ppermute | solution.py:193
  90.0 6.4 %collective-permute-start.5 = (f32[1,768]{1,0:T(1,128)S(1)}, f32[1,768]{1,0:T(1,128)S(1)}, u32[]{:S(2)}, u32[]{:S(2)}) collective-permute-start(f32[1,768]{1,0:T(1,128)S(1)} %squares.1.square_ref), channel_id=1, source_target_pairs={{0,1},{1,0},{2,3},{3,2},{4,5},{5,4},{6,7},{7,6},{8,9},{9,8},{10,11... | collective-permute-start | bytes 9224 | tf_op jit(solution)/shard_map/ppermute | solution.py:193
  96.4 17.1 %collective-permute-start.7 = (bf16[2,2,160,384]{3,2,1,0:T(8,128)(2,1)S(1)}, bf16[2,2,160,384]{3,2,1,0:T(8,128)(2,1)}, u32[]{:S(2)}, u32[]{:S(2)}) collective-permute-start(bf16[2,2,160,384]{3,2,1,0:T(8,128)(2,1)S(1)} %collective-permute-done.3.refs_2_), channel_id=1, source_target_pairs={{0,16},{16,32},{32,48},{48,64},{64,80},{80,96},{96,112},{112,0},{1... | collective-permute-start | bytes 1474568 | tf_op jit(solution)/shard_map/ppermute | solution.py:217
  101.7 14.1 %collective-permute-start.10 = (bf16[2,160,384]{2,1,0:T(8,128)(2,1)}, bf16[2,160,384]{2,1,0:T(8,128)(2,1)S(1)}, u32[]{:S(2)}, u32[]{:S(2)}) collective-permute-start(bf16[2,160,384]{2,1,0:T(8,128)(2,1)} %slice_bitcast_fusion), channel_id=1, source_target_pairs={{0,32},{16,48},{32,64},{48,80},{64,96},{80,112},{96,0},{112,16},{1... | collective-permute-start | bytes 737288 | tf_op jit(solution)/shard_map/ppermute | solution.py:217
  104.1 15.1 %collective-permute-start.8 = (bf16[2,2,160,384]{3,2,1,0:T(8,128)(2,1)S(1)}, bf16[2,2,160,384]{3,2,1,0:T(8,128)(2,1)}, u32[]{:S(2)}, u32[]{:S(2)}) collective-permute-start(bf16[2,2,160,384]{3,2,1,0:T(8,128)(2,1)S(1)} %collective-permute-done.3.refs_2_), channel_id=1, source_target_pairs={{0,128},{128,0},{1,129},{129,1},{2,130},{130,2},{3,131},{131,3},{4... | collective-permute-start | bytes 1474568 | tf_op jit(solution)/shard_map/ppermute | solution.py:193
  113.4 6.0 %collective-permute-start.9 = (bf16[2,2,160,384]{3,2,1,0:T(8,128)(2,1)}, bf16[2,2,160,384]{3,2,1,0:T(8,128)(2,1)S(1)}, u32[]{:S(2)}, u32[]{:S(2)}) collective-permute-start(bf16[2,2,160,384]{3,2,1,0:T(8,128)(2,1)} %collective-permute-done.7.refs_3_), channel_id=1, source_target_pairs={{0,128},{128,0},{1,129},{129,1},{2,130},{130,2},{3,131},{131,3},{4... | collective-permute-start | bytes 1474568 | tf_op jit(solution)/shard_map/ppermute | solution.py:193
  115.9 3.6 %collective-permute-start.11 = (bf16[2,160,384]{2,1,0:T(8,128)(2,1)S(1)}, bf16[2,160,384]{2,1,0:T(8,128)(2,1)S(1)}, u32[]{:S(2)}, u32[]{:S(2)}) collective-permute-start(bf16[2,160,384]{2,1,0:T(8,128)(2,1)S(1)} %collective-permute-done.10.refs_7_), channel_id=1, source_target_pairs={{0,128},{128,0},{1,129},{129,1},{2,130},{130,2},{3,131},{131,3},{4... | collective-permute-start | bytes 737288 | tf_op jit(solution)/shard_map/ppermute | solution.py:193
  118.4 3.1 %copy-start.4 = (bf16[2560,768]{1,0:T(8,128)(2,1)S(1)}, bf16[2560,768]{1,0:T(8,128)(2,1)}, u32[]{:S(2)}) copy-start(bf16[2560,768]{1,0:T(8,128)(2,1)} %normalise.1) | copy-start | bytes 11796484
  123.0 16.7 %collective-permute-start.13 = (bf16[512,512]{1,0:T(8,128)(2,1)S(1)}, bf16[512,512]{1,0:T(8,128)(2,1)S(1)}, u32[]{:S(2)}, u32[]{:S(2)}) collective-permute-start(bf16[512,512]{1,0:T(8,128)(2,1)S(1)} %fusion.4), channel_id=1, source_target_pairs={{0,1},{1,0},{2,3},{3,2},{4,5},{5,4},{6,7},{7,6},{8,9},{9,8},{10,11... | collective-permute-start | bytes 1572872 | tf_op jit(solution)/shard_map/ppermute | solution.py:193
  128.3 11.4 %copy-start.1 = (f32[768,128]{1,0:T(8,128)S(1)}, f32[768,128]{1,0:T(8,128)}, u32[]{:S(2)}) copy-start(f32[768,128]{1,0:T(8,128)} %constant.62.clone.cos_ref) | copy-start | bytes 1179652
  128.3 11.4 %copy-start.2 = (f32[768,128]{1,0:T(8,128)S(1)}, f32[768,128]{1,0:T(8,128)}, u32[]{:S(2)}) copy-start(f32[768,128]{1,0:T(8,128)} %constant.63.clone.sin_ref) | copy-start | bytes 1179652
  128.3 11.4 %copy-start.3 = (f32[2,128]{1,0:T(2,128)S(1)}, f32[2,128]{1,0:T(2,128)}, u32[]{:S(2)}) copy-start(f32[2,128]{1,0:T(2,128)} %query_gain_ref.3) | copy-start | bytes 3076
  128.3 17.0 %collective-permute-start.12 = (bf16[256,512]{1,0:T(8,128)(2,1)S(1)}, bf16[256,512]{1,0:T(8,128)(2,1)S(1)}, u32[]{:S(2)}, u32[]{:S(2)}) collective-permute-start(bf16[256,512]{1,0:T(8,128)(2,1)S(1)} %convolution_convert_fusion), channel_id=1, source_target_pairs={{0,1},{1,0},{2,3},{3,2},{4,5},{5,4},{6,7},{7,6},{8,9},{9,8},{10,11... | collective-permute-start | bytes 786440 | tf_op jit(solution)/shard_map/ppermute | solution.py:193
Sparse Core Ops, SparseCore 0:
  9.4 66.8 all-gather.1
